TPU v7x, 512 devices: a whole 4x4x16 slice. The times are simulated.
512 devices in a mesh: row: 8 (over y, core), col: 16 (over z_lo, x), layer: 4 (over z_hi).
Axes of the slice: x: 4, y: 4, z: 16 (z_hi: 4, z_lo: 4; z = z_hi * 4 + z_lo), core: 2. Of those that a mesh axis runs over, the one named last changes fastest.
Arguments:
- panel: bfloat16 [8192, 4, 4096], P('row', 'layer', 'col'), may hold values from -6 to 6
- in_pattern: int32 [64, 4, 32], P('row', 'layer', 'col'), may hold values 0 or 1
- slab: bfloat16 [4, 32, 128, 8192], P('layer', 'row', None, 'col'), may hold values from -0.046875 to 0.046875
- owner: int32 [4, 32], P('layer'), may hold values from 0 to 31, each once within a row
- out_pattern: int32 [64, 64], P(('row', 'layer'), 'col'), may hold values 0 or 1
Outputs:
- product: bfloat16 [8192, 8192], P(('row', 'layer'), 'col')
Inputs may be any that keep to these rules, and one draw needn't show every extreme that they name: `owner`: each row lists every number of 0 to 31 once.
All inputs are finite; a program needn't handle non-finite values. No bound on the sum of `in_pattern` or of `out_pattern` on one device may be relied on, other than what follows from the above.
Results may differ from a plain program's by a relative error of at most 0.001.
Values may be sent and summed in bfloat16 or wider, within the bound.
No kernel may reach another device: no remote copies, remote signals or barrier semaphores. Data moves between devices by JAX's collectives and lax.ppermute only.
A program may use at most 64 MiB of HBM per device.

v0:
```python
import jax
import jax.numpy as jnp
from jax import lax
from jax.sharding import PartitionSpec as P


def shards(panel, in_pattern, slab, owner, out_pattern):
    block_size = slab.shape[2]
    slab_cols = slab.shape[3]
    panel_rows = panel.shape[0]
    local_blocks = in_pattern.shape[2]
    shaped = panel.reshape(in_pattern.shape[0], block_size, 1, local_blocks, block_size)
    keeper = in_pattern.astype(jnp.bfloat16)[:, None, :, :, None]
    masked = (shaped * keeper).reshape(panel_rows, 1, local_blocks * block_size)
    mapping = owner[0]
    range_rows = lax.all_gather(slab, "row", axis=1, tiled=True)[0]
    portion = lax.all_gather(masked, "col", axis=2, tiled=True)
    amount = portion.shape[2] // block_size
    operand = jnp.take(range_rows, mapping, axis=0).reshape(amount * block_size, slab_cols)
    summed = jnp.dot(portion[:, 0, :], operand, preferred_element_type=jnp.float32)
    reduced = lax.psum_scatter(summed, "layer", scatter_dimension=0, tiled=True)
    out_rows = out_pattern.shape[0]
    out_cols = out_pattern.shape[1]
    blocked = reduced.reshape(out_rows, block_size, out_cols, block_size)
    blocked = blocked * out_pattern.astype(jnp.float32)[:, None, :, None]
    return blocked.reshape(out_rows * block_size, out_cols * block_size).astype(jnp.bfloat16)


def solution(mesh):
    in_specs = (
        P("row", "layer", "col"),
        P("row", "layer", "col"),
        P("layer", "row", None, "col"),
        P("layer", None),
        P(("row", "layer"), "col"),
    )
    out_specs = P(("row", "layer"), "col")
    return jax.shard_map(shards, mesh=mesh, in_specs=in_specs, out_specs=out_specs, check_vma=False)
```

profile of v0, /device:TPU:1, one launch (start us, length us, event | category | flops | bytes accessed | tf_op | source)
XLA Modules:
  0.0 299.8 jit_solution(10978592648681757918)
XLA Ops:
  6.5 0.0 copy-start.1
  6.5 0.0 all-gather.5.cloned.1.call-start
  6.5 0.7 all-gather.5.cloned.1.call-update
  7.3 0.0 all-gather.3.cloned.1.call-start
  7.3 0.7 convert_bitcast_fusion
  8.0 0.1 copy.7
  8.1 0.3 mul.27
  8.4 0.3 mul.28
  8.8 2.0 mul.29
  10.8 0.0 all-gather.3.cloned.1.call-update
  10.8 0.0 reduce-scatter.2.cloned.1.call-start
  10.8 0.0 copy-done.1
  10.9 44.2 %all-gather.5.cloned.1.call-done = bf16[1,32,128,512]{3,2,0,1:T(8,128)(2,1)} async-done(((bf16[1,4,128,512]{3,2,0,1:T(8,128)(2,1)}), bf16[1,32,128,512]{3,2,0,1:T(8,128)(2,1)}) %all-gather.5.cloned.1.call-update) | async-done | bytes 4194320 | tf_op jit(solution)/shard_map/all_gather | solution.py:16
  55.1 4.9 %gather_fusion = bf16[32,128,512]{2,1,0:T(8,128)(2,1)} fusion(bf16[32,128,512]{2,1,0:T(8,128)(2,1)} %bitcast.21, s32[1024]{0:T(1024)S(1)} %pad_clamp_fusion), kind=kCustom, calls=%fused_computation | custom fusion | bytes 8388736 | tf_op jit(solution)/shard_map/jit(_take)/gather | solution.py:19
  60.0 4.6 %broadcast_select_fusion = bf16[32,128,512]{2,1,0:T(8,128)(2,1)} fusion(bf16[32,128,512]{2,1,0:T(8,128)(2,1)} %gather_fusion, pred[32]{0:T(512)(128)(4,1)S(1)} %compare_and_fusion), kind=kLoop, calls=%fused_computation.3 | loop fusion | flops 2097152 | bytes 8388640 | tf_op jit(solution)/shard_map/jit(_take)/select_n | solution.py:19
  64.6 114.9 %all-gather.3.cloned.1.call-done = bf16[1024,1,4096]{2,0,1:T(8,128)(2,1)} async-done(((bf16[1024,1,256]{2,0,1:T(8,128)(2,1)}), bf16[1024,1,4096]{2,0,1:T(8,128)(2,1)}) %all-gather.3.cloned.1.call-update) | async-done | bytes 8388624 | tf_op jit(solution)/shard_map/all_gather | solution.py:17
  179.5 0.0 copy-start
  179.5 10.4 %fusion = f32[1024,512]{1,0:T(8,128)} fusion(bf16[4096,512]{1,0:T(8,128)(2,1)} %bitcast.22, bf16[1024,1,4096]{2,0,1:T(8,128)(2,1)} %all-gather.3.cloned.1.call-done), kind=kOutput, calls=%fused_computation.1 | convolution fusion | flops 4294967296 | bytes 14680064 | tf_op jit(solution)/shard_map/dot_general | solution.py:20
  189.9 0.0 reduce-scatter.2.cloned.1.call-update
  189.9 0.0 copy-done
  189.9 101.4 %reduce-scatter.2.cloned.1.call-done = f32[256,512]{1,0:T(8,128)} async-done(((f32[1024,512]{1,0:T(8,128)}), f32[256,512]{1,0:T(8,128)}) %reduce-scatter.2.cloned.1.call-update) | async-done | bytes 524304 | tf_op jit(solution)/shard_map/reduce_scatter | solution.py:21
  291.3 0.1 mul.30
  291.4 1.8 fusion.2
  (4 shorter events, 0.0 us)
Async XLA Ops:
  6.5 4.3 %copy-start.1 = (s32[1,32]{1,0:T(1,128)S(1)}, s32[1,32]{1,0:T(1,128)}, u32[]{:S(2)}) copy-start(s32[1,32]{1,0:T(1,128)} %param.8) | copy-start | bytes 388
  6.5 48.5 %all-gather.5.cloned.1.call-start = ((), (), s32[]{:S(2)}) async-start(), calls=%async_computation.2 | async-start | bytes 4718592 | tf_op jit(solution)/shard_map/all_gather | solution.py:16
  7.3 172.2 %all-gather.3.cloned.1.call-start = ((), (), s32[]{:S(2)}) async-start(), calls=%async_computation.1 | async-start | bytes 8912896 | tf_op jit(solution)/shard_map/all_gather | solution.py:17
  10.8 280.5 %reduce-scatter.2.cloned.1.call-start = ((), (), s32[]{:S(2)}) async-start(), calls=%async_computation.3 | async-start | bytes 2621440 | tf_op jit(solution)/shard_map/reduce_scatter | solution.py:21
  179.5 10.5 %copy-start = (s32[2,4]{1,0:T(2,128)S(1)}, s32[2,4]{1,0:T(2,128)}, u32[]{:S(2)}) copy-start(s32[2,4]{1,0:T(2,128)} %param.9) | copy-start | bytes 100
Sparse Core Ops, SparseCore 0:
  9.5 45.5 all-gather.4
  57.1 122.3 all-gather.2
  190.0 101.2 reduce-scatter.1
where the time goes:
time: 300 us
  waiting for transfers between devices  261 us (87%)
  between operations  13.2 us (4%)
  matrix products  10.4 us (3%)
  other arithmetic  9.09 us (3%)
  local copies, waits for them, and re-layouts  5.84 us (2%)
    all_gather x1, waiting for transfers between devices, shards(): portion = lax.all_gather(masked, 'col', axis=2, tiled=True)  115 us
    reduce_scatter x1, waiting for transfers between devices, shards(): reduced = lax.psum_scatter(summed, 'layer', scatter_dimension=0, tiled=True)  101 us
    all_gather x1, waiting for transfers between devices, shards(): range_rows = lax.all_gather(slab, 'row', axis=1, tiled=True)[0]  44.2 us
    dot_general x1, matrix products, shards(): jnp.dot(portion[:, 0, :], operand, preferred_element_type=jnp.float32)  10.4 us
  transfers between devices with their start and end apart: 3, of which 3 were waited for; matrix products, arithmetic and copies ran while one was open for 4% of the time, Pallas kernels for 0%

commit v1 on v0

v1 whole, which is shorter than its diff:
```python
import itertools

import jax
import jax.numpy as jnp
from jax import lax
from jax.experimental import pallas as pl
from jax.experimental.pallas import tpu as pltpu
from jax.sharding import PartitionSpec as P

AXES = ("row", "col", "layer")
BS = 128
LEVELS = 32700.0
TINY = 1e-33
STEPS = 8.0
PAD = 16


def moves(f):
    pairs = []
    for y, c, zl, x, zh in itertools.product(range(4), range(2), range(4), range(4), range(4)):
        y2, c2, zl2, x2 = f(y, c, zl, x)
        pairs.append((((y * 2 + c) * 16 + zl * 4 + x) * 4 + zh, ((y2 * 2 + c2) * 16 + zl2 * 4 + x2) * 4 + zh))
    return pairs


def send(v, f):
    return lax.ppermute(v, AXES, moves(f))


def mask_kernel(pat_ref, x_ref, o_ref):
    for b in range(x_ref.shape[0] // BS):
        for j in range(x_ref.shape[1] // BS):
            keep = pat_ref[b, j].astype(jnp.float32).astype(jnp.bfloat16)
            at = (pl.ds(b * BS, BS), pl.ds(j * BS, BS))
            o_ref[at] = x_ref[at] * keep


def mask(panel, pattern):
    return pl.pallas_call(
        mask_kernel,
        out_shape=jax.ShapeDtypeStruct(panel.shape, panel.dtype),
        in_specs=[pl.BlockSpec(memory_space=pltpu.SMEM), pl.BlockSpec(memory_space=pltpu.VMEM)],
        out_specs=pl.BlockSpec(memory_space=pltpu.VMEM),
        name="mask",
    )(pattern, panel)


def mm_kernel(owner_ref, pos_ref, a_ref, mine_ref, other_ref, o_ref, a_s, b_s, acc, sem_a, sem_b):
    rows = a_s.shape[0]
    pieces = a_ref.shape[0]
    kw = a_ref.shape[2]
    y, c = pos_ref[0], pos_ref[1]

    def copy_a(s):
        return pltpu.make_async_copy(a_ref.at[s], a_s.at[:, pl.ds(s * kw, kw)], sem_a.at[s])

    def dst_b(j):
        return b_s.at[pl.ds(j * BS, BS), :]

    for s in range(pieces):
        copy_a(s).start()
        for j in (2 * s, 2 * s + 1):
            n = owner_ref[j]
            row, i = n // 4, n % 4
            rel = (row // 2 + 4 - y) % 4
            same = (row % 2) == c

            @pl.when(same)
            def _():
                pltpu.make_async_copy(mine_ref.at[rel, i], dst_b(j), sem_b.at[j]).start()

            @pl.when(jnp.logical_not(same))
            def _():
                pltpu.make_async_copy(other_ref.at[rel, i], dst_b(j), sem_b.at[j]).start()

    tile = 256
    for k in range(pieces // 2):
        for s in (2 * k, 2 * k + 1):
            copy_a(s).wait()
            for j in (2 * s, 2 * s + 1):
                pltpu.make_async_copy(mine_ref.at[0, 0], dst_b(j), sem_b.at[j]).wait()

        @pl.loop(0, rows // tile)
        def _(t):
            at = pl.ds(pl.multiple_of(t * tile, tile), tile)
            part = jnp.dot(a_s[at, pl.ds(k * 2 * kw, 2 * kw)], b_s[pl.ds(k * 2 * kw, 2 * kw), :], preferred_element_type=jnp.float32)
            if k == 0:
                acc[at, :] = part
            else:
                acc[at, :] += part

    chunk = rows // 4
    for l in range(4):
        x = acc[pl.ds(l * chunk, chunk), :]
        top = jnp.max(jnp.abs(x), axis=0, keepdims=True)
        code = jnp.ceil(jnp.log2(jnp.maximum(top, TINY)) * STEPS)
        q = jnp.round(x * (jnp.exp2(code * (-1.0 / STEPS)) * LEVELS)).astype(jnp.int32)
        o_ref[l, pl.ds(0, chunk), :] = q.astype(jnp.int16)
        o_ref[l, pl.ds(chunk, PAD), :] = jnp.broadcast_to(code.astype(jnp.int32), (PAD, x.shape[1])).astype(jnp.int16)


def matmul(owner, pos, a, mine, other):
    pieces, rows, kw = a.shape
    cols = mine.shape[3]
    return pl.pallas_call(
        mm_kernel,
        out_shape=jax.ShapeDtypeStruct((4, rows // 4 + PAD, cols), jnp.int16),
        in_specs=[pl.BlockSpec(memory_space=pltpu.SMEM)] * 2 + [pl.BlockSpec(memory_space=pl.ANY)] * 3,
        out_specs=pl.BlockSpec(memory_space=pltpu.VMEM),
        scratch_shapes=[
            pltpu.VMEM((rows, pieces * kw), jnp.bfloat16),
            pltpu.VMEM((pieces * kw, cols), jnp.bfloat16),
            pltpu.VMEM((rows, cols), jnp.float32),
            pltpu.SemaphoreType.DMA((pieces,)),
            pltpu.SemaphoreType.DMA((2 * pieces,)),
        ],
        compiler_params=pltpu.CompilerParams(vmem_limit_bytes=40 << 20),
        cost_estimate=pl.CostEstimate(flops=2 * rows * cols * pieces * kw, bytes_accessed=14 << 20, transcendentals=0),
        name="matmul",
    )(owner, pos, a, mine, other)


def total_kernel(pat_ref, q_ref, o_ref):
    rows, cols = o_ref.shape
    total = jnp.zeros((rows, cols), jnp.float32)
    for l in range(4):
        code = q_ref[l, pl.ds(rows, PAD), :].astype(jnp.int32)[0:1, :].astype(jnp.float32)
        total = total + q_ref[l, pl.ds(0, rows), :].astype(jnp.int32).astype(jnp.float32) * (jnp.exp2(code * (1.0 / STEPS)) * (1.0 / LEVELS))
    for b in range(rows // BS):
        for n in range(cols // BS):
            keep = pat_ref[b, n].astype(jnp.float32)
            o_ref[pl.ds(b * BS, BS), pl.ds(n * BS, BS)] = (total[b * BS:(b + 1) * BS, n * BS:(n + 1) * BS] * keep).astype(jnp.bfloat16)


def total(pattern, q):
    _, rows, cols = q.shape
    return pl.pallas_call(
        total_kernel,
        out_shape=jax.ShapeDtypeStruct((rows - PAD, cols), jnp.bfloat16),
        in_specs=[pl.BlockSpec(memory_space=pltpu.SMEM), pl.BlockSpec(memory_space=pltpu.VMEM)],
        out_specs=pl.BlockSpec(memory_space=pltpu.VMEM),
        compiler_params=pltpu.CompilerParams(vmem_limit_bytes=16 << 20),
        name="total",
    )(pattern, q)


def shards(panel, in_pattern, slab, owner, out_pattern):
    row = lax.axis_index("row")
    pos = jnp.stack([row // 2, row % 2])
    own = slab[0]
    with jax.named_scope("slab_ring"):
        below = send(own, lambda y, c, zl, x: ((y + 1) % 4, c, zl, x))
        above = send(own, lambda y, c, zl, x: ((y + 3) % 4, c, zl, x))
        far = send(own, lambda y, c, zl, x: ((y + 2) % 4, c, zl, x))
        mine = jnp.stack([own, above, far, below])
        other = send(mine, lambda y, c, zl, x: (y, 1 - c, zl, x))
    masked = mask(panel[:, 0, :], in_pattern[:, 0, :])
    gathered = lax.all_gather(masked, "col", axis=0, tiled=False)
    q = matmul(owner[0], pos, gathered, mine, other)
    q = lax.all_to_all(q, "layer", 0, 0, tiled=True)
    return total(out_pattern, q)


def solution(mesh):
    in_specs = (
        P("row", "layer", "col"),
        P("row", "layer", "col"),
        P("layer", "row", None, "col"),
        P("layer", None),
        P(("row", "layer"), "col"),
    )
    out_specs = P(("row", "layer"), "col")
    return jax.shard_map(shards, mesh=mesh, in_specs=in_specs, out_specs=out_specs, check_vma=False)
```

time: 300 us -> 216 us (0.72)
  the two profiles are of different devices: /device:TPU:1 before, /device:TPU:32 now
where the time goes in v1:
time: 216 us
  waiting for transfers between devices  93.9 us (43%)
  blocking collectives  69.9 us (32%)
  Pallas kernels  19.1 us (9%)
  starting transfers between devices  13.5 us (6%)
  between operations  13.5 us (6%)
  local copies, waits for them, and re-layouts  4.74 us (2%)
    all_gather x1, waiting for transfers between devices, shards(): gathered = lax.all_gather(masked, 'col', axis=0, tiled=False)  70.4 us
    all_to_all x1, blocking collectives, shards(): q = lax.all_to_all(q, 'layer', 0, 0, tiled=True)  69.9 us
    ppermute x4, waiting for transfers between devices, send(): return lax.ppermute(v, AXES, moves(f))  23.4 us
    pallas_call x1, Pallas kernels, matmul(): pl.pallas_call(mm_kernel, out_shape=jax.ShapeDtypeStruct((4, rows // 4 +...  15.5 us
    ppermute x4, starting transfers between devices, send(): return lax.ppermute(v, AXES, moves(f))  13.5 us
  transfers between devices with their start and end apart: 5, of which 5 were waited for; matrix products, arithmetic and copies ran while one was open for 1% of the time, Pallas kernels for 0%

profile of v1, /device:TPU:32, one launch (start us, length us, event | category | flops | bytes accessed | tf_op | source)
XLA Modules:
  0.0 215.9 jit_solution(443996331001192488)
XLA Ops:
  6.5 0.0 all-gather.3.cloned.1.call-start
  6.5 1.3 copy.6.pat_ref
  7.9 2.0 mask.1
  9.9 0.0 all-gather.3.cloned.1.call-update
  9.9 3.5 %collective-permute-start.2 = (bf16[4,128,512]{2,1,0:T(8,128)(2,1)}, bf16[4,128,512]{2,1,0:T(8,128)(2,1)S(1)}, u32[]{:S(2)}, u32[]{:S(2)}) collective-permute-start(bf16[4,128,512]{2,1,0:T(8,128)(2,1)} %bitcast.13), channel_id=1, source_target_pairs={{0,128},{1,129},{2,130},{3,131},{4,132},{5,133},{6,134},{7,135},{8... | collective-permute-start | bytes 1572872 | tf_op jit(solution)/shard_map/slab_ring/ppermute | solution.py:27
  13.4 4.8 %collective-permute-start.1 = (bf16[4,128,512]{2,1,0:T(8,128)(2,1)}, bf16[4,128,512]{2,1,0:T(8,128)(2,1)S(1)}, u32[]{:S(2)}, u32[]{:S(2)}) collective-permute-start(bf16[4,128,512]{2,1,0:T(8,128)(2,1)} %bitcast.14), channel_id=1, source_target_pairs={{0,256},{1,257},{2,258},{3,259},{4,260},{5,261},{6,262},{7,263},{8... | collective-permute-start | bytes 1572872 | tf_op jit(solution)/shard_map/slab_ring/ppermute | solution.py:27
  18.2 3.3 %collective-permute-start = (bf16[4,128,512]{2,1,0:T(8,128)(2,1)}, bf16[4,128,512]{2,1,0:T(8,128)(2,1)S(1)}, u32[]{:S(2)}, u32[]{:S(2)}) collective-permute-start(bf16[4,128,512]{2,1,0:T(8,128)(2,1)} %bitcast.15), channel_id=1, source_target_pairs={{0,384},{1,385},{2,386},{3,387},{4,388},{5,389},{6,390},{7,391},{8... | collective-permute-start | bytes 1572872 | tf_op jit(solution)/shard_map/slab_ring/ppermute | solution.py:27
  21.5 5.5 %collective-permute-done.2 = bf16[4,128,512]{2,1,0:T(8,128)(2,1)S(1)} collective-permute-done((bf16[4,128,512]{2,1,0:T(8,128)(2,1)}, bf16[4,128,512]{2,1,0:T(8,128)(2,1)S(1)}, u32[]{:S(2)}, u32[]{:S(2)}) %collective-permute-start.2) | collective-permute-done | bytes 524320 | tf_op jit(solution)/shard_map/slab_ring/ppermute | solution.py:27
  26.9 12.4 %collective-permute-done.1 = bf16[4,128,512]{2,1,0:T(8,128)(2,1)S(1)} collective-permute-done((bf16[4,128,512]{2,1,0:T(8,128)(2,1)}, bf16[4,128,512]{2,1,0:T(8,128)(2,1)S(1)}, u32[]{:S(2)}, u32[]{:S(2)}) %collective-permute-start.1) | collective-permute-done | bytes 524320 | tf_op jit(solution)/shard_map/slab_ring/ppermute | solution.py:27
  39.3 1.4 collective-permute-done
  40.7 0.0 copy-start.2
  40.7 1.3 pad_maximum_fusion.mine_ref
  42.0 1.9 collective-permute-start.3
  44.0 0.1 pad_add_fusion.pos_ref
  44.0 4.2 %collective-permute-done.3.other_ref = bf16[4,4,128,512]{3,2,1,0:T(8,128)(2,1)} collective-permute-done((bf16[4,4,128,512]{3,2,1,0:T(8,128)(2,1)S(1)}, bf16[4,4,128,512]{3,2,1,0:T(8,128)(2,1)}, u32[]{:S(2)}, u32[]{:S(2)}) %collective-permute-start.3) | collective-permute-done | bytes 2097184 | tf_op jit(solution)/shard_map/slab_ring/ppermute | solution.py:27
  48.2 70.4 %all-gather.3.cloned.1.call-done = bf16[16384,256]{1,0:T(8,128)(2,1)} async-done(((bf16[1024,256]{1,0:T(8,128)(2,1)}), bf16[16384,256]{1,0:T(8,128)(2,1)}) %all-gather.3.cloned.1.call-update) | async-done | bytes 8388624 | tf_op jit(solution)/shard_map/all_gather | solution.py:158
  118.6 0.0 copy-done.2
  118.6 0.0 copy-start.1
  118.6 3.4 %copy-done.1 = bf16[16384,256]{1,0:T(8,128)(2,1)S(1)} copy-done((bf16[16384,256]{1,0:T(8,128)(2,1)S(1)}, bf16[16384,256]{1,0:T(8,128)(2,1)}, u32[]{:S(2)}) %copy-start.1) | copy-done | bytes 8388632
  122.0 15.5 %matmul.1 = s16[4,272,512]{2,1,0:T(8,128)(2,1)S(1)} custom-call(s32[32]{0:T(128)S(1)} %bitcast.11, s32[2]{0:T(128)S(1)} %pad_add_fusion.pos_ref, bf16[16,1024,256]{2,1,0:T(8,128)(2,1)S(1)} %bitcast.10, bf16[4,4,128,512]{3,2,1,0:T(8,128)(2,1)S(1)} %pad_maximum_fusion.mine_ref, bf16[4,4,128,512]{3,2,1,0:T(8,128)(2,1)} %collective-permute-done.3.other_ref), custom_call_target="tpu_custom_call" | custom-call | flops 4294967296 | bytes 14680064 | tf_op jit(solution)/shard_map/matmul/pallas_call | solution.py:105
  137.6 0.0 copy-start
  137.6 69.9 %all_to_all.5.q_ref = s16[4,272,512]{2,1,0:T(8,128)(2,1)S(1)} all-to-all(s16[4,272,512]{2,1,0:T(8,128)(2,1)S(1)} %matmul.1), channel_id=1, replica_groups=mesh['row'=8,'col'=16,'layer'=4] {'layer'}, dimensions={0} | all-to-all | bytes 2228224 | tf_op jit(solution)/shard_map/all_to_all | solution.py:160
  207.5 0.0 copy-done
  207.5 1.6 total.1
Async XLA Ops:
  6.5 112.1 %all-gather.3.cloned.1.call-start = ((), (), s32[]{:S(2)}) async-start(), calls=%async_computation.1 | async-start | bytes 8912896 | tf_op jit(solution)/shard_map/all_gather | solution.py:158
  9.9 17.1 %collective-permute-start.2 = (bf16[4,128,512]{2,1,0:T(8,128)(2,1)}, bf16[4,128,512]{2,1,0:T(8,128)(2,1)S(1)}, u32[]{:S(2)}, u32[]{:S(2)}) collective-permute-start(bf16[4,128,512]{2,1,0:T(8,128)(2,1)} %bitcast.13), channel_id=1, source_target_pairs={{0,128},{1,129},{2,130},{3,131},{4,132},{5,133},{6,134},{7,135},{8... | collective-permute-start | bytes 1572872 | tf_op jit(solution)/shard_map/slab_ring/ppermute | solution.py:27
  13.4 26.0 %collective-permute-start.1 = (bf16[4,128,512]{2,1,0:T(8,128)(2,1)}, bf16[4,128,512]{2,1,0:T(8,128)(2,1)S(1)}, u32[]{:S(2)}, u32[]{:S(2)}) collective-permute-start(bf16[4,128,512]{2,1,0:T(8,128)(2,1)} %bitcast.14), channel_id=1, source_target_pairs={{0,256},{1,257},{2,258},{3,259},{4,260},{5,261},{6,262},{7,263},{8... | collective-permute-start | bytes 1572872 | tf_op jit(solution)/shard_map/slab_ring/ppermute | solution.py:27
  18.2 22.5 %collective-permute-start = (bf16[4,128,512]{2,1,0:T(8,128)(2,1)}, bf16[4,128,512]{2,1,0:T(8,128)(2,1)S(1)}, u32[]{:S(2)}, u32[]{:S(2)}) collective-permute-start(bf16[4,128,512]{2,1,0:T(8,128)(2,1)} %bitcast.15), channel_id=1, source_target_pairs={{0,384},{1,385},{2,386},{3,387},{4,388},{5,389},{6,390},{7,391},{8... | collective-permute-start | bytes 1572872 | tf_op jit(solution)/shard_map/slab_ring/ppermute | solution.py:27
  40.7 77.9 %copy-start.2 = (s32[1,32]{1,0:T(1,128)S(1)}, s32[1,32]{1,0:T(1,128)}, u32[]{:S(2)}) copy-start(s32[1,32]{1,0:T(1,128)} %param.8) | copy-start | bytes 388
  42.0 6.2 %collective-permute-start.3 = (bf16[4,4,128,512]{3,2,1,0:T(8,128)(2,1)S(1)}, bf16[4,4,128,512]{3,2,1,0:T(8,128)(2,1)}, u32[]{:S(2)}, u32[]{:S(2)}) collective-permute-start(bf16[4,4,128,512]{3,2,1,0:T(8,128)(2,1)S(1)} %pad_maximum_fusion.mine_ref), channel_id=1, source_target_pairs={{0,64},{1,65},{2,66},{3,67},{4,68},{5,69},{6,70},{7,71},{8,72},{9,... | collective-permute-start | bytes 6291464 | tf_op jit(solution)/shard_map/slab_ring/ppermute | solution.py:27
  118.6 3.4 %copy-start.1 = (bf16[16384,256]{1,0:T(8,128)(2,1)S(1)}, bf16[16384,256]{1,0:T(8,128)(2,1)}, u32[]{:S(2)}) copy-start(bf16[16384,256]{1,0:T(8,128)(2,1)} %all-gather.3.cloned.1.call-done) | copy-start | bytes 25165828
  137.6 70.0 %copy-start = (s32[2,4]{1,0:T(2,128)S(1)}, s32[2,4]{1,0:T(2,128)}, u32[]{:S(2)}) copy-start(s32[2,4]{1,0:T(2,128)} %pat_ref.1) | copy-start | bytes 100
Sparse Core Ops, SparseCore 0:
  10.0 108.5 all-gather.2

commit v2 on v0

v2 whole, which is shorter than its diff:
```python
import itertools

import jax
import jax.numpy as jnp
from jax import lax
from jax.experimental import pallas as pl
from jax.experimental.pallas import tpu as pltpu
from jax.sharding import PartitionSpec as P

AXES = ("row", "col", "layer")
BS = 128
LEVELS = 32700.0
TINY = 1e-33
STEPS = 8.0
PAD = 16


def moves(f):
    pairs = []
    for y, c, zl, x, zh in itertools.product(range(4), range(2), range(4), range(4), range(4)):
        y2, c2, zl2, x2 = f(y, c, zl, x)
        pairs.append((((y * 2 + c) * 16 + zl * 4 + x) * 4 + zh, ((y2 * 2 + c2) * 16 + zl2 * 4 + x2) * 4 + zh))
    return pairs


def send(v, f):
    return lax.ppermute(v, AXES, moves(f))


def mask_kernel(pos_ref, pat_ref, x_ref, first_ref, second_ref):
    q = pos_ref[3]
    for h, o_ref in ((q, first_ref), (1 - q, second_ref)):
        for b in range(o_ref.shape[0] // BS):
            for j in range(x_ref.shape[1] // BS):
                block = 2 * b + h
                keep = pat_ref[block, j].astype(jnp.float32).astype(jnp.bfloat16)
                cols = pl.ds(j * BS, BS)
                o_ref[pl.ds(b * BS, BS), cols] = x_ref[pl.ds(pl.multiple_of(block * BS, BS), BS), cols] * keep


def mask(pos, panel, pattern):
    rows, width = panel.shape
    return pl.pallas_call(
        mask_kernel,
        out_shape=[jax.ShapeDtypeStruct((rows // 2, width), panel.dtype)] * 2,
        in_specs=[pl.BlockSpec(memory_space=pltpu.SMEM)] * 2 + [pl.BlockSpec(memory_space=pltpu.VMEM)],
        out_specs=[pl.BlockSpec(memory_space=pltpu.VMEM)] * 2,
        name="mask",
    )(pos, pattern, panel)


def mm_kernel(pos_ref, owner_ref, *refs):
    a_refs, mine, other = refs[:8], refs[8:12], refs[12:16]
    o_ref, place, a_s, b_s, acc, sem_a, sem_b = refs[16:]
    rows = a_s.shape[0]
    y, c, p, x = pos_ref[0], pos_ref[1], pos_ref[2], pos_ref[4]
    kw = 2 * BS

    def col(piece, i):
        batch, rel = piece // 4, piece % 4
        half = (p + batch) % 2
        return (2 * half + (c + i) % 2) * 4 + (x + rel) % 4

    def copy_a(piece, i):
        s = 2 * piece + i
        return pltpu.make_async_copy(a_refs[piece].at[i], a_s.at[:, pl.ds(s * kw, kw)], sem_a.at[s])

    for piece in range(8):
        for i in range(2):
            copy_a(piece, i).start()
            for u in range(2):
                place[owner_ref[2 * col(piece, i) + u]] = 2 * (2 * piece + i) + u

    def copy_b(ref, i, at):
        return pltpu.make_async_copy(ref.at[:, i], b_s.at[:, pl.ds(pl.multiple_of(at * BS, BS), BS), :], sem_b.at[at])

    for rel in range(4):
        for k, group in enumerate((mine, other)):
            for i in range(4):
                block = (((y + rel) % 4) * 2 + (c + k) % 2) * 4 + i
                copy_b(group[rel], i, place[block]).start()

    tile = 256
    for k in range(8):
        for i in range(2):
            copy_a(k, i).wait()
            for u in range(2):
                copy_b(mine[0], 0, 4 * k + 2 * i + u).wait()

        @pl.loop(0, rows // tile)
        def _(t):
            at = pl.ds(pl.multiple_of(t * tile, tile), tile)
            for g in range(2):
                part = jnp.dot(a_s[at, pl.ds(k * 2 * kw, 2 * kw)], b_s[g, pl.ds(k * 2 * kw, 2 * kw), :], preferred_element_type=jnp.float32)
                if k == 0:
                    acc[g, at, :] = part
                else:
                    acc[g, at, :] += part

    for l in range(4):
        codes = []
        for t in range(8):
            v = acc[t // 4, pl.ds(l * BS, BS), pl.ds((t % 4) * BS, BS)]
            top = jnp.max(jnp.abs(v), axis=0, keepdims=True)
            code = jnp.ceil(jnp.log2(jnp.maximum(top, TINY)) * STEPS)
            codes.append(code)
            v = jnp.round(v * (jnp.exp2(code * (-1.0 / STEPS)) * LEVELS)).astype(jnp.int32)
            o_ref[l, pl.ds(t * BS, BS), :] = v.astype(jnp.int16)
        codes = jnp.concatenate(codes + codes, axis=0)
        o_ref[l, pl.ds(8 * BS, PAD), :] = codes.astype(jnp.int32).astype(jnp.int16)


def matmul(pos, owner, a, mine, other):
    _, rows, kw = a[0].shape
    cols = mine[0].shape[3]
    depth = 16 * kw
    return pl.pallas_call(
        mm_kernel,
        out_shape=jax.ShapeDtypeStruct((4, 8 * BS + PAD, BS), jnp.int16),
        in_specs=[pl.BlockSpec(memory_space=pltpu.SMEM)] * 2 + [pl.BlockSpec(memory_space=pl.ANY)] * 16,
        out_specs=pl.BlockSpec(memory_space=pltpu.VMEM),
        scratch_shapes=[
            pltpu.SMEM((32,), jnp.int32),
            pltpu.VMEM((rows, depth), jnp.bfloat16),
            pltpu.VMEM((2, depth, cols), jnp.bfloat16),
            pltpu.VMEM((2, rows, cols), jnp.float32),
            pltpu.SemaphoreType.DMA((16,)),
            pltpu.SemaphoreType.DMA((32,)),
        ],
        compiler_params=pltpu.CompilerParams(vmem_limit_bytes=32 << 20),
        cost_estimate=pl.CostEstimate(flops=4 * rows * cols * depth, bytes_accessed=14 << 20, transcendentals=0),
        name="matmul",
    )(pos, owner, *a, *mine, *other)


def total_kernel(pos_ref, v_ref, first_ref, second_ref):
    other = (pos_ref[1] + pos_ref[3]) % 2
    for g, o_ref in ((other, first_ref), (1 - other, second_ref)):
        for n in range(4):
            t = g * 4 + n
            at = pl.ds(pl.multiple_of(t * BS, BS), BS)
            total = jnp.zeros((BS, BS), jnp.float32)
            for l in range(4):
                codes = v_ref[l, pl.ds(8 * BS, PAD), :].astype(jnp.int32).astype(jnp.float32)
                code = jnp.where(g == 0, codes[n:n + 1, :], codes[4 + n:5 + n, :])
                total = total + v_ref[l, at, :].astype(jnp.int32).astype(jnp.float32) * (jnp.exp2(code * (1.0 / STEPS)) * (1.0 / LEVELS))
            o_ref[:, pl.ds(n * BS, BS)] = total.astype(jnp.bfloat16)


def total(pos, v):
    return pl.pallas_call(
        total_kernel,
        out_shape=[jax.ShapeDtypeStruct((BS, 4 * BS), jnp.bfloat16)] * 2,
        in_specs=[pl.BlockSpec(memory_space=pltpu.SMEM), pl.BlockSpec(memory_space=pltpu.VMEM)],
        out_specs=[pl.BlockSpec(memory_space=pltpu.VMEM)] * 2,
        name="total",
    )(pos, v)


def place_kernel(pos_ref, pat_ref, first_ref, second_ref, o_ref):
    q = pos_ref[3]
    for b, ref in ((q, first_ref), (1 - q, second_ref)):
        for n in range(4):
            keep = pat_ref[b, n].astype(jnp.float32).astype(jnp.bfloat16)
            cols = pl.ds(n * BS, BS)
            o_ref[pl.ds(pl.multiple_of(b * BS, BS), BS), cols] = ref[:, cols] * keep


def place(pos, pattern, first, second):
    return pl.pallas_call(
        place_kernel,
        out_shape=jax.ShapeDtypeStruct((2 * BS, 4 * BS), jnp.bfloat16),
        in_specs=[pl.BlockSpec(memory_space=pltpu.SMEM)] * 2 + [pl.BlockSpec(memory_space=pltpu.VMEM)] * 2,
        out_specs=pl.BlockSpec(memory_space=pltpu.VMEM),
        name="place",
    )(pos, pattern, first, second)


def shards(panel, in_pattern, slab, owner, out_pattern):
    row, col = lax.axis_index("row"), lax.axis_index("col")
    zl = col // 4
    pos = jnp.stack([row // 2, row % 2, zl // 2, zl % 2, col % 4])
    first, second = mask(pos, panel[:, 0, :], in_pattern[:, 0, :])
    with jax.named_scope("panel_pair"):
        first = send(first, lambda y, c, zl, x: (y, zl % 2, zl - zl % 2 + c, x))
        second = send(second, lambda y, c, zl, x: (y, 1 - zl % 2, zl - zl % 2 + c, x))
        near = jnp.stack([first, second])
    with jax.named_scope("slab_pair"):
        own = slab[0]
        pair = send(own, lambda y, c, zl, x: (y, c, zl ^ 1, x))
        own = jnp.stack([own, pair])
    with jax.named_scope("panel_far"):
        beyond = send(near, lambda y, c, zl, x: (y, c, zl ^ 2, x))

    def ring_x(v):
        return [v] + [send(v, lambda y, c, zl, x, d=d: (y, c, zl, (x - d) % 4)) for d in (1, 2, 3)]

    with jax.named_scope("panel_near_ring"):
        a = ring_x(near)
    with jax.named_scope("slab_ring"):
        mine = [own] + [send(own, lambda y, c, zl, x, d=d: ((y - d) % 4, c, zl, x)) for d in (1, 2, 3)]
        other = [send(v, lambda y, c, zl, x: (y, 1 - c, zl, x)) for v in mine]
    with jax.named_scope("panel_far_ring"):
        a = a + ring_x(beyond)
    v = matmul(pos, owner[0], a, mine, other)
    v = lax.all_to_all(v, "layer", 0, 0, tiled=True)
    first, second = total(pos, v)
    with jax.named_scope("product_pair"):
        first = send(first, lambda y, c, zl, x: (y, zl % 2, zl - zl % 2 + c, x))
        second = send(second, lambda y, c, zl, x: (y, zl % 2, zl - zl % 2 + 1 - c, x))
    return place(pos, out_pattern, first, second)


def solution(mesh):
    in_specs = (
        P("row", "layer", "col"),
        P("row", "layer", "col"),
        P("layer", "row", None, "col"),
        P("layer", None),
        P(("row", "layer"), "col"),
    )
    out_specs = P(("row", "layer"), "col")
    return jax.shard_map(shards, mesh=mesh, in_specs=in_specs, out_specs=out_specs, check_vma=False)
```

time: 300 us -> 201 us (0.67)
  the two profiles are of different devices: /device:TPU:1 before, /device:TPU:15 now
where the time goes in v2:
time: 201 us; the launch traced here: 200 us
  blocking collectives  65 us (32%)
  starting transfers between devices  59.4 us (30%)
  waiting for transfers between devices  56.8 us (28%)
  Pallas kernels  15.7 us (8%)
  local copies, waits for them, and re-layouts  2.72 us (1%)
    all_to_all x1, blocking collectives, shards(): v = lax.all_to_all(v, 'layer', 0, 0, tiled=True)  65 us
    ppermute x19, starting transfers between devices, send(): return lax.ppermute(v, AXES, moves(f))  59.4 us
    ppermute x19, waiting for transfers between devices, send(): return lax.ppermute(v, AXES, moves(f))  56.8 us
    pallas_call x1, Pallas kernels, matmul(): pl.pallas_call(mm_kernel, out_shape=jax.ShapeDtypeStruct((4, 8 * BS + PAD...  9.78 us
  transfers between devices with their start and end apart: 19, of which 9 were waited for; matrix products, arithmetic and copies ran while one was open for 0% of the time, Pallas kernels for 0%

profile of v2, /device:TPU:15, one launch (start us, length us, event | category | flops | bytes accessed | tf_op | source)
XLA Modules:
  0.0 199.9 jit_solution(8990622034676622079)
XLA Ops:
  4.0 4.1 %collective-permute-start = (bf16[512,256]{1,0:T(8,128)(2,1)}, bf16[512,256]{1,0:T(8,128)(2,1)S(1)}, u32[]{:S(2)}, u32[]{:S(2)}) collective-permute-start(bf16[512,256]{1,0:T(8,128)(2,1)} %get-tuple-element.9), channel_id=1, source_target_pairs={{0,0},{1,1},{2,2},{3,3},{4,4},{5,5},{6,6},{7,7},{8,8},{9,9},{10,10... | collective-permute-start | bytes 786440 | tf_op jit(solution)/shard_map/panel_pair/ppermute | solution.py:27
  12.4 3.2 %collective-permute-done.1 = bf16[512,256]{1,0:T(8,128)(2,1)S(1)} collective-permute-done((bf16[512,256]{1,0:T(8,128)(2,1)}, bf16[512,256]{1,0:T(8,128)(2,1)S(1)}, u32[]{:S(2)}, u32[]{:S(2)}) %collective-permute-start.1) | collective-permute-done | bytes 262176 | tf_op jit(solution)/shard_map/panel_pair/ppermute | solution.py:27
  15.6 4.9 %collective-permute-start.5 = (bf16[2,512,256]{2,1,0:T(8,128)(2,1)S(1)}, bf16[2,512,256]{2,1,0:T(8,128)(2,1)S(1)}, u32[]{:S(2)}, u32[]{:S(2)}) collective-permute-start(bf16[2,512,256]{2,1,0:T(8,128)(2,1)S(1)} %pad_maximum_fusion.1.refs_0_), channel_id=1, source_target_pairs={{0,32},{1,33},{2,34},{3,35},{4,36},{5,37},{6,38},{7,39},{8,40},{9,... | collective-permute-start | bytes 1572872 | tf_op jit(solution)/shard_map/panel_far/ppermute | solution.py:27
  20.5 2.1 %collective-permute-start.4 = (bf16[2,512,256]{2,1,0:T(8,128)(2,1)S(1)}, bf16[2,512,256]{2,1,0:T(8,128)(2,1)S(1)}, u32[]{:S(2)}, u32[]{:S(2)}) collective-permute-start(bf16[2,512,256]{2,1,0:T(8,128)(2,1)S(1)} %pad_maximum_fusion.1.refs_0_), channel_id=1, source_target_pairs={{0,4},{1,5},{2,6},{3,7},{4,8},{5,9},{6,10},{7,11},{8,12},{9,13},{1... | collective-permute-start | bytes 1572872 | tf_op jit(solution)/shard_map/panel_near_ring/ppermute | solution.py:27
  22.6 4.0 %collective-permute-start.3 = (bf16[2,512,256]{2,1,0:T(8,128)(2,1)S(1)}, bf16[2,512,256]{2,1,0:T(8,128)(2,1)S(1)}, u32[]{:S(2)}, u32[]{:S(2)}) collective-permute-start(bf16[2,512,256]{2,1,0:T(8,128)(2,1)S(1)} %pad_maximum_fusion.1.refs_0_), channel_id=1, source_target_pairs={{0,8},{1,9},{2,10},{3,11},{4,12},{5,13},{6,14},{7,15},{8,0},{9,1},... | collective-permute-start | bytes 1572872 | tf_op jit(solution)/shard_map/panel_near_ring/ppermute | solution.py:27
  26.7 7.2 %collective-permute-done.9 = bf16[4,128,512]{2,1,0:T(8,128)(2,1)S(1)} collective-permute-done((bf16[4,128,512]{2,1,0:T(8,128)(2,1)}, bf16[4,128,512]{2,1,0:T(8,128)(2,1)S(1)}, u32[]{:S(2)}, u32[]{:S(2)}) %collective-permute-start.9) | collective-permute-done | bytes 524320 | tf_op jit(solution)/shard_map/slab_pair/ppermute | solution.py:27
  34.0 3.2 %collective-permute-start.12 = (bf16[2,4,128,512]{3,2,1,0:T(8,128)(2,1)S(1)}, bf16[2,4,128,512]{3,2,1,0:T(8,128)(2,1)S(1)}, u32[]{:S(2)}, u32[]{:S(2)}) collective-permute-start(bf16[2,4,128,512]{3,2,1,0:T(8,128)(2,1)S(1)} %pad_maximum_fusion.refs_8_), channel_id=1, source_target_pairs={{0,128},{1,129},{2,130},{3,131},{4,132},{5,133},{6,134},{7,135},{8... | collective-permute-start | bytes 3145736 | tf_op jit(solution)/shard_map/slab_ring/ppermute | solution.py:27
  37.2 2.6 %collective-permute-start.11 = (bf16[2,4,128,512]{3,2,1,0:T(8,128)(2,1)S(1)}, bf16[2,4,128,512]{3,2,1,0:T(8,128)(2,1)S(1)}, u32[]{:S(2)}, u32[]{:S(2)}) collective-permute-start(bf16[2,4,128,512]{3,2,1,0:T(8,128)(2,1)S(1)} %pad_maximum_fusion.refs_8_), channel_id=1, source_target_pairs={{0,256},{1,257},{2,258},{3,259},{4,260},{5,261},{6,262},{7,263},{8... | collective-permute-start | bytes 3145736 | tf_op jit(solution)/shard_map/slab_ring/ppermute | solution.py:27
  39.8 3.5 %collective-permute-done.5.refs_4_ = bf16[2,512,256]{2,1,0:T(8,128)(2,1)S(1)} collective-permute-done((bf16[2,512,256]{2,1,0:T(8,128)(2,1)S(1)}, bf16[2,512,256]{2,1,0:T(8,128)(2,1)S(1)}, u32[]{:S(2)}, u32[]{:S(2)}) %collective-permute-start.5) | collective-permute-done | bytes 524320 | tf_op jit(solution)/shard_map/panel_far/ppermute | solution.py:27
  43.3 2.1 %collective-permute-start.10 = (bf16[2,4,128,512]{3,2,1,0:T(8,128)(2,1)S(1)}, bf16[2,4,128,512]{3,2,1,0:T(8,128)(2,1)S(1)}, u32[]{:S(2)}, u32[]{:S(2)}) collective-permute-start(bf16[2,4,128,512]{3,2,1,0:T(8,128)(2,1)S(1)} %pad_maximum_fusion.refs_8_), channel_id=1, source_target_pairs={{0,384},{1,385},{2,386},{3,387},{4,388},{5,389},{6,390},{7,391},{8... | collective-permute-start | bytes 3145736 | tf_op jit(solution)/shard_map/slab_ring/ppermute | solution.py:27
  45.4 2.5 %collective-permute-start.2 = (bf16[2,512,256]{2,1,0:T(8,128)(2,1)S(1)}, bf16[2,512,256]{2,1,0:T(8,128)(2,1)S(1)}, u32[]{:S(2)}, u32[]{:S(2)}) collective-permute-start(bf16[2,512,256]{2,1,0:T(8,128)(2,1)S(1)} %pad_maximum_fusion.1.refs_0_), channel_id=1, source_target_pairs={{0,12},{1,13},{2,14},{3,15},{4,0},{5,1},{6,2},{7,3},{8,4},{9,5},{1... | collective-permute-start | bytes 1572872 | tf_op jit(solution)/shard_map/panel_near_ring/ppermute | solution.py:27
  47.8 4.0 %collective-permute-start.8 = (bf16[2,512,256]{2,1,0:T(8,128)(2,1)S(1)}, bf16[2,512,256]{2,1,0:T(8,128)(2,1)S(1)}, u32[]{:S(2)}, u32[]{:S(2)}) collective-permute-start(bf16[2,512,256]{2,1,0:T(8,128)(2,1)S(1)} %collective-permute-done.5.refs_4_), channel_id=1, source_target_pairs={{0,4},{1,5},{2,6},{3,7},{4,8},{5,9},{6,10},{7,11},{8,12},{9,13},{1... | collective-permute-start | bytes 1572872 | tf_op jit(solution)/shard_map/panel_far_ring/ppermute | solution.py:27
  51.9 8.3 %collective-permute-done.2.refs_1_ = bf16[2,512,256]{2,1,0:T(8,128)(2,1)S(1)} collective-permute-done((bf16[2,512,256]{2,1,0:T(8,128)(2,1)S(1)}, bf16[2,512,256]{2,1,0:T(8,128)(2,1)S(1)}, u32[]{:S(2)}, u32[]{:S(2)}) %collective-permute-start.2) | collective-permute-done | bytes 524320 | tf_op jit(solution)/shard_map/panel_near_ring/ppermute | solution.py:27
  60.2 4.5 %collective-permute-start.13 = (bf16[2,4,128,512]{3,2,1,0:T(8,128)(2,1)S(1)}, bf16[2,4,128,512]{3,2,1,0:T(8,128)(2,1)S(1)}, u32[]{:S(2)}, u32[]{:S(2)}) collective-permute-start(bf16[2,4,128,512]{3,2,1,0:T(8,128)(2,1)S(1)} %pad_maximum_fusion.refs_8_), channel_id=1, source_target_pairs={{0,64},{1,65},{2,66},{3,67},{4,68},{5,69},{6,70},{7,71},{8,72},{9,... | collective-permute-start | bytes 3145736 | tf_op jit(solution)/shard_map/slab_ring/ppermute | solution.py:27
  66.7 3.4 %collective-permute-start.16 = (bf16[2,4,128,512]{3,2,1,0:T(8,128)(2,1)S(1)}, bf16[2,4,128,512]{3,2,1,0:T(8,128)(2,1)S(1)}, u32[]{:S(2)}, u32[]{:S(2)}) collective-permute-start(bf16[2,4,128,512]{3,2,1,0:T(8,128)(2,1)S(1)} %collective-permute-done.12.refs_11_), channel_id=1, source_target_pairs={{0,64},{1,65},{2,66},{3,67},{4,68},{5,69},{6,70},{7,71},{8,72},{9,... | collective-permute-start | bytes 3145736 | tf_op jit(solution)/shard_map/slab_ring/ppermute | solution.py:27
  72.0 16.1 %collective-permute-done.10.refs_9_ = bf16[2,4,128,512]{3,2,1,0:T(8,128)(2,1)S(1)} collective-permute-done((bf16[2,4,128,512]{3,2,1,0:T(8,128)(2,1)S(1)}, bf16[2,4,128,512]{3,2,1,0:T(8,128)(2,1)S(1)}, u32[]{:S(2)}, u32[]{:S(2)}) %collective-permute-start.10) | collective-permute-done | bytes 1048608 | tf_op jit(solution)/shard_map/slab_ring/ppermute | solution.py:27
  88.1 2.4 %collective-permute-start.14 = (bf16[2,4,128,512]{3,2,1,0:T(8,128)(2,1)S(1)}, bf16[2,4,128,512]{3,2,1,0:T(8,128)(2,1)S(1)}, u32[]{:S(2)}, u32[]{:S(2)}) collective-permute-start(bf16[2,4,128,512]{3,2,1,0:T(8,128)(2,1)S(1)} %collective-permute-done.10.refs_9_), channel_id=1, source_target_pairs={{0,64},{1,65},{2,66},{3,67},{4,68},{5,69},{6,70},{7,71},{8,72},{9,... | collective-permute-start | bytes 3145736 | tf_op jit(solution)/shard_map/slab_ring/ppermute | solution.py:27
  90.5 2.5 %collective-permute-start.6 = (bf16[2,512,256]{2,1,0:T(8,128)(2,1)S(1)}, bf16[2,512,256]{2,1,0:T(8,128)(2,1)S(1)}, u32[]{:S(2)}, u32[]{:S(2)}) collective-permute-start(bf16[2,512,256]{2,1,0:T(8,128)(2,1)S(1)} %collective-permute-done.5.refs_4_), channel_id=1, source_target_pairs={{0,12},{1,13},{2,14},{3,15},{4,0},{5,1},{6,2},{7,3},{8,4},{9,5},{1... | collective-permute-start | bytes 1572872 | tf_op jit(solution)/shard_map/panel_far_ring/ppermute | solution.py:27
  93.0 14.2 %collective-permute-done.6.refs_5_ = bf16[2,512,256]{2,1,0:T(8,128)(2,1)S(1)} collective-permute-done((bf16[2,512,256]{2,1,0:T(8,128)(2,1)S(1)}, bf16[2,512,256]{2,1,0:T(8,128)(2,1)S(1)}, u32[]{:S(2)}, u32[]{:S(2)}) %collective-permute-start.6) | collective-permute-done | bytes 524320 | tf_op jit(solution)/shard_map/panel_far_ring/ppermute | solution.py:27
  107.2 9.8 %matmul.1 = s16[4,1040,128]{2,1,0:T(8,128)(2,1)S(1)} custom-call(s32[5]{0:T(128)S(1)} %copy-done, s32[32]{0:T(128)S(1)} %bitcast.12, bf16[2,512,256]{2,1,0:T(8,128)(2,1)S(1)} %pad_maximum_fusion.1.refs_0_, bf16[2,512,256]{2,1,0:T(8,128)(2,1)S(1)} %collective-permute-done.2.refs_1_, bf16[2,512,256]{2,1,0:T(8,128)(2,1)S(1)} %collective-permute-done.3.refs_2_, ...), custom_call_target="tpu_custom_call" | custom-call | flops 4294967296 | bytes 14680064 | tf_op jit(solution)/shard_map/matmul/pallas_call | solution.py:117
  117.0 65.0 %all_to_all.5.v_ref = s16[4,1040,128]{2,1,0:T(8,128)(2,1)} all-to-all(s16[4,1040,128]{2,1,0:T(8,128)(2,1)S(1)} %matmul.1), channel_id=1, replica_groups=mesh['row'=8,'col'=16,'layer'=4] {'layer'}, dimensions={0} | all-to-all | bytes 2129920 | tf_op jit(solution)/shard_map/all_to_all | solution.py:206
  182.0 2.2 %total.1 = (bf16[128,512]{1,0:T(8,128)(2,1)}, bf16[128,512]{1,0:T(8,128)(2,1)}) custom-call(s32[5]{0:T(128)} %stack.38.pos_ref, s16[4,1040,128]{2,1,0:T(8,128)(2,1)} %all_to_all.5.v_ref), custom_call_target="tpu_custom_call" | custom-call | tf_op jit(solution)/shard_map/total/pallas_call | solution.py:151
  184.1 7.4 %collective-permute-start.17 = (bf16[128,512]{1,0:T(8,128)(2,1)}, bf16[128,512]{1,0:T(8,128)(2,1)S(1)}, u32[]{:S(2)}, u32[]{:S(2)}) collective-permute-start(bf16[128,512]{1,0:T(8,128)(2,1)} %get-tuple-element.11), channel_id=1, source_target_pairs={{0,0},{1,1},{2,2},{3,3},{4,4},{5,5},{6,6},{7,7},{8,8},{9,9},{10,10... | collective-permute-start | bytes 393224 | tf_op jit(solution)/shard_map/product_pair/ppermute | solution.py:27
  194.5 3.1 %collective-permute-done.18.second_ref = bf16[128,512]{1,0:T(8,128)(2,1)S(1)} collective-permute-done((bf16[128,512]{1,0:T(8,128)(2,1)}, bf16[128,512]{1,0:T(8,128)(2,1)S(1)}, u32[]{:S(2)}, u32[]{:S(2)}) %collective-permute-start.18) | collective-permute-done | bytes 131104 | tf_op jit(solution)/shard_map/product_pair/ppermute | solution.py:27
  (33 shorter events, 17.5 us)
Async XLA Ops:
  0.0 33.9 %copy-start.2 = (bf16[1,4,128,512]{3,2,1,0:T(8,128)(2,1)S(1)}, bf16[1,4,128,512]{3,2,1,0:T(8,128)(2,1)}, u32[]{:S(2)}) copy-start(bf16[1,4,128,512]{3,2,1,0:T(8,128)(2,1)} %param.7) | copy-start | bytes 1572868
  4.0 8.4 %collective-permute-start = (bf16[512,256]{1,0:T(8,128)(2,1)}, bf16[512,256]{1,0:T(8,128)(2,1)S(1)}, u32[]{:S(2)}, u32[]{:S(2)}) collective-permute-start(bf16[512,256]{1,0:T(8,128)(2,1)} %get-tuple-element.9), channel_id=1, source_target_pairs={{0,0},{1,1},{2,2},{3,3},{4,4},{5,5},{6,6},{7,7},{8,8},{9,9},{10,10... | collective-permute-start | bytes 786440 | tf_op jit(solution)/shard_map/panel_pair/ppermute | solution.py:27
  8.1 7.4 %collective-permute-start.1 = (bf16[512,256]{1,0:T(8,128)(2,1)}, bf16[512,256]{1,0:T(8,128)(2,1)S(1)}, u32[]{:S(2)}, u32[]{:S(2)}) collective-permute-start(bf16[512,256]{1,0:T(8,128)(2,1)} %get-tuple-element.10), channel_id=1, source_target_pairs={{0,64},{1,65},{2,66},{3,67},{4,68},{5,69},{6,70},{7,71},{8,72},{9,... | collective-permute-start | bytes 786440 | tf_op jit(solution)/shard_map/panel_pair/ppermute | solution.py:27
  10.0 23.8 %collective-permute-start.9 = (bf16[4,128,512]{2,1,0:T(8,128)(2,1)}, bf16[4,128,512]{2,1,0:T(8,128)(2,1)S(1)}, u32[]{:S(2)}, u32[]{:S(2)}) collective-permute-start(bf16[4,128,512]{2,1,0:T(8,128)(2,1)} %bitcast.14), channel_id=1, source_target_pairs={{0,16},{1,17},{2,18},{3,19},{4,20},{5,21},{6,22},{7,23},{8,24},{9,... | collective-permute-start | bytes 1572872 | tf_op jit(solution)/shard_map/slab_pair/ppermute | solution.py:27
  15.6 91.6 %copy-start = (s32[5]{0:T(128)S(1)}, s32[5]{0:T(128)}, u32[]{:S(2)}) copy-start(s32[5]{0:T(128)} %stack.38.pos_ref) | copy-start | bytes 64
  15.6 91.6 %copy-start.1 = (s32[1,32]{1,0:T(1,128)S(1)}, s32[1,32]{1,0:T(1,128)}, u32[]{:S(2)}) copy-start(s32[1,32]{1,0:T(1,128)} %param.8) | copy-start | bytes 388
  15.6 27.7 %collective-permute-start.5 = (bf16[2,512,256]{2,1,0:T(8,128)(2,1)S(1)}, bf16[2,512,256]{2,1,0:T(8,128)(2,1)S(1)}, u32[]{:S(2)}, u32[]{:S(2)}) collective-permute-start(bf16[2,512,256]{2,1,0:T(8,128)(2,1)S(1)} %pad_maximum_fusion.1.refs_0_), channel_id=1, source_target_pairs={{0,32},{1,33},{2,34},{3,35},{4,36},{5,37},{6,38},{7,39},{8,40},{9,... | collective-permute-start | bytes 1572872 | tf_op jit(solution)/shard_map/panel_far/ppermute | solution.py:27
  20.5 24.8 %collective-permute-start.4 = (bf16[2,512,256]{2,1,0:T(8,128)(2,1)S(1)}, bf16[2,512,256]{2,1,0:T(8,128)(2,1)S(1)}, u32[]{:S(2)}, u32[]{:S(2)}) collective-permute-start(bf16[2,512,256]{2,1,0:T(8,128)(2,1)S(1)} %pad_maximum_fusion.1.refs_0_), channel_id=1, source_target_pairs={{0,4},{1,5},{2,6},{3,7},{4,8},{5,9},{6,10},{7,11},{8,12},{9,13},{1... | collective-permute-start | bytes 1572872 | tf_op jit(solution)/shard_map/panel_near_ring/ppermute | solution.py:27
  22.6 25.2 %collective-permute-start.3 = (bf16[2,512,256]{2,1,0:T(8,128)(2,1)S(1)}, bf16[2,512,256]{2,1,0:T(8,128)(2,1)S(1)}, u32[]{:S(2)}, u32[]{:S(2)}) collective-permute-start(bf16[2,512,256]{2,1,0:T(8,128)(2,1)S(1)} %pad_maximum_fusion.1.refs_0_), channel_id=1, source_target_pairs={{0,8},{1,9},{2,10},{3,11},{4,12},{5,13},{6,14},{7,15},{8,0},{9,1},... | collective-permute-start | bytes 1572872 | tf_op jit(solution)/shard_map/panel_near_ring/ppermute | solution.py:27
  34.0 32.7 %collective-permute-start.12 = (bf16[2,4,128,512]{3,2,1,0:T(8,128)(2,1)S(1)}, bf16[2,4,128,512]{3,2,1,0:T(8,128)(2,1)S(1)}, u32[]{:S(2)}, u32[]{:S(2)}) collective-permute-start(bf16[2,4,128,512]{3,2,1,0:T(8,128)(2,1)S(1)} %pad_maximum_fusion.refs_8_), channel_id=1, source_target_pairs={{0,128},{1,129},{2,130},{3,131},{4,132},{5,133},{6,134},{7,135},{8... | collective-permute-start | bytes 3145736 | tf_op jit(solution)/shard_map/slab_ring/ppermute | solution.py:27
  37.2 32.9 %collective-permute-start.11 = (bf16[2,4,128,512]{3,2,1,0:T(8,128)(2,1)S(1)}, bf16[2,4,128,512]{3,2,1,0:T(8,128)(2,1)S(1)}, u32[]{:S(2)}, u32[]{:S(2)}) collective-permute-start(bf16[2,4,128,512]{3,2,1,0:T(8,128)(2,1)S(1)} %pad_maximum_fusion.refs_8_), channel_id=1, source_target_pairs={{0,256},{1,257},{2,258},{3,259},{4,260},{5,261},{6,262},{7,263},{8... | collective-permute-start | bytes 3145736 | tf_op jit(solution)/shard_map/slab_ring/ppermute | solution.py:27
  43.3 44.8 %collective-permute-start.10 = (bf16[2,4,128,512]{3,2,1,0:T(8,128)(2,1)S(1)}, bf16[2,4,128,512]{3,2,1,0:T(8,128)(2,1)S(1)}, u32[]{:S(2)}, u32[]{:S(2)}) collective-permute-start(bf16[2,4,128,512]{3,2,1,0:T(8,128)(2,1)S(1)} %pad_maximum_fusion.refs_8_), channel_id=1, source_target_pairs={{0,384},{1,385},{2,386},{3,387},{4,388},{5,389},{6,390},{7,391},{8... | collective-permute-start | bytes 3145736 | tf_op jit(solution)/shard_map/slab_ring/ppermute | solution.py:27
  45.4 14.8 %collective-permute-start.2 = (bf16[2,512,256]{2,1,0:T(8,128)(2,1)S(1)}, bf16[2,512,256]{2,1,0:T(8,128)(2,1)S(1)}, u32[]{:S(2)}, u32[]{:S(2)}) collective-permute-start(bf16[2,512,256]{2,1,0:T(8,128)(2,1)S(1)} %pad_maximum_fusion.1.refs_0_), channel_id=1, source_target_pairs={{0,12},{1,13},{2,14},{3,15},{4,0},{5,1},{6,2},{7,3},{8,4},{9,5},{1... | collective-permute-start | bytes 1572872 | tf_op jit(solution)/shard_map/panel_near_ring/ppermute | solution.py:27
  47.8 16.9 %collective-permute-start.8 = (bf16[2,512,256]{2,1,0:T(8,128)(2,1)S(1)}, bf16[2,512,256]{2,1,0:T(8,128)(2,1)S(1)}, u32[]{:S(2)}, u32[]{:S(2)}) collective-permute-start(bf16[2,512,256]{2,1,0:T(8,128)(2,1)S(1)} %collective-permute-done.5.refs_4_), channel_id=1, source_target_pairs={{0,4},{1,5},{2,6},{3,7},{4,8},{5,9},{6,10},{7,11},{8,12},{9,13},{1... | collective-permute-start | bytes 1572872 | tf_op jit(solution)/shard_map/panel_far_ring/ppermute | solution.py:27
  60.2 47.0 %collective-permute-start.13 = (bf16[2,4,128,512]{3,2,1,0:T(8,128)(2,1)S(1)}, bf16[2,4,128,512]{3,2,1,0:T(8,128)(2,1)S(1)}, u32[]{:S(2)}, u32[]{:S(2)}) collective-permute-start(bf16[2,4,128,512]{3,2,1,0:T(8,128)(2,1)S(1)} %pad_maximum_fusion.refs_8_), channel_id=1, source_target_pairs={{0,64},{1,65},{2,66},{3,67},{4,68},{5,69},{6,70},{7,71},{8,72},{9,... | collective-permute-start | bytes 3145736 | tf_op jit(solution)/shard_map/slab_ring/ppermute | solution.py:27
  64.7 25.8 %collective-permute-start.7 = (bf16[2,512,256]{2,1,0:T(8,128)(2,1)S(1)}, bf16[2,512,256]{2,1,0:T(8,128)(2,1)S(1)}, u32[]{:S(2)}, u32[]{:S(2)}) collective-permute-start(bf16[2,512,256]{2,1,0:T(8,128)(2,1)S(1)} %collective-permute-done.5.refs_4_), channel_id=1, source_target_pairs={{0,8},{1,9},{2,10},{3,11},{4,12},{5,13},{6,14},{7,15},{8,0},{9,1},... | collective-permute-start | bytes 1572872 | tf_op jit(solution)/shard_map/panel_far_ring/ppermute | solution.py:27
  66.7 40.5 %collective-permute-start.16 = (bf16[2,4,128,512]{3,2,1,0:T(8,128)(2,1)S(1)}, bf16[2,4,128,512]{3,2,1,0:T(8,128)(2,1)S(1)}, u32[]{:S(2)}, u32[]{:S(2)}) collective-permute-start(bf16[2,4,128,512]{3,2,1,0:T(8,128)(2,1)S(1)} %collective-permute-done.12.refs_11_), channel_id=1, source_target_pairs={{0,64},{1,65},{2,66},{3,67},{4,68},{5,69},{6,70},{7,71},{8,72},{9,... | collective-permute-start | bytes 3145736 | tf_op jit(solution)/shard_map/slab_ring/ppermute | solution.py:27
  70.0 37.1 %collective-permute-start.15 = (bf16[2,4,128,512]{3,2,1,0:T(8,128)(2,1)S(1)}, bf16[2,4,128,512]{3,2,1,0:T(8,128)(2,1)S(1)}, u32[]{:S(2)}, u32[]{:S(2)}) collective-permute-start(bf16[2,4,128,512]{3,2,1,0:T(8,128)(2,1)S(1)} %collective-permute-done.11.refs_10_), channel_id=1, source_target_pairs={{0,64},{1,65},{2,66},{3,67},{4,68},{5,69},{6,70},{7,71},{8,72},{9,... | collective-permute-start | bytes 3145736 | tf_op jit(solution)/shard_map/slab_ring/ppermute | solution.py:27
  88.1 19.1 %collective-permute-start.14 = (bf16[2,4,128,512]{3,2,1,0:T(8,128)(2,1)S(1)}, bf16[2,4,128,512]{3,2,1,0:T(8,128)(2,1)S(1)}, u32[]{:S(2)}, u32[]{:S(2)}) collective-permute-start(bf16[2,4,128,512]{3,2,1,0:T(8,128)(2,1)S(1)} %collective-permute-done.10.refs_9_), channel_id=1, source_target_pairs={{0,64},{1,65},{2,66},{3,67},{4,68},{5,69},{6,70},{7,71},{8,72},{9,... | collective-permute-start | bytes 3145736 | tf_op jit(solution)/shard_map/slab_ring/ppermute | solution.py:27
  90.5 16.6 %collective-permute-start.6 = (bf16[2,512,256]{2,1,0:T(8,128)(2,1)S(1)}, bf16[2,512,256]{2,1,0:T(8,128)(2,1)S(1)}, u32[]{:S(2)}, u32[]{:S(2)}) collective-permute-start(bf16[2,512,256]{2,1,0:T(8,128)(2,1)S(1)} %collective-permute-done.5.refs_4_), channel_id=1, source_target_pairs={{0,12},{1,13},{2,14},{3,15},{4,0},{5,1},{6,2},{7,3},{8,4},{9,5},{1... | collective-permute-start | bytes 1572872 | tf_op jit(solution)/shard_map/panel_far_ring/ppermute | solution.py:27
  184.1 10.3 %collective-permute-start.17 = (bf16[128,512]{1,0:T(8,128)(2,1)}, bf16[128,512]{1,0:T(8,128)(2,1)S(1)}, u32[]{:S(2)}, u32[]{:S(2)}) collective-permute-start(bf16[128,512]{1,0:T(8,128)(2,1)} %get-tuple-element.11), channel_id=1, source_target_pairs={{0,0},{1,1},{2,2},{3,3},{4,4},{5,5},{6,6},{7,7},{8,8},{9,9},{10,10... | collective-permute-start | bytes 393224 | tf_op jit(solution)/shard_map/product_pair/ppermute | solution.py:27
  191.6 5.9 %collective-permute-start.18 = (bf16[128,512]{1,0:T(8,128)(2,1)}, bf16[128,512]{1,0:T(8,128)(2,1)S(1)}, u32[]{:S(2)}, u32[]{:S(2)}) collective-permute-start(bf16[128,512]{1,0:T(8,128)(2,1)} %get-tuple-element.12), channel_id=1, source_target_pairs={{0,16},{1,17},{2,18},{3,19},{4,20},{5,21},{6,22},{7,23},{8,24},{9,... | collective-permute-start | bytes 393224 | tf_op jit(solution)/shard_map/product_pair/ppermute | solution.py:27
  194.5 3.1 %copy-start.3 = (bf16[128,512]{1,0:T(8,128)(2,1)}, bf16[128,512]{1,0:T(8,128)(2,1)S(1)}, u32[]{:S(2)}) copy-start(bf16[128,512]{1,0:T(8,128)(2,1)S(1)} %collective-permute-done.17.first_ref) | copy-start | bytes 393220
  197.5 0.7 copy-start.4

commit v3 on v2

v3 whole, which is shorter than its diff:
```python
import itertools

import jax
import jax.numpy as jnp
from jax import lax
from jax.experimental import pallas as pl
from jax.experimental.pallas import tpu as pltpu
from jax.sharding import PartitionSpec as P

AXES = ("row", "col", "layer")
BS = 128
LEVELS = 32700.0
TINY = 1e-33
STEPS = 8.0
PAD = 16


def moves(f):
    pairs = []
    for y, c, zl, x, zh in itertools.product(range(4), range(2), range(4), range(4), range(4)):
        y2, c2, zl2, x2, zh2 = f(y, c, zl, x, zh)
        pairs.append((((y * 2 + c) * 16 + zl * 4 + x) * 4 + zh, ((y2 * 2 + c2) * 16 + zl2 * 4 + x2) * 4 + zh2))
    return pairs


def send(v, f):
    return lax.ppermute(v, AXES, moves(f))


def to_x(v, d):
    return send(v, lambda y, c, zl, x, zh: (y, c, zl, (x + d) % 4, zh))


def to_y(v, d):
    return send(v, lambda y, c, zl, x, zh: ((y + d) % 4, c, zl, x, zh))


def to_layer(v, d):
    return send(v, lambda y, c, zl, x, zh: (y, c, zl, x, (zh + d) % 4))


def to_core(v):
    return send(v, lambda y, c, zl, x, zh: (y, 1 - c, zl, x, zh))


def mask_kernel(pos_ref, pat_ref, x_ref, first_ref, second_ref):
    q = pos_ref[3]
    for h, o_ref in ((q, first_ref), (1 - q, second_ref)):
        for b in range(o_ref.shape[0] // BS):
            for j in range(x_ref.shape[1] // BS):
                block = 2 * b + h
                keep = pat_ref[j, block].astype(jnp.float32).astype(jnp.bfloat16)
                cols = pl.ds(j * BS, BS)
                o_ref[pl.ds(b * BS, BS), cols] = x_ref[pl.ds(pl.multiple_of(block * BS, BS), BS), cols] * keep


def mask(pos, panel, pattern):
    rows, width = panel.shape
    return pl.pallas_call(
        mask_kernel,
        out_shape=[jax.ShapeDtypeStruct((rows // 2, width), panel.dtype)] * 2,
        in_specs=[pl.BlockSpec(memory_space=pltpu.SMEM)] * 2 + [pl.BlockSpec(memory_space=pltpu.VMEM)],
        out_specs=[pl.BlockSpec(memory_space=pltpu.VMEM)] * 2,
        name="mask",
    )(pos, pattern, panel)


PANEL = (
    ((0, 0, 0), (0, 0, 1)),
    ((0, 3, 0), (0, 3, 1)),
    ((0, 1, 0), (0, 1, 1)),
    ((1, 0, 0), (1, 0, 1)),
    ((0, 2, 0), (1, 3, 0), (1, 3, 1)),
    ((0, 2, 1), (1, 1, 0), (1, 1, 1)),
    ((1, 2, 0),),
    ((1, 2, 1),),
)
R0 = tuple((0, g, i) for g in range(2) for i in range(4))
R1P = tuple((3, 0, i) for i in range(4))
R1M = tuple((1, 0, i) for i in range(4))
R2P = ((2, 0, 0), (2, 0, 1)) + tuple((3, 1, i) for i in range(4))
R2M = ((2, 0, 2), (2, 0, 3)) + tuple((1, 1, i) for i in range(4))
R3P = ((2, 1, 0), (2, 1, 1))
R3M = ((2, 1, 2), (2, 1, 3))
SLAB = (
    (0, R0[:4]),
    (0, R0[4:]),
    (0, R1P),
    (0, R1M),
    (0, R2P),
    (0, R2M),
    (0, R3P),
    (0, R3M),
    (1, R0),
    (1, R1P + R1M + R2P + R2M),
    (1, R3P + R3M),
)
NA, NB = len(PANEL), len(SLAB)


def quantize(v):
    top = jnp.max(jnp.abs(v), axis=0, keepdims=True)
    code = jnp.ceil(jnp.log2(jnp.maximum(top, TINY)) * STEPS)
    v = jnp.round(v * (jnp.exp2(code * (-1.0 / STEPS)) * LEVELS)).astype(jnp.int32)
    return v.astype(jnp.int16), code


def mm_kernel(pos_ref, owner_ref, *refs):
    a_refs, b_refs = refs[:NA], refs[NA:NA + NB]
    own_ref, *o_refs = refs[NA + NB:NA + NB + 4]
    place, a_s, b_s, acc, sem_a, sem_b = refs[NA + NB + 4:]
    rows = a_s.shape[0]
    y, c, p, x, layer = pos_ref[0], pos_ref[1], pos_ref[2], pos_ref[4], pos_ref[5]
    kw = 2 * BS
    pieces = [(n, at) + piece for n, group in enumerate(PANEL) for at, piece in enumerate(group)]

    def copy_a(s):
        n, at = pieces[s][:2]
        return pltpu.make_async_copy(a_refs[n].at[at], a_s.at[:, pl.ds(s * kw, kw)], sem_a.at[s])

    for s, (_, _, batch, rel, i) in enumerate(pieces):
        copy_a(s).start()
        col = (2 * ((p + batch) % 2) + (c + i) % 2) * 4 + (x + rel) % 4
        for u in range(2):
            place[owner_ref[2 * col + u]] = 2 * s + u

    def copy_b(ref, i, g, at):
        return pltpu.make_async_copy(ref.at[i], b_s.at[g, pl.ds(pl.multiple_of(at * BS, BS), BS), :], sem_b.at[g, at])

    for ref, (k, blocks) in zip(b_refs, SLAB):
        for n, (rel, g, i) in enumerate(blocks):
            block = (((y + rel) % 4) * 2 + (c + k) % 2) * 4 + i
            copy_b(ref, n, g, place[block]).start()

    tile = 256
    for k in range(8):
        for s in (2 * k, 2 * k + 1):
            copy_a(s).wait()
            for at in (2 * s, 2 * s + 1):
                for g in range(2):
                    copy_b(b_refs[0], 0, g, at).wait()

        @pl.loop(0, rows // tile)
        def _(t):
            at = pl.ds(pl.multiple_of(t * tile, tile), tile)
            for g in range(2):
                part = jnp.dot(a_s[at, pl.ds(k * 2 * kw, 2 * kw)], b_s[g, pl.ds(k * 2 * kw, 2 * kw), :], preferred_element_type=jnp.float32)
                if k == 0:
                    acc[g, at, :] = part
                else:
                    acc[g, at, :] += part

    def chunk(rel, t):
        at = pl.ds(pl.multiple_of(((layer + rel) % 4) * BS, BS), BS)
        return acc[t // 4, at, pl.ds((t % 4) * BS, BS)]

    for rel, o_ref in zip((1, 2, 3), o_refs):
        codes = []
        for t in range(8):
            v, code = quantize(chunk(rel, t))
            o_ref[pl.ds(t * BS, BS), :] = v
            codes.append(code)
        codes = jnp.concatenate(codes + codes, axis=0)
        o_ref[pl.ds(8 * BS, PAD), :] = codes.astype(jnp.int32).astype(jnp.int16)
    for t in range(8):
        own_ref[pl.ds(t * BS, BS), :] = chunk(0, t)


def matmul(pos, owner, a, b):
    _, rows, kw = a[0].shape
    cols = b[0].shape[2]
    depth = 16 * kw
    return pl.pallas_call(
        mm_kernel,
        out_shape=[jax.ShapeDtypeStruct((8 * BS, BS), jnp.float32)] + [jax.ShapeDtypeStruct((8 * BS + PAD, BS), jnp.int16)] * 3,
        in_specs=[pl.BlockSpec(memory_space=pltpu.SMEM)] * 2 + [pl.BlockSpec(memory_space=pl.ANY)] * (NA + NB),
        out_specs=[pl.BlockSpec(memory_space=pltpu.VMEM)] * 4,
        scratch_shapes=[
            pltpu.SMEM((32,), jnp.int32),
            pltpu.VMEM((rows, depth), jnp.bfloat16),
            pltpu.VMEM((2, depth, cols), jnp.bfloat16),
            pltpu.VMEM((2, rows, cols), jnp.float32),
            pltpu.SemaphoreType.DMA((16,)),
            pltpu.SemaphoreType.DMA((2, 32)),
        ],
        compiler_params=pltpu.CompilerParams(vmem_limit_bytes=32 << 20),
        cost_estimate=pl.CostEstimate(flops=4 * rows * cols * depth, bytes_accessed=14 << 20, transcendentals=0),
        name="matmul",
    )(pos, owner, *a, *b)


def total_kernel(pos_ref, own_ref, *refs):
    v_refs, o_refs = refs[:3], refs[3:]
    other = (pos_ref[1] + pos_ref[3]) % 2
    for g, o_ref in zip((other, 1 - other), o_refs):
        for n in range(4):
            at = pl.ds(pl.multiple_of((g * 4 + n) * BS, BS), BS)
            total = own_ref[at, :]
            for v_ref in v_refs:
                codes = v_ref[pl.ds(8 * BS, PAD), :].astype(jnp.int32).astype(jnp.float32)
                code = jnp.where(g == 0, codes[n:n + 1, :], codes[4 + n:5 + n, :])
                total = total + v_ref[at, :].astype(jnp.int32).astype(jnp.float32) * (jnp.exp2(code * (1.0 / STEPS)) * (1.0 / LEVELS))
            o_ref[:, pl.ds(n * BS, BS)] = total.astype(jnp.bfloat16)


def total(pos, own, v):
    return pl.pallas_call(
        total_kernel,
        out_shape=[jax.ShapeDtypeStruct((BS, 4 * BS), jnp.bfloat16)] * 2,
        in_specs=[pl.BlockSpec(memory_space=pltpu.SMEM)] + [pl.BlockSpec(memory_space=pltpu.VMEM)] * 4,
        out_specs=[pl.BlockSpec(memory_space=pltpu.VMEM)] * 2,
        name="total",
    )(pos, own, *v)


def place_kernel(pos_ref, pat_ref, first_ref, second_ref, o_ref):
    q = pos_ref[3]
    for b, ref in ((q, first_ref), (1 - q, second_ref)):
        for n in range(4):
            keep = pat_ref[b, n].astype(jnp.float32).astype(jnp.bfloat16)
            cols = pl.ds(n * BS, BS)
            o_ref[pl.ds(pl.multiple_of(b * BS, BS), BS), cols] = ref[:, cols] * keep


def place(pos, pattern, first, second):
    return pl.pallas_call(
        place_kernel,
        out_shape=jax.ShapeDtypeStruct((2 * BS, 4 * BS), jnp.bfloat16),
        in_specs=[pl.BlockSpec(memory_space=pltpu.SMEM)] * 2 + [pl.BlockSpec(memory_space=pltpu.VMEM)] * 2,
        out_specs=pl.BlockSpec(memory_space=pltpu.VMEM),
        name="place",
    )(pos, pattern, first, second)


def shards(panel, in_pattern, slab, owner, out_pattern):
    row, col = lax.axis_index("row"), lax.axis_index("col")
    zl = col // 4
    pos = jnp.stack([row // 2, row % 2, zl // 2, zl % 2, col % 4, lax.axis_index("layer")])
    cat = lambda *v: jnp.concatenate(v, axis=0)
    own = slab[0]
    first, second = mask(pos, panel[:, 0, :], in_pattern[:, 0, :].T)
    with jax.named_scope("round0"):
        first = send(first, lambda y, c, zl, x, zh: (y, zl % 2, zl - zl % 2 + c, x, zh))
        second = send(second, lambda y, c, zl, x, zh: (y, 1 - zl % 2, zl - zl % 2 + c, x, zh))
        pair = send(own, lambda y, c, zl, x, zh: (y, c, zl ^ 1, x, zh))
        b1p, b1m = to_y(own, 1), to_y(own, -1)
        first, second, pair, b1p, b1m = lax.optimization_barrier((first, second, pair, b1p, b1m))
        near = jnp.stack([first, second])
    with jax.named_scope("round1"):
        far = send(near, lambda y, c, zl, x, zh: (y, c, zl ^ 2, x, zh))
        a1p, a1m = to_x(near, 1), to_x(near, -1)
        b2p, b2m = to_y(cat(b1p[:2], pair), 1), to_y(cat(b1m[2:], pair), -1)
        far, a1p, a1m, b2p, b2m = lax.optimization_barrier((far, a1p, a1m, b2p, b2m))
    with jax.named_scope("round2"):
        a2p, a2m = to_x(cat(a1p[:1], far), 1), to_x(cat(a1m[1:], far), -1)
        b3p, b3m = to_y(b2p[2:4], 1), to_y(b2m[4:], -1)
        c12 = to_core(cat(b1p, b1m, b2p, b2m))
        a2p, a2m, b3p, b3m, c12 = lax.optimization_barrier((a2p, a2m, b3p, b3m, c12))
    with jax.named_scope("round3"):
        a3p, a3m = to_x(a2p[1:2], 1), to_x(a2m[2:], -1)
        c3, c0 = to_core(cat(b3p, b3m)), to_core(cat(own, pair))
    own_part, *parts = matmul(
        pos, owner[0], (near, a1p, a1m, far, a2p, a2m, a3p, a3m), (own, pair, b1p, b1m, b2p, b2m, b3p, b3m, c0, c12, c3)
    )
    with jax.named_scope("layer_sums"):
        far_part = to_layer(parts[1], 2)
        parts = [to_layer(parts[0], 1), far_part, to_layer(parts[2], 3)]
    first, second = total(pos, own_part, parts)
    with jax.named_scope("product_pair"):
        first = send(first, lambda y, c, zl, x, zh: (y, zl % 2, zl - zl % 2 + c, x, zh))
        second = send(second, lambda y, c, zl, x, zh: (y, zl % 2, zl - zl % 2 + 1 - c, x, zh))
    return place(pos, out_pattern, first, second)


def solution(mesh):
    in_specs = (
        P("row", "layer", "col"),
        P("row", "layer", "col"),
        P("layer", "row", None, "col"),
        P("layer", None),
        P(("row", "layer"), "col"),
    )
    out_specs = P(("row", "layer"), "col")
    return jax.shard_map(shards, mesh=mesh, in_specs=in_specs, out_specs=out_specs, check_vma=False)
```

time: 201 us -> 205 us (1.020)
  the two profiles are of different devices: /device:TPU:15 before, /device:TPU:102 now
where the time goes in v3:
time: 205 us; the launch traced here: 204 us
  starting transfers between devices  87 us (42%)
  waiting for transfers between devices  85.3 us (42%)
  Pallas kernels  27.9 us (14%)
  local copies, waits for them, and re-layouts  2.93 us (1%)
    ppermute x24, starting transfers between devices, send(): return lax.ppermute(v, AXES, moves(f))  87 us
    ppermute x24, waiting for transfers between devices, send(): return lax.ppermute(v, AXES, moves(f))  85.3 us
    pallas_call x1, Pallas kernels, matmul(): pl.pallas_call(mm_kernel, out_shape=[jax.ShapeDtypeStruct((8 * BS, BS), j...  22 us
  transfers between devices with their start and end apart: 24, of which 12 were waited for; matrix products, arithmetic and copies ran while one was open for 1% of the time, Pallas kernels for 1%

profile of v3, /device:TPU:102, one launch (start us, length us, event | category | flops | bytes accessed | tf_op | source)
XLA Modules:
  0.0 204.3 jit_solution(8300871970435646942)
XLA Ops:
  2.0 3.5 %collective-permute-start.3 = (bf16[4,128,512]{2,1,0:T(8,128)(2,1)}, bf16[4,128,512]{2,1,0:T(8,128)(2,1)S(1)}, u32[]{:S(2)}, u32[]{:S(2)}) collective-permute-start(bf16[4,128,512]{2,1,0:T(8,128)(2,1)} %bitcast.15), channel_id=1, source_target_pairs={{0,128},{1,129},{2,130},{3,131},{4,132},{5,133},{6,134},{7,135},{8... | collective-permute-start | bytes 1572872 | tf_op jit(solution)/shard_map/round0/ppermute | solution.py:27
  5.5 3.6 %collective-permute-start.4 = (bf16[4,128,512]{2,1,0:T(8,128)(2,1)}, bf16[4,128,512]{2,1,0:T(8,128)(2,1)S(1)}, u32[]{:S(2)}, u32[]{:S(2)}) collective-permute-start(bf16[4,128,512]{2,1,0:T(8,128)(2,1)} %bitcast.16), channel_id=1, source_target_pairs={{0,384},{1,385},{2,386},{3,387},{4,388},{5,389},{6,390},{7,391},{8... | collective-permute-start | bytes 1572872 | tf_op jit(solution)/shard_map/round0/ppermute | solution.py:27
  11.7 2.5 %collective-permute-start = (bf16[512,256]{1,0:T(8,128)(2,1)}, bf16[512,256]{1,0:T(8,128)(2,1)S(1)}, u32[]{:S(2)}, u32[]{:S(2)}) collective-permute-start(bf16[512,256]{1,0:T(8,128)(2,1)} %get-tuple-element.28), channel_id=1, source_target_pairs={{0,0},{1,1},{2,2},{3,3},{4,4},{5,5},{6,6},{7,7},{8,8},{9,9},{10,10... | collective-permute-start | bytes 786440 | tf_op jit(solution)/shard_map/round0/ppermute | solution.py:27
  14.2 2.9 %collective-permute-start.1 = (bf16[512,256]{1,0:T(8,128)(2,1)}, bf16[512,256]{1,0:T(8,128)(2,1)S(1)}, u32[]{:S(2)}, u32[]{:S(2)}) collective-permute-start(bf16[512,256]{1,0:T(8,128)(2,1)} %get-tuple-element.29), channel_id=1, source_target_pairs={{0,64},{1,65},{2,66},{3,67},{4,68},{5,69},{6,70},{7,71},{8,72},{9,... | collective-permute-start | bytes 786440 | tf_op jit(solution)/shard_map/round0/ppermute | solution.py:27
  17.1 2.5 %collective-permute-done = bf16[512,256]{1,0:T(8,128)(2,1)S(1)} collective-permute-done((bf16[512,256]{1,0:T(8,128)(2,1)}, bf16[512,256]{1,0:T(8,128)(2,1)S(1)}, u32[]{:S(2)}, u32[]{:S(2)}) %collective-permute-start) | collective-permute-done | bytes 262176 | tf_op jit(solution)/shard_map/round0/ppermute | solution.py:27
  21.5 3.1 %collective-permute-start.8 = (bf16[6,128,512]{2,1,0:T(8,128)(2,1)S(1)}, bf16[6,128,512]{2,1,0:T(8,128)(2,1)S(1)}, u32[]{:S(2)}, u32[]{:S(2)}) collective-permute-start(bf16[6,128,512]{2,1,0:T(8,128)(2,1)S(1)} %get-tuple-element.54), channel_id=1, source_target_pairs={{0,128},{1,129},{2,130},{3,131},{4,132},{5,133},{6,134},{7,135},{8... | collective-permute-start | bytes 2359304 | tf_op jit(solution)/shard_map/round1/ppermute | solution.py:27
  24.6 4.0 %collective-permute-start.9 = (bf16[6,128,512]{2,1,0:T(8,128)(2,1)S(1)}, bf16[6,128,512]{2,1,0:T(8,128)(2,1)S(1)}, u32[]{:S(2)}, u32[]{:S(2)}) collective-permute-start(bf16[6,128,512]{2,1,0:T(8,128)(2,1)S(1)} %get-tuple-element.53), channel_id=1, source_target_pairs={{0,384},{1,385},{2,386},{3,387},{4,388},{5,389},{6,390},{7,391},{8... | collective-permute-start | bytes 2359304 | tf_op jit(solution)/shard_map/round1/ppermute | solution.py:27
  30.6 6.7 %collective-permute-start.6 = (bf16[2,512,256]{2,1,0:T(8,128)(2,1)S(1)}, bf16[2,512,256]{2,1,0:T(8,128)(2,1)S(1)}, u32[]{:S(2)}, u32[]{:S(2)}) collective-permute-start(bf16[2,512,256]{2,1,0:T(8,128)(2,1)S(1)} %pad_maximum_fusion.6.refs_0_), channel_id=1, source_target_pairs={{0,4},{1,5},{2,6},{3,7},{4,8},{5,9},{6,10},{7,11},{8,12},{9,13},{1... | collective-permute-start | bytes 1572872 | tf_op jit(solution)/shard_map/round1/ppermute | solution.py:27
  39.2 17.0 %collective-permute-done.5.refs_3_ = bf16[2,512,256]{2,1,0:T(8,128)(2,1)S(1)} collective-permute-done((bf16[2,512,256]{2,1,0:T(8,128)(2,1)S(1)}, bf16[2,512,256]{2,1,0:T(8,128)(2,1)S(1)}, u32[]{:S(2)}, u32[]{:S(2)}) %collective-permute-start.5) | collective-permute-done | bytes 524320 | tf_op jit(solution)/shard_map/round1/ppermute | solution.py:27
  58.9 4.8 %collective-permute-start.10 = (bf16[3,512,256]{2,1,0:T(8,128)(2,1)S(1)}, bf16[3,512,256]{2,1,0:T(8,128)(2,1)S(1)}, u32[]{:S(2)}, u32[]{:S(2)}) collective-permute-start(bf16[3,512,256]{2,1,0:T(8,128)(2,1)S(1)} %get-tuple-element.52), channel_id=1, source_target_pairs={{0,4},{1,5},{2,6},{3,7},{4,8},{5,9},{6,10},{7,11},{8,12},{9,13},{1... | collective-permute-start | bytes 2359304 | tf_op jit(solution)/shard_map/round2/ppermute | solution.py:27
  69.8 7.3 %collective-permute-done.12.refs_14_ = bf16[2,128,512]{2,1,0:T(8,128)(2,1)S(1)} collective-permute-done((bf16[2,128,512]{2,1,0:T(8,128)(2,1)S(1)}, bf16[2,128,512]{2,1,0:T(8,128)(2,1)S(1)}, u32[]{:S(2)}, u32[]{:S(2)}) %collective-permute-start.12) | collective-permute-done | bytes 262176 | tf_op jit(solution)/shard_map/round2/ppermute | solution.py:27
  79.1 7.4 %collective-permute-done.13.refs_15_ = bf16[2,128,512]{2,1,0:T(8,128)(2,1)S(1)} collective-permute-done((bf16[2,128,512]{2,1,0:T(8,128)(2,1)S(1)}, bf16[2,128,512]{2,1,0:T(8,128)(2,1)S(1)}, u32[]{:S(2)}, u32[]{:S(2)}) %collective-permute-start.13) | collective-permute-done | bytes 262176 | tf_op jit(solution)/shard_map/round2/ppermute | solution.py:27
  88.5 4.5 %collective-permute-start.15 = (bf16[1,512,256]{2,1,0:T(8,128)(2,1)S(1)}, bf16[1,512,256]{2,1,0:T(8,128)(2,1)S(1)}, u32[]{:S(2)}, u32[]{:S(2)}) collective-permute-start(bf16[1,512,256]{2,1,0:T(8,128)(2,1)S(1)} %slice.30), channel_id=1, source_target_pairs={{0,4},{1,5},{2,6},{3,7},{4,8},{5,9},{6,10},{7,11},{8,12},{9,13},{1... | collective-permute-start | bytes 786440 | tf_op jit(solution)/shard_map/round3/ppermute | solution.py:27
  95.0 4.2 %collective-permute-done.15.refs_6_ = bf16[1,512,256]{2,1,0:T(8,128)(2,1)S(1)} collective-permute-done((bf16[1,512,256]{2,1,0:T(8,128)(2,1)S(1)}, bf16[1,512,256]{2,1,0:T(8,128)(2,1)S(1)}, u32[]{:S(2)}, u32[]{:S(2)}) %collective-permute-start.15) | collective-permute-done | bytes 262176 | tf_op jit(solution)/shard_map/round3/ppermute | solution.py:27
  99.2 5.4 %collective-permute-done.16.refs_7_ = bf16[1,512,256]{2,1,0:T(8,128)(2,1)S(1)} collective-permute-done((bf16[1,512,256]{2,1,0:T(8,128)(2,1)S(1)}, bf16[1,512,256]{2,1,0:T(8,128)(2,1)S(1)}, u32[]{:S(2)}, u32[]{:S(2)}) %collective-permute-start.16) | collective-permute-done | bytes 262176 | tf_op jit(solution)/shard_map/round3/ppermute | solution.py:27
  104.6 22.0 %matmul.1 = (f32[1024,128]{1,0:T(8,128)S(1)}, s16[1040,128]{1,0:T(8,128)(2,1)S(1)}, s16[1040,128]{1,0:T(8,128)(2,1)S(1)}, s16[1040,128]{1,0:T(8,128)(2,1)S(1)}) custom-call(s32[6]{0:T(128)S(1)} %copy-done.2, s32[32]{0:T(128)S(1)} %bitcast.19, bf16[2,512,256]{2,1,0:T(8,128)(2,1)S(1)} %pad_maximum_fusion.6.refs_0_, ...), custom_call_target="tpu_custom_call" | custom-call | flops 4294967296 | bytes 14680064 | tf_op jit(solution)/shard_map/matmul/pallas_call | solution.py:173
  127.4 6.8 %collective-permute-start.19 = (s16[1040,128]{1,0:T(8,128)(2,1)S(1)}, s16[1040,128]{1,0:T(8,128)(2,1)S(1)}, u32[]{:S(2)}, u32[]{:S(2)}) collective-permute-start(s16[1040,128]{1,0:T(8,128)(2,1)S(1)} %get-tuple-element.46), channel_id=1, source_target_pairs={{0,1},{1,2},{2,3},{3,0},{4,5},{5,6},{6,7},{7,4},{8,9},{9,10},{10,1... | collective-permute-start | bytes 798728 | tf_op jit(solution)/shard_map/layer_sums/ppermute | solution.py:27
  134.3 9.0 %collective-permute-start.20 = (s16[1040,128]{1,0:T(8,128)(2,1)S(1)}, s16[1040,128]{1,0:T(8,128)(2,1)S(1)}, u32[]{:S(2)}, u32[]{:S(2)}) collective-permute-start(s16[1040,128]{1,0:T(8,128)(2,1)S(1)} %get-tuple-element.47), channel_id=1, source_target_pairs={{0,2},{1,3},{2,0},{3,1},{4,6},{5,7},{6,4},{7,5},{8,10},{9,11},{10,... | collective-permute-start | bytes 798728 | tf_op jit(solution)/shard_map/layer_sums/ppermute | solution.py:27
  143.3 5.5 %collective-permute-start.21 = (s16[1040,128]{1,0:T(8,128)(2,1)S(1)}, s16[1040,128]{1,0:T(8,128)(2,1)S(1)}, u32[]{:S(2)}, u32[]{:S(2)}) collective-permute-start(s16[1040,128]{1,0:T(8,128)(2,1)S(1)} %get-tuple-element.48), channel_id=1, source_target_pairs={{0,3},{1,0},{2,1},{3,2},{4,7},{5,4},{6,5},{7,6},{8,11},{9,8},{10,9... | collective-permute-start | bytes 798728 | tf_op jit(solution)/shard_map/layer_sums/ppermute | solution.py:27
  148.7 23.4 %collective-permute-done.19.refs_0_ = s16[1040,128]{1,0:T(8,128)(2,1)S(1)} collective-permute-done((s16[1040,128]{1,0:T(8,128)(2,1)S(1)}, s16[1040,128]{1,0:T(8,128)(2,1)S(1)}, u32[]{:S(2)}, u32[]{:S(2)}) %collective-permute-start.19) | collective-permute-done | bytes 266272 | tf_op jit(solution)/shard_map/layer_sums/ppermute | solution.py:27
  172.1 8.1 %collective-permute-done.20.refs_1_ = s16[1040,128]{1,0:T(8,128)(2,1)S(1)} collective-permute-done((s16[1040,128]{1,0:T(8,128)(2,1)S(1)}, s16[1040,128]{1,0:T(8,128)(2,1)S(1)}, u32[]{:S(2)}, u32[]{:S(2)}) %collective-permute-start.20) | collective-permute-done | bytes 266272 | tf_op jit(solution)/shard_map/layer_sums/ppermute | solution.py:27
  180.2 3.1 %collective-permute-done.21.refs_2_ = s16[1040,128]{1,0:T(8,128)(2,1)S(1)} collective-permute-done((s16[1040,128]{1,0:T(8,128)(2,1)S(1)}, s16[1040,128]{1,0:T(8,128)(2,1)S(1)}, u32[]{:S(2)}, u32[]{:S(2)}) %collective-permute-start.21) | collective-permute-done | bytes 266272 | tf_op jit(solution)/shard_map/layer_sums/ppermute | solution.py:27
  186.2 8.6 %collective-permute-start.22 = (bf16[128,512]{1,0:T(8,128)(2,1)}, bf16[128,512]{1,0:T(8,128)(2,1)S(1)}, u32[]{:S(2)}, u32[]{:S(2)}) collective-permute-start(bf16[128,512]{1,0:T(8,128)(2,1)} %get-tuple-element.49), channel_id=1, source_target_pairs={{0,0},{1,1},{2,2},{3,3},{4,4},{5,5},{6,6},{7,7},{8,8},{9,9},{10,10... | collective-permute-start | bytes 393224 | tf_op jit(solution)/shard_map/product_pair/ppermute | solution.py:27
  197.7 4.2 %collective-permute-done.23.second_ref = bf16[128,512]{1,0:T(8,128)(2,1)S(1)} collective-permute-done((bf16[128,512]{1,0:T(8,128)(2,1)}, bf16[128,512]{1,0:T(8,128)(2,1)S(1)}, u32[]{:S(2)}, u32[]{:S(2)}) %collective-permute-start.23) | collective-permute-done | bytes 131104 | tf_op jit(solution)/shard_map/product_pair/ppermute | solution.py:27
  (61 shorter events, 33.7 us)
Async XLA Ops:
  0.0 21.3 %collective-permute-start.2 = (bf16[4,128,512]{2,1,0:T(8,128)(2,1)}, bf16[4,128,512]{2,1,0:T(8,128)(2,1)S(1)}, u32[]{:S(2)}, u32[]{:S(2)}) collective-permute-start(bf16[4,128,512]{2,1,0:T(8,128)(2,1)} %bitcast.14), channel_id=1, source_target_pairs={{0,16},{1,17},{2,18},{3,19},{4,20},{5,21},{6,22},{7,23},{8,24},{9,... | collective-permute-start | bytes 1572872 | tf_op jit(solution)/shard_map/round0/ppermute | solution.py:27
  2.0 19.3 %collective-permute-start.3 = (bf16[4,128,512]{2,1,0:T(8,128)(2,1)}, bf16[4,128,512]{2,1,0:T(8,128)(2,1)S(1)}, u32[]{:S(2)}, u32[]{:S(2)}) collective-permute-start(bf16[4,128,512]{2,1,0:T(8,128)(2,1)} %bitcast.15), channel_id=1, source_target_pairs={{0,128},{1,129},{2,130},{3,131},{4,132},{5,133},{6,134},{7,135},{8... | collective-permute-start | bytes 1572872 | tf_op jit(solution)/shard_map/round0/ppermute | solution.py:27
  5.5 15.8 %collective-permute-start.4 = (bf16[4,128,512]{2,1,0:T(8,128)(2,1)}, bf16[4,128,512]{2,1,0:T(8,128)(2,1)S(1)}, u32[]{:S(2)}, u32[]{:S(2)}) collective-permute-start(bf16[4,128,512]{2,1,0:T(8,128)(2,1)} %bitcast.16), channel_id=1, source_target_pairs={{0,384},{1,385},{2,386},{3,387},{4,388},{5,389},{6,390},{7,391},{8... | collective-permute-start | bytes 1572872 | tf_op jit(solution)/shard_map/round0/ppermute | solution.py:27
  11.7 7.9 %collective-permute-start = (bf16[512,256]{1,0:T(8,128)(2,1)}, bf16[512,256]{1,0:T(8,128)(2,1)S(1)}, u32[]{:S(2)}, u32[]{:S(2)}) collective-permute-start(bf16[512,256]{1,0:T(8,128)(2,1)} %get-tuple-element.28), channel_id=1, source_target_pairs={{0,0},{1,1},{2,2},{3,3},{4,4},{5,5},{6,6},{7,7},{8,8},{9,9},{10,10... | collective-permute-start | bytes 786440 | tf_op jit(solution)/shard_map/round0/ppermute | solution.py:27
  14.2 7.1 %collective-permute-start.1 = (bf16[512,256]{1,0:T(8,128)(2,1)}, bf16[512,256]{1,0:T(8,128)(2,1)S(1)}, u32[]{:S(2)}, u32[]{:S(2)}) collective-permute-start(bf16[512,256]{1,0:T(8,128)(2,1)} %get-tuple-element.29), channel_id=1, source_target_pairs={{0,64},{1,65},{2,66},{3,67},{4,68},{5,69},{6,70},{7,71},{8,72},{9,... | collective-permute-start | bytes 786440 | tf_op jit(solution)/shard_map/round0/ppermute | solution.py:27
  21.5 34.7 %collective-permute-start.8 = (bf16[6,128,512]{2,1,0:T(8,128)(2,1)S(1)}, bf16[6,128,512]{2,1,0:T(8,128)(2,1)S(1)}, u32[]{:S(2)}, u32[]{:S(2)}) collective-permute-start(bf16[6,128,512]{2,1,0:T(8,128)(2,1)S(1)} %get-tuple-element.54), channel_id=1, source_target_pairs={{0,128},{1,129},{2,130},{3,131},{4,132},{5,133},{6,134},{7,135},{8... | collective-permute-start | bytes 2359304 | tf_op jit(solution)/shard_map/round1/ppermute | solution.py:27
  24.6 31.7 %collective-permute-start.9 = (bf16[6,128,512]{2,1,0:T(8,128)(2,1)S(1)}, bf16[6,128,512]{2,1,0:T(8,128)(2,1)S(1)}, u32[]{:S(2)}, u32[]{:S(2)}) collective-permute-start(bf16[6,128,512]{2,1,0:T(8,128)(2,1)S(1)} %get-tuple-element.53), channel_id=1, source_target_pairs={{0,384},{1,385},{2,386},{3,387},{4,388},{5,389},{6,390},{7,391},{8... | collective-permute-start | bytes 2359304 | tf_op jit(solution)/shard_map/round1/ppermute | solution.py:27
  28.6 27.6 %collective-permute-start.5 = (bf16[2,512,256]{2,1,0:T(8,128)(2,1)S(1)}, bf16[2,512,256]{2,1,0:T(8,128)(2,1)S(1)}, u32[]{:S(2)}, u32[]{:S(2)}) collective-permute-start(bf16[2,512,256]{2,1,0:T(8,128)(2,1)S(1)} %pad_maximum_fusion.6.refs_0_), channel_id=1, source_target_pairs={{0,32},{1,33},{2,34},{3,35},{4,36},{5,37},{6,38},{7,39},{8,40},{9,... | collective-permute-start | bytes 1572872 | tf_op jit(solution)/shard_map/round1/ppermute | solution.py:27
  30.6 25.7 %collective-permute-start.6 = (bf16[2,512,256]{2,1,0:T(8,128)(2,1)S(1)}, bf16[2,512,256]{2,1,0:T(8,128)(2,1)S(1)}, u32[]{:S(2)}, u32[]{:S(2)}) collective-permute-start(bf16[2,512,256]{2,1,0:T(8,128)(2,1)S(1)} %pad_maximum_fusion.6.refs_0_), channel_id=1, source_target_pairs={{0,4},{1,5},{2,6},{3,7},{4,8},{5,9},{6,10},{7,11},{8,12},{9,13},{1... | collective-permute-start | bytes 1572872 | tf_op jit(solution)/shard_map/round1/ppermute | solution.py:27
  37.3 19.0 %collective-permute-start.7 = (bf16[2,512,256]{2,1,0:T(8,128)(2,1)S(1)}, bf16[2,512,256]{2,1,0:T(8,128)(2,1)S(1)}, u32[]{:S(2)}, u32[]{:S(2)}) collective-permute-start(bf16[2,512,256]{2,1,0:T(8,128)(2,1)S(1)} %pad_maximum_fusion.6.refs_0_), channel_id=1, source_target_pairs={{0,12},{1,13},{2,14},{3,15},{4,0},{5,1},{6,2},{7,3},{8,4},{9,5},{1... | collective-permute-start | bytes 1572872 | tf_op jit(solution)/shard_map/round1/ppermute | solution.py:27
  56.6 29.9 %collective-permute-start.14 = (bf16[20,128,512]{2,1,0:T(8,128)(2,1)S(1)}, bf16[20,128,512]{2,1,0:T(8,128)(2,1)S(1)}, u32[]{:S(2)}, u32[]{:S(2)}) collective-permute-start(bf16[20,128,512]{2,1,0:T(8,128)(2,1)S(1)} %pad_maximum_fusion), channel_id=1, source_target_pairs={{0,64},{1,65},{2,66},{3,67},{4,68},{5,69},{6,70},{7,71},{8,72},{9,... | collective-permute-start | bytes 7864328 | tf_op jit(solution)/shard_map/round2/ppermute | solution.py:27
  58.9 27.6 %collective-permute-start.10 = (bf16[3,512,256]{2,1,0:T(8,128)(2,1)S(1)}, bf16[3,512,256]{2,1,0:T(8,128)(2,1)S(1)}, u32[]{:S(2)}, u32[]{:S(2)}) collective-permute-start(bf16[3,512,256]{2,1,0:T(8,128)(2,1)S(1)} %get-tuple-element.52), channel_id=1, source_target_pairs={{0,4},{1,5},{2,6},{3,7},{4,8},{5,9},{6,10},{7,11},{8,12},{9,13},{1... | collective-permute-start | bytes 2359304 | tf_op jit(solution)/shard_map/round2/ppermute | solution.py:27
  63.8 22.7 %collective-permute-start.11 = (bf16[3,512,256]{2,1,0:T(8,128)(2,1)S(1)}, bf16[3,512,256]{2,1,0:T(8,128)(2,1)S(1)}, u32[]{:S(2)}, u32[]{:S(2)}) collective-permute-start(bf16[3,512,256]{2,1,0:T(8,128)(2,1)S(1)} %get-tuple-element.51), channel_id=1, source_target_pairs={{0,12},{1,13},{2,14},{3,15},{4,0},{5,1},{6,2},{7,3},{8,4},{9,5},{1... | collective-permute-start | bytes 2359304 | tf_op jit(solution)/shard_map/round2/ppermute | solution.py:27
  65.7 11.4 %collective-permute-start.12 = (bf16[2,128,512]{2,1,0:T(8,128)(2,1)S(1)}, bf16[2,128,512]{2,1,0:T(8,128)(2,1)S(1)}, u32[]{:S(2)}, u32[]{:S(2)}) collective-permute-start(bf16[2,128,512]{2,1,0:T(8,128)(2,1)S(1)} %slice.28), channel_id=1, source_target_pairs={{0,128},{1,129},{2,130},{3,131},{4,132},{5,133},{6,134},{7,135},{8... | collective-permute-start | bytes 786440 | tf_op jit(solution)/shard_map/round2/ppermute | solution.py:27
  67.8 27.2 %collective-permute-start.17 = (bf16[8,128,512]{2,1,0:T(8,128)(2,1)S(1)}, bf16[8,128,512]{2,1,0:T(8,128)(2,1)S(1)}, u32[]{:S(2)}, u32[]{:S(2)}) collective-permute-start(bf16[8,128,512]{2,1,0:T(8,128)(2,1)S(1)} %pad_maximum_fusion.1), channel_id=1, source_target_pairs={{0,64},{1,65},{2,66},{3,67},{4,68},{5,69},{6,70},{7,71},{8,72},{9,... | collective-permute-start | bytes 3145736 | tf_op jit(solution)/shard_map/round3/ppermute | solution.py:27
  77.1 9.3 %collective-permute-start.13 = (bf16[2,128,512]{2,1,0:T(8,128)(2,1)S(1)}, bf16[2,128,512]{2,1,0:T(8,128)(2,1)S(1)}, u32[]{:S(2)}, u32[]{:S(2)}) collective-permute-start(bf16[2,128,512]{2,1,0:T(8,128)(2,1)S(1)} %slice.29), channel_id=1, source_target_pairs={{0,384},{1,385},{2,386},{3,387},{4,388},{5,389},{6,390},{7,391},{8... | collective-permute-start | bytes 786440 | tf_op jit(solution)/shard_map/round2/ppermute | solution.py:27
  86.5 18.1 %collective-permute-start.18 = (bf16[4,128,512]{2,1,0:T(8,128)(2,1)S(1)}, bf16[4,128,512]{2,1,0:T(8,128)(2,1)S(1)}, u32[]{:S(2)}, u32[]{:S(2)}) collective-permute-start(bf16[4,128,512]{2,1,0:T(8,128)(2,1)S(1)} %pad_maximum_fusion.7), channel_id=1, source_target_pairs={{0,64},{1,65},{2,66},{3,67},{4,68},{5,69},{6,70},{7,71},{8,72},{9,... | collective-permute-start | bytes 1572872 | tf_op jit(solution)/shard_map/round3/ppermute | solution.py:27
  88.5 10.7 %collective-permute-start.15 = (bf16[1,512,256]{2,1,0:T(8,128)(2,1)S(1)}, bf16[1,512,256]{2,1,0:T(8,128)(2,1)S(1)}, u32[]{:S(2)}, u32[]{:S(2)}) collective-permute-start(bf16[1,512,256]{2,1,0:T(8,128)(2,1)S(1)} %slice.30), channel_id=1, source_target_pairs={{0,4},{1,5},{2,6},{3,7},{4,8},{5,9},{6,10},{7,11},{8,12},{9,13},{1... | collective-permute-start | bytes 786440 | tf_op jit(solution)/shard_map/round3/ppermute | solution.py:27
  93.1 11.5 %collective-permute-start.16 = (bf16[1,512,256]{2,1,0:T(8,128)(2,1)S(1)}, bf16[1,512,256]{2,1,0:T(8,128)(2,1)S(1)}, u32[]{:S(2)}, u32[]{:S(2)}) collective-permute-start(bf16[1,512,256]{2,1,0:T(8,128)(2,1)S(1)} %slice.31), channel_id=1, source_target_pairs={{0,12},{1,13},{2,14},{3,15},{4,0},{5,1},{6,2},{7,3},{8,4},{9,5},{1... | collective-permute-start | bytes 786440 | tf_op jit(solution)/shard_map/round3/ppermute | solution.py:27
  127.4 44.7 %collective-permute-start.19 = (s16[1040,128]{1,0:T(8,128)(2,1)S(1)}, s16[1040,128]{1,0:T(8,128)(2,1)S(1)}, u32[]{:S(2)}, u32[]{:S(2)}) collective-permute-start(s16[1040,128]{1,0:T(8,128)(2,1)S(1)} %get-tuple-element.46), channel_id=1, source_target_pairs={{0,1},{1,2},{2,3},{3,0},{4,5},{5,6},{6,7},{7,4},{8,9},{9,10},{10,1... | collective-permute-start | bytes 798728 | tf_op jit(solution)/shard_map/layer_sums/ppermute | solution.py:27
  134.3 46.0 %collective-permute-start.20 = (s16[1040,128]{1,0:T(8,128)(2,1)S(1)}, s16[1040,128]{1,0:T(8,128)(2,1)S(1)}, u32[]{:S(2)}, u32[]{:S(2)}) collective-permute-start(s16[1040,128]{1,0:T(8,128)(2,1)S(1)} %get-tuple-element.47), channel_id=1, source_target_pairs={{0,2},{1,3},{2,0},{3,1},{4,6},{5,7},{6,4},{7,5},{8,10},{9,11},{10,... | collective-permute-start | bytes 798728 | tf_op jit(solution)/shard_map/layer_sums/ppermute | solution.py:27
  143.3 40.0 %collective-permute-start.21 = (s16[1040,128]{1,0:T(8,128)(2,1)S(1)}, s16[1040,128]{1,0:T(8,128)(2,1)S(1)}, u32[]{:S(2)}, u32[]{:S(2)}) collective-permute-start(s16[1040,128]{1,0:T(8,128)(2,1)S(1)} %get-tuple-element.48), channel_id=1, source_target_pairs={{0,3},{1,0},{2,1},{3,2},{4,7},{5,4},{6,5},{7,6},{8,11},{9,8},{10,9... | collective-permute-start | bytes 798728 | tf_op jit(solution)/shard_map/layer_sums/ppermute | solution.py:27
  186.2 11.5 %collective-permute-start.22 = (bf16[128,512]{1,0:T(8,128)(2,1)}, bf16[128,512]{1,0:T(8,128)(2,1)S(1)}, u32[]{:S(2)}, u32[]{:S(2)}) collective-permute-start(bf16[128,512]{1,0:T(8,128)(2,1)} %get-tuple-element.49), channel_id=1, source_target_pairs={{0,0},{1,1},{2,2},{3,3},{4,4},{5,5},{6,6},{7,7},{8,8},{9,9},{10,10... | collective-permute-start | bytes 393224 | tf_op jit(solution)/shard_map/product_pair/ppermute | solution.py:27
  194.8 7.1 %collective-permute-start.23 = (bf16[128,512]{1,0:T(8,128)(2,1)}, bf16[128,512]{1,0:T(8,128)(2,1)S(1)}, u32[]{:S(2)}, u32[]{:S(2)}) collective-permute-start(bf16[128,512]{1,0:T(8,128)(2,1)} %get-tuple-element.50), channel_id=1, source_target_pairs={{0,16},{1,17},{2,18},{3,19},{4,20},{5,21},{6,22},{7,23},{8,24},{9,... | collective-permute-start | bytes 393224 | tf_op jit(solution)/shard_map/product_pair/ppermute | solution.py:27
  (9 other events, 113.4 us)

commit v4 on v3

v4 whole, which is shorter than its diff:
```python
import itertools

import jax
import jax.numpy as jnp
from jax import lax
from jax.experimental import pallas as pl
from jax.experimental.pallas import tpu as pltpu
from jax.sharding import PartitionSpec as P

AXES = ("row", "col", "layer")
BS = 128
LEVELS = 32700.0
TINY = 1e-33
STEPS = 8.0
PAD = 16


def moves(f):
    pairs = []
    for y, c, zl, x, zh in itertools.product(range(4), range(2), range(4), range(4), range(4)):
        y2, c2, zl2, x2, zh2 = f(y, c, zl, x, zh)
        pairs.append((((y * 2 + c) * 16 + zl * 4 + x) * 4 + zh, ((y2 * 2 + c2) * 16 + zl2 * 4 + x2) * 4 + zh2))
    return pairs


def send(v, f):
    return lax.ppermute(v, AXES, moves(f))


def to_x(v, d):
    return send(v, lambda y, c, zl, x, zh: (y, c, zl, (x + d) % 4, zh))


def to_y(v, d):
    return send(v, lambda y, c, zl, x, zh: ((y + d) % 4, c, zl, x, zh))


def to_layer(v, d):
    return send(v, lambda y, c, zl, x, zh: (y, c, zl, x, (zh + d) % 4))


def to_core(v):
    return send(v, lambda y, c, zl, x, zh: (y, 1 - c, zl, x, zh))


def mask_kernel(pos_ref, pat_ref, x_ref, first_ref, second_ref):
    q = pos_ref[3]
    for h, o_ref in ((q, first_ref), (1 - q, second_ref)):
        for b in range(o_ref.shape[0] // BS):
            for j in range(x_ref.shape[1] // BS):
                block = 2 * b + h
                keep = pat_ref[j, block].astype(jnp.float32).astype(jnp.bfloat16)
                cols = pl.ds(j * BS, BS)
                o_ref[pl.ds(b * BS, BS), cols] = x_ref[pl.ds(pl.multiple_of(block * BS, BS), BS), cols] * keep


def mask(pos, panel, pattern):
    rows, width = panel.shape
    return pl.pallas_call(
        mask_kernel,
        out_shape=[jax.ShapeDtypeStruct((rows // 2, width), panel.dtype)] * 2,
        in_specs=[pl.BlockSpec(memory_space=pltpu.SMEM)] * 2 + [pl.BlockSpec(memory_space=pltpu.VMEM)],
        out_specs=[pl.BlockSpec(memory_space=pltpu.VMEM)] * 2,
        name="mask",
    )(pos, pattern, panel)


PANEL = (
    ((0, 0, 0), (0, 0, 1)),
    ((0, 3, 0), (0, 3, 1)),
    ((0, 1, 0), (0, 1, 1)),
    ((1, 0, 0), (1, 0, 1)),
    ((0, 2, 0), (1, 3, 0), (1, 3, 1)),
    ((0, 2, 1), (1, 1, 0), (1, 1, 1)),
    ((1, 2, 0),),
    ((1, 2, 1),),
)
SLAB = (
    (0, 0, 4, 0, 0, 0, 0),
    (1, 0, 4, 1, 0, 0, 0),
    (2, 0, 4, 0, 0, 3, 0),
    (3, 0, 4, 0, 0, 1, 0),
    (4, 0, 2, 0, 0, 2, 0),
    (4, 2, 4, 1, 0, 3, 0),
    (5, 0, 2, 0, 0, 2, 2),
    (5, 2, 4, 1, 0, 1, 0),
    (6, 0, 2, 1, 0, 2, 0),
    (7, 0, 2, 1, 0, 2, 2),
    (8, 0, 4, 0, 1, 0, 0),
    (8, 4, 4, 1, 1, 0, 0),
    (9, 0, 4, 0, 1, 3, 0),
    (9, 4, 4, 0, 1, 1, 0),
    (9, 8, 2, 0, 1, 2, 0),
    (9, 10, 4, 1, 1, 3, 0),
    (9, 14, 2, 0, 1, 2, 2),
    (9, 16, 4, 1, 1, 1, 0),
    (10, 0, 2, 1, 1, 2, 0),
    (10, 2, 2, 1, 1, 2, 2),
)
NA, NB = 8, 11


def quantize(tiles, o_ref):
    codes = []
    for t, v in enumerate(tiles):
        top = jnp.max(jnp.abs(v), axis=0, keepdims=True)
        code = jnp.ceil(jnp.log2(jnp.maximum(top, TINY)) * STEPS)
        v = jnp.round(v * (jnp.exp2(code * (-1.0 / STEPS)) * LEVELS)).astype(jnp.int32)
        o_ref[pl.ds(t * BS, BS), :] = v.astype(jnp.int16)
        codes.append(code)
    codes = jnp.concatenate(codes * (PAD // len(codes)), axis=0)
    o_ref[pl.ds(len(tiles) * BS, PAD), :] = codes.astype(jnp.int32).astype(jnp.int16)


def scales(v_ref, tiles):
    codes = v_ref[pl.ds(tiles * BS, PAD), :].astype(jnp.int32).astype(jnp.float32)
    return jnp.exp2(codes * (1.0 / STEPS)) * (1.0 / LEVELS)


def values(v_ref, at):
    return v_ref[at, :].astype(jnp.int32).astype(jnp.float32)


def product(chunks, pos_ref, owner_ref, a_refs, b_refs, a_s):
    y, c, p, x, layer = pos_ref[0], pos_ref[1], pos_ref[2], pos_ref[4], pos_ref[5]
    for ref, group in zip(a_refs, PANEL):
        for n, (batch, rel, i) in enumerate(group):
            col = (2 * ((p + batch) % 2) + (c + i) % 2) * 4 + (x + rel) % 4
            for u in range(2):
                block = owner_ref[2 * col + u]
                row = block // 4
                at = ((row + c) % 2) * 16 + ((row // 2 + 4 - y) % 4) * 4 + block % 4
                at = pl.ds(pl.multiple_of(at * BS, BS), BS)
                for k, chunk in enumerate(chunks):
                    rows = pl.ds(pl.multiple_of(((layer + chunk) % 4) * BS, BS), BS)
                    a_s[pl.ds(k * BS, BS), at] = ref[n, rows, pl.ds(u * BS, BS)]
    for g in range(2):
        total = None
        for array, first, blocks, half, core, rel, i in SLAB:
            if half != g:
                continue
            at = pl.ds((core * 16 + rel * 4 + i) * BS, blocks * BS)
            b = b_refs[array][pl.ds(first, blocks)].reshape(blocks * BS, 4 * BS)
            part = jnp.dot(a_s[:, at], b, preferred_element_type=jnp.float32)
            total = part if total is None else total + part
        yield g, total


def far_kernel(pos_ref, owner_ref, *refs):
    a_refs, b_refs, (o0_ref, o1_ref, a_s) = refs[:NA], refs[NA:NA + NB], refs[NA + NB:]
    for g, total in product((2,), pos_ref, owner_ref, a_refs, b_refs, a_s):
        quantize([total[:, n * BS:(n + 1) * BS] for n in range(4)], (o0_ref, o1_ref)[g])


def rest_kernel(pos_ref, owner_ref, *refs):
    a_refs, b_refs, (*o_refs, a_s) = refs[:NA], refs[NA:NA + NB], refs[NA + NB:]
    for g, total in product((0, 1, 3), pos_ref, owner_ref, a_refs, b_refs, a_s):
        for k, o_ref in enumerate(o_refs):
            o_ref[g] = total[k * BS:(k + 1) * BS]


def matmul(kernel, name, chunks, out_shape, pos, owner, a, b):
    depth = 32 * BS
    return pl.pallas_call(
        kernel,
        out_shape=out_shape,
        in_specs=[pl.BlockSpec(memory_space=pltpu.SMEM)] * 2 + [pl.BlockSpec(memory_space=pltpu.VMEM)] * (NA + NB),
        out_specs=[pl.BlockSpec(memory_space=pltpu.VMEM)] * len(out_shape),
        scratch_shapes=[pltpu.VMEM((chunks * BS, depth), jnp.bfloat16)],
        compiler_params=pltpu.CompilerParams(vmem_limit_bytes=32 << 20),
        cost_estimate=pl.CostEstimate(flops=2 * chunks * BS * 8 * BS * depth, bytes_accessed=1 << 20, transcendentals=0),
        name=name,
    )(pos, owner, *a, *b)


def add_kernel(own1_ref, own3_ref, got1_ref, got3_ref, o1_ref, o3_ref):
    for half, own_ref, got_ref, o_ref in ((0, own1_ref, got1_ref, o1_ref), (1, own3_ref, got3_ref, o3_ref)):
        scale = scales(got_ref, 4)
        tiles = []
        for t in range(8):
            v = own_ref[t // 4, :, pl.ds((t % 4) * BS, BS)]
            if t // 4 == half:
                n = t % 4
                v = v + values(got_ref, pl.ds(n * BS, BS)) * scale[n:n + 1, :]
            tiles.append(v)
        quantize(tiles, o_ref)


def add(own1, own3, got1, got3):
    return pl.pallas_call(
        add_kernel,
        out_shape=[jax.ShapeDtypeStruct((8 * BS + PAD, BS), jnp.int16)] * 2,
        in_specs=[pl.BlockSpec(memory_space=pltpu.VMEM)] * 4,
        out_specs=[pl.BlockSpec(memory_space=pltpu.VMEM)] * 2,
        name="add",
    )(own1, own3, got1, got3)


def total_kernel(pos_ref, own_ref, *refs):
    v_refs, o_refs = refs[:2], refs[2:]
    other = (pos_ref[1] + pos_ref[3]) % 2
    found = [scales(v_ref, 8) for v_ref in v_refs]
    for g, o_ref in zip((other, 1 - other), o_refs):
        for n in range(4):
            at = pl.ds(pl.multiple_of((g * 4 + n) * BS, BS), BS)
            total = own_ref[g, :, pl.ds(n * BS, BS)]
            for v_ref, scale in zip(v_refs, found):
                total = total + values(v_ref, at) * jnp.where(g == 0, scale[n:n + 1, :], scale[4 + n:5 + n, :])
            o_ref[:, pl.ds(n * BS, BS)] = total.astype(jnp.bfloat16)


def total(pos, own, v):
    return pl.pallas_call(
        total_kernel,
        out_shape=[jax.ShapeDtypeStruct((BS, 4 * BS), jnp.bfloat16)] * 2,
        in_specs=[pl.BlockSpec(memory_space=pltpu.SMEM)] + [pl.BlockSpec(memory_space=pltpu.VMEM)] * 3,
        out_specs=[pl.BlockSpec(memory_space=pltpu.VMEM)] * 2,
        name="total",
    )(pos, own, *v)


def place_kernel(pos_ref, pat_ref, first_ref, second_ref, o_ref):
    q = pos_ref[3]
    for b, ref in ((q, first_ref), (1 - q, second_ref)):
        for n in range(4):
            keep = pat_ref[b, n].astype(jnp.float32).astype(jnp.bfloat16)
            cols = pl.ds(n * BS, BS)
            o_ref[pl.ds(pl.multiple_of(b * BS, BS), BS), cols] = ref[:, cols] * keep


def place(pos, pattern, first, second):
    return pl.pallas_call(
        place_kernel,
        out_shape=jax.ShapeDtypeStruct((2 * BS, 4 * BS), jnp.bfloat16),
        in_specs=[pl.BlockSpec(memory_space=pltpu.SMEM)] * 2 + [pl.BlockSpec(memory_space=pltpu.VMEM)] * 2,
        out_specs=pl.BlockSpec(memory_space=pltpu.VMEM),
        name="place",
    )(pos, pattern, first, second)


def shards(panel, in_pattern, slab, owner, out_pattern):
    row, col = lax.axis_index("row"), lax.axis_index("col")
    zl = col // 4
    pos = jnp.stack([row // 2, row % 2, zl // 2, zl % 2, col % 4, lax.axis_index("layer")])
    cat = lambda *v: jnp.concatenate(v, axis=0)
    own = slab[0]
    first, second = mask(pos, panel[:, 0, :], in_pattern[:, 0, :].T)
    with jax.named_scope("round0"):
        first = send(first, lambda y, c, zl, x, zh: (y, zl % 2, zl - zl % 2 + c, x, zh))
        second = send(second, lambda y, c, zl, x, zh: (y, 1 - zl % 2, zl - zl % 2 + c, x, zh))
        pair = send(own, lambda y, c, zl, x, zh: (y, c, zl ^ 1, x, zh))
        b1p, b1m = to_y(own, 1), to_y(own, -1)
        first, second, pair, b1p, b1m = lax.optimization_barrier((first, second, pair, b1p, b1m))
        near = jnp.stack([first, second])
    with jax.named_scope("round1"):
        far = send(near, lambda y, c, zl, x, zh: (y, c, zl ^ 2, x, zh))
        a1p, a1m = to_x(near, 1), to_x(near, -1)
        b2p, b2m = to_y(cat(b1p[:2], pair), 1), to_y(cat(b1m[2:], pair), -1)
        far, a1p, a1m, b2p, b2m = lax.optimization_barrier((far, a1p, a1m, b2p, b2m))
    with jax.named_scope("round2"):
        a2p, a2m = to_x(cat(a1p[:1], far), 1), to_x(cat(a1m[1:], far), -1)
        b3p, b3m = to_y(b2p[2:4], 1), to_y(b2m[4:], -1)
        c12 = to_core(cat(b1p, b1m, b2p, b2m))
        a2p, a2m, b3p, b3m, c12, late = lax.optimization_barrier((a2p, a2m, b3p, b3m, c12, pair))
    with jax.named_scope("round3"):
        a3p, a3m = to_x(a2p[1:2], 1), to_x(a2m[2:], -1)
        c3, c0 = to_core(cat(b3p, b3m)), to_core(cat(own, late))
    a = (near, a1p, a1m, far, a2p, a2m, a3p, a3m)
    b = (own, pair, b1p, b1m, b2p, b2m, b3p, b3m, c0, c12, c3)
    half_shape = [jax.ShapeDtypeStruct((4 * BS + PAD, BS), jnp.int16)] * 2
    whole_shape = [jax.ShapeDtypeStruct((2, BS, 4 * BS), jnp.float32)] * 3
    far1, far3 = matmul(far_kernel, "matmul_far", 1, half_shape, pos, owner[0], a, b)
    with jax.named_scope("layer_halves"):
        got1, got3 = to_layer(far1, 1), to_layer(far3, -1)
    own_part, part1, part3 = matmul(rest_kernel, "matmul_rest", 3, whole_shape, pos, owner[0], a, b)
    part1, part3 = add(part1, part3, got1, got3)
    with jax.named_scope("layer_sums"):
        got1, got3 = to_layer(part1, 1), to_layer(part3, -1)
    first, second = total(pos, own_part, (got1, got3))
    with jax.named_scope("product_pair"):
        first = send(first, lambda y, c, zl, x, zh: (y, zl % 2, zl - zl % 2 + c, x, zh))
        second = send(second, lambda y, c, zl, x, zh: (y, zl % 2, zl - zl % 2 + 1 - c, x, zh))
    return place(pos, out_pattern, first, second)


def solution(mesh):
    in_specs = (
        P("row", "layer", "col"),
        P("row", "layer", "col"),
        P("layer", "row", None, "col"),
        P("layer", None),
        P(("row", "layer"), "col"),
    )
    out_specs = P(("row", "layer"), "col")
    return jax.shard_map(shards, mesh=mesh, in_specs=in_specs, out_specs=out_specs, check_vma=False)
```

time: 205 us -> 181 us (0.88)
  the two profiles are of different devices: /device:TPU:102 before, /device:TPU:71 now
where the time goes in v4:
time: 181 us; the launch traced here: 180 us
  starting transfers between devices  109 us (60%)
  waiting for transfers between devices  49.1 us (27%)
  Pallas kernels  15.5 us (9%)
  local copies, waits for them, and re-layouts  5.2 us (3%)
    ppermute x25, starting transfers between devices, send(): return lax.ppermute(v, AXES, moves(f))  109 us
    ppermute x25, waiting for transfers between devices, send(): return lax.ppermute(v, AXES, moves(f))  49.1 us
    pallas_call x2, Pallas kernels, matmul(): pl.pallas_call(kernel, out_shape=out_shape, in_specs=[pl.BlockSpec(memory...  7.48 us
    unnamed x24, local copies, waits for them, and re-layouts  4.43 us
  transfers between devices with their start and end apart: 25, of which 13 were waited for; matrix products, arithmetic and copies ran while one was open for 1% of the time, Pallas kernels for 4%

profile of v4, /device:TPU:71, one launch (start us, length us, event | category | flops | bytes accessed | tf_op | source)
XLA Modules:
  0.0 180.2 jit_solution(4506556322841826)
XLA Ops:
  0.0 3.5 %collective-permute-start.2 = (bf16[4,128,512]{2,1,0:T(8,128)(2,1)}, bf16[4,128,512]{2,1,0:T(8,128)(2,1)S(1)}, u32[]{:S(2)}, u32[]{:S(2)}) collective-permute-start(bf16[4,128,512]{2,1,0:T(8,128)(2,1)} %bitcast.14), channel_id=1, source_target_pairs={{0,16},{1,17},{2,18},{3,19},{4,20},{5,21},{6,22},{7,23},{8,24},{9,... | collective-permute-start | bytes 1572872 | tf_op jit(solution)/shard_map/round0/ppermute | solution.py:27
  3.5 3.2 %collective-permute-start.3 = (bf16[4,128,512]{2,1,0:T(8,128)(2,1)}, bf16[4,128,512]{2,1,0:T(8,128)(2,1)S(1)}, u32[]{:S(2)}, u32[]{:S(2)}) collective-permute-start(bf16[4,128,512]{2,1,0:T(8,128)(2,1)} %bitcast.15), channel_id=1, source_target_pairs={{0,128},{1,129},{2,130},{3,131},{4,132},{5,133},{6,134},{7,135},{8... | collective-permute-start | bytes 1572872 | tf_op jit(solution)/shard_map/round0/ppermute | solution.py:27
  6.8 3.4 %collective-permute-start.4 = (bf16[4,128,512]{2,1,0:T(8,128)(2,1)}, bf16[4,128,512]{2,1,0:T(8,128)(2,1)S(1)}, u32[]{:S(2)}, u32[]{:S(2)}) collective-permute-start(bf16[4,128,512]{2,1,0:T(8,128)(2,1)} %bitcast.16), channel_id=1, source_target_pairs={{0,384},{1,385},{2,386},{3,387},{4,388},{5,389},{6,390},{7,391},{8... | collective-permute-start | bytes 1572872 | tf_op jit(solution)/shard_map/round0/ppermute | solution.py:27
  17.7 3.2 %collective-permute-done = bf16[512,256]{1,0:T(8,128)(2,1)S(1)} collective-permute-done((bf16[512,256]{1,0:T(8,128)(2,1)}, bf16[512,256]{1,0:T(8,128)(2,1)S(1)}, u32[]{:S(2)}, u32[]{:S(2)}) %collective-permute-start) | collective-permute-done | bytes 262176 | tf_op jit(solution)/shard_map/round0/ppermute | solution.py:27
  24.6 4.3 %collective-permute-start.9 = (bf16[6,128,512]{2,1,0:T(8,128)(2,1)S(1)}, bf16[6,128,512]{2,1,0:T(8,128)(2,1)S(1)}, u32[]{:S(2)}, u32[]{:S(2)}) collective-permute-start(bf16[6,128,512]{2,1,0:T(8,128)(2,1)S(1)} %get-tuple-element.61), channel_id=1, source_target_pairs={{0,384},{1,385},{2,386},{3,387},{4,388},{5,389},{6,390},{7,391},{8... | collective-permute-start | bytes 2359304 | tf_op jit(solution)/shard_map/round1/ppermute | solution.py:27
  30.9 6.8 %collective-permute-start.6 = (bf16[2,512,256]{2,1,0:T(8,128)(2,1)S(1)}, bf16[2,512,256]{2,1,0:T(8,128)(2,1)S(1)}, u32[]{:S(2)}, u32[]{:S(2)}) collective-permute-start(bf16[2,512,256]{2,1,0:T(8,128)(2,1)S(1)} %pad_maximum_fusion.6.refs_0_), channel_id=1, source_target_pairs={{0,4},{1,5},{2,6},{3,7},{4,8},{5,9},{6,10},{7,11},{8,12},{9,13},{1... | collective-permute-start | bytes 1572872 | tf_op jit(solution)/shard_map/round1/ppermute | solution.py:27
  39.7 12.5 %collective-permute-done.5.refs_3_ = bf16[2,512,256]{2,1,0:T(8,128)(2,1)S(1)} collective-permute-done((bf16[2,512,256]{2,1,0:T(8,128)(2,1)S(1)}, bf16[2,512,256]{2,1,0:T(8,128)(2,1)S(1)}, u32[]{:S(2)}, u32[]{:S(2)}) %collective-permute-start.5) | collective-permute-done | bytes 524320 | tf_op jit(solution)/shard_map/round1/ppermute | solution.py:27
  52.6 5.0 %collective-permute-start.14 = (bf16[20,128,512]{2,1,0:T(8,128)(2,1)S(1)}, bf16[20,128,512]{2,1,0:T(8,128)(2,1)S(1)}, u32[]{:S(2)}, u32[]{:S(2)}) collective-permute-start(bf16[20,128,512]{2,1,0:T(8,128)(2,1)S(1)} %pad_maximum_fusion), channel_id=1, source_target_pairs={{0,64},{1,65},{2,66},{3,67},{4,68},{5,69},{6,70},{7,71},{8,72},{9,... | collective-permute-start | bytes 7864328 | tf_op jit(solution)/shard_map/round2/ppermute | solution.py:27
  57.8 5.9 %collective-permute-start.10 = (bf16[3,512,256]{2,1,0:T(8,128)(2,1)S(1)}, bf16[3,512,256]{2,1,0:T(8,128)(2,1)S(1)}, u32[]{:S(2)}, u32[]{:S(2)}) collective-permute-start(bf16[3,512,256]{2,1,0:T(8,128)(2,1)S(1)} %get-tuple-element.60), channel_id=1, source_target_pairs={{0,4},{1,5},{2,6},{3,7},{4,8},{5,9},{6,10},{7,11},{8,12},{9,13},{1... | collective-permute-start | bytes 2359304 | tf_op jit(solution)/shard_map/round2/ppermute | solution.py:27
  67.7 4.6 %collective-permute-start.13 = (bf16[2,128,512]{2,1,0:T(8,128)(2,1)S(1)}, bf16[2,128,512]{2,1,0:T(8,128)(2,1)S(1)}, u32[]{:S(2)}, u32[]{:S(2)}) collective-permute-start(bf16[2,128,512]{2,1,0:T(8,128)(2,1)S(1)} %slice.29), channel_id=1, source_target_pairs={{0,384},{1,385},{2,386},{3,387},{4,388},{5,389},{6,390},{7,391},{8... | collective-permute-start | bytes 786440 | tf_op jit(solution)/shard_map/round2/ppermute | solution.py:27
  72.3 4.2 %collective-permute-done.12.refs_14_ = bf16[2,128,512]{2,1,0:T(8,128)(2,1)S(1)} collective-permute-done((bf16[2,128,512]{2,1,0:T(8,128)(2,1)S(1)}, bf16[2,128,512]{2,1,0:T(8,128)(2,1)S(1)}, u32[]{:S(2)}, u32[]{:S(2)}) %collective-permute-start.12) | collective-permute-done | bytes 262176 | tf_op jit(solution)/shard_map/round2/ppermute | solution.py:27
  77.3 3.4 %collective-permute-done.10.refs_4_ = bf16[3,512,256]{2,1,0:T(8,128)(2,1)S(1)} collective-permute-done((bf16[3,512,256]{2,1,0:T(8,128)(2,1)S(1)}, bf16[3,512,256]{2,1,0:T(8,128)(2,1)S(1)}, u32[]{:S(2)}, u32[]{:S(2)}) %collective-permute-start.10) | collective-permute-done | bytes 786464 | tf_op jit(solution)/shard_map/round2/ppermute | solution.py:27
  80.7 5.0 %collective-permute-done.11.refs_5_ = bf16[3,512,256]{2,1,0:T(8,128)(2,1)S(1)} collective-permute-done((bf16[3,512,256]{2,1,0:T(8,128)(2,1)S(1)}, bf16[3,512,256]{2,1,0:T(8,128)(2,1)S(1)}, u32[]{:S(2)}, u32[]{:S(2)}) %collective-permute-start.11) | collective-permute-done | bytes 786464 | tf_op jit(solution)/shard_map/round2/ppermute | solution.py:27
  92.8 3.4 %collective-permute-start.16 = (bf16[1,512,256]{2,1,0:T(8,128)(2,1)S(1)}, bf16[1,512,256]{2,1,0:T(8,128)(2,1)S(1)}, u32[]{:S(2)}, u32[]{:S(2)}) collective-permute-start(bf16[1,512,256]{2,1,0:T(8,128)(2,1)S(1)} %slice.31), channel_id=1, source_target_pairs={{0,12},{1,13},{2,14},{3,15},{4,0},{5,1},{6,2},{7,3},{8,4},{9,5},{1... | collective-permute-start | bytes 786440 | tf_op jit(solution)/shard_map/round3/ppermute | solution.py:27
  96.2 3.9 %collective-permute-done.15.refs_6_ = bf16[1,512,256]{2,1,0:T(8,128)(2,1)S(1)} collective-permute-done((bf16[1,512,256]{2,1,0:T(8,128)(2,1)S(1)}, bf16[1,512,256]{2,1,0:T(8,128)(2,1)S(1)}, u32[]{:S(2)}, u32[]{:S(2)}) %collective-permute-start.15) | collective-permute-done | bytes 262176 | tf_op jit(solution)/shard_map/round3/ppermute | solution.py:27
  100.1 3.2 %collective-permute-done.16.refs_7_ = bf16[1,512,256]{2,1,0:T(8,128)(2,1)S(1)} collective-permute-done((bf16[1,512,256]{2,1,0:T(8,128)(2,1)S(1)}, bf16[1,512,256]{2,1,0:T(8,128)(2,1)S(1)}, u32[]{:S(2)}, u32[]{:S(2)}) %collective-permute-start.16) | collective-permute-done | bytes 262176 | tf_op jit(solution)/shard_map/round3/ppermute | solution.py:27
  105.8 3.8 %collective-permute-start.19 = (s16[528,128]{1,0:T(8,128)(2,1)S(1)}, s16[528,128]{1,0:T(8,128)(2,1)S(1)}, u32[]{:S(2)}, u32[]{:S(2)}) collective-permute-start(s16[528,128]{1,0:T(8,128)(2,1)S(1)} %get-tuple-element.53), channel_id=1, source_target_pairs={{0,1},{1,2},{2,3},{3,0},{4,5},{5,6},{6,7},{7,4},{8,9},{9,10},{10,1... | collective-permute-start | bytes 405512 | tf_op jit(solution)/shard_map/layer_halves/ppermute | solution.py:27
  109.6 5.4 %collective-permute-start.20 = (s16[528,128]{1,0:T(8,128)(2,1)S(1)}, s16[528,128]{1,0:T(8,128)(2,1)S(1)}, u32[]{:S(2)}, u32[]{:S(2)}) collective-permute-start(s16[528,128]{1,0:T(8,128)(2,1)S(1)} %get-tuple-element.54), channel_id=1, source_target_pairs={{0,3},{1,0},{2,1},{3,2},{4,7},{5,4},{6,5},{7,6},{8,11},{9,8},{10,9... | collective-permute-start | bytes 405512 | tf_op jit(solution)/shard_map/layer_halves/ppermute | solution.py:27
  115.0 5.0 %matmul_rest.1 = (f32[2,128,512]{2,1,0:T(8,128)S(1)}, f32[2,128,512]{2,1,0:T(8,128)S(1)}, f32[2,128,512]{2,1,0:T(8,128)S(1)}) custom-call(s32[6]{0:T(128)S(1)} %copy-done.4, s32[32]{0:T(128)S(1)} %bitcast.21, bf16[2,512,256]{2,1,0:T(8,128)(2,1)S(1)} %pad_maximum_fusion.6.refs_0_, bf16[2,512,256]{2,1,0:T(8,128)(2,1)S(1)} %collective-permute-done.6.refs_1_, ...), custom_call_target="tpu_custom_call" | custom-call | flops 3221225472 | bytes 1048576 | tf_op jit(solution)/shard_map/matmul_rest/pallas_call | solution.py:164
  125.4 5.2 %collective-permute-start.21 = (s16[1040,128]{1,0:T(8,128)(2,1)}, s16[1040,128]{1,0:T(8,128)(2,1)S(1)}, u32[]{:S(2)}, u32[]{:S(2)}) collective-permute-start(s16[1040,128]{1,0:T(8,128)(2,1)} %get-tuple-element.55), channel_id=1, source_target_pairs={{0,1},{1,2},{2,3},{3,0},{4,5},{5,6},{6,7},{7,4},{8,9},{9,10},{10,1... | collective-permute-start | bytes 798728 | tf_op jit(solution)/shard_map/layer_sums/ppermute | solution.py:27
  130.6 4.0 %collective-permute-start.22 = (s16[1040,128]{1,0:T(8,128)(2,1)}, s16[1040,128]{1,0:T(8,128)(2,1)S(1)}, u32[]{:S(2)}, u32[]{:S(2)}) collective-permute-start(s16[1040,128]{1,0:T(8,128)(2,1)} %get-tuple-element.56), channel_id=1, source_target_pairs={{0,3},{1,0},{2,1},{3,2},{4,7},{5,4},{6,5},{7,6},{8,11},{9,8},{10,9... | collective-permute-start | bytes 798728 | tf_op jit(solution)/shard_map/layer_sums/ppermute | solution.py:27
  137.0 5.2 %collective-permute-done.22.refs_1_ = s16[1040,128]{1,0:T(8,128)(2,1)S(1)} collective-permute-done((s16[1040,128]{1,0:T(8,128)(2,1)}, s16[1040,128]{1,0:T(8,128)(2,1)S(1)}, u32[]{:S(2)}, u32[]{:S(2)}) %collective-permute-start.22) | collective-permute-done | bytes 266272 | tf_op jit(solution)/shard_map/layer_sums/ppermute | solution.py:27
  144.9 27.0 %collective-permute-start.23 = (bf16[128,512]{1,0:T(8,128)(2,1)}, bf16[128,512]{1,0:T(8,128)(2,1)S(1)}, u32[]{:S(2)}, u32[]{:S(2)}) collective-permute-start(bf16[128,512]{1,0:T(8,128)(2,1)} %get-tuple-element.57), channel_id=1, source_target_pairs={{0,0},{1,1},{2,2},{3,3},{4,4},{5,5},{6,6},{7,7},{8,8},{9,9},{10,10... | collective-permute-start | bytes 393224 | tf_op jit(solution)/shard_map/product_pair/ppermute | solution.py:27
  174.7 3.1 %collective-permute-done.24.second_ref = bf16[128,512]{1,0:T(8,128)(2,1)S(1)} collective-permute-done((bf16[128,512]{1,0:T(8,128)(2,1)}, bf16[128,512]{1,0:T(8,128)(2,1)S(1)}, u32[]{:S(2)}, u32[]{:S(2)}) %collective-permute-start.24) | collective-permute-done | bytes 131104 | tf_op jit(solution)/shard_map/product_pair/ppermute | solution.py:27
  (71 shorter events, 45.6 us)
Async XLA Ops:
  0.0 22.2 %collective-permute-start.2 = (bf16[4,128,512]{2,1,0:T(8,128)(2,1)}, bf16[4,128,512]{2,1,0:T(8,128)(2,1)S(1)}, u32[]{:S(2)}, u32[]{:S(2)}) collective-permute-start(bf16[4,128,512]{2,1,0:T(8,128)(2,1)} %bitcast.14), channel_id=1, source_target_pairs={{0,16},{1,17},{2,18},{3,19},{4,20},{5,21},{6,22},{7,23},{8,24},{9,... | collective-permute-start | bytes 1572872 | tf_op jit(solution)/shard_map/round0/ppermute | solution.py:27
  3.5 18.7 %collective-permute-start.3 = (bf16[4,128,512]{2,1,0:T(8,128)(2,1)}, bf16[4,128,512]{2,1,0:T(8,128)(2,1)S(1)}, u32[]{:S(2)}, u32[]{:S(2)}) collective-permute-start(bf16[4,128,512]{2,1,0:T(8,128)(2,1)} %bitcast.15), channel_id=1, source_target_pairs={{0,128},{1,129},{2,130},{3,131},{4,132},{5,133},{6,134},{7,135},{8... | collective-permute-start | bytes 1572872 | tf_op jit(solution)/shard_map/round0/ppermute | solution.py:27
  6.8 15.5 %collective-permute-start.4 = (bf16[4,128,512]{2,1,0:T(8,128)(2,1)}, bf16[4,128,512]{2,1,0:T(8,128)(2,1)S(1)}, u32[]{:S(2)}, u32[]{:S(2)}) collective-permute-start(bf16[4,128,512]{2,1,0:T(8,128)(2,1)} %bitcast.16), channel_id=1, source_target_pairs={{0,384},{1,385},{2,386},{3,387},{4,388},{5,389},{6,390},{7,391},{8... | collective-permute-start | bytes 1572872 | tf_op jit(solution)/shard_map/round0/ppermute | solution.py:27
  12.7 8.2 %collective-permute-start = (bf16[512,256]{1,0:T(8,128)(2,1)}, bf16[512,256]{1,0:T(8,128)(2,1)S(1)}, u32[]{:S(2)}, u32[]{:S(2)}) collective-permute-start(bf16[512,256]{1,0:T(8,128)(2,1)} %get-tuple-element.32), channel_id=1, source_target_pairs={{0,0},{1,1},{2,2},{3,3},{4,4},{5,5},{6,6},{7,7},{8,8},{9,9},{10,10... | collective-permute-start | bytes 786440 | tf_op jit(solution)/shard_map/round0/ppermute | solution.py:27
  15.8 6.4 %collective-permute-start.1 = (bf16[512,256]{1,0:T(8,128)(2,1)}, bf16[512,256]{1,0:T(8,128)(2,1)S(1)}, u32[]{:S(2)}, u32[]{:S(2)}) collective-permute-start(bf16[512,256]{1,0:T(8,128)(2,1)} %get-tuple-element.33), channel_id=1, source_target_pairs={{0,64},{1,65},{2,66},{3,67},{4,68},{5,69},{6,70},{7,71},{8,72},{9,... | collective-permute-start | bytes 786440 | tf_op jit(solution)/shard_map/round0/ppermute | solution.py:27
  22.4 29.8 %collective-permute-start.8 = (bf16[6,128,512]{2,1,0:T(8,128)(2,1)S(1)}, bf16[6,128,512]{2,1,0:T(8,128)(2,1)S(1)}, u32[]{:S(2)}, u32[]{:S(2)}) collective-permute-start(bf16[6,128,512]{2,1,0:T(8,128)(2,1)S(1)} %get-tuple-element.62), channel_id=1, source_target_pairs={{0,128},{1,129},{2,130},{3,131},{4,132},{5,133},{6,134},{7,135},{8... | collective-permute-start | bytes 2359304 | tf_op jit(solution)/shard_map/round1/ppermute | solution.py:27
  24.6 27.6 %collective-permute-start.9 = (bf16[6,128,512]{2,1,0:T(8,128)(2,1)S(1)}, bf16[6,128,512]{2,1,0:T(8,128)(2,1)S(1)}, u32[]{:S(2)}, u32[]{:S(2)}) collective-permute-start(bf16[6,128,512]{2,1,0:T(8,128)(2,1)S(1)} %get-tuple-element.61), channel_id=1, source_target_pairs={{0,384},{1,385},{2,386},{3,387},{4,388},{5,389},{6,390},{7,391},{8... | collective-permute-start | bytes 2359304 | tf_op jit(solution)/shard_map/round1/ppermute | solution.py:27
  29.0 23.2 %collective-permute-start.5 = (bf16[2,512,256]{2,1,0:T(8,128)(2,1)S(1)}, bf16[2,512,256]{2,1,0:T(8,128)(2,1)S(1)}, u32[]{:S(2)}, u32[]{:S(2)}) collective-permute-start(bf16[2,512,256]{2,1,0:T(8,128)(2,1)S(1)} %pad_maximum_fusion.6.refs_0_), channel_id=1, source_target_pairs={{0,32},{1,33},{2,34},{3,35},{4,36},{5,37},{6,38},{7,39},{8,40},{9,... | collective-permute-start | bytes 1572872 | tf_op jit(solution)/shard_map/round1/ppermute | solution.py:27
  30.9 21.3 %collective-permute-start.6 = (bf16[2,512,256]{2,1,0:T(8,128)(2,1)S(1)}, bf16[2,512,256]{2,1,0:T(8,128)(2,1)S(1)}, u32[]{:S(2)}, u32[]{:S(2)}) collective-permute-start(bf16[2,512,256]{2,1,0:T(8,128)(2,1)S(1)} %pad_maximum_fusion.6.refs_0_), channel_id=1, source_target_pairs={{0,4},{1,5},{2,6},{3,7},{4,8},{5,9},{6,10},{7,11},{8,12},{9,13},{1... | collective-permute-start | bytes 1572872 | tf_op jit(solution)/shard_map/round1/ppermute | solution.py:27
  37.8 14.4 %collective-permute-start.7 = (bf16[2,512,256]{2,1,0:T(8,128)(2,1)S(1)}, bf16[2,512,256]{2,1,0:T(8,128)(2,1)S(1)}, u32[]{:S(2)}, u32[]{:S(2)}) collective-permute-start(bf16[2,512,256]{2,1,0:T(8,128)(2,1)S(1)} %pad_maximum_fusion.6.refs_0_), channel_id=1, source_target_pairs={{0,12},{1,13},{2,14},{3,15},{4,0},{5,1},{6,2},{7,3},{8,4},{9,5},{1... | collective-permute-start | bytes 1572872 | tf_op jit(solution)/shard_map/round1/ppermute | solution.py:27
  52.6 33.1 %collective-permute-start.14 = (bf16[20,128,512]{2,1,0:T(8,128)(2,1)S(1)}, bf16[20,128,512]{2,1,0:T(8,128)(2,1)S(1)}, u32[]{:S(2)}, u32[]{:S(2)}) collective-permute-start(bf16[20,128,512]{2,1,0:T(8,128)(2,1)S(1)} %pad_maximum_fusion), channel_id=1, source_target_pairs={{0,64},{1,65},{2,66},{3,67},{4,68},{5,69},{6,70},{7,71},{8,72},{9,... | collective-permute-start | bytes 7864328 | tf_op jit(solution)/shard_map/round2/ppermute | solution.py:27
  57.8 22.9 %collective-permute-start.10 = (bf16[3,512,256]{2,1,0:T(8,128)(2,1)S(1)}, bf16[3,512,256]{2,1,0:T(8,128)(2,1)S(1)}, u32[]{:S(2)}, u32[]{:S(2)}) collective-permute-start(bf16[3,512,256]{2,1,0:T(8,128)(2,1)S(1)} %get-tuple-element.60), channel_id=1, source_target_pairs={{0,4},{1,5},{2,6},{3,7},{4,8},{5,9},{6,10},{7,11},{8,12},{9,13},{1... | collective-permute-start | bytes 2359304 | tf_op jit(solution)/shard_map/round2/ppermute | solution.py:27
  63.8 21.9 %collective-permute-start.11 = (bf16[3,512,256]{2,1,0:T(8,128)(2,1)S(1)}, bf16[3,512,256]{2,1,0:T(8,128)(2,1)S(1)}, u32[]{:S(2)}, u32[]{:S(2)}) collective-permute-start(bf16[3,512,256]{2,1,0:T(8,128)(2,1)S(1)} %get-tuple-element.59), channel_id=1, source_target_pairs={{0,12},{1,13},{2,14},{3,15},{4,0},{5,1},{6,2},{7,3},{8,4},{9,5},{1... | collective-permute-start | bytes 2359304 | tf_op jit(solution)/shard_map/round2/ppermute | solution.py:27
  65.7 10.7 %collective-permute-start.12 = (bf16[2,128,512]{2,1,0:T(8,128)(2,1)S(1)}, bf16[2,128,512]{2,1,0:T(8,128)(2,1)S(1)}, u32[]{:S(2)}, u32[]{:S(2)}) collective-permute-start(bf16[2,128,512]{2,1,0:T(8,128)(2,1)S(1)} %slice.28), channel_id=1, source_target_pairs={{0,128},{1,129},{2,130},{3,131},{4,132},{5,133},{6,134},{7,135},{8... | collective-permute-start | bytes 786440 | tf_op jit(solution)/shard_map/round2/ppermute | solution.py:27
  67.7 9.6 %collective-permute-start.13 = (bf16[2,128,512]{2,1,0:T(8,128)(2,1)S(1)}, bf16[2,128,512]{2,1,0:T(8,128)(2,1)S(1)}, u32[]{:S(2)}, u32[]{:S(2)}) collective-permute-start(bf16[2,128,512]{2,1,0:T(8,128)(2,1)S(1)} %slice.29), channel_id=1, source_target_pairs={{0,384},{1,385},{2,386},{3,387},{4,388},{5,389},{6,390},{7,391},{8... | collective-permute-start | bytes 786440 | tf_op jit(solution)/shard_map/round2/ppermute | solution.py:27
  85.8 17.5 %collective-permute-start.17 = (bf16[8,128,512]{2,1,0:T(8,128)(2,1)S(1)}, bf16[8,128,512]{2,1,0:T(8,128)(2,1)S(1)}, u32[]{:S(2)}, u32[]{:S(2)}) collective-permute-start(bf16[8,128,512]{2,1,0:T(8,128)(2,1)S(1)} %pad_maximum_fusion.1), channel_id=1, source_target_pairs={{0,64},{1,65},{2,66},{3,67},{4,68},{5,69},{6,70},{7,71},{8,72},{9,... | collective-permute-start | bytes 3145736 | tf_op jit(solution)/shard_map/round3/ppermute | solution.py:27
  88.9 14.4 %collective-permute-start.18 = (bf16[4,128,512]{2,1,0:T(8,128)(2,1)S(1)}, bf16[4,128,512]{2,1,0:T(8,128)(2,1)S(1)}, u32[]{:S(2)}, u32[]{:S(2)}) collective-permute-start(bf16[4,128,512]{2,1,0:T(8,128)(2,1)S(1)} %pad_maximum_fusion.7), channel_id=1, source_target_pairs={{0,64},{1,65},{2,66},{3,67},{4,68},{5,69},{6,70},{7,71},{8,72},{9,... | collective-permute-start | bytes 1572872 | tf_op jit(solution)/shard_map/round3/ppermute | solution.py:27
  90.9 9.3 %collective-permute-start.15 = (bf16[1,512,256]{2,1,0:T(8,128)(2,1)S(1)}, bf16[1,512,256]{2,1,0:T(8,128)(2,1)S(1)}, u32[]{:S(2)}, u32[]{:S(2)}) collective-permute-start(bf16[1,512,256]{2,1,0:T(8,128)(2,1)S(1)} %slice.30), channel_id=1, source_target_pairs={{0,4},{1,5},{2,6},{3,7},{4,8},{5,9},{6,10},{7,11},{8,12},{9,13},{1... | collective-permute-start | bytes 786440 | tf_op jit(solution)/shard_map/round3/ppermute | solution.py:27
  92.8 10.5 %collective-permute-start.16 = (bf16[1,512,256]{2,1,0:T(8,128)(2,1)S(1)}, bf16[1,512,256]{2,1,0:T(8,128)(2,1)S(1)}, u32[]{:S(2)}, u32[]{:S(2)}) collective-permute-start(bf16[1,512,256]{2,1,0:T(8,128)(2,1)S(1)} %slice.31), channel_id=1, source_target_pairs={{0,12},{1,13},{2,14},{3,15},{4,0},{5,1},{6,2},{7,3},{8,4},{9,5},{1... | collective-permute-start | bytes 786440 | tf_op jit(solution)/shard_map/round3/ppermute | solution.py:27
  105.8 16.6 %collective-permute-start.19 = (s16[528,128]{1,0:T(8,128)(2,1)S(1)}, s16[528,128]{1,0:T(8,128)(2,1)S(1)}, u32[]{:S(2)}, u32[]{:S(2)}) collective-permute-start(s16[528,128]{1,0:T(8,128)(2,1)S(1)} %get-tuple-element.53), channel_id=1, source_target_pairs={{0,1},{1,2},{2,3},{3,0},{4,5},{5,6},{6,7},{7,4},{8,9},{9,10},{10,1... | collective-permute-start | bytes 405512 | tf_op jit(solution)/shard_map/layer_halves/ppermute | solution.py:27
  109.6 12.8 %collective-permute-start.20 = (s16[528,128]{1,0:T(8,128)(2,1)S(1)}, s16[528,128]{1,0:T(8,128)(2,1)S(1)}, u32[]{:S(2)}, u32[]{:S(2)}) collective-permute-start(s16[528,128]{1,0:T(8,128)(2,1)S(1)} %get-tuple-element.54), channel_id=1, source_target_pairs={{0,3},{1,0},{2,1},{3,2},{4,7},{5,4},{6,5},{7,6},{8,11},{9,8},{10,9... | collective-permute-start | bytes 405512 | tf_op jit(solution)/shard_map/layer_halves/ppermute | solution.py:27
  125.4 11.6 %collective-permute-start.21 = (s16[1040,128]{1,0:T(8,128)(2,1)}, s16[1040,128]{1,0:T(8,128)(2,1)S(1)}, u32[]{:S(2)}, u32[]{:S(2)}) collective-permute-start(s16[1040,128]{1,0:T(8,128)(2,1)} %get-tuple-element.55), channel_id=1, source_target_pairs={{0,1},{1,2},{2,3},{3,0},{4,5},{5,6},{6,7},{7,4},{8,9},{9,10},{10,1... | collective-permute-start | bytes 798728 | tf_op jit(solution)/shard_map/layer_sums/ppermute | solution.py:27
  130.6 11.6 %collective-permute-start.22 = (s16[1040,128]{1,0:T(8,128)(2,1)}, s16[1040,128]{1,0:T(8,128)(2,1)S(1)}, u32[]{:S(2)}, u32[]{:S(2)}) collective-permute-start(s16[1040,128]{1,0:T(8,128)(2,1)} %get-tuple-element.56), channel_id=1, source_target_pairs={{0,3},{1,0},{2,1},{3,2},{4,7},{5,4},{6,5},{7,6},{8,11},{9,8},{10,9... | collective-permute-start | bytes 798728 | tf_op jit(solution)/shard_map/layer_sums/ppermute | solution.py:27
  144.9 29.9 %collective-permute-start.23 = (bf16[128,512]{1,0:T(8,128)(2,1)}, bf16[128,512]{1,0:T(8,128)(2,1)S(1)}, u32[]{:S(2)}, u32[]{:S(2)}) collective-permute-start(bf16[128,512]{1,0:T(8,128)(2,1)} %get-tuple-element.57), channel_id=1, source_target_pairs={{0,0},{1,1},{2,2},{3,3},{4,4},{5,5},{6,6},{7,7},{8,8},{9,9},{10,10... | collective-permute-start | bytes 393224 | tf_op jit(solution)/shard_map/product_pair/ppermute | solution.py:27
  (13 other events, 131.5 us)

commit v5 on v4

--- a/solution.py
+++ b/solution.py
@@ -31,16 +31,8 @@
     return send(v, lambda y, c, zl, x, zh: (y, c, zl, (x + d) % 4, zh))
 
 
-def to_y(v, d):
-    return send(v, lambda y, c, zl, x, zh: ((y + d) % 4, c, zl, x, zh))
-
-
 def to_layer(v, d):
     return send(v, lambda y, c, zl, x, zh: (y, c, zl, x, (zh + d) % 4))
-
-
-def to_core(v):
-    return send(v, lambda y, c, zl, x, zh: (y, 1 - c, zl, x, zh))
 
 
 def mask_kernel(pos_ref, pat_ref, x_ref, first_ref, second_ref):
@@ -65,39 +57,8 @@
     )(pos, pattern, panel)
 
 
-PANEL = (
-    ((0, 0, 0), (0, 0, 1)),
-    ((0, 3, 0), (0, 3, 1)),
-    ((0, 1, 0), (0, 1, 1)),
-    ((1, 0, 0), (1, 0, 1)),
-    ((0, 2, 0), (1, 3, 0), (1, 3, 1)),
-    ((0, 2, 1), (1, 1, 0), (1, 1, 1)),
-    ((1, 2, 0),),
-    ((1, 2, 1),),
-)
-SLAB = (
-    (0, 0, 4, 0, 0, 0, 0),
-    (1, 0, 4, 1, 0, 0, 0),
-    (2, 0, 4, 0, 0, 3, 0),
-    (3, 0, 4, 0, 0, 1, 0),
-    (4, 0, 2, 0, 0, 2, 0),
-    (4, 2, 4, 1, 0, 3, 0),
-    (5, 0, 2, 0, 0, 2, 2),
-    (5, 2, 4, 1, 0, 1, 0),
-    (6, 0, 2, 1, 0, 2, 0),
-    (7, 0, 2, 1, 0, 2, 2),
-    (8, 0, 4, 0, 1, 0, 0),
-    (8, 4, 4, 1, 1, 0, 0),
-    (9, 0, 4, 0, 1, 3, 0),
-    (9, 4, 4, 0, 1, 1, 0),
-    (9, 8, 2, 0, 1, 2, 0),
-    (9, 10, 4, 1, 1, 3, 0),
-    (9, 14, 2, 0, 1, 2, 2),
-    (9, 16, 4, 1, 1, 1, 0),
-    (10, 0, 2, 1, 1, 2, 0),
-    (10, 2, 2, 1, 1, 2, 2),
-)
-NA, NB = 8, 11
+PANEL = ((0, 0), (0, 3), (0, 1), (0, 2), (1, 0), (1, 3), (1, 1), (1, 2))
+NA = len(PANEL)
 
 
 def quantize(tiles, o_ref):
@@ -121,40 +82,34 @@
     return v_ref[at, :].astype(jnp.int32).astype(jnp.float32)
 
 
-def product(chunks, pos_ref, owner_ref, a_refs, b_refs, a_s):
-    y, c, p, x, layer = pos_ref[0], pos_ref[1], pos_ref[2], pos_ref[4], pos_ref[5]
-    for ref, group in zip(a_refs, PANEL):
-        for n, (batch, rel, i) in enumerate(group):
+def product(chunks, pos_ref, owner_ref, a_refs, b_ref, a_s):
+    c, p, x, layer = pos_ref[1], pos_ref[2], pos_ref[4], pos_ref[5]
+    for ref, (batch, rel) in zip(a_refs, PANEL):
+        for i in range(2):
             col = (2 * ((p + batch) % 2) + (c + i) % 2) * 4 + (x + rel) % 4
             for u in range(2):
-                block = owner_ref[2 * col + u]
-                row = block // 4
-                at = ((row + c) % 2) * 16 + ((row // 2 + 4 - y) % 4) * 4 + block % 4
-                at = pl.ds(pl.multiple_of(at * BS, BS), BS)
+                at = pl.ds(pl.multiple_of(owner_ref[2 * col + u] * BS, BS), BS)
                 for k, chunk in enumerate(chunks):
                     rows = pl.ds(pl.multiple_of(((layer + chunk) % 4) * BS, BS), BS)
-                    a_s[pl.ds(k * BS, BS), at] = ref[n, rows, pl.ds(u * BS, BS)]
+                    a_s[pl.ds(k * BS, BS), at] = ref[i, rows, pl.ds(u * BS, BS)]
     for g in range(2):
         total = None
-        for array, first, blocks, half, core, rel, i in SLAB:
-            if half != g:
-                continue
-            at = pl.ds((core * 16 + rel * 4 + i) * BS, blocks * BS)
-            b = b_refs[array][pl.ds(first, blocks)].reshape(blocks * BS, 4 * BS)
-            part = jnp.dot(a_s[:, at], b, preferred_element_type=jnp.float32)
+        for row in range(8):
+            b = b_ref[row, pl.ds(4 * g, 4)].reshape(4 * BS, 4 * BS)
+            part = jnp.dot(a_s[:, pl.ds(row * 4 * BS, 4 * BS)], b, preferred_element_type=jnp.float32)
             total = part if total is None else total + part
         yield g, total
 
 
 def far_kernel(pos_ref, owner_ref, *refs):
-    a_refs, b_refs, (o0_ref, o1_ref, a_s) = refs[:NA], refs[NA:NA + NB], refs[NA + NB:]
-    for g, total in product((2,), pos_ref, owner_ref, a_refs, b_refs, a_s):
+    a_refs, (b_ref, o0_ref, o1_ref, a_s) = refs[:NA], refs[NA:]
+    for g, total in product((2,), pos_ref, owner_ref, a_refs, b_ref, a_s):
         quantize([total[:, n * BS:(n + 1) * BS] for n in range(4)], (o0_ref, o1_ref)[g])
 
 
 def rest_kernel(pos_ref, owner_ref, *refs):
-    a_refs, b_refs, (*o_refs, a_s) = refs[:NA], refs[NA:NA + NB], refs[NA + NB:]
-    for g, total in product((0, 1, 3), pos_ref, owner_ref, a_refs, b_refs, a_s):
+    a_refs, (b_ref, *o_refs, a_s) = refs[:NA], refs[NA:]
+    for g, total in product((0, 1, 3), pos_ref, owner_ref, a_refs, b_ref, a_s):
         for k, o_ref in enumerate(o_refs):
             o_ref[g] = total[k * BS:(k + 1) * BS]
 
@@ -164,13 +119,13 @@
     return pl.pallas_call(
         kernel,
         out_shape=out_shape,
-        in_specs=[pl.BlockSpec(memory_space=pltpu.SMEM)] * 2 + [pl.BlockSpec(memory_space=pltpu.VMEM)] * (NA + NB),
+        in_specs=[pl.BlockSpec(memory_space=pltpu.SMEM)] * 2 + [pl.BlockSpec(memory_space=pltpu.VMEM)] * (NA + 1),
         out_specs=[pl.BlockSpec(memory_space=pltpu.VMEM)] * len(out_shape),
         scratch_shapes=[pltpu.VMEM((chunks * BS, depth), jnp.bfloat16)],
         compiler_params=pltpu.CompilerParams(vmem_limit_bytes=32 << 20),
         cost_estimate=pl.CostEstimate(flops=2 * chunks * BS * 8 * BS * depth, bytes_accessed=1 << 20, transcendentals=0),
         name=name,
-    )(pos, owner, *a, *b)
+    )(pos, owner, *a, b)
 
 
 def add_kernel(own1_ref, own3_ref, got1_ref, got3_ref, o1_ref, o3_ref):
@@ -242,31 +197,24 @@
     row, col = lax.axis_index("row"), lax.axis_index("col")
     zl = col // 4
     pos = jnp.stack([row // 2, row % 2, zl // 2, zl % 2, col % 4, lax.axis_index("layer")])
-    cat = lambda *v: jnp.concatenate(v, axis=0)
+    first, second = mask(pos, panel[:, 0, :], in_pattern[:, 0, :].T)
     own = slab[0]
-    first, second = mask(pos, panel[:, 0, :], in_pattern[:, 0, :].T)
-    with jax.named_scope("round0"):
+    with jax.named_scope("slab_pair"):
+        pair = send(own, lambda y, c, zl, x, zh: (y, c, zl ^ 1, x, zh))
+    with jax.named_scope("panel_pair"):
         first = send(first, lambda y, c, zl, x, zh: (y, zl % 2, zl - zl % 2 + c, x, zh))
         second = send(second, lambda y, c, zl, x, zh: (y, 1 - zl % 2, zl - zl % 2 + c, x, zh))
-        pair = send(own, lambda y, c, zl, x, zh: (y, c, zl ^ 1, x, zh))
-        b1p, b1m = to_y(own, 1), to_y(own, -1)
-        first, second, pair, b1p, b1m = lax.optimization_barrier((first, second, pair, b1p, b1m))
+        pair, first, second = lax.optimization_barrier((pair, first, second))
         near = jnp.stack([first, second])
-    with jax.named_scope("round1"):
+    with jax.named_scope("slab_rows"):
+        b = lax.all_gather(jnp.concatenate([own, pair]), "row", axis=0)
+    with jax.named_scope("panel_far"):
         far = send(near, lambda y, c, zl, x, zh: (y, c, zl ^ 2, x, zh))
-        a1p, a1m = to_x(near, 1), to_x(near, -1)
-        b2p, b2m = to_y(cat(b1p[:2], pair), 1), to_y(cat(b1m[2:], pair), -1)
-        far, a1p, a1m, b2p, b2m = lax.optimization_barrier((far, a1p, a1m, b2p, b2m))
-    with jax.named_scope("round2"):
-        a2p, a2m = to_x(cat(a1p[:1], far), 1), to_x(cat(a1m[1:], far), -1)
-        b3p, b3m = to_y(b2p[2:4], 1), to_y(b2m[4:], -1)
-        c12 = to_core(cat(b1p, b1m, b2p, b2m))
-        a2p, a2m, b3p, b3m, c12, late = lax.optimization_barrier((a2p, a2m, b3p, b3m, c12, pair))
-    with jax.named_scope("round3"):
-        a3p, a3m = to_x(a2p[1:2], 1), to_x(a2m[2:], -1)
-        c3, c0 = to_core(cat(b3p, b3m)), to_core(cat(own, late))
-    a = (near, a1p, a1m, far, a2p, a2m, a3p, a3m)
-    b = (own, pair, b1p, b1m, b2p, b2m, b3p, b3m, c0, c12, c3)
+    with jax.named_scope("panel_near_x"):
+        near_x = [to_x(near, d) for d in (1, 3, 2)]
+    with jax.named_scope("panel_far_x"):
+        far_x = [to_x(far, d) for d in (1, 3, 2)]
+    a = (near, *near_x, far, *far_x)
     half_shape = [jax.ShapeDtypeStruct((4 * BS + PAD, BS), jnp.int16)] * 2
     whole_shape = [jax.ShapeDtypeStruct((2, BS, 4 * BS), jnp.float32)] * 3
     far1, far3 = matmul(far_kernel, "matmul_far", 1, half_shape, pos, owner[0], a, b)

time: 181 us -> 190 us (1.050)
  the two profiles are of different devices: /device:TPU:71 before, /device:TPU:1 now
where the time goes in v5:
time: 190 us; the launch traced here: 189 us
  waiting for transfers between devices  79.5 us (42%)
  starting transfers between devices  65.2 us (34%)
  Pallas kernels  15 us (8%)
  between operations  13.7 us (7%)
  local copies, waits for them, and re-layouts  13.4 us (7%)
  other arithmetic  2.18 us (1%)
    ppermute x16, waiting for transfers between devices, send(): return lax.ppermute(v, AXES, moves(f))  74.1 us
    ppermute x16, starting transfers between devices, send(): return lax.ppermute(v, AXES, moves(f))  65.2 us
    unnamed x32, local copies, waits for them, and re-layouts  12.8 us
    pallas_call x2, Pallas kernels, matmul(): pl.pallas_call(kernel, out_shape=out_shape, in_specs=[pl.BlockSpec(memory...  6.99 us
    all_gather x1, waiting for transfers between devices, shards(): b = lax.all_gather(jnp.concatenate([own, pair]), 'row', axis=0)  5.43 us
  transfers between devices with their start and end apart: 17, of which 12 were waited for; matrix products, arithmetic and copies ran while one was open for 0% of the time, Pallas kernels for 4%

profile of v5, /device:TPU:1, one launch (start us, length us, event | category | flops | bytes accessed | tf_op | source)
XLA Modules:
  0.0 189.0 jit_solution(9722460409056048766)
XLA Ops:
  6.5 4.4 %collective-permute-start = (bf16[4,128,512]{2,1,0:T(8,128)(2,1)}, bf16[4,128,512]{2,1,0:T(8,128)(2,1)S(1)}, u32[]{:S(2)}, u32[]{:S(2)}) collective-permute-start(bf16[4,128,512]{2,1,0:T(8,128)(2,1)} %bitcast.20), channel_id=1, source_target_pairs={{0,16},{1,17},{2,18},{3,19},{4,20},{5,21},{6,22},{7,23},{8,24},{9,... | collective-permute-start | bytes 1572872 | tf_op jit(solution)/shard_map/slab_pair/ppermute | solution.py:27
  13.5 7.9 %collective-permute-start.1 = (bf16[512,256]{1,0:T(8,128)(2,1)}, bf16[512,256]{1,0:T(8,128)(2,1)S(1)}, u32[]{:S(2)}, u32[]{:S(2)}) collective-permute-start(bf16[512,256]{1,0:T(8,128)(2,1)} %get-tuple-element.19), channel_id=1, source_target_pairs={{0,0},{1,1},{2,2},{3,3},{4,4},{5,5},{6,6},{7,7},{8,8},{9,9},{10,10... | collective-permute-start | bytes 786440 | tf_op jit(solution)/shard_map/panel_pair/ppermute | solution.py:27
  23.4 3.4 %collective-permute-done.1 = bf16[512,256]{1,0:T(8,128)(2,1)S(1)} collective-permute-done((bf16[512,256]{1,0:T(8,128)(2,1)}, bf16[512,256]{1,0:T(8,128)(2,1)S(1)}, u32[]{:S(2)}, u32[]{:S(2)}) %collective-permute-start.1) | collective-permute-done | bytes 262176 | tf_op jit(solution)/shard_map/panel_pair/ppermute | solution.py:27
  30.8 4.9 %collective-permute-start.6 = (bf16[2,512,256]{2,1,0:T(8,128)(2,1)S(1)}, bf16[2,512,256]{2,1,0:T(8,128)(2,1)S(1)}, u32[]{:S(2)}, u32[]{:S(2)}) collective-permute-start(bf16[2,512,256]{2,1,0:T(8,128)(2,1)S(1)} %pad_maximum_fusion.1.refs_0_), channel_id=1, source_target_pairs={{0,32},{1,33},{2,34},{3,35},{4,36},{5,37},{6,38},{7,39},{8,40},{9,... | collective-permute-start | bytes 1572872 | tf_op jit(solution)/shard_map/panel_far/ppermute | solution.py:27
  35.7 3.1 %collective-permute-start.3 = (bf16[2,512,256]{2,1,0:T(8,128)(2,1)S(1)}, bf16[2,512,256]{2,1,0:T(8,128)(2,1)S(1)}, u32[]{:S(2)}, u32[]{:S(2)}) collective-permute-start(bf16[2,512,256]{2,1,0:T(8,128)(2,1)S(1)} %pad_maximum_fusion.1.refs_0_), channel_id=1, source_target_pairs={{0,4},{1,5},{2,6},{3,7},{4,8},{5,9},{6,10},{7,11},{8,12},{9,13},{1... | collective-permute-start | bytes 1572872 | tf_op jit(solution)/shard_map/panel_near_x/ppermute | solution.py:27
  38.8 3.4 %collective-permute-start.4 = (bf16[2,512,256]{2,1,0:T(8,128)(2,1)S(1)}, bf16[2,512,256]{2,1,0:T(8,128)(2,1)S(1)}, u32[]{:S(2)}, u32[]{:S(2)}) collective-permute-start(bf16[2,512,256]{2,1,0:T(8,128)(2,1)S(1)} %pad_maximum_fusion.1.refs_0_), channel_id=1, source_target_pairs={{0,12},{1,13},{2,14},{3,15},{4,0},{5,1},{6,2},{7,3},{8,4},{9,5},{1... | collective-permute-start | bytes 1572872 | tf_op jit(solution)/shard_map/panel_near_x/ppermute | solution.py:27
  42.2 3.4 %collective-permute-start.5 = (bf16[2,512,256]{2,1,0:T(8,128)(2,1)S(1)}, bf16[2,512,256]{2,1,0:T(8,128)(2,1)S(1)}, u32[]{:S(2)}, u32[]{:S(2)}) collective-permute-start(bf16[2,512,256]{2,1,0:T(8,128)(2,1)S(1)} %pad_maximum_fusion.1.refs_0_), channel_id=1, source_target_pairs={{0,8},{1,9},{2,10},{3,11},{4,12},{5,13},{6,14},{7,15},{8,0},{9,1},... | collective-permute-start | bytes 1572872 | tf_op jit(solution)/shard_map/panel_near_x/ppermute | solution.py:27
  45.6 13.0 %collective-permute-done.6.refs_4_ = bf16[2,512,256]{2,1,0:T(8,128)(2,1)S(1)} collective-permute-done((bf16[2,512,256]{2,1,0:T(8,128)(2,1)S(1)}, bf16[2,512,256]{2,1,0:T(8,128)(2,1)S(1)}, u32[]{:S(2)}, u32[]{:S(2)}) %collective-permute-start.6) | collective-permute-done | bytes 524320 | tf_op jit(solution)/shard_map/panel_far/ppermute | solution.py:27
  58.7 3.5 %collective-permute-start.7 = (bf16[2,512,256]{2,1,0:T(8,128)(2,1)S(1)}, bf16[2,512,256]{2,1,0:T(8,128)(2,1)S(1)}, u32[]{:S(2)}, u32[]{:S(2)}) collective-permute-start(bf16[2,512,256]{2,1,0:T(8,128)(2,1)S(1)} %collective-permute-done.6.refs_4_), channel_id=1, source_target_pairs={{0,4},{1,5},{2,6},{3,7},{4,8},{5,9},{6,10},{7,11},{8,12},{9,13},{1... | collective-permute-start | bytes 1572872 | tf_op jit(solution)/shard_map/panel_far_x/ppermute | solution.py:27
  62.2 3.2 %collective-permute-start.8 = (bf16[2,512,256]{2,1,0:T(8,128)(2,1)S(1)}, bf16[2,512,256]{2,1,0:T(8,128)(2,1)S(1)}, u32[]{:S(2)}, u32[]{:S(2)}) collective-permute-start(bf16[2,512,256]{2,1,0:T(8,128)(2,1)S(1)} %collective-permute-done.6.refs_4_), channel_id=1, source_target_pairs={{0,12},{1,13},{2,14},{3,15},{4,0},{5,1},{6,2},{7,3},{8,4},{9,5},{1... | collective-permute-start | bytes 1572872 | tf_op jit(solution)/shard_map/panel_far_x/ppermute | solution.py:27
  65.4 3.6 %collective-permute-start.9 = (bf16[2,512,256]{2,1,0:T(8,128)(2,1)S(1)}, bf16[2,512,256]{2,1,0:T(8,128)(2,1)S(1)}, u32[]{:S(2)}, u32[]{:S(2)}) collective-permute-start(bf16[2,512,256]{2,1,0:T(8,128)(2,1)S(1)} %collective-permute-done.6.refs_4_), channel_id=1, source_target_pairs={{0,8},{1,9},{2,10},{3,11},{4,12},{5,13},{6,14},{7,15},{8,0},{9,1},... | collective-permute-start | bytes 1572872 | tf_op jit(solution)/shard_map/panel_far_x/ppermute | solution.py:27
  69.0 6.1 %collective-permute-done.7.refs_5_ = bf16[2,512,256]{2,1,0:T(8,128)(2,1)S(1)} collective-permute-done((bf16[2,512,256]{2,1,0:T(8,128)(2,1)S(1)}, bf16[2,512,256]{2,1,0:T(8,128)(2,1)S(1)}, u32[]{:S(2)}, u32[]{:S(2)}) %collective-permute-start.7) | collective-permute-done | bytes 524320 | tf_op jit(solution)/shard_map/panel_far_x/ppermute | solution.py:27
  77.4 9.7 %collective-permute-done.9.refs_7_ = bf16[2,512,256]{2,1,0:T(8,128)(2,1)S(1)} collective-permute-done((bf16[2,512,256]{2,1,0:T(8,128)(2,1)S(1)}, bf16[2,512,256]{2,1,0:T(8,128)(2,1)S(1)}, u32[]{:S(2)}, u32[]{:S(2)}) %collective-permute-start.9) | collective-permute-done | bytes 524320 | tf_op jit(solution)/shard_map/panel_far_x/ppermute | solution.py:27
  87.9 5.4 %all-gather.3.cloned.1.call-done = bf16[64,128,512]{2,1,0:T(8,128)(2,1)} async-done(((bf16[8,128,512]{2,1,0:T(8,128)(2,1)}), bf16[64,128,512]{2,1,0:T(8,128)(2,1)}) %all-gather.3.cloned.1.call-update) | async-done | bytes 8388624 | tf_op jit(solution)/shard_map/slab_rows/all_gather | solution.py:210
  93.4 3.4 %copy-done = bf16[64,128,512]{2,1,0:T(8,128)(2,1)S(1)} copy-done((bf16[64,128,512]{2,1,0:T(8,128)(2,1)S(1)}, bf16[64,128,512]{2,1,0:T(8,128)(2,1)}, u32[]{:S(2)}) %copy-start) | copy-done | bytes 8388632
  102.3 7.3 %collective-permute-start.10 = (s16[528,128]{1,0:T(8,128)(2,1)S(1)}, s16[528,128]{1,0:T(8,128)(2,1)S(1)}, u32[]{:S(2)}, u32[]{:S(2)}) collective-permute-start(s16[528,128]{1,0:T(8,128)(2,1)S(1)} %get-tuple-element.27), channel_id=1, source_target_pairs={{0,1},{1,2},{2,3},{3,0},{4,5},{5,6},{6,7},{7,4},{8,9},{9,10},{10,1... | collective-permute-start | bytes 405512 | tf_op jit(solution)/shard_map/layer_halves/ppermute | solution.py:27
  109.6 2.7 %collective-permute-start.11 = (s16[528,128]{1,0:T(8,128)(2,1)S(1)}, s16[528,128]{1,0:T(8,128)(2,1)S(1)}, u32[]{:S(2)}, u32[]{:S(2)}) collective-permute-start(s16[528,128]{1,0:T(8,128)(2,1)S(1)} %get-tuple-element.28), channel_id=1, source_target_pairs={{0,3},{1,0},{2,1},{3,2},{4,7},{5,4},{6,5},{7,6},{8,11},{9,8},{10,9... | collective-permute-start | bytes 405512 | tf_op jit(solution)/shard_map/layer_halves/ppermute | solution.py:27
  112.3 4.9 %matmul_rest.1 = (f32[2,128,512]{2,1,0:T(8,128)S(1)}, f32[2,128,512]{2,1,0:T(8,128)S(1)}, f32[2,128,512]{2,1,0:T(8,128)S(1)}) custom-call(s32[6]{0:T(128)S(1)} %copy-done.8, s32[32]{0:T(128)S(1)} %bitcast.18, bf16[2,512,256]{2,1,0:T(8,128)(2,1)S(1)} %pad_maximum_fusion.1.refs_0_, bf16[2,512,256]{2,1,0:T(8,128)(2,1)S(1)} %collective-permute-done.3.refs_1_, ...), custom_call_target="tpu_custom_call" | custom-call | flops 3221225472 | bytes 1048576 | tf_op jit(solution)/shard_map/matmul_rest/pallas_call | solution.py:119
  119.6 9.4 %collective-permute-done.11.got3_ref = s16[528,128]{1,0:T(8,128)(2,1)S(1)} collective-permute-done((s16[528,128]{1,0:T(8,128)(2,1)S(1)}, s16[528,128]{1,0:T(8,128)(2,1)S(1)}, u32[]{:S(2)}, u32[]{:S(2)}) %collective-permute-start.11) | collective-permute-done | bytes 135200 | tf_op jit(solution)/shard_map/layer_halves/ppermute | solution.py:27
  131.9 7.8 %collective-permute-start.12 = (s16[1040,128]{1,0:T(8,128)(2,1)}, s16[1040,128]{1,0:T(8,128)(2,1)S(1)}, u32[]{:S(2)}, u32[]{:S(2)}) collective-permute-start(s16[1040,128]{1,0:T(8,128)(2,1)} %get-tuple-element.29), channel_id=1, source_target_pairs={{0,1},{1,2},{2,3},{3,0},{4,5},{5,6},{6,7},{7,4},{8,9},{9,10},{10,1... | collective-permute-start | bytes 798728 | tf_op jit(solution)/shard_map/layer_sums/ppermute | solution.py:27
  141.7 17.0 %collective-permute-done.12.refs_0_ = s16[1040,128]{1,0:T(8,128)(2,1)S(1)} collective-permute-done((s16[1040,128]{1,0:T(8,128)(2,1)}, s16[1040,128]{1,0:T(8,128)(2,1)S(1)}, u32[]{:S(2)}, u32[]{:S(2)}) %collective-permute-start.12) | collective-permute-done | bytes 266272 | tf_op jit(solution)/shard_map/layer_sums/ppermute | solution.py:27
  158.7 8.2 %collective-permute-done.13.refs_1_ = s16[1040,128]{1,0:T(8,128)(2,1)S(1)} collective-permute-done((s16[1040,128]{1,0:T(8,128)(2,1)}, s16[1040,128]{1,0:T(8,128)(2,1)S(1)}, u32[]{:S(2)}, u32[]{:S(2)}) %collective-permute-start.13) | collective-permute-done | bytes 266272 | tf_op jit(solution)/shard_map/layer_sums/ppermute | solution.py:27
  169.6 4.2 %collective-permute-start.14 = (bf16[128,512]{1,0:T(8,128)(2,1)}, bf16[128,512]{1,0:T(8,128)(2,1)S(1)}, u32[]{:S(2)}, u32[]{:S(2)}) collective-permute-start(bf16[128,512]{1,0:T(8,128)(2,1)} %get-tuple-element.31), channel_id=1, source_target_pairs={{0,0},{1,1},{2,2},{3,3},{4,4},{5,5},{6,6},{7,7},{8,8},{9,9},{10,10... | collective-permute-start | bytes 393224 | tf_op jit(solution)/shard_map/product_pair/ppermute | solution.py:27
  176.6 3.1 %collective-permute-done.15.second_ref = bf16[128,512]{1,0:T(8,128)(2,1)S(1)} collective-permute-done((bf16[128,512]{1,0:T(8,128)(2,1)}, bf16[128,512]{1,0:T(8,128)(2,1)S(1)}, u32[]{:S(2)}, u32[]{:S(2)}) %collective-permute-start.15) | collective-permute-done | bytes 131104 | tf_op jit(solution)/shard_map/product_pair/ppermute | solution.py:27
  (52 shorter events, 32.2 us)
Async XLA Ops:
  6.5 86.8 %all-gather.3.cloned.1.call-start = ((), (), s32[]{:S(2)}) async-start(), calls=%async_computation | async-start | bytes 9437184 | tf_op jit(solution)/shard_map/slab_rows/all_gather | solution.py:210
  6.5 22.0 %collective-permute-start = (bf16[4,128,512]{2,1,0:T(8,128)(2,1)}, bf16[4,128,512]{2,1,0:T(8,128)(2,1)S(1)}, u32[]{:S(2)}, u32[]{:S(2)}) collective-permute-start(bf16[4,128,512]{2,1,0:T(8,128)(2,1)} %bitcast.20), channel_id=1, source_target_pairs={{0,16},{1,17},{2,18},{3,19},{4,20},{5,21},{6,22},{7,23},{8,24},{9,... | collective-permute-start | bytes 1572872 | tf_op jit(solution)/shard_map/slab_pair/ppermute | solution.py:27
  13.5 13.3 %collective-permute-start.1 = (bf16[512,256]{1,0:T(8,128)(2,1)}, bf16[512,256]{1,0:T(8,128)(2,1)S(1)}, u32[]{:S(2)}, u32[]{:S(2)}) collective-permute-start(bf16[512,256]{1,0:T(8,128)(2,1)} %get-tuple-element.19), channel_id=1, source_target_pairs={{0,0},{1,1},{2,2},{3,3},{4,4},{5,5},{6,6},{7,7},{8,8},{9,9},{10,10... | collective-permute-start | bytes 786440 | tf_op jit(solution)/shard_map/panel_pair/ppermute | solution.py:27
  21.5 7.1 %collective-permute-start.2 = (bf16[512,256]{1,0:T(8,128)(2,1)}, bf16[512,256]{1,0:T(8,128)(2,1)S(1)}, u32[]{:S(2)}, u32[]{:S(2)}) collective-permute-start(bf16[512,256]{1,0:T(8,128)(2,1)} %get-tuple-element.20), channel_id=1, source_target_pairs={{0,64},{1,65},{2,66},{3,67},{4,68},{5,69},{6,70},{7,71},{8,72},{9,... | collective-permute-start | bytes 786440 | tf_op jit(solution)/shard_map/panel_pair/ppermute | solution.py:27
  30.8 27.9 %collective-permute-start.6 = (bf16[2,512,256]{2,1,0:T(8,128)(2,1)S(1)}, bf16[2,512,256]{2,1,0:T(8,128)(2,1)S(1)}, u32[]{:S(2)}, u32[]{:S(2)}) collective-permute-start(bf16[2,512,256]{2,1,0:T(8,128)(2,1)S(1)} %pad_maximum_fusion.1.refs_0_), channel_id=1, source_target_pairs={{0,32},{1,33},{2,34},{3,35},{4,36},{5,37},{6,38},{7,39},{8,40},{9,... | collective-permute-start | bytes 1572872 | tf_op jit(solution)/shard_map/panel_far/ppermute | solution.py:27
  35.7 29.7 %collective-permute-start.3 = (bf16[2,512,256]{2,1,0:T(8,128)(2,1)S(1)}, bf16[2,512,256]{2,1,0:T(8,128)(2,1)S(1)}, u32[]{:S(2)}, u32[]{:S(2)}) collective-permute-start(bf16[2,512,256]{2,1,0:T(8,128)(2,1)S(1)} %pad_maximum_fusion.1.refs_0_), channel_id=1, source_target_pairs={{0,4},{1,5},{2,6},{3,7},{4,8},{5,9},{6,10},{7,11},{8,12},{9,13},{1... | collective-permute-start | bytes 1572872 | tf_op jit(solution)/shard_map/panel_near_x/ppermute | solution.py:27
  38.8 30.2 %collective-permute-start.4 = (bf16[2,512,256]{2,1,0:T(8,128)(2,1)S(1)}, bf16[2,512,256]{2,1,0:T(8,128)(2,1)S(1)}, u32[]{:S(2)}, u32[]{:S(2)}) collective-permute-start(bf16[2,512,256]{2,1,0:T(8,128)(2,1)S(1)} %pad_maximum_fusion.1.refs_0_), channel_id=1, source_target_pairs={{0,12},{1,13},{2,14},{3,15},{4,0},{5,1},{6,2},{7,3},{8,4},{9,5},{1... | collective-permute-start | bytes 1572872 | tf_op jit(solution)/shard_map/panel_near_x/ppermute | solution.py:27
  42.2 26.8 %collective-permute-start.5 = (bf16[2,512,256]{2,1,0:T(8,128)(2,1)S(1)}, bf16[2,512,256]{2,1,0:T(8,128)(2,1)S(1)}, u32[]{:S(2)}, u32[]{:S(2)}) collective-permute-start(bf16[2,512,256]{2,1,0:T(8,128)(2,1)S(1)} %pad_maximum_fusion.1.refs_0_), channel_id=1, source_target_pairs={{0,8},{1,9},{2,10},{3,11},{4,12},{5,13},{6,14},{7,15},{8,0},{9,1},... | collective-permute-start | bytes 1572872 | tf_op jit(solution)/shard_map/panel_near_x/ppermute | solution.py:27
  58.7 16.5 %collective-permute-start.7 = (bf16[2,512,256]{2,1,0:T(8,128)(2,1)S(1)}, bf16[2,512,256]{2,1,0:T(8,128)(2,1)S(1)}, u32[]{:S(2)}, u32[]{:S(2)}) collective-permute-start(bf16[2,512,256]{2,1,0:T(8,128)(2,1)S(1)} %collective-permute-done.6.refs_4_), channel_id=1, source_target_pairs={{0,4},{1,5},{2,6},{3,7},{4,8},{5,9},{6,10},{7,11},{8,12},{9,13},{1... | collective-permute-start | bytes 1572872 | tf_op jit(solution)/shard_map/panel_far_x/ppermute | solution.py:27
  62.2 14.4 %collective-permute-start.8 = (bf16[2,512,256]{2,1,0:T(8,128)(2,1)S(1)}, bf16[2,512,256]{2,1,0:T(8,128)(2,1)S(1)}, u32[]{:S(2)}, u32[]{:S(2)}) collective-permute-start(bf16[2,512,256]{2,1,0:T(8,128)(2,1)S(1)} %collective-permute-done.6.refs_4_), channel_id=1, source_target_pairs={{0,12},{1,13},{2,14},{3,15},{4,0},{5,1},{6,2},{7,3},{8,4},{9,5},{1... | collective-permute-start | bytes 1572872 | tf_op jit(solution)/shard_map/panel_far_x/ppermute | solution.py:27
  65.4 21.7 %collective-permute-start.9 = (bf16[2,512,256]{2,1,0:T(8,128)(2,1)S(1)}, bf16[2,512,256]{2,1,0:T(8,128)(2,1)S(1)}, u32[]{:S(2)}, u32[]{:S(2)}) collective-permute-start(bf16[2,512,256]{2,1,0:T(8,128)(2,1)S(1)} %collective-permute-done.6.refs_4_), channel_id=1, source_target_pairs={{0,8},{1,9},{2,10},{3,11},{4,12},{5,13},{6,14},{7,15},{8,0},{9,1},... | collective-permute-start | bytes 1572872 | tf_op jit(solution)/shard_map/panel_far_x/ppermute | solution.py:27
  87.1 0.8 copy-start.3
  93.4 3.4 %copy-start = (bf16[64,128,512]{2,1,0:T(8,128)(2,1)S(1)}, bf16[64,128,512]{2,1,0:T(8,128)(2,1)}, u32[]{:S(2)}) copy-start(bf16[64,128,512]{2,1,0:T(8,128)(2,1)} %all-gather.3.cloned.1.call-done) | copy-start | bytes 25165828
  96.8 1.0 copy-start.2
  97.8 1.0 copy-start.4
  102.3 17.3 %collective-permute-start.10 = (s16[528,128]{1,0:T(8,128)(2,1)S(1)}, s16[528,128]{1,0:T(8,128)(2,1)S(1)}, u32[]{:S(2)}, u32[]{:S(2)}) collective-permute-start(s16[528,128]{1,0:T(8,128)(2,1)S(1)} %get-tuple-element.27), channel_id=1, source_target_pairs={{0,1},{1,2},{2,3},{3,0},{4,5},{5,6},{6,7},{7,4},{8,9},{9,10},{10,1... | collective-permute-start | bytes 405512 | tf_op jit(solution)/shard_map/layer_halves/ppermute | solution.py:27
  109.6 19.4 %collective-permute-start.11 = (s16[528,128]{1,0:T(8,128)(2,1)S(1)}, s16[528,128]{1,0:T(8,128)(2,1)S(1)}, u32[]{:S(2)}, u32[]{:S(2)}) collective-permute-start(s16[528,128]{1,0:T(8,128)(2,1)S(1)} %get-tuple-element.28), channel_id=1, source_target_pairs={{0,3},{1,0},{2,1},{3,2},{4,7},{5,4},{6,5},{7,6},{8,11},{9,8},{10,9... | collective-permute-start | bytes 405512 | tf_op jit(solution)/shard_map/layer_halves/ppermute | solution.py:27
  119.6 9.4 %copy-start.12 = (s16[528,128]{1,0:T(8,128)(2,1)}, s16[528,128]{1,0:T(8,128)(2,1)S(1)}, u32[]{:S(2)}) copy-start(s16[528,128]{1,0:T(8,128)(2,1)S(1)} %collective-permute-done.10.got1_ref) | copy-start | bytes 405508
  131.9 26.7 %collective-permute-start.12 = (s16[1040,128]{1,0:T(8,128)(2,1)}, s16[1040,128]{1,0:T(8,128)(2,1)S(1)}, u32[]{:S(2)}, u32[]{:S(2)}) collective-permute-start(s16[1040,128]{1,0:T(8,128)(2,1)} %get-tuple-element.29), channel_id=1, source_target_pairs={{0,1},{1,2},{2,3},{3,0},{4,5},{5,6},{6,7},{7,4},{8,9},{9,10},{10,1... | collective-permute-start | bytes 798728 | tf_op jit(solution)/shard_map/layer_sums/ppermute | solution.py:27
  139.7 27.1 %collective-permute-start.13 = (s16[1040,128]{1,0:T(8,128)(2,1)}, s16[1040,128]{1,0:T(8,128)(2,1)S(1)}, u32[]{:S(2)}, u32[]{:S(2)}) collective-permute-start(s16[1040,128]{1,0:T(8,128)(2,1)} %get-tuple-element.30), channel_id=1, source_target_pairs={{0,3},{1,0},{2,1},{3,2},{4,7},{5,4},{6,5},{7,6},{8,11},{9,8},{10,9... | collective-permute-start | bytes 798728 | tf_op jit(solution)/shard_map/layer_sums/ppermute | solution.py:27
  158.7 8.2 %copy-start.10 = (s16[1040,128]{1,0:T(8,128)(2,1)}, s16[1040,128]{1,0:T(8,128)(2,1)S(1)}, u32[]{:S(2)}) copy-start(s16[1040,128]{1,0:T(8,128)(2,1)S(1)} %collective-permute-done.12.refs_0_) | copy-start | bytes 798724
  169.6 7.1 %collective-permute-start.14 = (bf16[128,512]{1,0:T(8,128)(2,1)}, bf16[128,512]{1,0:T(8,128)(2,1)S(1)}, u32[]{:S(2)}, u32[]{:S(2)}) collective-permute-start(bf16[128,512]{1,0:T(8,128)(2,1)} %get-tuple-element.31), channel_id=1, source_target_pairs={{0,0},{1,1},{2,2},{3,3},{4,4},{5,5},{6,6},{7,7},{8,8},{9,9},{10,10... | collective-permute-start | bytes 393224 | tf_op jit(solution)/shard_map/product_pair/ppermute | solution.py:27
  173.8 5.9 %collective-permute-start.15 = (bf16[128,512]{1,0:T(8,128)(2,1)}, bf16[128,512]{1,0:T(8,128)(2,1)S(1)}, u32[]{:S(2)}, u32[]{:S(2)}) collective-permute-start(bf16[128,512]{1,0:T(8,128)(2,1)} %get-tuple-element.32), channel_id=1, source_target_pairs={{0,16},{1,17},{2,18},{3,19},{4,20},{5,21},{6,22},{7,23},{8,24},{9,... | collective-permute-start | bytes 393224 | tf_op jit(solution)/shard_map/product_pair/ppermute | solution.py:27
  176.6 3.1 %copy-start.14 = (bf16[128,512]{1,0:T(8,128)(2,1)}, bf16[128,512]{1,0:T(8,128)(2,1)S(1)}, u32[]{:S(2)}) copy-start(bf16[128,512]{1,0:T(8,128)(2,1)S(1)} %collective-permute-done.14.first_ref) | copy-start | bytes 393220
  (9 other events, 6.5 us)
Sparse Core Ops, SparseCore 0:
  30.8 62.4 all-gather.2

commit v6 on v4

--- a/solution.py
+++ b/solution.py
@@ -72,8 +72,7 @@
     ((1, 0, 0), (1, 0, 1)),
     ((0, 2, 0), (1, 3, 0), (1, 3, 1)),
     ((0, 2, 1), (1, 1, 0), (1, 1, 1)),
-    ((1, 2, 0),),
-    ((1, 2, 1),),
+    ((1, 2, 0), (1, 2, 1)),
 )
 SLAB = (
     (0, 0, 4, 0, 0, 0, 0),
@@ -84,20 +83,18 @@
     (4, 2, 4, 1, 0, 3, 0),
     (5, 0, 2, 0, 0, 2, 2),
     (5, 2, 4, 1, 0, 1, 0),
-    (6, 0, 2, 1, 0, 2, 0),
-    (7, 0, 2, 1, 0, 2, 2),
-    (8, 0, 4, 0, 1, 0, 0),
-    (8, 4, 4, 1, 1, 0, 0),
-    (9, 0, 4, 0, 1, 3, 0),
-    (9, 4, 4, 0, 1, 1, 0),
-    (9, 8, 2, 0, 1, 2, 0),
-    (9, 10, 4, 1, 1, 3, 0),
-    (9, 14, 2, 0, 1, 2, 2),
-    (9, 16, 4, 1, 1, 1, 0),
-    (10, 0, 2, 1, 1, 2, 0),
-    (10, 2, 2, 1, 1, 2, 2),
+    (6, 0, 4, 1, 0, 2, 0),
+    (7, 0, 4, 0, 1, 0, 0),
+    (7, 4, 4, 1, 1, 0, 0),
+    (7, 8, 4, 0, 1, 3, 0),
+    (7, 12, 4, 0, 1, 1, 0),
+    (7, 16, 2, 0, 1, 2, 0),
+    (7, 18, 4, 1, 1, 3, 0),
+    (7, 22, 2, 0, 1, 2, 2),
+    (7, 24, 4, 1, 1, 1, 0),
+    (8, 0, 4, 1, 1, 2, 0),
 )
-NA, NB = 8, 11
+NA, NB = 7, 9
 
 
 def quantize(tiles, o_ref):
@@ -147,9 +144,11 @@
 
 
 def far_kernel(pos_ref, owner_ref, *refs):
-    a_refs, b_refs, (o0_ref, o1_ref, a_s) = refs[:NA], refs[NA:NA + NB], refs[NA + NB:]
+    a_refs, b_refs, (o_ref, a_s) = refs[:NA], refs[NA:NA + NB], refs[NA + NB:]
+    tiles = []
     for g, total in product((2,), pos_ref, owner_ref, a_refs, b_refs, a_s):
-        quantize([total[:, n * BS:(n + 1) * BS] for n in range(4)], (o0_ref, o1_ref)[g])
+        tiles += [total[:, n * BS:(n + 1) * BS] for n in range(4)]
+    quantize(tiles, o_ref)
 
 
 def rest_kernel(pos_ref, owner_ref, *refs):
@@ -173,27 +172,25 @@
     )(pos, owner, *a, *b)
 
 
-def add_kernel(own1_ref, own3_ref, got1_ref, got3_ref, o1_ref, o3_ref):
-    for half, own_ref, got_ref, o_ref in ((0, own1_ref, got1_ref, o1_ref), (1, own3_ref, got3_ref, o3_ref)):
-        scale = scales(got_ref, 4)
+def add_kernel(pos_ref, own1_ref, own3_ref, got_ref, o1_ref, o3_ref):
+    scale = scales(got_ref, 8)
+    for core, own_ref, o_ref in ((0, own1_ref, o1_ref), (1, own3_ref, o3_ref)):
+        mine = pos_ref[1] == core
         tiles = []
         for t in range(8):
-            v = own_ref[t // 4, :, pl.ds((t % 4) * BS, BS)]
-            if t // 4 == half:
-                n = t % 4
-                v = v + values(got_ref, pl.ds(n * BS, BS)) * scale[n:n + 1, :]
-            tiles.append(v)
+            got = values(got_ref, pl.ds(t * BS, BS)) * scale[t:t + 1, :]
+            tiles.append(own_ref[t // 4, :, pl.ds((t % 4) * BS, BS)] + jnp.where(mine, got, 0.0))
         quantize(tiles, o_ref)
 
 
-def add(own1, own3, got1, got3):
+def add(pos, own1, own3, got):
     return pl.pallas_call(
         add_kernel,
         out_shape=[jax.ShapeDtypeStruct((8 * BS + PAD, BS), jnp.int16)] * 2,
-        in_specs=[pl.BlockSpec(memory_space=pltpu.VMEM)] * 4,
+        in_specs=[pl.BlockSpec(memory_space=pltpu.SMEM)] + [pl.BlockSpec(memory_space=pltpu.VMEM)] * 3,
         out_specs=[pl.BlockSpec(memory_space=pltpu.VMEM)] * 2,
         name="add",
-    )(own1, own3, got1, got3)
+    )(pos, own1, own3, got)
 
 
 def total_kernel(pos_ref, own_ref, *refs):
@@ -244,36 +241,38 @@
     pos = jnp.stack([row // 2, row % 2, zl // 2, zl % 2, col % 4, lax.axis_index("layer")])
     cat = lambda *v: jnp.concatenate(v, axis=0)
     own = slab[0]
-    first, second = mask(pos, panel[:, 0, :], in_pattern[:, 0, :].T)
     with jax.named_scope("round0"):
+        pair = send(own, lambda y, c, zl, x, zh: (y, c, zl ^ 1, x, zh))
+        first, second = mask(pos, panel[:, 0, :], in_pattern[:, 0, :].T)
         first = send(first, lambda y, c, zl, x, zh: (y, zl % 2, zl - zl % 2 + c, x, zh))
         second = send(second, lambda y, c, zl, x, zh: (y, 1 - zl % 2, zl - zl % 2 + c, x, zh))
-        pair = send(own, lambda y, c, zl, x, zh: (y, c, zl ^ 1, x, zh))
-        b1p, b1m = to_y(own, 1), to_y(own, -1)
-        first, second, pair, b1p, b1m = lax.optimization_barrier((first, second, pair, b1p, b1m))
+        first, second, pair, late = lax.optimization_barrier((first, second, pair, own))
         near = jnp.stack([first, second])
     with jax.named_scope("round1"):
         far = send(near, lambda y, c, zl, x, zh: (y, c, zl ^ 2, x, zh))
         a1p, a1m = to_x(near, 1), to_x(near, -1)
-        b2p, b2m = to_y(cat(b1p[:2], pair), 1), to_y(cat(b1m[2:], pair), -1)
-        far, a1p, a1m, b2p, b2m = lax.optimization_barrier((far, a1p, a1m, b2p, b2m))
+        b1p, b1m = to_y(late, 1), to_y(late, -1)
+        far, a1p, a1m, b1p, b1m = lax.optimization_barrier((far, a1p, a1m, b1p, b1m))
     with jax.named_scope("round2"):
         a2p, a2m = to_x(cat(a1p[:1], far), 1), to_x(cat(a1m[1:], far), -1)
-        b3p, b3m = to_y(b2p[2:4], 1), to_y(b2m[4:], -1)
-        c12 = to_core(cat(b1p, b1m, b2p, b2m))
-        a2p, a2m, b3p, b3m, c12, late = lax.optimization_barrier((a2p, a2m, b3p, b3m, c12, pair))
+        b2p, b2m = to_y(cat(b1p[:2], pair), 1), to_y(cat(b1m[2:], pair), -1)
+        a2p, a2m, b2p, b2m = lax.optimization_barrier((a2p, a2m, b2p, b2m))
     with jax.named_scope("round3"):
-        a3p, a3m = to_x(a2p[1:2], 1), to_x(a2m[2:], -1)
-        c3, c0 = to_core(cat(b3p, b3m)), to_core(cat(own, late))
-    a = (near, a1p, a1m, far, a2p, a2m, a3p, a3m)
-    b = (own, pair, b1p, b1m, b2p, b2m, b3p, b3m, c0, c12, c3)
-    half_shape = [jax.ShapeDtypeStruct((4 * BS + PAD, BS), jnp.int16)] * 2
-    whole_shape = [jax.ShapeDtypeStruct((2, BS, 4 * BS), jnp.float32)] * 3
-    far1, far3 = matmul(far_kernel, "matmul_far", 1, half_shape, pos, owner[0], a, b)
-    with jax.named_scope("layer_halves"):
-        got1, got3 = to_layer(far1, 1), to_layer(far3, -1)
-    own_part, part1, part3 = matmul(rest_kernel, "matmul_rest", 3, whole_shape, pos, owner[0], a, b)
-    part1, part3 = add(part1, part3, got1, got3)
+        even = row % 2 == 0
+        hand_a, hand_b = jnp.where(even, a2p[1:], a2m[1:]), jnp.where(even, b2p[2:], b2m[2:])
+        a3 = send(hand_a, lambda y, c, zl, x, zh: (y, c, zl, (x + 1 - 2 * c) % 4, zh))
+        b3 = send(hand_b, lambda y, c, zl, x, zh: ((y + 1 - 2 * c) % 4, c, zl, x, zh))
+        b3x = send(hand_b, lambda y, c, zl, x, zh: ((y + 1 - 2 * c) % 4, 1 - c, zl, x, zh))
+        swap = to_core(cat(late, pair, b1p, b1m, b2p, b2m))
+    a = (near, a1p, a1m, far, a2p, a2m, a3)
+    b = (late, pair, b1p, b1m, b2p, b2m, b3, swap, b3x)
+    far_shape = [jax.ShapeDtypeStruct((8 * BS + PAD, BS), jnp.int16)]
+    rest_shape = [jax.ShapeDtypeStruct((2, BS, 4 * BS), jnp.float32)] * 3
+    got, = matmul(far_kernel, "matmul_far", 1, far_shape, pos, owner[0], a, b)
+    with jax.named_scope("layer_far"):
+        got = send(got, lambda y, c, zl, x, zh: (y, c, zl, x, (zh + 1 - 2 * c) % 4))
+    own_part, part1, part3 = matmul(rest_kernel, "matmul_rest", 3, rest_shape, pos, owner[0], a, b)
+    part1, part3 = add(pos, part1, part3, got)
     with jax.named_scope("layer_sums"):
         got1, got3 = to_layer(part1, 1), to_layer(part3, -1)
     first, second = total(pos, own_part, (got1, got3))

time: 181 us -> 187 us (1.033)
  starting transfers between devices: 109 us -> 91.8 us
  local copies, waits for them, and re-layouts: 5.2 us -> 16.6 us
  waiting for transfers between devices: 49.1 us -> 55.6 us
  Pallas kernels: 15.5 us -> 19.6 us
    ppermute x25 -> x21, starting transfers between devices: 109 us -> 91.8 us  [send(): return lax.ppermute(v, AXES, moves(f))]
    unnamed x24 -> x45, local copies, waits for them, and re-layouts: 4.43 us -> 15 us
    ppermute x25 -> x21, waiting for transfers between devices: 49.1 us -> 55.6 us  [send(): return lax.ppermute(v, AXES, moves(f))]
    pallas_call x2, Pallas kernels: 7.48 us -> 11.4 us  [matmul(): pl.pallas_call(kernel, out_shape=out_shape, in_specs=[pl.BlockSpec(memory...]
  transfers between devices with their start and end apart: 25 -> 21, of which waited for: 13 -> 14; matrix products, arithmetic and copies ran while one was open for 1% -> 3% of each run, Pallas kernels for 4% -> 5%
where the time goes in v6:
time: 187 us; the launch traced here: 186 us
  starting transfers between devices  91.8 us (49%)
  waiting for transfers between devices  55.6 us (30%)
  Pallas kernels  19.6 us (10%)
  local copies, waits for them, and re-layouts  16.6 us (9%)
    ppermute x21, starting transfers between devices, send(): return lax.ppermute(v, AXES, moves(f))  91.8 us
    ppermute x21, waiting for transfers between devices, send(): return lax.ppermute(v, AXES, moves(f))  55.6 us
    unnamed x45, local copies, waits for them, and re-layouts  15 us
    pallas_call x2, Pallas kernels, matmul(): pl.pallas_call(kernel, out_shape=out_shape, in_specs=[pl.BlockSpec(memory...  11.4 us
  transfers between devices with their start and end apart: 21, of which 14 were waited for; matrix products, arithmetic and copies ran while one was open for 3% of the time, Pallas kernels for 5%

profile of v6, /device:TPU:71, one launch (start us, length us, event | category | flops | bytes accessed | tf_op | source)
XLA Modules:
  0.0 185.7 jit_solution(18169593342434626811)
XLA Ops:
  0.0 3.5 %collective-permute-start.2 = (bf16[4,128,512]{2,1,0:T(8,128)(2,1)}, bf16[4,128,512]{2,1,0:T(8,128)(2,1)S(1)}, u32[]{:S(2)}, u32[]{:S(2)}) collective-permute-start(bf16[4,128,512]{2,1,0:T(8,128)(2,1)} %bitcast.14), channel_id=1, source_target_pairs={{0,16},{1,17},{2,18},{3,19},{4,20},{5,21},{6,22},{7,23},{8,24},{9,... | collective-permute-start | bytes 1572872 | tf_op jit(solution)/shard_map/round0/ppermute | solution.py:27
  6.2 2.6 %collective-permute-start = (bf16[512,256]{1,0:T(8,128)(2,1)}, bf16[512,256]{1,0:T(8,128)(2,1)S(1)}, u32[]{:S(2)}, u32[]{:S(2)}) collective-permute-start(bf16[512,256]{1,0:T(8,128)(2,1)} %get-tuple-element.27), channel_id=1, source_target_pairs={{0,0},{1,1},{2,2},{3,3},{4,4},{5,5},{6,6},{7,7},{8,8},{9,9},{10,10... | collective-permute-start | bytes 786440 | tf_op jit(solution)/shard_map/round0/ppermute | solution.py:27
  10.7 8.0 %collective-permute-done = bf16[512,256]{1,0:T(8,128)(2,1)S(1)} collective-permute-done((bf16[512,256]{1,0:T(8,128)(2,1)}, bf16[512,256]{1,0:T(8,128)(2,1)S(1)}, u32[]{:S(2)}, u32[]{:S(2)}) %collective-permute-start) | collective-permute-done | bytes 262176 | tf_op jit(solution)/shard_map/round0/ppermute | solution.py:27
  25.4 3.2 %collective-permute-start.5 = (bf16[2,512,256]{2,1,0:T(8,128)(2,1)S(1)}, bf16[2,512,256]{2,1,0:T(8,128)(2,1)S(1)}, u32[]{:S(2)}, u32[]{:S(2)}) collective-permute-start(bf16[2,512,256]{2,1,0:T(8,128)(2,1)S(1)} %pad_maximum_fusion.4.refs_0_), channel_id=1, source_target_pairs={{0,12},{1,13},{2,14},{3,15},{4,0},{5,1},{6,2},{7,3},{8,4},{9,5},{1... | collective-permute-start | bytes 1572872 | tf_op jit(solution)/shard_map/round1/ppermute | solution.py:27
  29.4 3.2 %collective-permute-start.6 = (bf16[4,128,512]{2,1,0:T(8,128)(2,1)}, bf16[4,128,512]{2,1,0:T(8,128)(2,1)S(1)}, u32[]{:S(2)}, u32[]{:S(2)}) collective-permute-start(bf16[4,128,512]{2,1,0:T(8,128)(2,1)} %bitcast.15), channel_id=1, source_target_pairs={{0,128},{1,129},{2,130},{3,131},{4,132},{5,133},{6,134},{7,135},{8... | collective-permute-start | bytes 1572872 | tf_op jit(solution)/shard_map/round1/ppermute | solution.py:27
  32.6 3.4 %collective-permute-start.7 = (bf16[4,128,512]{2,1,0:T(8,128)(2,1)}, bf16[4,128,512]{2,1,0:T(8,128)(2,1)S(1)}, u32[]{:S(2)}, u32[]{:S(2)}) collective-permute-start(bf16[4,128,512]{2,1,0:T(8,128)(2,1)} %bitcast.16), channel_id=1, source_target_pairs={{0,384},{1,385},{2,386},{3,387},{4,388},{5,389},{6,390},{7,391},{8... | collective-permute-start | bytes 1572872 | tf_op jit(solution)/shard_map/round1/ppermute | solution.py:27
  36.0 9.9 %collective-permute-done.3.refs_3_ = bf16[2,512,256]{2,1,0:T(8,128)(2,1)S(1)} collective-permute-done((bf16[2,512,256]{2,1,0:T(8,128)(2,1)S(1)}, bf16[2,512,256]{2,1,0:T(8,128)(2,1)S(1)}, u32[]{:S(2)}, u32[]{:S(2)}) %collective-permute-start.3) | collective-permute-done | bytes 524320 | tf_op jit(solution)/shard_map/round1/ppermute | solution.py:27
  46.5 3.2 %collective-permute-start.10 = (bf16[6,128,512]{2,1,0:T(8,128)(2,1)S(1)}, bf16[6,128,512]{2,1,0:T(8,128)(2,1)S(1)}, u32[]{:S(2)}, u32[]{:S(2)}) collective-permute-start(bf16[6,128,512]{2,1,0:T(8,128)(2,1)S(1)} %get-tuple-element.50), channel_id=1, source_target_pairs={{0,128},{1,129},{2,130},{3,131},{4,132},{5,133},{6,134},{7,135},{8... | collective-permute-start | bytes 2359304 | tf_op jit(solution)/shard_map/round2/ppermute | solution.py:27
  49.7 3.4 %collective-permute-start.11 = (bf16[6,128,512]{2,1,0:T(8,128)(2,1)S(1)}, bf16[6,128,512]{2,1,0:T(8,128)(2,1)S(1)}, u32[]{:S(2)}, u32[]{:S(2)}) collective-permute-start(bf16[6,128,512]{2,1,0:T(8,128)(2,1)S(1)} %get-tuple-element.49), channel_id=1, source_target_pairs={{0,384},{1,385},{2,386},{3,387},{4,388},{5,389},{6,390},{7,391},{8... | collective-permute-start | bytes 2359304 | tf_op jit(solution)/shard_map/round2/ppermute | solution.py:27
  53.2 3.3 %collective-permute-start.8 = (bf16[3,512,256]{2,1,0:T(8,128)(2,1)S(1)}, bf16[3,512,256]{2,1,0:T(8,128)(2,1)}, u32[]{:S(2)}, u32[]{:S(2)}) collective-permute-start(bf16[3,512,256]{2,1,0:T(8,128)(2,1)S(1)} %get-tuple-element.52), channel_id=1, source_target_pairs={{0,4},{1,5},{2,6},{3,7},{4,8},{5,9},{6,10},{7,11},{8,12},{9,13},{1... | collective-permute-start | bytes 2359304 | tf_op jit(solution)/shard_map/round2/ppermute | solution.py:27
  61.9 4.0 %collective-permute-done.10.refs_11_ = bf16[6,128,512]{2,1,0:T(8,128)(2,1)S(1)} collective-permute-done((bf16[6,128,512]{2,1,0:T(8,128)(2,1)S(1)}, bf16[6,128,512]{2,1,0:T(8,128)(2,1)S(1)}, u32[]{:S(2)}, u32[]{:S(2)}) %collective-permute-start.10) | collective-permute-done | bytes 786464 | tf_op jit(solution)/shard_map/round2/ppermute | solution.py:27
  67.6 3.3 %collective-permute-done.8.refs_4_ = bf16[3,512,256]{2,1,0:T(8,128)(2,1)} collective-permute-done((bf16[3,512,256]{2,1,0:T(8,128)(2,1)S(1)}, bf16[3,512,256]{2,1,0:T(8,128)(2,1)}, u32[]{:S(2)}, u32[]{:S(2)}) %collective-permute-start.8) | collective-permute-done | bytes 786464 | tf_op jit(solution)/shard_map/round2/ppermute | solution.py:27
  71.0 4.1 %collective-permute-done.9.refs_5_ = bf16[3,512,256]{2,1,0:T(8,128)(2,1)} collective-permute-done((bf16[3,512,256]{2,1,0:T(8,128)(2,1)S(1)}, bf16[3,512,256]{2,1,0:T(8,128)(2,1)}, u32[]{:S(2)}, u32[]{:S(2)}) %collective-permute-start.9) | collective-permute-done | bytes 786464 | tf_op jit(solution)/shard_map/round2/ppermute | solution.py:27
  77.0 6.5 %collective-permute-start.14 = (bf16[28,128,512]{2,1,0:T(8,128)(2,1)}, bf16[28,128,512]{2,1,0:T(8,128)(2,1)}, u32[]{:S(2)}, u32[]{:S(2)}) collective-permute-start(bf16[28,128,512]{2,1,0:T(8,128)(2,1)} %constant_dynamic-update-slice_fusion), channel_id=1, source_target_pairs={{0,64},{1,65},{2,66},{3,67},{4,68},{5,69},{6,70},{7,71},{8,72},{9,... | collective-permute-start | bytes 11010056 | tf_op jit(solution)/shard_map/round3/ppermute | solution.py:27
  83.5 3.1 %collective-permute-start.13 = (bf16[4,128,512]{2,1,0:T(8,128)(2,1)S(1)}, bf16[4,128,512]{2,1,0:T(8,128)(2,1)S(1)}, u32[]{:S(2)}, u32[]{:S(2)}) collective-permute-start(bf16[4,128,512]{2,1,0:T(8,128)(2,1)S(1)} %slice_select_fusion), channel_id=1, source_target_pairs={{0,128},{1,129},{2,130},{3,131},{4,132},{5,133},{6,134},{7,135},{8... | collective-permute-start | bytes 1572872 | tf_op jit(solution)/shard_map/round3/ppermute | solution.py:27
  86.6 3.6 %collective-permute-start.15 = (bf16[4,128,512]{2,1,0:T(8,128)(2,1)S(1)}, bf16[4,128,512]{2,1,0:T(8,128)(2,1)S(1)}, u32[]{:S(2)}, u32[]{:S(2)}) collective-permute-start(bf16[4,128,512]{2,1,0:T(8,128)(2,1)S(1)} %slice_select_fusion), channel_id=1, source_target_pairs={{0,192},{1,193},{2,194},{3,195},{4,196},{5,197},{6,198},{7,199},{8... | collective-permute-start | bytes 1572872 | tf_op jit(solution)/shard_map/round3/ppermute | solution.py:27
  93.7 7.0 %collective-permute-done.15.refs_15_ = bf16[4,128,512]{2,1,0:T(8,128)(2,1)S(1)} collective-permute-done((bf16[4,128,512]{2,1,0:T(8,128)(2,1)S(1)}, bf16[4,128,512]{2,1,0:T(8,128)(2,1)S(1)}, u32[]{:S(2)}, u32[]{:S(2)}) %collective-permute-start.15) | collective-permute-done | bytes 524320 | tf_op jit(solution)/shard_map/round3/ppermute | solution.py:27
  107.8 4.4 %matmul_far.1 = s16[1040,128]{1,0:T(8,128)(2,1)S(1)} custom-call(s32[6]{0:T(128)S(1)} %copy-done.13, s32[32]{0:T(128)S(1)} %bitcast.20, bf16[2,512,256]{2,1,0:T(8,128)(2,1)S(1)} %copy-done.5, bf16[2,512,256]{2,1,0:T(8,128)(2,1)S(1)} %copy-done.7, bf16[2,512,256]{2,1,0:T(8,128)(2,1)S(1)} %copy-done.9, bf16[2,512,256]{2,1,0:T(8,128)(2,1)S(1)} %copy-done.1, ...), custom_call_target="tpu_custom_call" | custom-call | flops 1073741824 | bytes 1048576 | tf_op jit(solution)/shard_map/matmul_far/pallas_call | solution.py:163
  112.3 10.0 %collective-permute-start.16 = (s16[1040,128]{1,0:T(8,128)(2,1)S(1)}, s16[1040,128]{1,0:T(8,128)(2,1)S(1)}, u32[]{:S(2)}, u32[]{:S(2)}) collective-permute-start(s16[1040,128]{1,0:T(8,128)(2,1)S(1)} %matmul_far.1), channel_id=1, source_target_pairs={{0,1},{1,2},{2,3},{3,0},{4,5},{5,6},{6,7},{7,4},{8,9},{9,10},{10,1... | collective-permute-start | bytes 798728 | tf_op jit(solution)/shard_map/layer_far/ppermute | solution.py:27
  122.3 7.0 %matmul_rest.1 = (f32[2,128,512]{2,1,0:T(8,128)S(1)}, f32[2,128,512]{2,1,0:T(8,128)S(1)}, f32[2,128,512]{2,1,0:T(8,128)S(1)}) custom-call(s32[6]{0:T(128)S(1)} %copy-done.13, s32[32]{0:T(128)S(1)} %bitcast.21, bf16[2,512,256]{2,1,0:T(8,128)(2,1)S(1)} %copy-done.5, bf16[2,512,256]{2,1,0:T(8,128)(2,1)S(1)} %copy-done.7, bf16[2,512,256]{2,1,0:T(8,128)(2,1)S(1)} %copy-done.9, ...), custom_call_target="tpu_custom_call" | custom-call | flops 3221225472 | bytes 1048576 | tf_op jit(solution)/shard_map/matmul_rest/pallas_call | solution.py:163
  136.7 7.3 %collective-permute-start.18 = (s16[1040,128]{1,0:T(8,128)(2,1)}, s16[1040,128]{1,0:T(8,128)(2,1)S(1)}, u32[]{:S(2)}, u32[]{:S(2)}) collective-permute-start(s16[1040,128]{1,0:T(8,128)(2,1)} %get-tuple-element.46), channel_id=1, source_target_pairs={{0,3},{1,0},{2,1},{3,2},{4,7},{5,4},{6,5},{7,6},{8,11},{9,8},{10,9... | collective-permute-start | bytes 798728 | tf_op jit(solution)/shard_map/layer_sums/ppermute | solution.py:27
  144.0 8.5 %collective-permute-done.17.refs_0_ = s16[1040,128]{1,0:T(8,128)(2,1)S(1)} collective-permute-done((s16[1040,128]{1,0:T(8,128)(2,1)}, s16[1040,128]{1,0:T(8,128)(2,1)S(1)}, u32[]{:S(2)}, u32[]{:S(2)}) %collective-permute-start.17) | collective-permute-done | bytes 266272 | tf_op jit(solution)/shard_map/layer_sums/ppermute | solution.py:27
  155.4 22.0 %collective-permute-start.19 = (bf16[128,512]{1,0:T(8,128)(2,1)}, bf16[128,512]{1,0:T(8,128)(2,1)S(1)}, u32[]{:S(2)}, u32[]{:S(2)}) collective-permute-start(bf16[128,512]{1,0:T(8,128)(2,1)} %get-tuple-element.47), channel_id=1, source_target_pairs={{0,0},{1,1},{2,2},{3,3},{4,4},{5,5},{6,6},{7,7},{8,8},{9,9},{10,10... | collective-permute-start | bytes 393224 | tf_op jit(solution)/shard_map/product_pair/ppermute | solution.py:27
  180.2 3.1 %collective-permute-done.20.second_ref = bf16[128,512]{1,0:T(8,128)(2,1)S(1)} collective-permute-done((bf16[128,512]{1,0:T(8,128)(2,1)}, bf16[128,512]{1,0:T(8,128)(2,1)S(1)}, u32[]{:S(2)}, u32[]{:S(2)}) %collective-permute-start.20) | collective-permute-done | bytes 131104 | tf_op jit(solution)/shard_map/product_pair/ppermute | solution.py:27
  (80 shorter events, 47.9 us)
Async XLA Ops:
  0.0 21.2 %collective-permute-start.2 = (bf16[4,128,512]{2,1,0:T(8,128)(2,1)}, bf16[4,128,512]{2,1,0:T(8,128)(2,1)S(1)}, u32[]{:S(2)}, u32[]{:S(2)}) collective-permute-start(bf16[4,128,512]{2,1,0:T(8,128)(2,1)} %bitcast.14), channel_id=1, source_target_pairs={{0,16},{1,17},{2,18},{3,19},{4,20},{5,21},{6,22},{7,23},{8,24},{9,... | collective-permute-start | bytes 1572872 | tf_op jit(solution)/shard_map/round0/ppermute | solution.py:27
  6.2 12.5 %collective-permute-start = (bf16[512,256]{1,0:T(8,128)(2,1)}, bf16[512,256]{1,0:T(8,128)(2,1)S(1)}, u32[]{:S(2)}, u32[]{:S(2)}) collective-permute-start(bf16[512,256]{1,0:T(8,128)(2,1)} %get-tuple-element.27), channel_id=1, source_target_pairs={{0,0},{1,1},{2,2},{3,3},{4,4},{5,5},{6,6},{7,7},{8,8},{9,9},{10,10... | collective-permute-start | bytes 786440 | tf_op jit(solution)/shard_map/round0/ppermute | solution.py:27
  8.8 12.4 %collective-permute-start.1 = (bf16[512,256]{1,0:T(8,128)(2,1)}, bf16[512,256]{1,0:T(8,128)(2,1)S(1)}, u32[]{:S(2)}, u32[]{:S(2)}) collective-permute-start(bf16[512,256]{1,0:T(8,128)(2,1)} %get-tuple-element.28), channel_id=1, source_target_pairs={{0,64},{1,65},{2,66},{3,67},{4,68},{5,69},{6,70},{7,71},{8,72},{9,... | collective-permute-start | bytes 786440 | tf_op jit(solution)/shard_map/round0/ppermute | solution.py:27
  21.3 37.3 %copy-start.2 = (bf16[1,4,128,512]{3,2,1,0:T(8,128)(2,1)S(1)}, bf16[1,4,128,512]{3,2,1,0:T(8,128)(2,1)}, u32[]{:S(2)}) copy-start(bf16[1,4,128,512]{3,2,1,0:T(8,128)(2,1)} %param.7) | copy-start | bytes 1572868
  21.3 24.6 %collective-permute-start.3 = (bf16[2,512,256]{2,1,0:T(8,128)(2,1)S(1)}, bf16[2,512,256]{2,1,0:T(8,128)(2,1)S(1)}, u32[]{:S(2)}, u32[]{:S(2)}) collective-permute-start(bf16[2,512,256]{2,1,0:T(8,128)(2,1)S(1)} %pad_maximum_fusion.4.refs_0_), channel_id=1, source_target_pairs={{0,32},{1,33},{2,34},{3,35},{4,36},{5,37},{6,38},{7,39},{8,40},{9,... | collective-permute-start | bytes 1572872 | tf_op jit(solution)/shard_map/round1/ppermute | solution.py:27
  23.3 22.5 %collective-permute-start.4 = (bf16[2,512,256]{2,1,0:T(8,128)(2,1)S(1)}, bf16[2,512,256]{2,1,0:T(8,128)(2,1)S(1)}, u32[]{:S(2)}, u32[]{:S(2)}) collective-permute-start(bf16[2,512,256]{2,1,0:T(8,128)(2,1)S(1)} %pad_maximum_fusion.4.refs_0_), channel_id=1, source_target_pairs={{0,4},{1,5},{2,6},{3,7},{4,8},{5,9},{6,10},{7,11},{8,12},{9,13},{1... | collective-permute-start | bytes 1572872 | tf_op jit(solution)/shard_map/round1/ppermute | solution.py:27
  25.4 20.4 %collective-permute-start.5 = (bf16[2,512,256]{2,1,0:T(8,128)(2,1)S(1)}, bf16[2,512,256]{2,1,0:T(8,128)(2,1)S(1)}, u32[]{:S(2)}, u32[]{:S(2)}) collective-permute-start(bf16[2,512,256]{2,1,0:T(8,128)(2,1)S(1)} %pad_maximum_fusion.4.refs_0_), channel_id=1, source_target_pairs={{0,12},{1,13},{2,14},{3,15},{4,0},{5,1},{6,2},{7,3},{8,4},{9,5},{1... | collective-permute-start | bytes 1572872 | tf_op jit(solution)/shard_map/round1/ppermute | solution.py:27
  29.4 16.5 %collective-permute-start.6 = (bf16[4,128,512]{2,1,0:T(8,128)(2,1)}, bf16[4,128,512]{2,1,0:T(8,128)(2,1)S(1)}, u32[]{:S(2)}, u32[]{:S(2)}) collective-permute-start(bf16[4,128,512]{2,1,0:T(8,128)(2,1)} %bitcast.15), channel_id=1, source_target_pairs={{0,128},{1,129},{2,130},{3,131},{4,132},{5,133},{6,134},{7,135},{8... | collective-permute-start | bytes 1572872 | tf_op jit(solution)/shard_map/round1/ppermute | solution.py:27
  32.6 13.6 %collective-permute-start.7 = (bf16[4,128,512]{2,1,0:T(8,128)(2,1)}, bf16[4,128,512]{2,1,0:T(8,128)(2,1)S(1)}, u32[]{:S(2)}, u32[]{:S(2)}) collective-permute-start(bf16[4,128,512]{2,1,0:T(8,128)(2,1)} %bitcast.16), channel_id=1, source_target_pairs={{0,384},{1,385},{2,386},{3,387},{4,388},{5,389},{6,390},{7,391},{8... | collective-permute-start | bytes 1572872 | tf_op jit(solution)/shard_map/round1/ppermute | solution.py:27
  46.5 19.5 %collective-permute-start.10 = (bf16[6,128,512]{2,1,0:T(8,128)(2,1)S(1)}, bf16[6,128,512]{2,1,0:T(8,128)(2,1)S(1)}, u32[]{:S(2)}, u32[]{:S(2)}) collective-permute-start(bf16[6,128,512]{2,1,0:T(8,128)(2,1)S(1)} %get-tuple-element.50), channel_id=1, source_target_pairs={{0,128},{1,129},{2,130},{3,131},{4,132},{5,133},{6,134},{7,135},{8... | collective-permute-start | bytes 2359304 | tf_op jit(solution)/shard_map/round2/ppermute | solution.py:27
  49.7 18.0 %collective-permute-start.11 = (bf16[6,128,512]{2,1,0:T(8,128)(2,1)S(1)}, bf16[6,128,512]{2,1,0:T(8,128)(2,1)S(1)}, u32[]{:S(2)}, u32[]{:S(2)}) collective-permute-start(bf16[6,128,512]{2,1,0:T(8,128)(2,1)S(1)} %get-tuple-element.49), channel_id=1, source_target_pairs={{0,384},{1,385},{2,386},{3,387},{4,388},{5,389},{6,390},{7,391},{8... | collective-permute-start | bytes 2359304 | tf_op jit(solution)/shard_map/round2/ppermute | solution.py:27
  53.2 17.7 %collective-permute-start.8 = (bf16[3,512,256]{2,1,0:T(8,128)(2,1)S(1)}, bf16[3,512,256]{2,1,0:T(8,128)(2,1)}, u32[]{:S(2)}, u32[]{:S(2)}) collective-permute-start(bf16[3,512,256]{2,1,0:T(8,128)(2,1)S(1)} %get-tuple-element.52), channel_id=1, source_target_pairs={{0,4},{1,5},{2,6},{3,7},{4,8},{5,9},{6,10},{7,11},{8,12},{9,13},{1... | collective-permute-start | bytes 2359304 | tf_op jit(solution)/shard_map/round2/ppermute | solution.py:27
  56.5 18.6 %collective-permute-start.9 = (bf16[3,512,256]{2,1,0:T(8,128)(2,1)S(1)}, bf16[3,512,256]{2,1,0:T(8,128)(2,1)}, u32[]{:S(2)}, u32[]{:S(2)}) collective-permute-start(bf16[3,512,256]{2,1,0:T(8,128)(2,1)S(1)} %get-tuple-element.51), channel_id=1, source_target_pairs={{0,12},{1,13},{2,14},{3,15},{4,0},{5,1},{6,2},{7,3},{8,4},{9,5},{1... | collective-permute-start | bytes 2359304 | tf_op jit(solution)/shard_map/round2/ppermute | solution.py:27
  61.1 41.5 %copy-start.13 = (s32[6]{0:T(128)S(1)}, s32[6]{0:T(128)}, u32[]{:S(2)}) copy-start(s32[6]{0:T(128)} %stack.36.pos_ref) | copy-start | bytes 76
  61.1 41.5 %copy-start.14 = (s32[1,32]{1,0:T(1,128)S(1)}, s32[1,32]{1,0:T(1,128)}, u32[]{:S(2)}) copy-start(s32[1,32]{1,0:T(1,128)} %param.8) | copy-start | bytes 388
  77.0 25.6 %collective-permute-start.14 = (bf16[28,128,512]{2,1,0:T(8,128)(2,1)}, bf16[28,128,512]{2,1,0:T(8,128)(2,1)}, u32[]{:S(2)}, u32[]{:S(2)}) collective-permute-start(bf16[28,128,512]{2,1,0:T(8,128)(2,1)} %constant_dynamic-update-slice_fusion), channel_id=1, source_target_pairs={{0,64},{1,65},{2,66},{3,67},{4,68},{5,69},{6,70},{7,71},{8,72},{9,... | collective-permute-start | bytes 11010056 | tf_op jit(solution)/shard_map/round3/ppermute | solution.py:27
  83.5 10.2 %collective-permute-start.13 = (bf16[4,128,512]{2,1,0:T(8,128)(2,1)S(1)}, bf16[4,128,512]{2,1,0:T(8,128)(2,1)S(1)}, u32[]{:S(2)}, u32[]{:S(2)}) collective-permute-start(bf16[4,128,512]{2,1,0:T(8,128)(2,1)S(1)} %slice_select_fusion), channel_id=1, source_target_pairs={{0,128},{1,129},{2,130},{3,131},{4,132},{5,133},{6,134},{7,135},{8... | collective-permute-start | bytes 1572872 | tf_op jit(solution)/shard_map/round3/ppermute | solution.py:27
  86.6 14.1 %collective-permute-start.15 = (bf16[4,128,512]{2,1,0:T(8,128)(2,1)S(1)}, bf16[4,128,512]{2,1,0:T(8,128)(2,1)S(1)}, u32[]{:S(2)}, u32[]{:S(2)}) collective-permute-start(bf16[4,128,512]{2,1,0:T(8,128)(2,1)S(1)} %slice_select_fusion), channel_id=1, source_target_pairs={{0,192},{1,193},{2,194},{3,195},{4,196},{5,197},{6,198},{7,199},{8... | collective-permute-start | bytes 1572872 | tf_op jit(solution)/shard_map/round3/ppermute | solution.py:27
  91.5 11.1 %collective-permute-start.12 = (bf16[2,512,256]{2,1,0:T(8,128)(2,1)S(1)}, bf16[2,512,256]{2,1,0:T(8,128)(2,1)S(1)}, u32[]{:S(2)}, u32[]{:S(2)}) collective-permute-start(bf16[2,512,256]{2,1,0:T(8,128)(2,1)S(1)} %slice_select_fusion.1), channel_id=1, source_target_pairs={{0,4},{1,5},{2,6},{3,7},{4,8},{5,9},{6,10},{7,11},{8,12},{9,13},{1... | collective-permute-start | bytes 1572872 | tf_op jit(solution)/shard_map/round3/ppermute | solution.py:27
  112.3 19.4 %collective-permute-start.16 = (s16[1040,128]{1,0:T(8,128)(2,1)S(1)}, s16[1040,128]{1,0:T(8,128)(2,1)S(1)}, u32[]{:S(2)}, u32[]{:S(2)}) collective-permute-start(s16[1040,128]{1,0:T(8,128)(2,1)S(1)} %matmul_far.1), channel_id=1, source_target_pairs={{0,1},{1,2},{2,3},{3,0},{4,5},{5,6},{6,7},{7,4},{8,9},{9,10},{10,1... | collective-permute-start | bytes 798728 | tf_op jit(solution)/shard_map/layer_far/ppermute | solution.py:27
  134.8 17.7 %collective-permute-start.17 = (s16[1040,128]{1,0:T(8,128)(2,1)}, s16[1040,128]{1,0:T(8,128)(2,1)S(1)}, u32[]{:S(2)}, u32[]{:S(2)}) collective-permute-start(s16[1040,128]{1,0:T(8,128)(2,1)} %get-tuple-element.45), channel_id=1, source_target_pairs={{0,1},{1,2},{2,3},{3,0},{4,5},{5,6},{6,7},{7,4},{8,9},{9,10},{10,1... | collective-permute-start | bytes 798728 | tf_op jit(solution)/shard_map/layer_sums/ppermute | solution.py:27
  136.7 15.8 %collective-permute-start.18 = (s16[1040,128]{1,0:T(8,128)(2,1)}, s16[1040,128]{1,0:T(8,128)(2,1)S(1)}, u32[]{:S(2)}, u32[]{:S(2)}) collective-permute-start(s16[1040,128]{1,0:T(8,128)(2,1)} %get-tuple-element.46), channel_id=1, source_target_pairs={{0,3},{1,0},{2,1},{3,2},{4,7},{5,4},{6,5},{7,6},{8,11},{9,8},{10,9... | collective-permute-start | bytes 798728 | tf_op jit(solution)/shard_map/layer_sums/ppermute | solution.py:27
  155.4 24.8 %collective-permute-start.19 = (bf16[128,512]{1,0:T(8,128)(2,1)}, bf16[128,512]{1,0:T(8,128)(2,1)S(1)}, u32[]{:S(2)}, u32[]{:S(2)}) collective-permute-start(bf16[128,512]{1,0:T(8,128)(2,1)} %get-tuple-element.47), channel_id=1, source_target_pairs={{0,0},{1,1},{2,2},{3,3},{4,4},{5,5},{6,6},{7,7},{8,8},{9,9},{10,10... | collective-permute-start | bytes 393224 | tf_op jit(solution)/shard_map/product_pair/ppermute | solution.py:27
  177.4 5.9 %collective-permute-start.20 = (bf16[128,512]{1,0:T(8,128)(2,1)}, bf16[128,512]{1,0:T(8,128)(2,1)S(1)}, u32[]{:S(2)}, u32[]{:S(2)}) collective-permute-start(bf16[128,512]{1,0:T(8,128)(2,1)} %get-tuple-element.48), channel_id=1, source_target_pairs={{0,16},{1,17},{2,18},{3,19},{4,20},{5,21},{6,22},{7,23},{8,24},{9,... | collective-permute-start | bytes 393224 | tf_op jit(solution)/shard_map/product_pair/ppermute | solution.py:27
  (17 other events, 36.5 us)

commit v7 on v6

--- a/solution.py
+++ b/solution.py
@@ -61,6 +61,7 @@
         out_shape=[jax.ShapeDtypeStruct((rows // 2, width), panel.dtype)] * 2,
         in_specs=[pl.BlockSpec(memory_space=pltpu.SMEM)] * 2 + [pl.BlockSpec(memory_space=pltpu.VMEM)],
         out_specs=[pl.BlockSpec(memory_space=pltpu.VMEM)] * 2,
+        compiler_params=pltpu.CompilerParams(vmem_limit_bytes=4 << 20),
         name="mask",
     )(pos, pattern, panel)
 
@@ -166,7 +167,7 @@
         in_specs=[pl.BlockSpec(memory_space=pltpu.SMEM)] * 2 + [pl.BlockSpec(memory_space=pltpu.VMEM)] * (NA + NB),
         out_specs=[pl.BlockSpec(memory_space=pltpu.VMEM)] * len(out_shape),
         scratch_shapes=[pltpu.VMEM((chunks * BS, depth), jnp.bfloat16)],
-        compiler_params=pltpu.CompilerParams(vmem_limit_bytes=32 << 20),
+        compiler_params=pltpu.CompilerParams(vmem_limit_bytes=24 << 20),
         cost_estimate=pl.CostEstimate(flops=2 * chunks * BS * 8 * BS * depth, bytes_accessed=1 << 20, transcendentals=0),
         name=name,
     )(pos, owner, *a, *b)
@@ -189,6 +190,7 @@
         out_shape=[jax.ShapeDtypeStruct((8 * BS + PAD, BS), jnp.int16)] * 2,
         in_specs=[pl.BlockSpec(memory_space=pltpu.SMEM)] + [pl.BlockSpec(memory_space=pltpu.VMEM)] * 3,
         out_specs=[pl.BlockSpec(memory_space=pltpu.VMEM)] * 2,
+        compiler_params=pltpu.CompilerParams(vmem_limit_bytes=8 << 20),
         name="add",
     )(pos, own1, own3, got)
 
@@ -212,6 +214,7 @@
         out_shape=[jax.ShapeDtypeStruct((BS, 4 * BS), jnp.bfloat16)] * 2,
         in_specs=[pl.BlockSpec(memory_space=pltpu.SMEM)] + [pl.BlockSpec(memory_space=pltpu.VMEM)] * 3,
         out_specs=[pl.BlockSpec(memory_space=pltpu.VMEM)] * 2,
+        compiler_params=pltpu.CompilerParams(vmem_limit_bytes=4 << 20),
         name="total",
     )(pos, own, *v)
 
@@ -231,6 +234,7 @@
         out_shape=jax.ShapeDtypeStruct((2 * BS, 4 * BS), jnp.bfloat16),
         in_specs=[pl.BlockSpec(memory_space=pltpu.SMEM)] * 2 + [pl.BlockSpec(memory_space=pltpu.VMEM)] * 2,
         out_specs=pl.BlockSpec(memory_space=pltpu.VMEM),
+        compiler_params=pltpu.CompilerParams(vmem_limit_bytes=4 << 20),
         name="place",
     )(pos, pattern, first, second)
 

time: 187 us -> 180 us (0.963)
  Pallas kernels: 19.6 us -> 15 us
  local copies, waits for them, and re-layouts: 16.6 us -> 13.1 us
  starting transfers between devices: 91.8 us -> 95 us
    ppermute x21, starting transfers between devices: 91.8 us -> 95 us  [send(): return lax.ppermute(v, AXES, moves(f))]
    unnamed x45 -> x33, local copies, waits for them, and re-layouts: 15 us -> 12.1 us
  transfers between devices with their start and end apart: 21 -> 21, of which waited for: 14 -> 14; matrix products, arithmetic and copies ran while one was open for 3% -> 3% of each run, Pallas kernels for 5% -> 4%
where the time goes in v7:
time: 180 us; the launch traced here: 179 us
  starting transfers between devices  95 us (53%)
  waiting for transfers between devices  54 us (30%)
  Pallas kernels  15 us (8%)
  local copies, waits for them, and re-layouts  13.1 us (7%)
    ppermute x21, starting transfers between devices, send(): return lax.ppermute(v, AXES, moves(f))  95 us
    ppermute x21, waiting for transfers between devices, send(): return lax.ppermute(v, AXES, moves(f))  54 us
    unnamed x33, local copies, waits for them, and re-layouts  12.1 us
    pallas_call x2, Pallas kernels, matmul(): pl.pallas_call(kernel, out_shape=out_shape, in_specs=[pl.BlockSpec(memory...  11.4 us
  transfers between devices with their start and end apart: 21, of which 14 were waited for; matrix products, arithmetic and copies ran while one was open for 3% of the time, Pallas kernels for 4%

profile of v7, /device:TPU:71, one launch (start us, length us, event | category | flops | bytes accessed | tf_op | source)
XLA Modules:
  0.0 179.2 jit_solution(11876712692197436186)
XLA Ops:
  0.0 3.5 %collective-permute-start.2 = (bf16[4,128,512]{2,1,0:T(8,128)(2,1)}, bf16[4,128,512]{2,1,0:T(8,128)(2,1)S(1)}, u32[]{:S(2)}, u32[]{:S(2)}) collective-permute-start(bf16[4,128,512]{2,1,0:T(8,128)(2,1)} %bitcast.14), channel_id=1, source_target_pairs={{0,16},{1,17},{2,18},{3,19},{4,20},{5,21},{6,22},{7,23},{8,24},{9,... | collective-permute-start | bytes 1572872 | tf_op jit(solution)/shard_map/round0/ppermute | solution.py:27
  10.6 8.1 %collective-permute-done = bf16[512,256]{1,0:T(8,128)(2,1)S(1)} collective-permute-done((bf16[512,256]{1,0:T(8,128)(2,1)S(1)}, bf16[512,256]{1,0:T(8,128)(2,1)S(1)}, u32[]{:S(2)}, u32[]{:S(2)}) %collective-permute-start) | collective-permute-done | bytes 262176 | tf_op jit(solution)/shard_map/round0/ppermute | solution.py:27
  25.3 3.2 %collective-permute-start.5 = (bf16[2,512,256]{2,1,0:T(8,128)(2,1)S(1)}, bf16[2,512,256]{2,1,0:T(8,128)(2,1)S(1)}, u32[]{:S(2)}, u32[]{:S(2)}) collective-permute-start(bf16[2,512,256]{2,1,0:T(8,128)(2,1)S(1)} %pad_maximum_fusion.4.refs_0_), channel_id=1, source_target_pairs={{0,12},{1,13},{2,14},{3,15},{4,0},{5,1},{6,2},{7,3},{8,4},{9,5},{1... | collective-permute-start | bytes 1572872 | tf_op jit(solution)/shard_map/round1/ppermute | solution.py:27
  29.3 3.2 %collective-permute-start.6 = (bf16[4,128,512]{2,1,0:T(8,128)(2,1)}, bf16[4,128,512]{2,1,0:T(8,128)(2,1)S(1)}, u32[]{:S(2)}, u32[]{:S(2)}) collective-permute-start(bf16[4,128,512]{2,1,0:T(8,128)(2,1)} %bitcast.15), channel_id=1, source_target_pairs={{0,128},{1,129},{2,130},{3,131},{4,132},{5,133},{6,134},{7,135},{8... | collective-permute-start | bytes 1572872 | tf_op jit(solution)/shard_map/round1/ppermute | solution.py:27
  32.5 3.4 %collective-permute-start.7 = (bf16[4,128,512]{2,1,0:T(8,128)(2,1)}, bf16[4,128,512]{2,1,0:T(8,128)(2,1)S(1)}, u32[]{:S(2)}, u32[]{:S(2)}) collective-permute-start(bf16[4,128,512]{2,1,0:T(8,128)(2,1)} %bitcast.16), channel_id=1, source_target_pairs={{0,384},{1,385},{2,386},{3,387},{4,388},{5,389},{6,390},{7,391},{8... | collective-permute-start | bytes 1572872 | tf_op jit(solution)/shard_map/round1/ppermute | solution.py:27
  35.9 9.8 %collective-permute-done.3.refs_3_ = bf16[2,512,256]{2,1,0:T(8,128)(2,1)S(1)} collective-permute-done((bf16[2,512,256]{2,1,0:T(8,128)(2,1)S(1)}, bf16[2,512,256]{2,1,0:T(8,128)(2,1)S(1)}, u32[]{:S(2)}, u32[]{:S(2)}) %collective-permute-start.3) | collective-permute-done | bytes 524320 | tf_op jit(solution)/shard_map/round1/ppermute | solution.py:27
  46.2 3.2 %collective-permute-start.10 = (bf16[6,128,512]{2,1,0:T(8,128)(2,1)S(1)}, bf16[6,128,512]{2,1,0:T(8,128)(2,1)S(1)}, u32[]{:S(2)}, u32[]{:S(2)}) collective-permute-start(bf16[6,128,512]{2,1,0:T(8,128)(2,1)S(1)} %get-tuple-element.50), channel_id=1, source_target_pairs={{0,128},{1,129},{2,130},{3,131},{4,132},{5,133},{6,134},{7,135},{8... | collective-permute-start | bytes 2359304 | tf_op jit(solution)/shard_map/round2/ppermute | solution.py:27
  49.4 3.4 %collective-permute-start.11 = (bf16[6,128,512]{2,1,0:T(8,128)(2,1)S(1)}, bf16[6,128,512]{2,1,0:T(8,128)(2,1)S(1)}, u32[]{:S(2)}, u32[]{:S(2)}) collective-permute-start(bf16[6,128,512]{2,1,0:T(8,128)(2,1)S(1)} %get-tuple-element.49), channel_id=1, source_target_pairs={{0,384},{1,385},{2,386},{3,387},{4,388},{5,389},{6,390},{7,391},{8... | collective-permute-start | bytes 2359304 | tf_op jit(solution)/shard_map/round2/ppermute | solution.py:27
  53.0 3.3 %collective-permute-start.8 = (bf16[3,512,256]{2,1,0:T(8,128)(2,1)S(1)}, bf16[3,512,256]{2,1,0:T(8,128)(2,1)}, u32[]{:S(2)}, u32[]{:S(2)}) collective-permute-start(bf16[3,512,256]{2,1,0:T(8,128)(2,1)S(1)} %get-tuple-element.52), channel_id=1, source_target_pairs={{0,4},{1,5},{2,6},{3,7},{4,8},{5,9},{6,10},{7,11},{8,12},{9,13},{1... | collective-permute-start | bytes 2359304 | tf_op jit(solution)/shard_map/round2/ppermute | solution.py:27
  61.7 3.9 %collective-permute-done.10.refs_11_ = bf16[6,128,512]{2,1,0:T(8,128)(2,1)S(1)} collective-permute-done((bf16[6,128,512]{2,1,0:T(8,128)(2,1)S(1)}, bf16[6,128,512]{2,1,0:T(8,128)(2,1)S(1)}, u32[]{:S(2)}, u32[]{:S(2)}) %collective-permute-start.10) | collective-permute-done | bytes 786464 | tf_op jit(solution)/shard_map/round2/ppermute | solution.py:27
  67.3 3.4 %collective-permute-done.8.refs_4_ = bf16[3,512,256]{2,1,0:T(8,128)(2,1)} collective-permute-done((bf16[3,512,256]{2,1,0:T(8,128)(2,1)S(1)}, bf16[3,512,256]{2,1,0:T(8,128)(2,1)}, u32[]{:S(2)}, u32[]{:S(2)}) %collective-permute-start.8) | collective-permute-done | bytes 786464 | tf_op jit(solution)/shard_map/round2/ppermute | solution.py:27
  70.7 4.1 %collective-permute-done.9.refs_5_ = bf16[3,512,256]{2,1,0:T(8,128)(2,1)} collective-permute-done((bf16[3,512,256]{2,1,0:T(8,128)(2,1)S(1)}, bf16[3,512,256]{2,1,0:T(8,128)(2,1)}, u32[]{:S(2)}, u32[]{:S(2)}) %collective-permute-start.9) | collective-permute-done | bytes 786464 | tf_op jit(solution)/shard_map/round2/ppermute | solution.py:27
  76.7 6.6 %collective-permute-start.14 = (bf16[28,128,512]{2,1,0:T(8,128)(2,1)}, bf16[28,128,512]{2,1,0:T(8,128)(2,1)}, u32[]{:S(2)}, u32[]{:S(2)}) collective-permute-start(bf16[28,128,512]{2,1,0:T(8,128)(2,1)} %constant_dynamic-update-slice_fusion), channel_id=1, source_target_pairs={{0,64},{1,65},{2,66},{3,67},{4,68},{5,69},{6,70},{7,71},{8,72},{9,... | collective-permute-start | bytes 11010056 | tf_op jit(solution)/shard_map/round3/ppermute | solution.py:27
  83.3 3.1 %collective-permute-start.13 = (bf16[4,128,512]{2,1,0:T(8,128)(2,1)S(1)}, bf16[4,128,512]{2,1,0:T(8,128)(2,1)S(1)}, u32[]{:S(2)}, u32[]{:S(2)}) collective-permute-start(bf16[4,128,512]{2,1,0:T(8,128)(2,1)S(1)} %slice_select_fusion), channel_id=1, source_target_pairs={{0,128},{1,129},{2,130},{3,131},{4,132},{5,133},{6,134},{7,135},{8... | collective-permute-start | bytes 1572872 | tf_op jit(solution)/shard_map/round3/ppermute | solution.py:27
  86.4 3.6 %collective-permute-start.15 = (bf16[4,128,512]{2,1,0:T(8,128)(2,1)S(1)}, bf16[4,128,512]{2,1,0:T(8,128)(2,1)S(1)}, u32[]{:S(2)}, u32[]{:S(2)}) collective-permute-start(bf16[4,128,512]{2,1,0:T(8,128)(2,1)S(1)} %slice_select_fusion), channel_id=1, source_target_pairs={{0,192},{1,193},{2,194},{3,195},{4,196},{5,197},{6,198},{7,199},{8... | collective-permute-start | bytes 1572872 | tf_op jit(solution)/shard_map/round3/ppermute | solution.py:27
  93.5 7.0 %collective-permute-done.15.refs_15_ = bf16[4,128,512]{2,1,0:T(8,128)(2,1)S(1)} collective-permute-done((bf16[4,128,512]{2,1,0:T(8,128)(2,1)S(1)}, bf16[4,128,512]{2,1,0:T(8,128)(2,1)S(1)}, u32[]{:S(2)}, u32[]{:S(2)}) %collective-permute-start.15) | collective-permute-done | bytes 524320 | tf_op jit(solution)/shard_map/round3/ppermute | solution.py:27
  107.6 4.4 %matmul_far.1 = s16[1040,128]{1,0:T(8,128)(2,1)S(1)} custom-call(s32[6]{0:T(128)S(1)} %stack.36.pos_ref, s32[32]{0:T(128)S(1)} %bitcast.21, bf16[2,512,256]{2,1,0:T(8,128)(2,1)S(1)} %copy-done.5, bf16[2,512,256]{2,1,0:T(8,128)(2,1)S(1)} %copy-done.7, bf16[2,512,256]{2,1,0:T(8,128)(2,1)S(1)} %copy-done.9, bf16[2,512,256]{2,1,0:T(8,128)(2,1)S(1)} %copy-done.1, ...), custom_call_target="tpu_custom_call" | custom-call | flops 1073741824 | bytes 1048576 | tf_op jit(solution)/shard_map/matmul_far/pallas_call | solution.py:164
  112.1 10.0 %collective-permute-start.16 = (s16[1040,128]{1,0:T(8,128)(2,1)S(1)}, s16[1040,128]{1,0:T(8,128)(2,1)S(1)}, u32[]{:S(2)}, u32[]{:S(2)}) collective-permute-start(s16[1040,128]{1,0:T(8,128)(2,1)S(1)} %matmul_far.1), channel_id=1, source_target_pairs={{0,1},{1,2},{2,3},{3,0},{4,5},{5,6},{6,7},{7,4},{8,9},{9,10},{10,1... | collective-permute-start | bytes 798728 | tf_op jit(solution)/shard_map/layer_far/ppermute | solution.py:27
  122.0 7.0 %matmul_rest.1 = (f32[2,128,512]{2,1,0:T(8,128)S(1)}, f32[2,128,512]{2,1,0:T(8,128)S(1)}, f32[2,128,512]{2,1,0:T(8,128)S(1)}) custom-call(s32[6]{0:T(128)S(1)} %stack.36.pos_ref, s32[32]{0:T(128)S(1)} %bitcast.22, bf16[2,512,256]{2,1,0:T(8,128)(2,1)S(1)} %copy-done.5, bf16[2,512,256]{2,1,0:T(8,128)(2,1)S(1)} %copy-done.7, ...), custom_call_target="tpu_custom_call" | custom-call | flops 3221225472 | bytes 1048576 | tf_op jit(solution)/shard_map/matmul_rest/pallas_call | solution.py:164
  130.0 3.2 %collective-permute-start.17 = (s16[1040,128]{1,0:T(8,128)(2,1)S(1)}, s16[1040,128]{1,0:T(8,128)(2,1)S(1)}, u32[]{:S(2)}, u32[]{:S(2)}) collective-permute-start(s16[1040,128]{1,0:T(8,128)(2,1)S(1)} %get-tuple-element.45), channel_id=1, source_target_pairs={{0,1},{1,2},{2,3},{3,0},{4,5},{5,6},{6,7},{7,4},{8,9},{9,10},{10,1... | collective-permute-start | bytes 798728 | tf_op jit(solution)/shard_map/layer_sums/ppermute | solution.py:27
  133.2 6.0 %collective-permute-start.18 = (s16[1040,128]{1,0:T(8,128)(2,1)S(1)}, s16[1040,128]{1,0:T(8,128)(2,1)S(1)}, u32[]{:S(2)}, u32[]{:S(2)}) collective-permute-start(s16[1040,128]{1,0:T(8,128)(2,1)S(1)} %get-tuple-element.46), channel_id=1, source_target_pairs={{0,3},{1,0},{2,1},{3,2},{4,7},{5,4},{6,5},{7,6},{8,11},{9,8},{10,9... | collective-permute-start | bytes 798728 | tf_op jit(solution)/shard_map/layer_sums/ppermute | solution.py:27
  139.2 7.3 %collective-permute-done.17.refs_0_ = s16[1040,128]{1,0:T(8,128)(2,1)S(1)} collective-permute-done((s16[1040,128]{1,0:T(8,128)(2,1)S(1)}, s16[1040,128]{1,0:T(8,128)(2,1)S(1)}, u32[]{:S(2)}, u32[]{:S(2)}) %collective-permute-start.17) | collective-permute-done | bytes 266272 | tf_op jit(solution)/shard_map/layer_sums/ppermute | solution.py:27
  147.2 25.0 %collective-permute-start.19 = (bf16[128,512]{1,0:T(8,128)(2,1)S(1)}, bf16[128,512]{1,0:T(8,128)(2,1)S(1)}, u32[]{:S(2)}, u32[]{:S(2)}) collective-permute-start(bf16[128,512]{1,0:T(8,128)(2,1)S(1)} %get-tuple-element.47), channel_id=1, source_target_pairs={{0,0},{1,1},{2,2},{3,3},{4,4},{5,5},{6,6},{7,7},{8,8},{9,9},{10,10... | collective-permute-start | bytes 393224 | tf_op jit(solution)/shard_map/product_pair/ppermute | solution.py:27
  174.8 3.1 %collective-permute-done.20.second_ref = bf16[128,512]{1,0:T(8,128)(2,1)S(1)} collective-permute-done((bf16[128,512]{1,0:T(8,128)(2,1)S(1)}, bf16[128,512]{1,0:T(8,128)(2,1)S(1)}, u32[]{:S(2)}, u32[]{:S(2)}) %collective-permute-start.20) | collective-permute-done | bytes 131104 | tf_op jit(solution)/shard_map/product_pair/ppermute | solution.py:27
  (68 shorter events, 40.1 us)
Async XLA Ops:
  0.0 21.1 %collective-permute-start.2 = (bf16[4,128,512]{2,1,0:T(8,128)(2,1)}, bf16[4,128,512]{2,1,0:T(8,128)(2,1)S(1)}, u32[]{:S(2)}, u32[]{:S(2)}) collective-permute-start(bf16[4,128,512]{2,1,0:T(8,128)(2,1)} %bitcast.14), channel_id=1, source_target_pairs={{0,16},{1,17},{2,18},{3,19},{4,20},{5,21},{6,22},{7,23},{8,24},{9,... | collective-permute-start | bytes 1572872 | tf_op jit(solution)/shard_map/round0/ppermute | solution.py:27
  6.1 12.6 %collective-permute-start = (bf16[512,256]{1,0:T(8,128)(2,1)S(1)}, bf16[512,256]{1,0:T(8,128)(2,1)S(1)}, u32[]{:S(2)}, u32[]{:S(2)}) collective-permute-start(bf16[512,256]{1,0:T(8,128)(2,1)S(1)} %get-tuple-element.27), channel_id=1, source_target_pairs={{0,0},{1,1},{2,2},{3,3},{4,4},{5,5},{6,6},{7,7},{8,8},{9,9},{10,10... | collective-permute-start | bytes 786440 | tf_op jit(solution)/shard_map/round0/ppermute | solution.py:27
  8.7 12.4 %collective-permute-start.1 = (bf16[512,256]{1,0:T(8,128)(2,1)S(1)}, bf16[512,256]{1,0:T(8,128)(2,1)S(1)}, u32[]{:S(2)}, u32[]{:S(2)}) collective-permute-start(bf16[512,256]{1,0:T(8,128)(2,1)S(1)} %get-tuple-element.28), channel_id=1, source_target_pairs={{0,64},{1,65},{2,66},{3,67},{4,68},{5,69},{6,70},{7,71},{8,72},{9,... | collective-permute-start | bytes 786440 | tf_op jit(solution)/shard_map/round0/ppermute | solution.py:27
  21.2 37.2 %copy-start.2 = (bf16[1,4,128,512]{3,2,1,0:T(8,128)(2,1)S(1)}, bf16[1,4,128,512]{3,2,1,0:T(8,128)(2,1)}, u32[]{:S(2)}) copy-start(bf16[1,4,128,512]{3,2,1,0:T(8,128)(2,1)} %param.7) | copy-start | bytes 1572868
  21.2 24.6 %collective-permute-start.3 = (bf16[2,512,256]{2,1,0:T(8,128)(2,1)S(1)}, bf16[2,512,256]{2,1,0:T(8,128)(2,1)S(1)}, u32[]{:S(2)}, u32[]{:S(2)}) collective-permute-start(bf16[2,512,256]{2,1,0:T(8,128)(2,1)S(1)} %pad_maximum_fusion.4.refs_0_), channel_id=1, source_target_pairs={{0,32},{1,33},{2,34},{3,35},{4,36},{5,37},{6,38},{7,39},{8,40},{9,... | collective-permute-start | bytes 1572872 | tf_op jit(solution)/shard_map/round1/ppermute | solution.py:27
  23.2 22.5 %collective-permute-start.4 = (bf16[2,512,256]{2,1,0:T(8,128)(2,1)S(1)}, bf16[2,512,256]{2,1,0:T(8,128)(2,1)S(1)}, u32[]{:S(2)}, u32[]{:S(2)}) collective-permute-start(bf16[2,512,256]{2,1,0:T(8,128)(2,1)S(1)} %pad_maximum_fusion.4.refs_0_), channel_id=1, source_target_pairs={{0,4},{1,5},{2,6},{3,7},{4,8},{5,9},{6,10},{7,11},{8,12},{9,13},{1... | collective-permute-start | bytes 1572872 | tf_op jit(solution)/shard_map/round1/ppermute | solution.py:27
  25.3 20.4 %collective-permute-start.5 = (bf16[2,512,256]{2,1,0:T(8,128)(2,1)S(1)}, bf16[2,512,256]{2,1,0:T(8,128)(2,1)S(1)}, u32[]{:S(2)}, u32[]{:S(2)}) collective-permute-start(bf16[2,512,256]{2,1,0:T(8,128)(2,1)S(1)} %pad_maximum_fusion.4.refs_0_), channel_id=1, source_target_pairs={{0,12},{1,13},{2,14},{3,15},{4,0},{5,1},{6,2},{7,3},{8,4},{9,5},{1... | collective-permute-start | bytes 1572872 | tf_op jit(solution)/shard_map/round1/ppermute | solution.py:27
  29.3 16.4 %collective-permute-start.6 = (bf16[4,128,512]{2,1,0:T(8,128)(2,1)}, bf16[4,128,512]{2,1,0:T(8,128)(2,1)S(1)}, u32[]{:S(2)}, u32[]{:S(2)}) collective-permute-start(bf16[4,128,512]{2,1,0:T(8,128)(2,1)} %bitcast.15), channel_id=1, source_target_pairs={{0,128},{1,129},{2,130},{3,131},{4,132},{5,133},{6,134},{7,135},{8... | collective-permute-start | bytes 1572872 | tf_op jit(solution)/shard_map/round1/ppermute | solution.py:27
  32.5 13.5 %collective-permute-start.7 = (bf16[4,128,512]{2,1,0:T(8,128)(2,1)}, bf16[4,128,512]{2,1,0:T(8,128)(2,1)S(1)}, u32[]{:S(2)}, u32[]{:S(2)}) collective-permute-start(bf16[4,128,512]{2,1,0:T(8,128)(2,1)} %bitcast.16), channel_id=1, source_target_pairs={{0,384},{1,385},{2,386},{3,387},{4,388},{5,389},{6,390},{7,391},{8... | collective-permute-start | bytes 1572872 | tf_op jit(solution)/shard_map/round1/ppermute | solution.py:27
  46.2 19.4 %collective-permute-start.10 = (bf16[6,128,512]{2,1,0:T(8,128)(2,1)S(1)}, bf16[6,128,512]{2,1,0:T(8,128)(2,1)S(1)}, u32[]{:S(2)}, u32[]{:S(2)}) collective-permute-start(bf16[6,128,512]{2,1,0:T(8,128)(2,1)S(1)} %get-tuple-element.50), channel_id=1, source_target_pairs={{0,128},{1,129},{2,130},{3,131},{4,132},{5,133},{6,134},{7,135},{8... | collective-permute-start | bytes 2359304 | tf_op jit(solution)/shard_map/round2/ppermute | solution.py:27
  49.4 17.8 %collective-permute-start.11 = (bf16[6,128,512]{2,1,0:T(8,128)(2,1)S(1)}, bf16[6,128,512]{2,1,0:T(8,128)(2,1)S(1)}, u32[]{:S(2)}, u32[]{:S(2)}) collective-permute-start(bf16[6,128,512]{2,1,0:T(8,128)(2,1)S(1)} %get-tuple-element.49), channel_id=1, source_target_pairs={{0,384},{1,385},{2,386},{3,387},{4,388},{5,389},{6,390},{7,391},{8... | collective-permute-start | bytes 2359304 | tf_op jit(solution)/shard_map/round2/ppermute | solution.py:27
  53.0 17.6 %collective-permute-start.8 = (bf16[3,512,256]{2,1,0:T(8,128)(2,1)S(1)}, bf16[3,512,256]{2,1,0:T(8,128)(2,1)}, u32[]{:S(2)}, u32[]{:S(2)}) collective-permute-start(bf16[3,512,256]{2,1,0:T(8,128)(2,1)S(1)} %get-tuple-element.52), channel_id=1, source_target_pairs={{0,4},{1,5},{2,6},{3,7},{4,8},{5,9},{6,10},{7,11},{8,12},{9,13},{1... | collective-permute-start | bytes 2359304 | tf_op jit(solution)/shard_map/round2/ppermute | solution.py:27
  56.3 18.5 %collective-permute-start.9 = (bf16[3,512,256]{2,1,0:T(8,128)(2,1)S(1)}, bf16[3,512,256]{2,1,0:T(8,128)(2,1)}, u32[]{:S(2)}, u32[]{:S(2)}) collective-permute-start(bf16[3,512,256]{2,1,0:T(8,128)(2,1)S(1)} %get-tuple-element.51), channel_id=1, source_target_pairs={{0,12},{1,13},{2,14},{3,15},{4,0},{5,1},{6,2},{7,3},{8,4},{9,5},{1... | collective-permute-start | bytes 2359304 | tf_op jit(solution)/shard_map/round2/ppermute | solution.py:27
  60.9 41.5 %copy-start.11 = (s32[1,32]{1,0:T(1,128)S(1)}, s32[1,32]{1,0:T(1,128)}, u32[]{:S(2)}) copy-start(s32[1,32]{1,0:T(1,128)} %param.8) | copy-start | bytes 388
  76.7 25.7 %collective-permute-start.14 = (bf16[28,128,512]{2,1,0:T(8,128)(2,1)}, bf16[28,128,512]{2,1,0:T(8,128)(2,1)}, u32[]{:S(2)}, u32[]{:S(2)}) collective-permute-start(bf16[28,128,512]{2,1,0:T(8,128)(2,1)} %constant_dynamic-update-slice_fusion), channel_id=1, source_target_pairs={{0,64},{1,65},{2,66},{3,67},{4,68},{5,69},{6,70},{7,71},{8,72},{9,... | collective-permute-start | bytes 11010056 | tf_op jit(solution)/shard_map/round3/ppermute | solution.py:27
  83.3 10.2 %collective-permute-start.13 = (bf16[4,128,512]{2,1,0:T(8,128)(2,1)S(1)}, bf16[4,128,512]{2,1,0:T(8,128)(2,1)S(1)}, u32[]{:S(2)}, u32[]{:S(2)}) collective-permute-start(bf16[4,128,512]{2,1,0:T(8,128)(2,1)S(1)} %slice_select_fusion), channel_id=1, source_target_pairs={{0,128},{1,129},{2,130},{3,131},{4,132},{5,133},{6,134},{7,135},{8... | collective-permute-start | bytes 1572872 | tf_op jit(solution)/shard_map/round3/ppermute | solution.py:27
  86.4 14.1 %collective-permute-start.15 = (bf16[4,128,512]{2,1,0:T(8,128)(2,1)S(1)}, bf16[4,128,512]{2,1,0:T(8,128)(2,1)S(1)}, u32[]{:S(2)}, u32[]{:S(2)}) collective-permute-start(bf16[4,128,512]{2,1,0:T(8,128)(2,1)S(1)} %slice_select_fusion), channel_id=1, source_target_pairs={{0,192},{1,193},{2,194},{3,195},{4,196},{5,197},{6,198},{7,199},{8... | collective-permute-start | bytes 1572872 | tf_op jit(solution)/shard_map/round3/ppermute | solution.py:27
  91.2 11.1 %collective-permute-start.12 = (bf16[2,512,256]{2,1,0:T(8,128)(2,1)S(1)}, bf16[2,512,256]{2,1,0:T(8,128)(2,1)S(1)}, u32[]{:S(2)}, u32[]{:S(2)}) collective-permute-start(bf16[2,512,256]{2,1,0:T(8,128)(2,1)S(1)} %slice_select_fusion.1), channel_id=1, source_target_pairs={{0,4},{1,5},{2,6},{3,7},{4,8},{5,9},{6,10},{7,11},{8,12},{9,13},{1... | collective-permute-start | bytes 1572872 | tf_op jit(solution)/shard_map/round3/ppermute | solution.py:27
  112.0 65.9 %copy-start.13 = (s32[2,4]{1,0:T(2,128)S(1)}, s32[2,4]{1,0:T(2,128)}, u32[]{:S(2)}) copy-start(s32[2,4]{1,0:T(2,128)} %pat_ref.1) | copy-start | bytes 100
  112.1 17.0 %collective-permute-start.16 = (s16[1040,128]{1,0:T(8,128)(2,1)S(1)}, s16[1040,128]{1,0:T(8,128)(2,1)S(1)}, u32[]{:S(2)}, u32[]{:S(2)}) collective-permute-start(s16[1040,128]{1,0:T(8,128)(2,1)S(1)} %matmul_far.1), channel_id=1, source_target_pairs={{0,1},{1,2},{2,3},{3,0},{4,5},{5,6},{6,7},{7,4},{8,9},{9,10},{10,1... | collective-permute-start | bytes 798728 | tf_op jit(solution)/shard_map/layer_far/ppermute | solution.py:27
  130.0 16.5 %collective-permute-start.17 = (s16[1040,128]{1,0:T(8,128)(2,1)S(1)}, s16[1040,128]{1,0:T(8,128)(2,1)S(1)}, u32[]{:S(2)}, u32[]{:S(2)}) collective-permute-start(s16[1040,128]{1,0:T(8,128)(2,1)S(1)} %get-tuple-element.45), channel_id=1, source_target_pairs={{0,1},{1,2},{2,3},{3,0},{4,5},{5,6},{6,7},{7,4},{8,9},{9,10},{10,1... | collective-permute-start | bytes 798728 | tf_op jit(solution)/shard_map/layer_sums/ppermute | solution.py:27
  133.2 13.3 %collective-permute-start.18 = (s16[1040,128]{1,0:T(8,128)(2,1)S(1)}, s16[1040,128]{1,0:T(8,128)(2,1)S(1)}, u32[]{:S(2)}, u32[]{:S(2)}) collective-permute-start(s16[1040,128]{1,0:T(8,128)(2,1)S(1)} %get-tuple-element.46), channel_id=1, source_target_pairs={{0,3},{1,0},{2,1},{3,2},{4,7},{5,4},{6,5},{7,6},{8,11},{9,8},{10,9... | collective-permute-start | bytes 798728 | tf_op jit(solution)/shard_map/layer_sums/ppermute | solution.py:27
  147.2 27.7 %collective-permute-start.19 = (bf16[128,512]{1,0:T(8,128)(2,1)S(1)}, bf16[128,512]{1,0:T(8,128)(2,1)S(1)}, u32[]{:S(2)}, u32[]{:S(2)}) collective-permute-start(bf16[128,512]{1,0:T(8,128)(2,1)S(1)} %get-tuple-element.47), channel_id=1, source_target_pairs={{0,0},{1,1},{2,2},{3,3},{4,4},{5,5},{6,6},{7,7},{8,8},{9,9},{10,10... | collective-permute-start | bytes 393224 | tf_op jit(solution)/shard_map/product_pair/ppermute | solution.py:27
  172.2 5.7 %collective-permute-start.20 = (bf16[128,512]{1,0:T(8,128)(2,1)S(1)}, bf16[128,512]{1,0:T(8,128)(2,1)S(1)}, u32[]{:S(2)}, u32[]{:S(2)}) collective-permute-start(bf16[128,512]{1,0:T(8,128)(2,1)S(1)} %get-tuple-element.48), channel_id=1, source_target_pairs={{0,16},{1,17},{2,18},{3,19},{4,20},{5,21},{6,22},{7,23},{8,24},{9,... | collective-permute-start | bytes 393224 | tf_op jit(solution)/shard_map/product_pair/ppermute | solution.py:27
  (11 other events, 29.5 us)

commit v8 on v7

--- a/solution.py
+++ b/solution.py
@@ -89,13 +89,13 @@
     (7, 4, 4, 1, 1, 0, 0),
     (7, 8, 4, 0, 1, 3, 0),
     (7, 12, 4, 0, 1, 1, 0),
-    (7, 16, 2, 0, 1, 2, 0),
-    (7, 18, 4, 1, 1, 3, 0),
-    (7, 22, 2, 0, 1, 2, 2),
-    (7, 24, 4, 1, 1, 1, 0),
-    (8, 0, 4, 1, 1, 2, 0),
+    (8, 0, 2, 0, 1, 2, 0),
+    (8, 2, 4, 1, 1, 3, 0),
+    (8, 6, 2, 0, 1, 2, 2),
+    (8, 8, 4, 1, 1, 1, 0),
+    (9, 0, 4, 1, 1, 2, 0),
 )
-NA, NB = 7, 9
+NA, NB = 7, 10
 
 
 def quantize(tiles, o_ref):
@@ -260,16 +260,17 @@
     with jax.named_scope("round2"):
         a2p, a2m = to_x(cat(a1p[:1], far), 1), to_x(cat(a1m[1:], far), -1)
         b2p, b2m = to_y(cat(b1p[:2], pair), 1), to_y(cat(b1m[2:], pair), -1)
-        a2p, a2m, b2p, b2m = lax.optimization_barrier((a2p, a2m, b2p, b2m))
+        swap1 = to_core(cat(late, pair, b1p, b1m))
+        a2p, a2m, b2p, b2m, swap1 = lax.optimization_barrier((a2p, a2m, b2p, b2m, swap1))
     with jax.named_scope("round3"):
         even = row % 2 == 0
         hand_a, hand_b = jnp.where(even, a2p[1:], a2m[1:]), jnp.where(even, b2p[2:], b2m[2:])
         a3 = send(hand_a, lambda y, c, zl, x, zh: (y, c, zl, (x + 1 - 2 * c) % 4, zh))
         b3 = send(hand_b, lambda y, c, zl, x, zh: ((y + 1 - 2 * c) % 4, c, zl, x, zh))
         b3x = send(hand_b, lambda y, c, zl, x, zh: ((y + 1 - 2 * c) % 4, 1 - c, zl, x, zh))
-        swap = to_core(cat(late, pair, b1p, b1m, b2p, b2m))
+        swap2 = to_core(cat(b2p, b2m))
     a = (near, a1p, a1m, far, a2p, a2m, a3)
-    b = (late, pair, b1p, b1m, b2p, b2m, b3, swap, b3x)
+    b = (late, pair, b1p, b1m, b2p, b2m, b3, swap1, swap2, b3x)
     far_shape = [jax.ShapeDtypeStruct((8 * BS + PAD, BS), jnp.int16)]
     rest_shape = [jax.ShapeDtypeStruct((2, BS, 4 * BS), jnp.float32)] * 3
     got, = matmul(far_kernel, "matmul_far", 1, far_shape, pos, owner[0], a, b)

time: 180 us -> 192 us (1.067)
  the two profiles are of different devices: /device:TPU:71 before, /device:TPU:65 now
where the time goes in v8:
time: 192 us; the launch traced here: 191 us
  starting transfers between devices  94.4 us (49%)
  waiting for transfers between devices  67.2 us (35%)
  Pallas kernels  12.9 us (7%)
  local copies, waits for them, and re-layouts  11.5 us (6%)
  other arithmetic  4.54 us (2%)
    ppermute x22, starting transfers between devices, send(): return lax.ppermute(v, AXES, moves(f))  94.4 us
    ppermute x22, waiting for transfers between devices, send(): return lax.ppermute(v, AXES, moves(f))  67.2 us
    unnamed x48, local copies, waits for them, and re-layouts  11.3 us
    pallas_call x2, Pallas kernels, matmul(): pl.pallas_call(kernel, out_shape=out_shape, in_specs=[pl.BlockSpec(memory...  9.25 us
  transfers between devices with their start and end apart: 22, of which 14 were waited for; matrix products, arithmetic and copies ran while one was open for 1% of the time, Pallas kernels for 3%

profile of v8, /device:TPU:65, one launch (start us, length us, event | category | flops | bytes accessed | tf_op | source)
XLA Modules:
  0.0 191.0 jit_solution(3118602528757414977)
XLA Ops:
  0.0 3.5 %collective-permute-start.2 = (bf16[4,128,512]{2,1,0:T(8,128)(2,1)}, bf16[4,128,512]{2,1,0:T(8,128)(2,1)S(1)}, u32[]{:S(2)}, u32[]{:S(2)}) collective-permute-start(bf16[4,128,512]{2,1,0:T(8,128)(2,1)} %bitcast.14), channel_id=1, source_target_pairs={{0,16},{1,17},{2,18},{3,19},{4,20},{5,21},{6,22},{7,23},{8,24},{9,... | collective-permute-start | bytes 1572872 | tf_op jit(solution)/shard_map/round0/ppermute | solution.py:27
  6.1 2.6 %collective-permute-start = (bf16[512,256]{1,0:T(8,128)(2,1)S(1)}, bf16[512,256]{1,0:T(8,128)(2,1)S(1)}, u32[]{:S(2)}, u32[]{:S(2)}) collective-permute-start(bf16[512,256]{1,0:T(8,128)(2,1)S(1)} %get-tuple-element.28), channel_id=1, source_target_pairs={{0,0},{1,1},{2,2},{3,3},{4,4},{5,5},{6,6},{7,7},{8,8},{9,9},{10,10... | collective-permute-start | bytes 786440 | tf_op jit(solution)/shard_map/round0/ppermute | solution.py:27
  10.6 8.1 %collective-permute-done = bf16[512,256]{1,0:T(8,128)(2,1)S(1)} collective-permute-done((bf16[512,256]{1,0:T(8,128)(2,1)S(1)}, bf16[512,256]{1,0:T(8,128)(2,1)S(1)}, u32[]{:S(2)}, u32[]{:S(2)}) %collective-permute-start) | collective-permute-done | bytes 262176 | tf_op jit(solution)/shard_map/round0/ppermute | solution.py:27
  23.1 3.1 %collective-permute-start.4 = (bf16[2,512,256]{2,1,0:T(8,128)(2,1)S(1)}, bf16[2,512,256]{2,1,0:T(8,128)(2,1)S(1)}, u32[]{:S(2)}, u32[]{:S(2)}) collective-permute-start(bf16[2,512,256]{2,1,0:T(8,128)(2,1)S(1)} %pad_maximum_fusion.6.refs_0_), channel_id=1, source_target_pairs={{0,4},{1,5},{2,6},{3,7},{4,8},{5,9},{6,10},{7,11},{8,12},{9,13},{1... | collective-permute-start | bytes 1572872 | tf_op jit(solution)/shard_map/round1/ppermute | solution.py:27
  26.2 3.4 %collective-permute-start.5 = (bf16[2,512,256]{2,1,0:T(8,128)(2,1)S(1)}, bf16[2,512,256]{2,1,0:T(8,128)(2,1)S(1)}, u32[]{:S(2)}, u32[]{:S(2)}) collective-permute-start(bf16[2,512,256]{2,1,0:T(8,128)(2,1)S(1)} %pad_maximum_fusion.6.refs_0_), channel_id=1, source_target_pairs={{0,12},{1,13},{2,14},{3,15},{4,0},{5,1},{6,2},{7,3},{8,4},{9,5},{1... | collective-permute-start | bytes 1572872 | tf_op jit(solution)/shard_map/round1/ppermute | solution.py:27
  30.4 3.2 %collective-permute-start.6 = (bf16[4,128,512]{2,1,0:T(8,128)(2,1)}, bf16[4,128,512]{2,1,0:T(8,128)(2,1)S(1)}, u32[]{:S(2)}, u32[]{:S(2)}) collective-permute-start(bf16[4,128,512]{2,1,0:T(8,128)(2,1)} %bitcast.15), channel_id=1, source_target_pairs={{0,128},{1,129},{2,130},{3,131},{4,132},{5,133},{6,134},{7,135},{8... | collective-permute-start | bytes 1572872 | tf_op jit(solution)/shard_map/round1/ppermute | solution.py:27
  33.6 3.4 %collective-permute-start.7 = (bf16[4,128,512]{2,1,0:T(8,128)(2,1)}, bf16[4,128,512]{2,1,0:T(8,128)(2,1)S(1)}, u32[]{:S(2)}, u32[]{:S(2)}) collective-permute-start(bf16[4,128,512]{2,1,0:T(8,128)(2,1)} %bitcast.16), channel_id=1, source_target_pairs={{0,384},{1,385},{2,386},{3,387},{4,388},{5,389},{6,390},{7,391},{8... | collective-permute-start | bytes 1572872 | tf_op jit(solution)/shard_map/round1/ppermute | solution.py:27
  36.9 8.3 %collective-permute-done.3.refs_3_ = bf16[2,512,256]{2,1,0:T(8,128)(2,1)S(1)} collective-permute-done((bf16[2,512,256]{2,1,0:T(8,128)(2,1)S(1)}, bf16[2,512,256]{2,1,0:T(8,128)(2,1)S(1)}, u32[]{:S(2)}, u32[]{:S(2)}) %collective-permute-start.3) | collective-permute-done | bytes 524320 | tf_op jit(solution)/shard_map/round1/ppermute | solution.py:27
  48.6 4.8 %collective-permute-start.12 = (bf16[16,128,512]{2,1,0:T(8,128)(2,1)S(1)}, bf16[16,128,512]{2,1,0:T(8,128)(2,1)S(1)}, u32[]{:S(2)}, u32[]{:S(2)}) collective-permute-start(bf16[16,128,512]{2,1,0:T(8,128)(2,1)S(1)} %pad_maximum_fusion), channel_id=1, source_target_pairs={{0,64},{1,65},{2,66},{3,67},{4,68},{5,69},{6,70},{7,71},{8,72},{9,... | collective-permute-start | bytes 6291464 | tf_op jit(solution)/shard_map/round2/ppermute | solution.py:27
  55.6 4.6 %collective-permute-start.9 = (bf16[3,512,256]{2,1,0:T(8,128)(2,1)S(1)}, bf16[3,512,256]{2,1,0:T(8,128)(2,1)S(1)}, u32[]{:S(2)}, u32[]{:S(2)}) collective-permute-start(bf16[3,512,256]{2,1,0:T(8,128)(2,1)S(1)} %get-tuple-element.53), channel_id=1, source_target_pairs={{0,12},{1,13},{2,14},{3,15},{4,0},{5,1},{6,2},{7,3},{8,4},{9,5},{1... | collective-permute-start | bytes 2359304 | tf_op jit(solution)/shard_map/round2/ppermute | solution.py:27
  60.3 3.2 %collective-permute-start.10 = (bf16[6,128,512]{2,1,0:T(8,128)(2,1)S(1)}, bf16[6,128,512]{2,1,0:T(8,128)(2,1)S(1)}, u32[]{:S(2)}, u32[]{:S(2)}) collective-permute-start(bf16[6,128,512]{2,1,0:T(8,128)(2,1)S(1)} %get-tuple-element.52), channel_id=1, source_target_pairs={{0,128},{1,129},{2,130},{3,131},{4,132},{5,133},{6,134},{7,135},{8... | collective-permute-start | bytes 2359304 | tf_op jit(solution)/shard_map/round2/ppermute | solution.py:27
  63.6 3.3 %collective-permute-start.11 = (bf16[6,128,512]{2,1,0:T(8,128)(2,1)S(1)}, bf16[6,128,512]{2,1,0:T(8,128)(2,1)S(1)}, u32[]{:S(2)}, u32[]{:S(2)}) collective-permute-start(bf16[6,128,512]{2,1,0:T(8,128)(2,1)S(1)} %get-tuple-element.51), channel_id=1, source_target_pairs={{0,384},{1,385},{2,386},{3,387},{4,388},{5,389},{6,390},{7,391},{8... | collective-permute-start | bytes 2359304 | tf_op jit(solution)/shard_map/round2/ppermute | solution.py:27
  66.8 9.1 %collective-permute-done.8.refs_4_ = bf16[3,512,256]{2,1,0:T(8,128)(2,1)S(1)} collective-permute-done((bf16[3,512,256]{2,1,0:T(8,128)(2,1)S(1)}, bf16[3,512,256]{2,1,0:T(8,128)(2,1)S(1)}, u32[]{:S(2)}, u32[]{:S(2)}) %collective-permute-start.8) | collective-permute-done | bytes 786464 | tf_op jit(solution)/shard_map/round2/ppermute | solution.py:27
  76.8 5.1 %collective-permute-done.10.refs_11_ = bf16[6,128,512]{2,1,0:T(8,128)(2,1)S(1)} collective-permute-done((bf16[6,128,512]{2,1,0:T(8,128)(2,1)S(1)}, bf16[6,128,512]{2,1,0:T(8,128)(2,1)S(1)}, u32[]{:S(2)}, u32[]{:S(2)}) %collective-permute-start.10) | collective-permute-done | bytes 786464 | tf_op jit(solution)/shard_map/round2/ppermute | solution.py:27
  86.3 3.8 %collective-permute-start.15 = (bf16[12,128,512]{2,1,0:T(8,128)(2,1)}, bf16[12,128,512]{2,1,0:T(8,128)(2,1)}, u32[]{:S(2)}, u32[]{:S(2)}) collective-permute-start(bf16[12,128,512]{2,1,0:T(8,128)(2,1)} %pad_maximum_fusion.1), channel_id=1, source_target_pairs={{0,64},{1,65},{2,66},{3,67},{4,68},{5,69},{6,70},{7,71},{8,72},{9,... | collective-permute-start | bytes 4718600 | tf_op jit(solution)/shard_map/round3/ppermute | solution.py:27
  93.6 4.5 %collective-permute-start.14 = (bf16[4,128,512]{2,1,0:T(8,128)(2,1)S(1)}, bf16[4,128,512]{2,1,0:T(8,128)(2,1)S(1)}, u32[]{:S(2)}, u32[]{:S(2)}) collective-permute-start(bf16[4,128,512]{2,1,0:T(8,128)(2,1)S(1)} %slice_select_fusion), channel_id=1, source_target_pairs={{0,128},{1,129},{2,130},{3,131},{4,132},{5,133},{6,134},{7,135},{8... | collective-permute-start | bytes 1572872 | tf_op jit(solution)/shard_map/round3/ppermute | solution.py:27
  104.2 6.6 %collective-permute-done.16.refs_16_ = bf16[4,128,512]{2,1,0:T(8,128)(2,1)S(1)} collective-permute-done((bf16[4,128,512]{2,1,0:T(8,128)(2,1)S(1)}, bf16[4,128,512]{2,1,0:T(8,128)(2,1)S(1)}, u32[]{:S(2)}, u32[]{:S(2)}) %collective-permute-start.16) | collective-permute-done | bytes 524320 | tf_op jit(solution)/shard_map/round3/ppermute | solution.py:27
  118.3 3.4 %matmul_far.1 = s16[1040,128]{1,0:T(8,128)(2,1)S(1)} custom-call(s32[6]{0:T(128)S(1)} %stack.36.pos_ref, s32[32]{0:T(128)S(1)} %bitcast.21, bf16[2,512,256]{2,1,0:T(8,128)(2,1)S(1)} %copy-done.13, bf16[2,512,256]{2,1,0:T(8,128)(2,1)S(1)} %copy-done.17, bf16[2,512,256]{2,1,0:T(8,128)(2,1)S(1)} %copy-done.19, bf16[2,512,256]{2,1,0:T(8,128)(2,1)S(1)} %copy-done.11, ...), custom_call_target="tpu_custom_call" | custom-call | flops 1073741824 | bytes 1048576 | tf_op jit(solution)/shard_map/matmul_far/pallas_call | solution.py:164
  121.6 10.9 %collective-permute-start.17 = (s16[1040,128]{1,0:T(8,128)(2,1)S(1)}, s16[1040,128]{1,0:T(8,128)(2,1)S(1)}, u32[]{:S(2)}, u32[]{:S(2)}) collective-permute-start(s16[1040,128]{1,0:T(8,128)(2,1)S(1)} %matmul_far.1), channel_id=1, source_target_pairs={{0,1},{1,2},{2,3},{3,0},{4,5},{5,6},{6,7},{7,4},{8,9},{9,10},{10,1... | collective-permute-start | bytes 798728 | tf_op jit(solution)/shard_map/layer_far/ppermute | solution.py:27
  132.6 5.9 %matmul_rest.1 = (f32[2,128,512]{2,1,0:T(8,128)S(1)}, f32[2,128,512]{2,1,0:T(8,128)S(1)}, f32[2,128,512]{2,1,0:T(8,128)S(1)}) custom-call(s32[6]{0:T(128)S(1)} %stack.36.pos_ref, s32[32]{0:T(128)S(1)} %bitcast.22, bf16[2,512,256]{2,1,0:T(8,128)(2,1)S(1)} %copy-done.13, bf16[2,512,256]{2,1,0:T(8,128)(2,1)S(1)} %copy-done.17, ...), custom_call_target="tpu_custom_call" | custom-call | flops 3221225472 | bytes 1048576 | tf_op jit(solution)/shard_map/matmul_rest/pallas_call | solution.py:164
  139.4 7.7 %collective-permute-start.18 = (s16[1040,128]{1,0:T(8,128)(2,1)S(1)}, s16[1040,128]{1,0:T(8,128)(2,1)S(1)}, u32[]{:S(2)}, u32[]{:S(2)}) collective-permute-start(s16[1040,128]{1,0:T(8,128)(2,1)S(1)} %get-tuple-element.47), channel_id=1, source_target_pairs={{0,1},{1,2},{2,3},{3,0},{4,5},{5,6},{6,7},{7,4},{8,9},{9,10},{10,1... | collective-permute-start | bytes 798728 | tf_op jit(solution)/shard_map/layer_sums/ppermute | solution.py:27
  149.0 15.5 %collective-permute-done.18.refs_0_ = s16[1040,128]{1,0:T(8,128)(2,1)S(1)} collective-permute-done((s16[1040,128]{1,0:T(8,128)(2,1)S(1)}, s16[1040,128]{1,0:T(8,128)(2,1)S(1)}, u32[]{:S(2)}, u32[]{:S(2)}) %collective-permute-start.18) | collective-permute-done | bytes 266272 | tf_op jit(solution)/shard_map/layer_sums/ppermute | solution.py:27
  165.2 18.8 %collective-permute-start.20 = (bf16[128,512]{1,0:T(8,128)(2,1)S(1)}, bf16[128,512]{1,0:T(8,128)(2,1)S(1)}, u32[]{:S(2)}, u32[]{:S(2)}) collective-permute-start(bf16[128,512]{1,0:T(8,128)(2,1)S(1)} %get-tuple-element.49), channel_id=1, source_target_pairs={{0,0},{1,1},{2,2},{3,3},{4,4},{5,5},{6,6},{7,7},{8,8},{9,9},{10,10... | collective-permute-start | bytes 393224 | tf_op jit(solution)/shard_map/product_pair/ppermute | solution.py:27
  186.6 3.1 %collective-permute-done.21.second_ref = bf16[128,512]{1,0:T(8,128)(2,1)S(1)} collective-permute-done((bf16[128,512]{1,0:T(8,128)(2,1)S(1)}, bf16[128,512]{1,0:T(8,128)(2,1)S(1)}, u32[]{:S(2)}, u32[]{:S(2)}) %collective-permute-start.21) | collective-permute-done | bytes 131104 | tf_op jit(solution)/shard_map/product_pair/ppermute | solution.py:27
  (88 shorter events, 44.8 us)
Async XLA Ops:
  0.0 21.1 %collective-permute-start.2 = (bf16[4,128,512]{2,1,0:T(8,128)(2,1)}, bf16[4,128,512]{2,1,0:T(8,128)(2,1)S(1)}, u32[]{:S(2)}, u32[]{:S(2)}) collective-permute-start(bf16[4,128,512]{2,1,0:T(8,128)(2,1)} %bitcast.14), channel_id=1, source_target_pairs={{0,16},{1,17},{2,18},{3,19},{4,20},{5,21},{6,22},{7,23},{8,24},{9,... | collective-permute-start | bytes 1572872 | tf_op jit(solution)/shard_map/round0/ppermute | solution.py:27
  6.1 12.6 %collective-permute-start = (bf16[512,256]{1,0:T(8,128)(2,1)S(1)}, bf16[512,256]{1,0:T(8,128)(2,1)S(1)}, u32[]{:S(2)}, u32[]{:S(2)}) collective-permute-start(bf16[512,256]{1,0:T(8,128)(2,1)S(1)} %get-tuple-element.28), channel_id=1, source_target_pairs={{0,0},{1,1},{2,2},{3,3},{4,4},{5,5},{6,6},{7,7},{8,8},{9,9},{10,10... | collective-permute-start | bytes 786440 | tf_op jit(solution)/shard_map/round0/ppermute | solution.py:27
  8.7 12.4 %collective-permute-start.1 = (bf16[512,256]{1,0:T(8,128)(2,1)S(1)}, bf16[512,256]{1,0:T(8,128)(2,1)S(1)}, u32[]{:S(2)}, u32[]{:S(2)}) collective-permute-start(bf16[512,256]{1,0:T(8,128)(2,1)S(1)} %get-tuple-element.29), channel_id=1, source_target_pairs={{0,64},{1,65},{2,66},{3,67},{4,68},{5,69},{6,70},{7,71},{8,72},{9,... | collective-permute-start | bytes 786440 | tf_op jit(solution)/shard_map/round0/ppermute | solution.py:27
  21.2 24.1 %collective-permute-start.3 = (bf16[2,512,256]{2,1,0:T(8,128)(2,1)S(1)}, bf16[2,512,256]{2,1,0:T(8,128)(2,1)S(1)}, u32[]{:S(2)}, u32[]{:S(2)}) collective-permute-start(bf16[2,512,256]{2,1,0:T(8,128)(2,1)S(1)} %pad_maximum_fusion.6.refs_0_), channel_id=1, source_target_pairs={{0,32},{1,33},{2,34},{3,35},{4,36},{5,37},{6,38},{7,39},{8,40},{9,... | collective-permute-start | bytes 1572872 | tf_op jit(solution)/shard_map/round1/ppermute | solution.py:27
  23.1 22.1 %collective-permute-start.4 = (bf16[2,512,256]{2,1,0:T(8,128)(2,1)S(1)}, bf16[2,512,256]{2,1,0:T(8,128)(2,1)S(1)}, u32[]{:S(2)}, u32[]{:S(2)}) collective-permute-start(bf16[2,512,256]{2,1,0:T(8,128)(2,1)S(1)} %pad_maximum_fusion.6.refs_0_), channel_id=1, source_target_pairs={{0,4},{1,5},{2,6},{3,7},{4,8},{5,9},{6,10},{7,11},{8,12},{9,13},{1... | collective-permute-start | bytes 1572872 | tf_op jit(solution)/shard_map/round1/ppermute | solution.py:27
  26.2 19.0 %collective-permute-start.5 = (bf16[2,512,256]{2,1,0:T(8,128)(2,1)S(1)}, bf16[2,512,256]{2,1,0:T(8,128)(2,1)S(1)}, u32[]{:S(2)}, u32[]{:S(2)}) collective-permute-start(bf16[2,512,256]{2,1,0:T(8,128)(2,1)S(1)} %pad_maximum_fusion.6.refs_0_), channel_id=1, source_target_pairs={{0,12},{1,13},{2,14},{3,15},{4,0},{5,1},{6,2},{7,3},{8,4},{9,5},{1... | collective-permute-start | bytes 1572872 | tf_op jit(solution)/shard_map/round1/ppermute | solution.py:27
  30.4 14.9 %collective-permute-start.6 = (bf16[4,128,512]{2,1,0:T(8,128)(2,1)}, bf16[4,128,512]{2,1,0:T(8,128)(2,1)S(1)}, u32[]{:S(2)}, u32[]{:S(2)}) collective-permute-start(bf16[4,128,512]{2,1,0:T(8,128)(2,1)} %bitcast.15), channel_id=1, source_target_pairs={{0,128},{1,129},{2,130},{3,131},{4,132},{5,133},{6,134},{7,135},{8... | collective-permute-start | bytes 1572872 | tf_op jit(solution)/shard_map/round1/ppermute | solution.py:27
  33.6 13.5 %collective-permute-start.7 = (bf16[4,128,512]{2,1,0:T(8,128)(2,1)}, bf16[4,128,512]{2,1,0:T(8,128)(2,1)S(1)}, u32[]{:S(2)}, u32[]{:S(2)}) collective-permute-start(bf16[4,128,512]{2,1,0:T(8,128)(2,1)} %bitcast.16), channel_id=1, source_target_pairs={{0,384},{1,385},{2,386},{3,387},{4,388},{5,389},{6,390},{7,391},{8... | collective-permute-start | bytes 1572872 | tf_op jit(solution)/shard_map/round1/ppermute | solution.py:27
  48.6 35.0 %collective-permute-start.12 = (bf16[16,128,512]{2,1,0:T(8,128)(2,1)S(1)}, bf16[16,128,512]{2,1,0:T(8,128)(2,1)S(1)}, u32[]{:S(2)}, u32[]{:S(2)}) collective-permute-start(bf16[16,128,512]{2,1,0:T(8,128)(2,1)S(1)} %pad_maximum_fusion), channel_id=1, source_target_pairs={{0,64},{1,65},{2,66},{3,67},{4,68},{5,69},{6,70},{7,71},{8,72},{9,... | collective-permute-start | bytes 6291464 | tf_op jit(solution)/shard_map/round2/ppermute | solution.py:27
  53.7 22.3 %collective-permute-start.8 = (bf16[3,512,256]{2,1,0:T(8,128)(2,1)S(1)}, bf16[3,512,256]{2,1,0:T(8,128)(2,1)S(1)}, u32[]{:S(2)}, u32[]{:S(2)}) collective-permute-start(bf16[3,512,256]{2,1,0:T(8,128)(2,1)S(1)} %get-tuple-element.54), channel_id=1, source_target_pairs={{0,4},{1,5},{2,6},{3,7},{4,8},{5,9},{6,10},{7,11},{8,12},{9,13},{1... | collective-permute-start | bytes 2359304 | tf_op jit(solution)/shard_map/round2/ppermute | solution.py:27
  55.6 21.2 %collective-permute-start.9 = (bf16[3,512,256]{2,1,0:T(8,128)(2,1)S(1)}, bf16[3,512,256]{2,1,0:T(8,128)(2,1)S(1)}, u32[]{:S(2)}, u32[]{:S(2)}) collective-permute-start(bf16[3,512,256]{2,1,0:T(8,128)(2,1)S(1)} %get-tuple-element.53), channel_id=1, source_target_pairs={{0,12},{1,13},{2,14},{3,15},{4,0},{5,1},{6,2},{7,3},{8,4},{9,5},{1... | collective-permute-start | bytes 2359304 | tf_op jit(solution)/shard_map/round2/ppermute | solution.py:27
  60.3 21.6 %collective-permute-start.10 = (bf16[6,128,512]{2,1,0:T(8,128)(2,1)S(1)}, bf16[6,128,512]{2,1,0:T(8,128)(2,1)S(1)}, u32[]{:S(2)}, u32[]{:S(2)}) collective-permute-start(bf16[6,128,512]{2,1,0:T(8,128)(2,1)S(1)} %get-tuple-element.52), channel_id=1, source_target_pairs={{0,128},{1,129},{2,130},{3,131},{4,132},{5,133},{6,134},{7,135},{8... | collective-permute-start | bytes 2359304 | tf_op jit(solution)/shard_map/round2/ppermute | solution.py:27
  63.6 20.1 %collective-permute-start.11 = (bf16[6,128,512]{2,1,0:T(8,128)(2,1)S(1)}, bf16[6,128,512]{2,1,0:T(8,128)(2,1)S(1)}, u32[]{:S(2)}, u32[]{:S(2)}) collective-permute-start(bf16[6,128,512]{2,1,0:T(8,128)(2,1)S(1)} %get-tuple-element.51), channel_id=1, source_target_pairs={{0,384},{1,385},{2,386},{3,387},{4,388},{5,389},{6,390},{7,391},{8... | collective-permute-start | bytes 2359304 | tf_op jit(solution)/shard_map/round2/ppermute | solution.py:27
  86.3 24.4 %copy-start.21 = (s32[1,32]{1,0:T(1,128)S(1)}, s32[1,32]{1,0:T(1,128)}, u32[]{:S(2)}) copy-start(s32[1,32]{1,0:T(1,128)} %param.8) | copy-start | bytes 388
  86.3 24.4 %collective-permute-start.15 = (bf16[12,128,512]{2,1,0:T(8,128)(2,1)}, bf16[12,128,512]{2,1,0:T(8,128)(2,1)}, u32[]{:S(2)}, u32[]{:S(2)}) collective-permute-start(bf16[12,128,512]{2,1,0:T(8,128)(2,1)} %pad_maximum_fusion.1), channel_id=1, source_target_pairs={{0,64},{1,65},{2,66},{3,67},{4,68},{5,69},{6,70},{7,71},{8,72},{9,... | collective-permute-start | bytes 4718600 | tf_op jit(solution)/shard_map/round3/ppermute | solution.py:27
  91.6 10.2 %collective-permute-start.13 = (bf16[2,512,256]{2,1,0:T(8,128)(2,1)S(1)}, bf16[2,512,256]{2,1,0:T(8,128)(2,1)S(1)}, u32[]{:S(2)}, u32[]{:S(2)}) collective-permute-start(bf16[2,512,256]{2,1,0:T(8,128)(2,1)S(1)} %slice_select_fusion.1), channel_id=1, source_target_pairs={{0,4},{1,5},{2,6},{3,7},{4,8},{5,9},{6,10},{7,11},{8,12},{9,13},{1... | collective-permute-start | bytes 1572872 | tf_op jit(solution)/shard_map/round3/ppermute | solution.py:27
  93.6 10.6 %collective-permute-start.14 = (bf16[4,128,512]{2,1,0:T(8,128)(2,1)S(1)}, bf16[4,128,512]{2,1,0:T(8,128)(2,1)S(1)}, u32[]{:S(2)}, u32[]{:S(2)}) collective-permute-start(bf16[4,128,512]{2,1,0:T(8,128)(2,1)S(1)} %slice_select_fusion), channel_id=1, source_target_pairs={{0,128},{1,129},{2,130},{3,131},{4,132},{5,133},{6,134},{7,135},{8... | collective-permute-start | bytes 1572872 | tf_op jit(solution)/shard_map/round3/ppermute | solution.py:27
  98.1 12.7 %collective-permute-start.16 = (bf16[4,128,512]{2,1,0:T(8,128)(2,1)S(1)}, bf16[4,128,512]{2,1,0:T(8,128)(2,1)S(1)}, u32[]{:S(2)}, u32[]{:S(2)}) collective-permute-start(bf16[4,128,512]{2,1,0:T(8,128)(2,1)S(1)} %slice_select_fusion), channel_id=1, source_target_pairs={{0,192},{1,193},{2,194},{3,195},{4,196},{5,197},{6,198},{7,199},{8... | collective-permute-start | bytes 1572872 | tf_op jit(solution)/shard_map/round3/ppermute | solution.py:27
  121.6 16.9 %collective-permute-start.17 = (s16[1040,128]{1,0:T(8,128)(2,1)S(1)}, s16[1040,128]{1,0:T(8,128)(2,1)S(1)}, u32[]{:S(2)}, u32[]{:S(2)}) collective-permute-start(s16[1040,128]{1,0:T(8,128)(2,1)S(1)} %matmul_far.1), channel_id=1, source_target_pairs={{0,1},{1,2},{2,3},{3,0},{4,5},{5,6},{6,7},{7,4},{8,9},{9,10},{10,1... | collective-permute-start | bytes 798728 | tf_op jit(solution)/shard_map/layer_far/ppermute | solution.py:27
  138.5 51.2 %copy-start.23 = (s32[2,4]{1,0:T(2,128)S(1)}, s32[2,4]{1,0:T(2,128)}, u32[]{:S(2)}) copy-start(s32[2,4]{1,0:T(2,128)} %pat_ref.1) | copy-start | bytes 100
  139.4 25.1 %collective-permute-start.18 = (s16[1040,128]{1,0:T(8,128)(2,1)S(1)}, s16[1040,128]{1,0:T(8,128)(2,1)S(1)}, u32[]{:S(2)}, u32[]{:S(2)}) collective-permute-start(s16[1040,128]{1,0:T(8,128)(2,1)S(1)} %get-tuple-element.47), channel_id=1, source_target_pairs={{0,1},{1,2},{2,3},{3,0},{4,5},{5,6},{6,7},{7,4},{8,9},{9,10},{10,1... | collective-permute-start | bytes 798728 | tf_op jit(solution)/shard_map/layer_sums/ppermute | solution.py:27
  147.1 17.4 %collective-permute-start.19 = (s16[1040,128]{1,0:T(8,128)(2,1)S(1)}, s16[1040,128]{1,0:T(8,128)(2,1)S(1)}, u32[]{:S(2)}, u32[]{:S(2)}) collective-permute-start(s16[1040,128]{1,0:T(8,128)(2,1)S(1)} %get-tuple-element.48), channel_id=1, source_target_pairs={{0,3},{1,0},{2,1},{3,2},{4,7},{5,4},{6,5},{7,6},{8,11},{9,8},{10,9... | collective-permute-start | bytes 798728 | tf_op jit(solution)/shard_map/layer_sums/ppermute | solution.py:27
  165.2 21.4 %collective-permute-start.20 = (bf16[128,512]{1,0:T(8,128)(2,1)S(1)}, bf16[128,512]{1,0:T(8,128)(2,1)S(1)}, u32[]{:S(2)}, u32[]{:S(2)}) collective-permute-start(bf16[128,512]{1,0:T(8,128)(2,1)S(1)} %get-tuple-element.49), channel_id=1, source_target_pairs={{0,0},{1,1},{2,2},{3,3},{4,4},{5,5},{6,6},{7,7},{8,8},{9,9},{10,10... | collective-permute-start | bytes 393224 | tf_op jit(solution)/shard_map/product_pair/ppermute | solution.py:27
  184.0 5.7 %collective-permute-start.21 = (bf16[128,512]{1,0:T(8,128)(2,1)S(1)}, bf16[128,512]{1,0:T(8,128)(2,1)S(1)}, u32[]{:S(2)}, u32[]{:S(2)}) collective-permute-start(bf16[128,512]{1,0:T(8,128)(2,1)S(1)} %get-tuple-element.50), channel_id=1, source_target_pairs={{0,16},{1,17},{2,18},{3,19},{4,20},{5,21},{6,22},{7,23},{8,24},{9,... | collective-permute-start | bytes 393224 | tf_op jit(solution)/shard_map/product_pair/ppermute | solution.py:27
  (24 other events, 162.5 us)

commit v9 on v4

--- a/solution.py
+++ b/solution.py
@@ -61,6 +61,7 @@
         out_shape=[jax.ShapeDtypeStruct((rows // 2, width), panel.dtype)] * 2,
         in_specs=[pl.BlockSpec(memory_space=pltpu.SMEM)] * 2 + [pl.BlockSpec(memory_space=pltpu.VMEM)],
         out_specs=[pl.BlockSpec(memory_space=pltpu.VMEM)] * 2,
+        compiler_params=pltpu.CompilerParams(vmem_limit_bytes=4 << 20),
         name="mask",
     )(pos, pattern, panel)
 
@@ -147,9 +148,11 @@
 
 
 def far_kernel(pos_ref, owner_ref, *refs):
-    a_refs, b_refs, (o0_ref, o1_ref, a_s) = refs[:NA], refs[NA:NA + NB], refs[NA + NB:]
+    a_refs, b_refs, (o_ref, a_s) = refs[:NA], refs[NA:NA + NB], refs[NA + NB:]
+    tiles = []
     for g, total in product((2,), pos_ref, owner_ref, a_refs, b_refs, a_s):
-        quantize([total[:, n * BS:(n + 1) * BS] for n in range(4)], (o0_ref, o1_ref)[g])
+        tiles += [total[:, n * BS:(n + 1) * BS] for n in range(4)]
+    quantize(tiles, o_ref)
 
 
 def rest_kernel(pos_ref, owner_ref, *refs):
@@ -167,33 +170,32 @@
         in_specs=[pl.BlockSpec(memory_space=pltpu.SMEM)] * 2 + [pl.BlockSpec(memory_space=pltpu.VMEM)] * (NA + NB),
         out_specs=[pl.BlockSpec(memory_space=pltpu.VMEM)] * len(out_shape),
         scratch_shapes=[pltpu.VMEM((chunks * BS, depth), jnp.bfloat16)],
-        compiler_params=pltpu.CompilerParams(vmem_limit_bytes=32 << 20),
+        compiler_params=pltpu.CompilerParams(vmem_limit_bytes=24 << 20),
         cost_estimate=pl.CostEstimate(flops=2 * chunks * BS * 8 * BS * depth, bytes_accessed=1 << 20, transcendentals=0),
         name=name,
     )(pos, owner, *a, *b)
 
 
-def add_kernel(own1_ref, own3_ref, got1_ref, got3_ref, o1_ref, o3_ref):
-    for half, own_ref, got_ref, o_ref in ((0, own1_ref, got1_ref, o1_ref), (1, own3_ref, got3_ref, o3_ref)):
-        scale = scales(got_ref, 4)
+def add_kernel(pos_ref, own1_ref, own3_ref, got_ref, o1_ref, o3_ref):
+    scale = scales(got_ref, 8)
+    for core, own_ref, o_ref in ((0, own1_ref, o1_ref), (1, own3_ref, o3_ref)):
+        mine = pos_ref[1] == core
         tiles = []
         for t in range(8):
-            v = own_ref[t // 4, :, pl.ds((t % 4) * BS, BS)]
-            if t // 4 == half:
-                n = t % 4
-                v = v + values(got_ref, pl.ds(n * BS, BS)) * scale[n:n + 1, :]
-            tiles.append(v)
+            got = values(got_ref, pl.ds(t * BS, BS)) * scale[t:t + 1, :]
+            tiles.append(own_ref[t // 4, :, pl.ds((t % 4) * BS, BS)] + jnp.where(mine, got, 0.0))
         quantize(tiles, o_ref)
 
 
-def add(own1, own3, got1, got3):
+def add(pos, own1, own3, got):
     return pl.pallas_call(
         add_kernel,
         out_shape=[jax.ShapeDtypeStruct((8 * BS + PAD, BS), jnp.int16)] * 2,
-        in_specs=[pl.BlockSpec(memory_space=pltpu.VMEM)] * 4,
+        in_specs=[pl.BlockSpec(memory_space=pltpu.SMEM)] + [pl.BlockSpec(memory_space=pltpu.VMEM)] * 3,
         out_specs=[pl.BlockSpec(memory_space=pltpu.VMEM)] * 2,
+        compiler_params=pltpu.CompilerParams(vmem_limit_bytes=8 << 20),
         name="add",
-    )(own1, own3, got1, got3)
+    )(pos, own1, own3, got)
 
 
 def total_kernel(pos_ref, own_ref, *refs):
@@ -215,6 +217,7 @@
         out_shape=[jax.ShapeDtypeStruct((BS, 4 * BS), jnp.bfloat16)] * 2,
         in_specs=[pl.BlockSpec(memory_space=pltpu.SMEM)] + [pl.BlockSpec(memory_space=pltpu.VMEM)] * 3,
         out_specs=[pl.BlockSpec(memory_space=pltpu.VMEM)] * 2,
+        compiler_params=pltpu.CompilerParams(vmem_limit_bytes=4 << 20),
         name="total",
     )(pos, own, *v)
 
@@ -234,6 +237,7 @@
         out_shape=jax.ShapeDtypeStruct((2 * BS, 4 * BS), jnp.bfloat16),
         in_specs=[pl.BlockSpec(memory_space=pltpu.SMEM)] * 2 + [pl.BlockSpec(memory_space=pltpu.VMEM)] * 2,
         out_specs=pl.BlockSpec(memory_space=pltpu.VMEM),
+        compiler_params=pltpu.CompilerParams(vmem_limit_bytes=4 << 20),
         name="place",
     )(pos, pattern, first, second)
 
@@ -267,13 +271,13 @@
         c3, c0 = to_core(cat(b3p, b3m)), to_core(cat(own, late))
     a = (near, a1p, a1m, far, a2p, a2m, a3p, a3m)
     b = (own, pair, b1p, b1m, b2p, b2m, b3p, b3m, c0, c12, c3)
-    half_shape = [jax.ShapeDtypeStruct((4 * BS + PAD, BS), jnp.int16)] * 2
-    whole_shape = [jax.ShapeDtypeStruct((2, BS, 4 * BS), jnp.float32)] * 3
-    far1, far3 = matmul(far_kernel, "matmul_far", 1, half_shape, pos, owner[0], a, b)
-    with jax.named_scope("layer_halves"):
-        got1, got3 = to_layer(far1, 1), to_layer(far3, -1)
-    own_part, part1, part3 = matmul(rest_kernel, "matmul_rest", 3, whole_shape, pos, owner[0], a, b)
-    part1, part3 = add(part1, part3, got1, got3)
+    far_shape = [jax.ShapeDtypeStruct((8 * BS + PAD, BS), jnp.int16)]
+    rest_shape = [jax.ShapeDtypeStruct((2, BS, 4 * BS), jnp.float32)] * 3
+    got, = matmul(far_kernel, "matmul_far", 1, far_shape, pos, owner[0], a, b)
+    with jax.named_scope("layer_far"):
+        got = send(got, lambda y, c, zl, x, zh: (y, c, zl, x, (zh + 1 - 2 * c) % 4))
+    own_part, part1, part3 = matmul(rest_kernel, "matmul_rest", 3, rest_shape, pos, owner[0], a, b)
+    part1, part3 = add(pos, part1, part3, got)
     with jax.named_scope("layer_sums"):
         got1, got3 = to_layer(part1, 1), to_layer(part3, -1)
     first, second = total(pos, own_part, (got1, got3))

time: 181 us -> 171 us (0.945)
  the two profiles are of different devices: /device:TPU:71 before, /device:TPU:81 now
where the time goes in v9:
time: 171 us; the launch traced here: 170 us
  starting transfers between devices  97.9 us (57%)
  waiting for transfers between devices  57.9 us (34%)
  Pallas kernels  11.1 us (6%)
  local copies, waits for them, and re-layouts  1.98 us (1%)
    ppermute x24, starting transfers between devices, send(): return lax.ppermute(v, AXES, moves(f))  97.9 us
    ppermute x24, waiting for transfers between devices, send(): return lax.ppermute(v, AXES, moves(f))  57.9 us
    pallas_call x2, Pallas kernels, matmul(): pl.pallas_call(kernel, out_shape=out_shape, in_specs=[pl.BlockSpec(memory...  7.47 us
  transfers between devices with their start and end apart: 24, of which 14 were waited for; matrix products, arithmetic and copies ran while one was open for 0% of the time, Pallas kernels for 3%

profile of v9, /device:TPU:81, one launch (start us, length us, event | category | flops | bytes accessed | tf_op | source)
XLA Modules:
  0.0 170.1 jit_solution(5209918446177458943)
XLA Ops:
  0.0 3.5 %collective-permute-start.2 = (bf16[4,128,512]{2,1,0:T(8,128)(2,1)}, bf16[4,128,512]{2,1,0:T(8,128)(2,1)S(1)}, u32[]{:S(2)}, u32[]{:S(2)}) collective-permute-start(bf16[4,128,512]{2,1,0:T(8,128)(2,1)} %bitcast.14), channel_id=1, source_target_pairs={{0,16},{1,17},{2,18},{3,19},{4,20},{5,21},{6,22},{7,23},{8,24},{9,... | collective-permute-start | bytes 1572872 | tf_op jit(solution)/shard_map/round0/ppermute | solution.py:27
  3.5 2.9 %collective-permute-start.3 = (bf16[4,128,512]{2,1,0:T(8,128)(2,1)}, bf16[4,128,512]{2,1,0:T(8,128)(2,1)S(1)}, u32[]{:S(2)}, u32[]{:S(2)}) collective-permute-start(bf16[4,128,512]{2,1,0:T(8,128)(2,1)} %bitcast.15), channel_id=1, source_target_pairs={{0,128},{1,129},{2,130},{3,131},{4,132},{5,133},{6,134},{7,135},{8... | collective-permute-start | bytes 1572872 | tf_op jit(solution)/shard_map/round0/ppermute | solution.py:27
  11.4 3.1 %collective-permute-start = (bf16[512,256]{1,0:T(8,128)(2,1)S(1)}, bf16[512,256]{1,0:T(8,128)(2,1)S(1)}, u32[]{:S(2)}, u32[]{:S(2)}) collective-permute-start(bf16[512,256]{1,0:T(8,128)(2,1)S(1)} %get-tuple-element.30), channel_id=1, source_target_pairs={{0,0},{1,1},{2,2},{3,3},{4,4},{5,5},{6,6},{7,7},{8,8},{9,9},{10,10... | collective-permute-start | bytes 786440 | tf_op jit(solution)/shard_map/round0/ppermute | solution.py:27
  16.5 2.9 %collective-permute-done = bf16[512,256]{1,0:T(8,128)(2,1)S(1)} collective-permute-done((bf16[512,256]{1,0:T(8,128)(2,1)S(1)}, bf16[512,256]{1,0:T(8,128)(2,1)S(1)}, u32[]{:S(2)}, u32[]{:S(2)}) %collective-permute-start) | collective-permute-done | bytes 262176 | tf_op jit(solution)/shard_map/round0/ppermute | solution.py:27
  21.3 2.9 %collective-permute-start.8 = (bf16[6,128,512]{2,1,0:T(8,128)(2,1)S(1)}, bf16[6,128,512]{2,1,0:T(8,128)(2,1)S(1)}, u32[]{:S(2)}, u32[]{:S(2)}) collective-permute-start(bf16[6,128,512]{2,1,0:T(8,128)(2,1)S(1)} %get-tuple-element.58), channel_id=1, source_target_pairs={{0,128},{1,129},{2,130},{3,131},{4,132},{5,133},{6,134},{7,135},{8... | collective-permute-start | bytes 2359304 | tf_op jit(solution)/shard_map/round1/ppermute | solution.py:27
  26.6 4.0 %collective-permute-start.5 = (bf16[2,512,256]{2,1,0:T(8,128)(2,1)S(1)}, bf16[2,512,256]{2,1,0:T(8,128)(2,1)S(1)}, u32[]{:S(2)}, u32[]{:S(2)}) collective-permute-start(bf16[2,512,256]{2,1,0:T(8,128)(2,1)S(1)} %pad_maximum_fusion.6.refs_0_), channel_id=1, source_target_pairs={{0,32},{1,33},{2,34},{3,35},{4,36},{5,37},{6,38},{7,39},{8,40},{9,... | collective-permute-start | bytes 1572872 | tf_op jit(solution)/shard_map/round1/ppermute | solution.py:27
  32.5 4.6 %collective-permute-start.7 = (bf16[2,512,256]{2,1,0:T(8,128)(2,1)S(1)}, bf16[2,512,256]{2,1,0:T(8,128)(2,1)S(1)}, u32[]{:S(2)}, u32[]{:S(2)}) collective-permute-start(bf16[2,512,256]{2,1,0:T(8,128)(2,1)S(1)} %pad_maximum_fusion.6.refs_0_), channel_id=1, source_target_pairs={{0,12},{1,13},{2,14},{3,15},{4,0},{5,1},{6,2},{7,3},{8,4},{9,5},{1... | collective-permute-start | bytes 1572872 | tf_op jit(solution)/shard_map/round1/ppermute | solution.py:27
  37.1 15.1 %collective-permute-done.5.refs_3_ = bf16[2,512,256]{2,1,0:T(8,128)(2,1)S(1)} collective-permute-done((bf16[2,512,256]{2,1,0:T(8,128)(2,1)S(1)}, bf16[2,512,256]{2,1,0:T(8,128)(2,1)S(1)}, u32[]{:S(2)}, u32[]{:S(2)}) %collective-permute-start.5) | collective-permute-done | bytes 524320 | tf_op jit(solution)/shard_map/round1/ppermute | solution.py:27
  52.6 3.8 %collective-permute-start.14 = (bf16[20,128,512]{2,1,0:T(8,128)(2,1)S(1)}, bf16[20,128,512]{2,1,0:T(8,128)(2,1)S(1)}, u32[]{:S(2)}, u32[]{:S(2)}) collective-permute-start(bf16[20,128,512]{2,1,0:T(8,128)(2,1)S(1)} %pad_maximum_fusion), channel_id=1, source_target_pairs={{0,64},{1,65},{2,66},{3,67},{4,68},{5,69},{6,70},{7,71},{8,72},{9,... | collective-permute-start | bytes 7864328 | tf_op jit(solution)/shard_map/round2/ppermute | solution.py:27
  58.5 4.6 %collective-permute-start.11 = (bf16[3,512,256]{2,1,0:T(8,128)(2,1)S(1)}, bf16[3,512,256]{2,1,0:T(8,128)(2,1)S(1)}, u32[]{:S(2)}, u32[]{:S(2)}) collective-permute-start(bf16[3,512,256]{2,1,0:T(8,128)(2,1)S(1)} %get-tuple-element.55), channel_id=1, source_target_pairs={{0,12},{1,13},{2,14},{3,15},{4,0},{5,1},{6,2},{7,3},{8,4},{9,5},{1... | collective-permute-start | bytes 2359304 | tf_op jit(solution)/shard_map/round2/ppermute | solution.py:27
  63.2 4.9 %collective-permute-start.12 = (bf16[2,128,512]{2,1,0:T(8,128)(2,1)S(1)}, bf16[2,128,512]{2,1,0:T(8,128)(2,1)S(1)}, u32[]{:S(2)}, u32[]{:S(2)}) collective-permute-start(bf16[2,128,512]{2,1,0:T(8,128)(2,1)S(1)} %slice.28), channel_id=1, source_target_pairs={{0,128},{1,129},{2,130},{3,131},{4,132},{5,133},{6,134},{7,135},{8... | collective-permute-start | bytes 786440 | tf_op jit(solution)/shard_map/round2/ppermute | solution.py:27
  69.9 3.6 %collective-permute-done.12.refs_14_ = bf16[2,128,512]{2,1,0:T(8,128)(2,1)S(1)} collective-permute-done((bf16[2,128,512]{2,1,0:T(8,128)(2,1)S(1)}, bf16[2,128,512]{2,1,0:T(8,128)(2,1)S(1)}, u32[]{:S(2)}, u32[]{:S(2)}) %collective-permute-start.12) | collective-permute-done | bytes 262176 | tf_op jit(solution)/shard_map/round2/ppermute | solution.py:27
  73.5 4.9 %collective-permute-done.13.refs_15_ = bf16[2,128,512]{2,1,0:T(8,128)(2,1)S(1)} collective-permute-done((bf16[2,128,512]{2,1,0:T(8,128)(2,1)S(1)}, bf16[2,128,512]{2,1,0:T(8,128)(2,1)S(1)}, u32[]{:S(2)}, u32[]{:S(2)}) %collective-permute-start.13) | collective-permute-done | bytes 262176 | tf_op jit(solution)/shard_map/round2/ppermute | solution.py:27
  79.8 3.0 %collective-permute-start.17 = (bf16[8,128,512]{2,1,0:T(8,128)(2,1)S(1)}, bf16[8,128,512]{2,1,0:T(8,128)(2,1)S(1)}, u32[]{:S(2)}, u32[]{:S(2)}) collective-permute-start(bf16[8,128,512]{2,1,0:T(8,128)(2,1)S(1)} %pad_maximum_fusion.1), channel_id=1, source_target_pairs={{0,64},{1,65},{2,66},{3,67},{4,68},{5,69},{6,70},{7,71},{8,72},{9,... | collective-permute-start | bytes 3145736 | tf_op jit(solution)/shard_map/round3/ppermute | solution.py:27
  86.8 5.3 %collective-permute-start.16 = (bf16[1,512,256]{2,1,0:T(8,128)(2,1)S(1)}, bf16[1,512,256]{2,1,0:T(8,128)(2,1)S(1)}, u32[]{:S(2)}, u32[]{:S(2)}) collective-permute-start(bf16[1,512,256]{2,1,0:T(8,128)(2,1)S(1)} %slice.31), channel_id=1, source_target_pairs={{0,12},{1,13},{2,14},{3,15},{4,0},{5,1},{6,2},{7,3},{8,4},{9,5},{1... | collective-permute-start | bytes 786440 | tf_op jit(solution)/shard_map/round3/ppermute | solution.py:27
  92.2 4.3 %collective-permute-done.15.refs_6_ = bf16[1,512,256]{2,1,0:T(8,128)(2,1)S(1)} collective-permute-done((bf16[1,512,256]{2,1,0:T(8,128)(2,1)S(1)}, bf16[1,512,256]{2,1,0:T(8,128)(2,1)S(1)}, u32[]{:S(2)}, u32[]{:S(2)}) %collective-permute-start.15) | collective-permute-done | bytes 262176 | tf_op jit(solution)/shard_map/round3/ppermute | solution.py:27
  97.3 2.5 %matmul_far.1 = s16[1040,128]{1,0:T(8,128)(2,1)S(1)} custom-call(s32[6]{0:T(128)S(1)} %stack.36.pos_ref, s32[32]{0:T(128)S(1)} %bitcast.21, bf16[2,512,256]{2,1,0:T(8,128)(2,1)S(1)} %pad_maximum_fusion.6.refs_0_, bf16[2,512,256]{2,1,0:T(8,128)(2,1)S(1)} %collective-permute-done.6.refs_1_, bf16[2,512,256]{2,1,0:T(8,128)(2,1)S(1)} %collective-permute-done.7.refs_2_, ...), custom_call_target="tpu_custom_call" | custom-call | flops 1073741824 | bytes 1048576 | tf_op jit(solution)/shard_map/matmul_far/pallas_call | solution.py:167
  99.8 9.7 %collective-permute-start.19 = (s16[1040,128]{1,0:T(8,128)(2,1)S(1)}, s16[1040,128]{1,0:T(8,128)(2,1)S(1)}, u32[]{:S(2)}, u32[]{:S(2)}) collective-permute-start(s16[1040,128]{1,0:T(8,128)(2,1)S(1)} %matmul_far.1), channel_id=1, source_target_pairs={{0,1},{1,2},{2,3},{3,0},{4,5},{5,6},{6,7},{7,4},{8,9},{9,10},{10,1... | collective-permute-start | bytes 798728 | tf_op jit(solution)/shard_map/layer_far/ppermute | solution.py:27
  109.5 5.0 %matmul_rest.1 = (f32[2,128,512]{2,1,0:T(8,128)S(1)}, f32[2,128,512]{2,1,0:T(8,128)S(1)}, f32[2,128,512]{2,1,0:T(8,128)S(1)}) custom-call(s32[6]{0:T(128)S(1)} %stack.36.pos_ref, s32[32]{0:T(128)S(1)} %bitcast.22, bf16[2,512,256]{2,1,0:T(8,128)(2,1)S(1)} %pad_maximum_fusion.6.refs_0_, bf16[2,512,256]{2,1,0:T(8,128)(2,1)S(1)} %collective-permute-done.6.refs_1_, ...), custom_call_target="tpu_custom_call" | custom-call | flops 3221225472 | bytes 1048576 | tf_op jit(solution)/shard_map/matmul_rest/pallas_call | solution.py:167
  114.6 6.8 %collective-permute-done.19.got_ref = s16[1040,128]{1,0:T(8,128)(2,1)S(1)} collective-permute-done((s16[1040,128]{1,0:T(8,128)(2,1)S(1)}, s16[1040,128]{1,0:T(8,128)(2,1)S(1)}, u32[]{:S(2)}, u32[]{:S(2)}) %collective-permute-start.19) | collective-permute-done | bytes 266272 | tf_op jit(solution)/shard_map/layer_far/ppermute | solution.py:27
  124.2 7.8 %collective-permute-start.21 = (s16[1040,128]{1,0:T(8,128)(2,1)S(1)}, s16[1040,128]{1,0:T(8,128)(2,1)S(1)}, u32[]{:S(2)}, u32[]{:S(2)}) collective-permute-start(s16[1040,128]{1,0:T(8,128)(2,1)S(1)} %get-tuple-element.52), channel_id=1, source_target_pairs={{0,3},{1,0},{2,1},{3,2},{4,7},{5,4},{6,5},{7,6},{8,11},{9,8},{10,9... | collective-permute-start | bytes 798728 | tf_op jit(solution)/shard_map/layer_sums/ppermute | solution.py:27
  132.0 10.6 %collective-permute-done.20.refs_0_ = s16[1040,128]{1,0:T(8,128)(2,1)S(1)} collective-permute-done((s16[1040,128]{1,0:T(8,128)(2,1)S(1)}, s16[1040,128]{1,0:T(8,128)(2,1)S(1)}, u32[]{:S(2)}, u32[]{:S(2)}) %collective-permute-start.20) | collective-permute-done | bytes 266272 | tf_op jit(solution)/shard_map/layer_sums/ppermute | solution.py:27
  145.4 17.7 %collective-permute-start.22 = (bf16[128,512]{1,0:T(8,128)(2,1)S(1)}, bf16[128,512]{1,0:T(8,128)(2,1)S(1)}, u32[]{:S(2)}, u32[]{:S(2)}) collective-permute-start(bf16[128,512]{1,0:T(8,128)(2,1)S(1)} %get-tuple-element.53), channel_id=1, source_target_pairs={{0,0},{1,1},{2,2},{3,3},{4,4},{5,5},{6,6},{7,7},{8,8},{9,9},{10,10... | collective-permute-start | bytes 393224 | tf_op jit(solution)/shard_map/product_pair/ppermute | solution.py:27
  165.7 3.1 %collective-permute-done.23.second_ref = bf16[128,512]{1,0:T(8,128)(2,1)S(1)} collective-permute-done((bf16[128,512]{1,0:T(8,128)(2,1)S(1)}, bf16[128,512]{1,0:T(8,128)(2,1)S(1)}, u32[]{:S(2)}, u32[]{:S(2)}) %collective-permute-start.23) | collective-permute-done | bytes 131104 | tf_op jit(solution)/shard_map/product_pair/ppermute | solution.py:27
  (55 shorter events, 33.1 us)
Async XLA Ops:
  0.0 21.1 %collective-permute-start.2 = (bf16[4,128,512]{2,1,0:T(8,128)(2,1)}, bf16[4,128,512]{2,1,0:T(8,128)(2,1)S(1)}, u32[]{:S(2)}, u32[]{:S(2)}) collective-permute-start(bf16[4,128,512]{2,1,0:T(8,128)(2,1)} %bitcast.14), channel_id=1, source_target_pairs={{0,16},{1,17},{2,18},{3,19},{4,20},{5,21},{6,22},{7,23},{8,24},{9,... | collective-permute-start | bytes 1572872 | tf_op jit(solution)/shard_map/round0/ppermute | solution.py:27
  3.5 17.6 %collective-permute-start.3 = (bf16[4,128,512]{2,1,0:T(8,128)(2,1)}, bf16[4,128,512]{2,1,0:T(8,128)(2,1)S(1)}, u32[]{:S(2)}, u32[]{:S(2)}) collective-permute-start(bf16[4,128,512]{2,1,0:T(8,128)(2,1)} %bitcast.15), channel_id=1, source_target_pairs={{0,128},{1,129},{2,130},{3,131},{4,132},{5,133},{6,134},{7,135},{8... | collective-permute-start | bytes 1572872 | tf_op jit(solution)/shard_map/round0/ppermute | solution.py:27
  6.5 14.6 %collective-permute-start.4 = (bf16[4,128,512]{2,1,0:T(8,128)(2,1)}, bf16[4,128,512]{2,1,0:T(8,128)(2,1)S(1)}, u32[]{:S(2)}, u32[]{:S(2)}) collective-permute-start(bf16[4,128,512]{2,1,0:T(8,128)(2,1)} %bitcast.16), channel_id=1, source_target_pairs={{0,384},{1,385},{2,386},{3,387},{4,388},{5,389},{6,390},{7,391},{8... | collective-permute-start | bytes 1572872 | tf_op jit(solution)/shard_map/round0/ppermute | solution.py:27
  11.4 8.0 %collective-permute-start = (bf16[512,256]{1,0:T(8,128)(2,1)S(1)}, bf16[512,256]{1,0:T(8,128)(2,1)S(1)}, u32[]{:S(2)}, u32[]{:S(2)}) collective-permute-start(bf16[512,256]{1,0:T(8,128)(2,1)S(1)} %get-tuple-element.30), channel_id=1, source_target_pairs={{0,0},{1,1},{2,2},{3,3},{4,4},{5,5},{6,6},{7,7},{8,8},{9,9},{10,10... | collective-permute-start | bytes 786440 | tf_op jit(solution)/shard_map/round0/ppermute | solution.py:27
  14.5 6.6 %collective-permute-start.1 = (bf16[512,256]{1,0:T(8,128)(2,1)S(1)}, bf16[512,256]{1,0:T(8,128)(2,1)S(1)}, u32[]{:S(2)}, u32[]{:S(2)}) collective-permute-start(bf16[512,256]{1,0:T(8,128)(2,1)S(1)} %get-tuple-element.31), channel_id=1, source_target_pairs={{0,64},{1,65},{2,66},{3,67},{4,68},{5,69},{6,70},{7,71},{8,72},{9,... | collective-permute-start | bytes 786440 | tf_op jit(solution)/shard_map/round0/ppermute | solution.py:27
  21.3 31.0 %collective-permute-start.8 = (bf16[6,128,512]{2,1,0:T(8,128)(2,1)S(1)}, bf16[6,128,512]{2,1,0:T(8,128)(2,1)S(1)}, u32[]{:S(2)}, u32[]{:S(2)}) collective-permute-start(bf16[6,128,512]{2,1,0:T(8,128)(2,1)S(1)} %get-tuple-element.58), channel_id=1, source_target_pairs={{0,128},{1,129},{2,130},{3,131},{4,132},{5,133},{6,134},{7,135},{8... | collective-permute-start | bytes 2359304 | tf_op jit(solution)/shard_map/round1/ppermute | solution.py:27
  24.2 28.1 %collective-permute-start.9 = (bf16[6,128,512]{2,1,0:T(8,128)(2,1)S(1)}, bf16[6,128,512]{2,1,0:T(8,128)(2,1)S(1)}, u32[]{:S(2)}, u32[]{:S(2)}) collective-permute-start(bf16[6,128,512]{2,1,0:T(8,128)(2,1)S(1)} %get-tuple-element.57), channel_id=1, source_target_pairs={{0,384},{1,385},{2,386},{3,387},{4,388},{5,389},{6,390},{7,391},{8... | collective-permute-start | bytes 2359304 | tf_op jit(solution)/shard_map/round1/ppermute | solution.py:27
  26.6 25.6 %collective-permute-start.5 = (bf16[2,512,256]{2,1,0:T(8,128)(2,1)S(1)}, bf16[2,512,256]{2,1,0:T(8,128)(2,1)S(1)}, u32[]{:S(2)}, u32[]{:S(2)}) collective-permute-start(bf16[2,512,256]{2,1,0:T(8,128)(2,1)S(1)} %pad_maximum_fusion.6.refs_0_), channel_id=1, source_target_pairs={{0,32},{1,33},{2,34},{3,35},{4,36},{5,37},{6,38},{7,39},{8,40},{9,... | collective-permute-start | bytes 1572872 | tf_op jit(solution)/shard_map/round1/ppermute | solution.py:27
  30.6 21.6 %collective-permute-start.6 = (bf16[2,512,256]{2,1,0:T(8,128)(2,1)S(1)}, bf16[2,512,256]{2,1,0:T(8,128)(2,1)S(1)}, u32[]{:S(2)}, u32[]{:S(2)}) collective-permute-start(bf16[2,512,256]{2,1,0:T(8,128)(2,1)S(1)} %pad_maximum_fusion.6.refs_0_), channel_id=1, source_target_pairs={{0,4},{1,5},{2,6},{3,7},{4,8},{5,9},{6,10},{7,11},{8,12},{9,13},{1... | collective-permute-start | bytes 1572872 | tf_op jit(solution)/shard_map/round1/ppermute | solution.py:27
  32.5 19.7 %collective-permute-start.7 = (bf16[2,512,256]{2,1,0:T(8,128)(2,1)S(1)}, bf16[2,512,256]{2,1,0:T(8,128)(2,1)S(1)}, u32[]{:S(2)}, u32[]{:S(2)}) collective-permute-start(bf16[2,512,256]{2,1,0:T(8,128)(2,1)S(1)} %pad_maximum_fusion.6.refs_0_), channel_id=1, source_target_pairs={{0,12},{1,13},{2,14},{3,15},{4,0},{5,1},{6,2},{7,3},{8,4},{9,5},{1... | collective-permute-start | bytes 1572872 | tf_op jit(solution)/shard_map/round1/ppermute | solution.py:27
  52.6 27.1 %collective-permute-start.14 = (bf16[20,128,512]{2,1,0:T(8,128)(2,1)S(1)}, bf16[20,128,512]{2,1,0:T(8,128)(2,1)S(1)}, u32[]{:S(2)}, u32[]{:S(2)}) collective-permute-start(bf16[20,128,512]{2,1,0:T(8,128)(2,1)S(1)} %pad_maximum_fusion), channel_id=1, source_target_pairs={{0,64},{1,65},{2,66},{3,67},{4,68},{5,69},{6,70},{7,71},{8,72},{9,... | collective-permute-start | bytes 7864328 | tf_op jit(solution)/shard_map/round2/ppermute | solution.py:27
  56.6 22.3 %collective-permute-start.10 = (bf16[3,512,256]{2,1,0:T(8,128)(2,1)S(1)}, bf16[3,512,256]{2,1,0:T(8,128)(2,1)S(1)}, u32[]{:S(2)}, u32[]{:S(2)}) collective-permute-start(bf16[3,512,256]{2,1,0:T(8,128)(2,1)S(1)} %get-tuple-element.56), channel_id=1, source_target_pairs={{0,4},{1,5},{2,6},{3,7},{4,8},{5,9},{6,10},{7,11},{8,12},{9,13},{1... | collective-permute-start | bytes 2359304 | tf_op jit(solution)/shard_map/round2/ppermute | solution.py:27
  58.5 21.2 %collective-permute-start.11 = (bf16[3,512,256]{2,1,0:T(8,128)(2,1)S(1)}, bf16[3,512,256]{2,1,0:T(8,128)(2,1)S(1)}, u32[]{:S(2)}, u32[]{:S(2)}) collective-permute-start(bf16[3,512,256]{2,1,0:T(8,128)(2,1)S(1)} %get-tuple-element.55), channel_id=1, source_target_pairs={{0,12},{1,13},{2,14},{3,15},{4,0},{5,1},{6,2},{7,3},{8,4},{9,5},{1... | collective-permute-start | bytes 2359304 | tf_op jit(solution)/shard_map/round2/ppermute | solution.py:27
  63.2 10.4 %collective-permute-start.12 = (bf16[2,128,512]{2,1,0:T(8,128)(2,1)S(1)}, bf16[2,128,512]{2,1,0:T(8,128)(2,1)S(1)}, u32[]{:S(2)}, u32[]{:S(2)}) collective-permute-start(bf16[2,128,512]{2,1,0:T(8,128)(2,1)S(1)} %slice.28), channel_id=1, source_target_pairs={{0,128},{1,129},{2,130},{3,131},{4,132},{5,133},{6,134},{7,135},{8... | collective-permute-start | bytes 786440 | tf_op jit(solution)/shard_map/round2/ppermute | solution.py:27
  68.0 10.4 %collective-permute-start.13 = (bf16[2,128,512]{2,1,0:T(8,128)(2,1)S(1)}, bf16[2,128,512]{2,1,0:T(8,128)(2,1)S(1)}, u32[]{:S(2)}, u32[]{:S(2)}) collective-permute-start(bf16[2,128,512]{2,1,0:T(8,128)(2,1)S(1)} %slice.29), channel_id=1, source_target_pairs={{0,384},{1,385},{2,386},{3,387},{4,388},{5,389},{6,390},{7,391},{8... | collective-permute-start | bytes 786440 | tf_op jit(solution)/shard_map/round2/ppermute | solution.py:27
  79.8 17.5 %collective-permute-start.17 = (bf16[8,128,512]{2,1,0:T(8,128)(2,1)S(1)}, bf16[8,128,512]{2,1,0:T(8,128)(2,1)S(1)}, u32[]{:S(2)}, u32[]{:S(2)}) collective-permute-start(bf16[8,128,512]{2,1,0:T(8,128)(2,1)S(1)} %pad_maximum_fusion.1), channel_id=1, source_target_pairs={{0,64},{1,65},{2,66},{3,67},{4,68},{5,69},{6,70},{7,71},{8,72},{9,... | collective-permute-start | bytes 3145736 | tf_op jit(solution)/shard_map/round3/ppermute | solution.py:27
  82.9 14.4 %collective-permute-start.18 = (bf16[4,128,512]{2,1,0:T(8,128)(2,1)S(1)}, bf16[4,128,512]{2,1,0:T(8,128)(2,1)S(1)}, u32[]{:S(2)}, u32[]{:S(2)}) collective-permute-start(bf16[4,128,512]{2,1,0:T(8,128)(2,1)S(1)} %pad_maximum_fusion.7), channel_id=1, source_target_pairs={{0,64},{1,65},{2,66},{3,67},{4,68},{5,69},{6,70},{7,71},{8,72},{9,... | collective-permute-start | bytes 1572872 | tf_op jit(solution)/shard_map/round3/ppermute | solution.py:27
  84.9 11.5 %collective-permute-start.15 = (bf16[1,512,256]{2,1,0:T(8,128)(2,1)S(1)}, bf16[1,512,256]{2,1,0:T(8,128)(2,1)S(1)}, u32[]{:S(2)}, u32[]{:S(2)}) collective-permute-start(bf16[1,512,256]{2,1,0:T(8,128)(2,1)S(1)} %slice.30), channel_id=1, source_target_pairs={{0,4},{1,5},{2,6},{3,7},{4,8},{5,9},{6,10},{7,11},{8,12},{9,13},{1... | collective-permute-start | bytes 786440 | tf_op jit(solution)/shard_map/round3/ppermute | solution.py:27
  86.8 10.5 %collective-permute-start.16 = (bf16[1,512,256]{2,1,0:T(8,128)(2,1)S(1)}, bf16[1,512,256]{2,1,0:T(8,128)(2,1)S(1)}, u32[]{:S(2)}, u32[]{:S(2)}) collective-permute-start(bf16[1,512,256]{2,1,0:T(8,128)(2,1)S(1)} %slice.31), channel_id=1, source_target_pairs={{0,12},{1,13},{2,14},{3,15},{4,0},{5,1},{6,2},{7,3},{8,4},{9,5},{1... | collective-permute-start | bytes 786440 | tf_op jit(solution)/shard_map/round3/ppermute | solution.py:27
  99.8 21.6 %collective-permute-start.19 = (s16[1040,128]{1,0:T(8,128)(2,1)S(1)}, s16[1040,128]{1,0:T(8,128)(2,1)S(1)}, u32[]{:S(2)}, u32[]{:S(2)}) collective-permute-start(s16[1040,128]{1,0:T(8,128)(2,1)S(1)} %matmul_far.1), channel_id=1, source_target_pairs={{0,1},{1,2},{2,3},{3,0},{4,5},{5,6},{6,7},{7,4},{8,9},{9,10},{10,1... | collective-permute-start | bytes 798728 | tf_op jit(solution)/shard_map/layer_far/ppermute | solution.py:27
  122.3 20.4 %collective-permute-start.20 = (s16[1040,128]{1,0:T(8,128)(2,1)S(1)}, s16[1040,128]{1,0:T(8,128)(2,1)S(1)}, u32[]{:S(2)}, u32[]{:S(2)}) collective-permute-start(s16[1040,128]{1,0:T(8,128)(2,1)S(1)} %get-tuple-element.51), channel_id=1, source_target_pairs={{0,1},{1,2},{2,3},{3,0},{4,5},{5,6},{6,7},{7,4},{8,9},{9,10},{10,1... | collective-permute-start | bytes 798728 | tf_op jit(solution)/shard_map/layer_sums/ppermute | solution.py:27
  124.2 20.5 %collective-permute-start.21 = (s16[1040,128]{1,0:T(8,128)(2,1)S(1)}, s16[1040,128]{1,0:T(8,128)(2,1)S(1)}, u32[]{:S(2)}, u32[]{:S(2)}) collective-permute-start(s16[1040,128]{1,0:T(8,128)(2,1)S(1)} %get-tuple-element.52), channel_id=1, source_target_pairs={{0,3},{1,0},{2,1},{3,2},{4,7},{5,4},{6,5},{7,6},{8,11},{9,8},{10,9... | collective-permute-start | bytes 798728 | tf_op jit(solution)/shard_map/layer_sums/ppermute | solution.py:27
  145.4 20.3 %collective-permute-start.22 = (bf16[128,512]{1,0:T(8,128)(2,1)S(1)}, bf16[128,512]{1,0:T(8,128)(2,1)S(1)}, u32[]{:S(2)}, u32[]{:S(2)}) collective-permute-start(bf16[128,512]{1,0:T(8,128)(2,1)S(1)} %get-tuple-element.53), channel_id=1, source_target_pairs={{0,0},{1,1},{2,2},{3,3},{4,4},{5,5},{6,6},{7,7},{8,8},{9,9},{10,10... | collective-permute-start | bytes 393224 | tf_op jit(solution)/shard_map/product_pair/ppermute | solution.py:27
  163.1 5.7 %collective-permute-start.23 = (bf16[128,512]{1,0:T(8,128)(2,1)S(1)}, bf16[128,512]{1,0:T(8,128)(2,1)S(1)}, u32[]{:S(2)}, u32[]{:S(2)}) collective-permute-start(bf16[128,512]{1,0:T(8,128)(2,1)S(1)} %get-tuple-element.54), channel_id=1, source_target_pairs={{0,16},{1,17},{2,18},{3,19},{4,20},{5,21},{6,22},{7,23},{8,24},{9,... | collective-permute-start | bytes 393224 | tf_op jit(solution)/shard_map/product_pair/ppermute | solution.py:27
  (5 other events, 136.6 us)

commit v10 on v9

--- a/solution.py
+++ b/solution.py
@@ -81,24 +81,24 @@
     (1, 0, 4, 1, 0, 0, 0),
     (2, 0, 4, 0, 0, 3, 0),
     (3, 0, 4, 0, 0, 1, 0),
-    (4, 0, 2, 0, 0, 2, 0),
-    (4, 2, 4, 1, 0, 3, 0),
-    (5, 0, 2, 0, 0, 2, 2),
-    (5, 2, 4, 1, 0, 1, 0),
-    (6, 0, 2, 1, 0, 2, 0),
-    (7, 0, 2, 1, 0, 2, 2),
-    (8, 0, 4, 0, 1, 0, 0),
-    (8, 4, 4, 1, 1, 0, 0),
-    (9, 0, 4, 0, 1, 3, 0),
-    (9, 4, 4, 0, 1, 1, 0),
+    (4, 0, 4, 1, 0, 3, 0),
+    (5, 0, 4, 1, 0, 1, 0),
+    (6, 0, 2, 0, 0, 2, 0),
+    (6, 2, 2, 1, 0, 2, 0),
+    (7, 0, 2, 0, 0, 2, 2),
+    (7, 2, 2, 1, 0, 2, 2),
+    (8, 0, 4, 0, 1, 3, 0),
+    (8, 4, 4, 0, 1, 1, 0),
+    (8, 8, 4, 1, 1, 3, 0),
+    (8, 12, 4, 1, 1, 1, 0),
+    (9, 0, 4, 0, 1, 0, 0),
+    (9, 4, 4, 1, 1, 0, 0),
     (9, 8, 2, 0, 1, 2, 0),
-    (9, 10, 4, 1, 1, 3, 0),
-    (9, 14, 2, 0, 1, 2, 2),
-    (9, 16, 4, 1, 1, 1, 0),
-    (10, 0, 2, 1, 1, 2, 0),
-    (10, 2, 2, 1, 1, 2, 2),
+    (9, 10, 2, 1, 1, 2, 0),
+    (9, 12, 2, 0, 1, 2, 2),
+    (9, 14, 2, 1, 1, 2, 2),
 )
-NA, NB = 8, 11
+NA, NB = 8, 10
 
 
 def quantize(tiles, o_ref):
@@ -259,18 +259,18 @@
     with jax.named_scope("round1"):
         far = send(near, lambda y, c, zl, x, zh: (y, c, zl ^ 2, x, zh))
         a1p, a1m = to_x(near, 1), to_x(near, -1)
-        b2p, b2m = to_y(cat(b1p[:2], pair), 1), to_y(cat(b1m[2:], pair), -1)
+        b2p, b2m = to_y(pair, 1), to_y(pair, -1)
         far, a1p, a1m, b2p, b2m = lax.optimization_barrier((far, a1p, a1m, b2p, b2m))
     with jax.named_scope("round2"):
         a2p, a2m = to_x(cat(a1p[:1], far), 1), to_x(cat(a1m[1:], far), -1)
-        b3p, b3m = to_y(b2p[2:4], 1), to_y(b2m[4:], -1)
+        b3p, b3m = to_y(cat(b1p[:2], b2p[:2]), 1), to_y(cat(b1m[2:], b2m[2:]), -1)
         c12 = to_core(cat(b1p, b1m, b2p, b2m))
         a2p, a2m, b3p, b3m, c12, late = lax.optimization_barrier((a2p, a2m, b3p, b3m, c12, pair))
     with jax.named_scope("round3"):
         a3p, a3m = to_x(a2p[1:2], 1), to_x(a2m[2:], -1)
-        c3, c0 = to_core(cat(b3p, b3m)), to_core(cat(own, late))
+        c03 = to_core(cat(own, late, b3p, b3m))
     a = (near, a1p, a1m, far, a2p, a2m, a3p, a3m)
-    b = (own, pair, b1p, b1m, b2p, b2m, b3p, b3m, c0, c12, c3)
+    b = (own, pair, b1p, b1m, b2p, b2m, b3p, b3m, c12, c03)
     far_shape = [jax.ShapeDtypeStruct((8 * BS + PAD, BS), jnp.int16)]
     rest_shape = [jax.ShapeDtypeStruct((2, BS, 4 * BS), jnp.float32)] * 3
     got, = matmul(far_kernel, "matmul_far", 1, far_shape, pos, owner[0], a, b)

time: 171 us -> 168 us (0.982)
  the two profiles are of different devices: /device:TPU:81 before, /device:TPU:31 now
where the time goes in v10:
time: 168 us; the launch traced here: 167 us
  starting transfers between devices  87.2 us (52%)
  waiting for transfers between devices  65.5 us (39%)
  Pallas kernels  11.1 us (7%)
  local copies, waits for them, and re-layouts  1.97 us (1%)
    ppermute x23, starting transfers between devices, send(): return lax.ppermute(v, AXES, moves(f))  87.2 us
    ppermute x23, waiting for transfers between devices, send(): return lax.ppermute(v, AXES, moves(f))  65.5 us
    pallas_call x2, Pallas kernels, matmul(): pl.pallas_call(kernel, out_shape=out_shape, in_specs=[pl.BlockSpec(memory...  7.48 us
  transfers between devices with their start and end apart: 23, of which 14 were waited for; matrix products, arithmetic and copies ran while one was open for 0% of the time, Pallas kernels for 3%

profile of v10, /device:TPU:31, one launch (start us, length us, event | category | flops | bytes accessed | tf_op | source)
XLA Modules:
  0.0 167.0 jit_solution(14581963215981286143)
XLA Ops:
  0.0 3.5 %collective-permute-start.2 = (bf16[4,128,512]{2,1,0:T(8,128)(2,1)}, bf16[4,128,512]{2,1,0:T(8,128)(2,1)S(1)}, u32[]{:S(2)}, u32[]{:S(2)}) collective-permute-start(bf16[4,128,512]{2,1,0:T(8,128)(2,1)} %bitcast.14), channel_id=1, source_target_pairs={{0,16},{1,17},{2,18},{3,19},{4,20},{5,21},{6,22},{7,23},{8,24},{9,... | collective-permute-start | bytes 1572872 | tf_op jit(solution)/shard_map/round0/ppermute | solution.py:27
  5.5 3.4 %collective-permute-start.4 = (bf16[4,128,512]{2,1,0:T(8,128)(2,1)}, bf16[4,128,512]{2,1,0:T(8,128)(2,1)S(1)}, u32[]{:S(2)}, u32[]{:S(2)}) collective-permute-start(bf16[4,128,512]{2,1,0:T(8,128)(2,1)} %bitcast.16), channel_id=1, source_target_pairs={{0,384},{1,385},{2,386},{3,387},{4,388},{5,389},{6,390},{7,391},{8... | collective-permute-start | bytes 1572872 | tf_op jit(solution)/shard_map/round0/ppermute | solution.py:27
  11.4 3.1 %collective-permute-start = (bf16[512,256]{1,0:T(8,128)(2,1)S(1)}, bf16[512,256]{1,0:T(8,128)(2,1)S(1)}, u32[]{:S(2)}, u32[]{:S(2)}) collective-permute-start(bf16[512,256]{1,0:T(8,128)(2,1)S(1)} %get-tuple-element.30), channel_id=1, source_target_pairs={{0,0},{1,1},{2,2},{3,3},{4,4},{5,5},{6,6},{7,7},{8,8},{9,9},{10,10... | collective-permute-start | bytes 786440 | tf_op jit(solution)/shard_map/round0/ppermute | solution.py:27
  21.2 4.9 %collective-permute-start.5 = (bf16[2,512,256]{2,1,0:T(8,128)(2,1)S(1)}, bf16[2,512,256]{2,1,0:T(8,128)(2,1)S(1)}, u32[]{:S(2)}, u32[]{:S(2)}) collective-permute-start(bf16[2,512,256]{2,1,0:T(8,128)(2,1)S(1)} %pad_maximum_fusion.4.refs_0_), channel_id=1, source_target_pairs={{0,32},{1,33},{2,34},{3,35},{4,36},{5,37},{6,38},{7,39},{8,40},{9,... | collective-permute-start | bytes 1572872 | tf_op jit(solution)/shard_map/round1/ppermute | solution.py:27
  28.3 3.0 %collective-permute-start.7 = (bf16[2,512,256]{2,1,0:T(8,128)(2,1)S(1)}, bf16[2,512,256]{2,1,0:T(8,128)(2,1)S(1)}, u32[]{:S(2)}, u32[]{:S(2)}) collective-permute-start(bf16[2,512,256]{2,1,0:T(8,128)(2,1)S(1)} %pad_maximum_fusion.4.refs_0_), channel_id=1, source_target_pairs={{0,12},{1,13},{2,14},{3,15},{4,0},{5,1},{6,2},{7,3},{8,4},{9,5},{1... | collective-permute-start | bytes 1572872 | tf_op jit(solution)/shard_map/round1/ppermute | solution.py:27
  31.4 3.7 %collective-permute-start.8 = (bf16[4,128,512]{2,1,0:T(8,128)(2,1)S(1)}, bf16[4,128,512]{2,1,0:T(8,128)(2,1)S(1)}, u32[]{:S(2)}, u32[]{:S(2)}) collective-permute-start(bf16[4,128,512]{2,1,0:T(8,128)(2,1)S(1)} %collective-permute-done.2.refs_9_), channel_id=1, source_target_pairs={{0,128},{1,129},{2,130},{3,131},{4,132},{5,133},{6,134},{7,135},{8... | collective-permute-start | bytes 1572872 | tf_op jit(solution)/shard_map/round1/ppermute | solution.py:27
  37.1 10.9 %collective-permute-done.5.refs_3_ = bf16[2,512,256]{2,1,0:T(8,128)(2,1)S(1)} collective-permute-done((bf16[2,512,256]{2,1,0:T(8,128)(2,1)S(1)}, bf16[2,512,256]{2,1,0:T(8,128)(2,1)S(1)}, u32[]{:S(2)}, u32[]{:S(2)}) %collective-permute-start.5) | collective-permute-done | bytes 524320 | tf_op jit(solution)/shard_map/round1/ppermute | solution.py:27
  49.9 4.8 %collective-permute-start.14 = (bf16[16,128,512]{2,1,0:T(8,128)(2,1)S(1)}, bf16[16,128,512]{2,1,0:T(8,128)(2,1)S(1)}, u32[]{:S(2)}, u32[]{:S(2)}) collective-permute-start(bf16[16,128,512]{2,1,0:T(8,128)(2,1)S(1)} %pad_maximum_fusion), channel_id=1, source_target_pairs={{0,64},{1,65},{2,66},{3,67},{4,68},{5,69},{6,70},{7,71},{8,72},{9,... | collective-permute-start | bytes 6291464 | tf_op jit(solution)/shard_map/round2/ppermute | solution.py:27
  54.9 4.6 %collective-permute-start.10 = (bf16[3,512,256]{2,1,0:T(8,128)(2,1)S(1)}, bf16[3,512,256]{2,1,0:T(8,128)(2,1)S(1)}, u32[]{:S(2)}, u32[]{:S(2)}) collective-permute-start(bf16[3,512,256]{2,1,0:T(8,128)(2,1)S(1)} %get-tuple-element.56), channel_id=1, source_target_pairs={{0,4},{1,5},{2,6},{3,7},{4,8},{5,9},{6,10},{7,11},{8,12},{9,13},{1... | collective-permute-start | bytes 2359304 | tf_op jit(solution)/shard_map/round2/ppermute | solution.py:27
  67.3 9.6 %collective-permute-done.12.refs_14_ = bf16[4,128,512]{2,1,0:T(8,128)(2,1)S(1)} collective-permute-done((bf16[4,128,512]{2,1,0:T(8,128)(2,1)S(1)}, bf16[4,128,512]{2,1,0:T(8,128)(2,1)S(1)}, u32[]{:S(2)}, u32[]{:S(2)}) %collective-permute-start.12) | collective-permute-done | bytes 524320 | tf_op jit(solution)/shard_map/round2/ppermute | solution.py:27
  76.9 3.6 %collective-permute-done.13.refs_15_ = bf16[4,128,512]{2,1,0:T(8,128)(2,1)S(1)} collective-permute-done((bf16[4,128,512]{2,1,0:T(8,128)(2,1)S(1)}, bf16[4,128,512]{2,1,0:T(8,128)(2,1)S(1)}, u32[]{:S(2)}, u32[]{:S(2)}) %collective-permute-start.13) | collective-permute-done | bytes 524320 | tf_op jit(solution)/shard_map/round2/ppermute | solution.py:27
  81.9 3.0 %collective-permute-start.17 = (bf16[16,128,512]{2,1,0:T(8,128)(2,1)S(1)}, bf16[16,128,512]{2,1,0:T(8,128)(2,1)S(1)}, u32[]{:S(2)}, u32[]{:S(2)}) collective-permute-start(bf16[16,128,512]{2,1,0:T(8,128)(2,1)S(1)} %pad_maximum_fusion.1), channel_id=1, source_target_pairs={{0,64},{1,65},{2,66},{3,67},{4,68},{5,69},{6,70},{7,71},{8,72},{9,... | collective-permute-start | bytes 6291464 | tf_op jit(solution)/shard_map/round3/ppermute | solution.py:27
  84.9 3.8 %collective-permute-start.15 = (bf16[1,512,256]{2,1,0:T(8,128)(2,1)S(1)}, bf16[1,512,256]{2,1,0:T(8,128)(2,1)S(1)}, u32[]{:S(2)}, u32[]{:S(2)}) collective-permute-start(bf16[1,512,256]{2,1,0:T(8,128)(2,1)S(1)} %slice.30), channel_id=1, source_target_pairs={{0,4},{1,5},{2,6},{3,7},{4,8},{5,9},{6,10},{7,11},{8,12},{9,13},{1... | collective-permute-start | bytes 786440 | tf_op jit(solution)/shard_map/round3/ppermute | solution.py:27
  90.7 4.1 %collective-permute-done.15.refs_6_ = bf16[1,512,256]{2,1,0:T(8,128)(2,1)S(1)} collective-permute-done((bf16[1,512,256]{2,1,0:T(8,128)(2,1)S(1)}, bf16[1,512,256]{2,1,0:T(8,128)(2,1)S(1)}, u32[]{:S(2)}, u32[]{:S(2)}) %collective-permute-start.15) | collective-permute-done | bytes 262176 | tf_op jit(solution)/shard_map/round3/ppermute | solution.py:27
  94.8 4.7 %collective-permute-done.16.refs_7_ = bf16[1,512,256]{2,1,0:T(8,128)(2,1)S(1)} collective-permute-done((bf16[1,512,256]{2,1,0:T(8,128)(2,1)S(1)}, bf16[1,512,256]{2,1,0:T(8,128)(2,1)S(1)}, u32[]{:S(2)}, u32[]{:S(2)}) %collective-permute-start.16) | collective-permute-done | bytes 262176 | tf_op jit(solution)/shard_map/round3/ppermute | solution.py:27
  102.0 7.7 %collective-permute-start.18 = (s16[1040,128]{1,0:T(8,128)(2,1)S(1)}, s16[1040,128]{1,0:T(8,128)(2,1)S(1)}, u32[]{:S(2)}, u32[]{:S(2)}) collective-permute-start(s16[1040,128]{1,0:T(8,128)(2,1)S(1)} %matmul_far.1), channel_id=1, source_target_pairs={{0,1},{1,2},{2,3},{3,0},{4,5},{5,6},{6,7},{7,4},{8,9},{9,10},{10,1... | collective-permute-start | bytes 798728 | tf_op jit(solution)/shard_map/layer_far/ppermute | solution.py:27
  109.7 5.0 %matmul_rest.1 = (f32[2,128,512]{2,1,0:T(8,128)S(1)}, f32[2,128,512]{2,1,0:T(8,128)S(1)}, f32[2,128,512]{2,1,0:T(8,128)S(1)}) custom-call(s32[6]{0:T(128)S(1)} %stack.36.pos_ref, s32[32]{0:T(128)S(1)} %bitcast.22, bf16[2,512,256]{2,1,0:T(8,128)(2,1)S(1)} %pad_maximum_fusion.4.refs_0_, bf16[2,512,256]{2,1,0:T(8,128)(2,1)S(1)} %collective-permute-done.6.refs_1_, ...), custom_call_target="tpu_custom_call" | custom-call | flops 3221225472 | bytes 1048576 | tf_op jit(solution)/shard_map/matmul_rest/pallas_call | solution.py:167
  114.7 6.6 %collective-permute-done.18.got_ref = s16[1040,128]{1,0:T(8,128)(2,1)S(1)} collective-permute-done((s16[1040,128]{1,0:T(8,128)(2,1)S(1)}, s16[1040,128]{1,0:T(8,128)(2,1)S(1)}, u32[]{:S(2)}, u32[]{:S(2)}) %collective-permute-start.18) | collective-permute-done | bytes 266272 | tf_op jit(solution)/shard_map/layer_far/ppermute | solution.py:27
  122.1 5.2 %collective-permute-start.19 = (s16[1040,128]{1,0:T(8,128)(2,1)S(1)}, s16[1040,128]{1,0:T(8,128)(2,1)S(1)}, u32[]{:S(2)}, u32[]{:S(2)}) collective-permute-start(s16[1040,128]{1,0:T(8,128)(2,1)S(1)} %get-tuple-element.51), channel_id=1, source_target_pairs={{0,1},{1,2},{2,3},{3,0},{4,5},{5,6},{6,7},{7,4},{8,9},{9,10},{10,1... | collective-permute-start | bytes 798728 | tf_op jit(solution)/shard_map/layer_sums/ppermute | solution.py:27
  127.4 4.7 %collective-permute-start.20 = (s16[1040,128]{1,0:T(8,128)(2,1)S(1)}, s16[1040,128]{1,0:T(8,128)(2,1)S(1)}, u32[]{:S(2)}, u32[]{:S(2)}) collective-permute-start(s16[1040,128]{1,0:T(8,128)(2,1)S(1)} %get-tuple-element.52), channel_id=1, source_target_pairs={{0,3},{1,0},{2,1},{3,2},{4,7},{5,4},{6,5},{7,6},{8,11},{9,8},{10,9... | collective-permute-start | bytes 798728 | tf_op jit(solution)/shard_map/layer_sums/ppermute | solution.py:27
  132.1 5.4 %collective-permute-done.19.refs_0_ = s16[1040,128]{1,0:T(8,128)(2,1)S(1)} collective-permute-done((s16[1040,128]{1,0:T(8,128)(2,1)S(1)}, s16[1040,128]{1,0:T(8,128)(2,1)S(1)}, u32[]{:S(2)}, u32[]{:S(2)}) %collective-permute-start.19) | collective-permute-done | bytes 266272 | tf_op jit(solution)/shard_map/layer_sums/ppermute | solution.py:27
  137.5 9.4 %collective-permute-done.20.refs_1_ = s16[1040,128]{1,0:T(8,128)(2,1)S(1)} collective-permute-done((s16[1040,128]{1,0:T(8,128)(2,1)S(1)}, s16[1040,128]{1,0:T(8,128)(2,1)S(1)}, u32[]{:S(2)}, u32[]{:S(2)}) %collective-permute-start.20) | collective-permute-done | bytes 266272 | tf_op jit(solution)/shard_map/layer_sums/ppermute | solution.py:27
  147.6 12.3 %collective-permute-start.21 = (bf16[128,512]{1,0:T(8,128)(2,1)S(1)}, bf16[128,512]{1,0:T(8,128)(2,1)S(1)}, u32[]{:S(2)}, u32[]{:S(2)}) collective-permute-start(bf16[128,512]{1,0:T(8,128)(2,1)S(1)} %get-tuple-element.53), channel_id=1, source_target_pairs={{0,0},{1,1},{2,2},{3,3},{4,4},{5,5},{6,6},{7,7},{8,8},{9,9},{10,10... | collective-permute-start | bytes 393224 | tf_op jit(solution)/shard_map/product_pair/ppermute | solution.py:27
  162.6 3.1 %collective-permute-done.22.second_ref = bf16[128,512]{1,0:T(8,128)(2,1)S(1)} collective-permute-done((bf16[128,512]{1,0:T(8,128)(2,1)S(1)}, bf16[128,512]{1,0:T(8,128)(2,1)S(1)}, u32[]{:S(2)}, u32[]{:S(2)}) %collective-permute-start.22) | collective-permute-done | bytes 131104 | tf_op jit(solution)/shard_map/product_pair/ppermute | solution.py:27
  (58 shorter events, 36.3 us)
Async XLA Ops:
  0.0 21.1 %collective-permute-start.2 = (bf16[4,128,512]{2,1,0:T(8,128)(2,1)}, bf16[4,128,512]{2,1,0:T(8,128)(2,1)S(1)}, u32[]{:S(2)}, u32[]{:S(2)}) collective-permute-start(bf16[4,128,512]{2,1,0:T(8,128)(2,1)} %bitcast.14), channel_id=1, source_target_pairs={{0,16},{1,17},{2,18},{3,19},{4,20},{5,21},{6,22},{7,23},{8,24},{9,... | collective-permute-start | bytes 1572872 | tf_op jit(solution)/shard_map/round0/ppermute | solution.py:27
  3.5 17.6 %collective-permute-start.3 = (bf16[4,128,512]{2,1,0:T(8,128)(2,1)}, bf16[4,128,512]{2,1,0:T(8,128)(2,1)S(1)}, u32[]{:S(2)}, u32[]{:S(2)}) collective-permute-start(bf16[4,128,512]{2,1,0:T(8,128)(2,1)} %bitcast.15), channel_id=1, source_target_pairs={{0,128},{1,129},{2,130},{3,131},{4,132},{5,133},{6,134},{7,135},{8... | collective-permute-start | bytes 1572872 | tf_op jit(solution)/shard_map/round0/ppermute | solution.py:27
  5.5 15.6 %collective-permute-start.4 = (bf16[4,128,512]{2,1,0:T(8,128)(2,1)}, bf16[4,128,512]{2,1,0:T(8,128)(2,1)S(1)}, u32[]{:S(2)}, u32[]{:S(2)}) collective-permute-start(bf16[4,128,512]{2,1,0:T(8,128)(2,1)} %bitcast.16), channel_id=1, source_target_pairs={{0,384},{1,385},{2,386},{3,387},{4,388},{5,389},{6,390},{7,391},{8... | collective-permute-start | bytes 1572872 | tf_op jit(solution)/shard_map/round0/ppermute | solution.py:27
  11.4 8.0 %collective-permute-start = (bf16[512,256]{1,0:T(8,128)(2,1)S(1)}, bf16[512,256]{1,0:T(8,128)(2,1)S(1)}, u32[]{:S(2)}, u32[]{:S(2)}) collective-permute-start(bf16[512,256]{1,0:T(8,128)(2,1)S(1)} %get-tuple-element.30), channel_id=1, source_target_pairs={{0,0},{1,1},{2,2},{3,3},{4,4},{5,5},{6,6},{7,7},{8,8},{9,9},{10,10... | collective-permute-start | bytes 786440 | tf_op jit(solution)/shard_map/round0/ppermute | solution.py:27
  14.5 6.6 %collective-permute-start.1 = (bf16[512,256]{1,0:T(8,128)(2,1)S(1)}, bf16[512,256]{1,0:T(8,128)(2,1)S(1)}, u32[]{:S(2)}, u32[]{:S(2)}) collective-permute-start(bf16[512,256]{1,0:T(8,128)(2,1)S(1)} %get-tuple-element.31), channel_id=1, source_target_pairs={{0,64},{1,65},{2,66},{3,67},{4,68},{5,69},{6,70},{7,71},{8,72},{9,... | collective-permute-start | bytes 786440 | tf_op jit(solution)/shard_map/round0/ppermute | solution.py:27
  21.2 26.8 %collective-permute-start.5 = (bf16[2,512,256]{2,1,0:T(8,128)(2,1)S(1)}, bf16[2,512,256]{2,1,0:T(8,128)(2,1)S(1)}, u32[]{:S(2)}, u32[]{:S(2)}) collective-permute-start(bf16[2,512,256]{2,1,0:T(8,128)(2,1)S(1)} %pad_maximum_fusion.4.refs_0_), channel_id=1, source_target_pairs={{0,32},{1,33},{2,34},{3,35},{4,36},{5,37},{6,38},{7,39},{8,40},{9,... | collective-permute-start | bytes 1572872 | tf_op jit(solution)/shard_map/round1/ppermute | solution.py:27
  26.1 21.9 %collective-permute-start.6 = (bf16[2,512,256]{2,1,0:T(8,128)(2,1)S(1)}, bf16[2,512,256]{2,1,0:T(8,128)(2,1)S(1)}, u32[]{:S(2)}, u32[]{:S(2)}) collective-permute-start(bf16[2,512,256]{2,1,0:T(8,128)(2,1)S(1)} %pad_maximum_fusion.4.refs_0_), channel_id=1, source_target_pairs={{0,4},{1,5},{2,6},{3,7},{4,8},{5,9},{6,10},{7,11},{8,12},{9,13},{1... | collective-permute-start | bytes 1572872 | tf_op jit(solution)/shard_map/round1/ppermute | solution.py:27
  28.3 19.7 %collective-permute-start.7 = (bf16[2,512,256]{2,1,0:T(8,128)(2,1)S(1)}, bf16[2,512,256]{2,1,0:T(8,128)(2,1)S(1)}, u32[]{:S(2)}, u32[]{:S(2)}) collective-permute-start(bf16[2,512,256]{2,1,0:T(8,128)(2,1)S(1)} %pad_maximum_fusion.4.refs_0_), channel_id=1, source_target_pairs={{0,12},{1,13},{2,14},{3,15},{4,0},{5,1},{6,2},{7,3},{8,4},{9,5},{1... | collective-permute-start | bytes 1572872 | tf_op jit(solution)/shard_map/round1/ppermute | solution.py:27
  31.4 16.6 %collective-permute-start.8 = (bf16[4,128,512]{2,1,0:T(8,128)(2,1)S(1)}, bf16[4,128,512]{2,1,0:T(8,128)(2,1)S(1)}, u32[]{:S(2)}, u32[]{:S(2)}) collective-permute-start(bf16[4,128,512]{2,1,0:T(8,128)(2,1)S(1)} %collective-permute-done.2.refs_9_), channel_id=1, source_target_pairs={{0,128},{1,129},{2,130},{3,131},{4,132},{5,133},{6,134},{7,135},{8... | collective-permute-start | bytes 1572872 | tf_op jit(solution)/shard_map/round1/ppermute | solution.py:27
  35.1 14.5 %collective-permute-start.9 = (bf16[4,128,512]{2,1,0:T(8,128)(2,1)S(1)}, bf16[4,128,512]{2,1,0:T(8,128)(2,1)S(1)}, u32[]{:S(2)}, u32[]{:S(2)}) collective-permute-start(bf16[4,128,512]{2,1,0:T(8,128)(2,1)S(1)} %collective-permute-done.2.refs_9_), channel_id=1, source_target_pairs={{0,384},{1,385},{2,386},{3,387},{4,388},{5,389},{6,390},{7,391},{8... | collective-permute-start | bytes 1572872 | tf_op jit(solution)/shard_map/round1/ppermute | solution.py:27
  49.9 31.7 %collective-permute-start.14 = (bf16[16,128,512]{2,1,0:T(8,128)(2,1)S(1)}, bf16[16,128,512]{2,1,0:T(8,128)(2,1)S(1)}, u32[]{:S(2)}, u32[]{:S(2)}) collective-permute-start(bf16[16,128,512]{2,1,0:T(8,128)(2,1)S(1)} %pad_maximum_fusion), channel_id=1, source_target_pairs={{0,64},{1,65},{2,66},{3,67},{4,68},{5,69},{6,70},{7,71},{8,72},{9,... | collective-permute-start | bytes 6291464 | tf_op jit(solution)/shard_map/round2/ppermute | solution.py:27
  54.9 25.6 %collective-permute-start.10 = (bf16[3,512,256]{2,1,0:T(8,128)(2,1)S(1)}, bf16[3,512,256]{2,1,0:T(8,128)(2,1)S(1)}, u32[]{:S(2)}, u32[]{:S(2)}) collective-permute-start(bf16[3,512,256]{2,1,0:T(8,128)(2,1)S(1)} %get-tuple-element.56), channel_id=1, source_target_pairs={{0,4},{1,5},{2,6},{3,7},{4,8},{5,9},{6,10},{7,11},{8,12},{9,13},{1... | collective-permute-start | bytes 2359304 | tf_op jit(solution)/shard_map/round2/ppermute | solution.py:27
  59.5 22.1 %collective-permute-start.11 = (bf16[3,512,256]{2,1,0:T(8,128)(2,1)S(1)}, bf16[3,512,256]{2,1,0:T(8,128)(2,1)S(1)}, u32[]{:S(2)}, u32[]{:S(2)}) collective-permute-start(bf16[3,512,256]{2,1,0:T(8,128)(2,1)S(1)} %get-tuple-element.55), channel_id=1, source_target_pairs={{0,12},{1,13},{2,14},{3,15},{4,0},{5,1},{6,2},{7,3},{8,4},{9,5},{1... | collective-permute-start | bytes 2359304 | tf_op jit(solution)/shard_map/round2/ppermute | solution.py:27
  61.7 15.1 %collective-permute-start.12 = (bf16[4,128,512]{2,1,0:T(8,128)(2,1)S(1)}, bf16[4,128,512]{2,1,0:T(8,128)(2,1)S(1)}, u32[]{:S(2)}, u32[]{:S(2)}) collective-permute-start(bf16[4,128,512]{2,1,0:T(8,128)(2,1)S(1)} %pad_maximum_fusion.5), channel_id=1, source_target_pairs={{0,128},{1,129},{2,130},{3,131},{4,132},{5,133},{6,134},{7,135},{8... | collective-permute-start | bytes 1572872 | tf_op jit(solution)/shard_map/round2/ppermute | solution.py:27
  64.4 16.1 %collective-permute-start.13 = (bf16[4,128,512]{2,1,0:T(8,128)(2,1)S(1)}, bf16[4,128,512]{2,1,0:T(8,128)(2,1)S(1)}, u32[]{:S(2)}, u32[]{:S(2)}) collective-permute-start(bf16[4,128,512]{2,1,0:T(8,128)(2,1)S(1)} %pad_maximum_fusion.6), channel_id=1, source_target_pairs={{0,384},{1,385},{2,386},{3,387},{4,388},{5,389},{6,390},{7,391},{8... | collective-permute-start | bytes 1572872 | tf_op jit(solution)/shard_map/round2/ppermute | solution.py:27
  81.9 17.6 %collective-permute-start.17 = (bf16[16,128,512]{2,1,0:T(8,128)(2,1)S(1)}, bf16[16,128,512]{2,1,0:T(8,128)(2,1)S(1)}, u32[]{:S(2)}, u32[]{:S(2)}) collective-permute-start(bf16[16,128,512]{2,1,0:T(8,128)(2,1)S(1)} %pad_maximum_fusion.1), channel_id=1, source_target_pairs={{0,64},{1,65},{2,66},{3,67},{4,68},{5,69},{6,70},{7,71},{8,72},{9,... | collective-permute-start | bytes 6291464 | tf_op jit(solution)/shard_map/round3/ppermute | solution.py:27
  84.9 9.8 %collective-permute-start.15 = (bf16[1,512,256]{2,1,0:T(8,128)(2,1)S(1)}, bf16[1,512,256]{2,1,0:T(8,128)(2,1)S(1)}, u32[]{:S(2)}, u32[]{:S(2)}) collective-permute-start(bf16[1,512,256]{2,1,0:T(8,128)(2,1)S(1)} %slice.30), channel_id=1, source_target_pairs={{0,4},{1,5},{2,6},{3,7},{4,8},{5,9},{6,10},{7,11},{8,12},{9,13},{1... | collective-permute-start | bytes 786440 | tf_op jit(solution)/shard_map/round3/ppermute | solution.py:27
  88.8 10.7 %collective-permute-start.16 = (bf16[1,512,256]{2,1,0:T(8,128)(2,1)S(1)}, bf16[1,512,256]{2,1,0:T(8,128)(2,1)S(1)}, u32[]{:S(2)}, u32[]{:S(2)}) collective-permute-start(bf16[1,512,256]{2,1,0:T(8,128)(2,1)S(1)} %slice.31), channel_id=1, source_target_pairs={{0,12},{1,13},{2,14},{3,15},{4,0},{5,1},{6,2},{7,3},{8,4},{9,5},{1... | collective-permute-start | bytes 786440 | tf_op jit(solution)/shard_map/round3/ppermute | solution.py:27
  102.0 19.3 %collective-permute-start.18 = (s16[1040,128]{1,0:T(8,128)(2,1)S(1)}, s16[1040,128]{1,0:T(8,128)(2,1)S(1)}, u32[]{:S(2)}, u32[]{:S(2)}) collective-permute-start(s16[1040,128]{1,0:T(8,128)(2,1)S(1)} %matmul_far.1), channel_id=1, source_target_pairs={{0,1},{1,2},{2,3},{3,0},{4,5},{5,6},{6,7},{7,4},{8,9},{9,10},{10,1... | collective-permute-start | bytes 798728 | tf_op jit(solution)/shard_map/layer_far/ppermute | solution.py:27
  114.7 51.0 %copy-start.6 = (s32[2,4]{1,0:T(2,128)S(1)}, s32[2,4]{1,0:T(2,128)}, u32[]{:S(2)}) copy-start(s32[2,4]{1,0:T(2,128)} %pat_ref.1) | copy-start | bytes 100
  122.1 15.4 %collective-permute-start.19 = (s16[1040,128]{1,0:T(8,128)(2,1)S(1)}, s16[1040,128]{1,0:T(8,128)(2,1)S(1)}, u32[]{:S(2)}, u32[]{:S(2)}) collective-permute-start(s16[1040,128]{1,0:T(8,128)(2,1)S(1)} %get-tuple-element.51), channel_id=1, source_target_pairs={{0,1},{1,2},{2,3},{3,0},{4,5},{5,6},{6,7},{7,4},{8,9},{9,10},{10,1... | collective-permute-start | bytes 798728 | tf_op jit(solution)/shard_map/layer_sums/ppermute | solution.py:27
  127.4 19.5 %collective-permute-start.20 = (s16[1040,128]{1,0:T(8,128)(2,1)S(1)}, s16[1040,128]{1,0:T(8,128)(2,1)S(1)}, u32[]{:S(2)}, u32[]{:S(2)}) collective-permute-start(s16[1040,128]{1,0:T(8,128)(2,1)S(1)} %get-tuple-element.52), channel_id=1, source_target_pairs={{0,3},{1,0},{2,1},{3,2},{4,7},{5,4},{6,5},{7,6},{8,11},{9,8},{10,9... | collective-permute-start | bytes 798728 | tf_op jit(solution)/shard_map/layer_sums/ppermute | solution.py:27
  147.6 15.0 %collective-permute-start.21 = (bf16[128,512]{1,0:T(8,128)(2,1)S(1)}, bf16[128,512]{1,0:T(8,128)(2,1)S(1)}, u32[]{:S(2)}, u32[]{:S(2)}) collective-permute-start(bf16[128,512]{1,0:T(8,128)(2,1)S(1)} %get-tuple-element.53), channel_id=1, source_target_pairs={{0,0},{1,1},{2,2},{3,3},{4,4},{5,5},{6,6},{7,7},{8,8},{9,9},{10,10... | collective-permute-start | bytes 393224 | tf_op jit(solution)/shard_map/product_pair/ppermute | solution.py:27
  160.0 5.7 %collective-permute-start.22 = (bf16[128,512]{1,0:T(8,128)(2,1)S(1)}, bf16[128,512]{1,0:T(8,128)(2,1)S(1)}, u32[]{:S(2)}, u32[]{:S(2)}) collective-permute-start(bf16[128,512]{1,0:T(8,128)(2,1)S(1)} %get-tuple-element.54), channel_id=1, source_target_pairs={{0,16},{1,17},{2,18},{3,19},{4,20},{5,21},{6,22},{7,23},{8,24},{9,... | collective-permute-start | bytes 393224 | tf_op jit(solution)/shard_map/product_pair/ppermute | solution.py:27
  (7 other events, 137.3 us)

commit v11 on v10

--- a/solution.py
+++ b/solution.py
@@ -73,8 +73,7 @@
     ((1, 0, 0), (1, 0, 1)),
     ((0, 2, 0), (1, 3, 0), (1, 3, 1)),
     ((0, 2, 1), (1, 1, 0), (1, 1, 1)),
-    ((1, 2, 0),),
-    ((1, 2, 1),),
+    ((1, 2, 0), (1, 2, 1)),
 )
 SLAB = (
     (0, 0, 4, 0, 0, 0, 0),
@@ -83,22 +82,18 @@
     (3, 0, 4, 0, 0, 1, 0),
     (4, 0, 4, 1, 0, 3, 0),
     (5, 0, 4, 1, 0, 1, 0),
-    (6, 0, 2, 0, 0, 2, 0),
-    (6, 2, 2, 1, 0, 2, 0),
-    (7, 0, 2, 0, 0, 2, 2),
-    (7, 2, 2, 1, 0, 2, 2),
-    (8, 0, 4, 0, 1, 3, 0),
-    (8, 4, 4, 0, 1, 1, 0),
-    (8, 8, 4, 1, 1, 3, 0),
-    (8, 12, 4, 1, 1, 1, 0),
-    (9, 0, 4, 0, 1, 0, 0),
-    (9, 4, 4, 1, 1, 0, 0),
-    (9, 8, 2, 0, 1, 2, 0),
-    (9, 10, 2, 1, 1, 2, 0),
-    (9, 12, 2, 0, 1, 2, 2),
-    (9, 14, 2, 1, 1, 2, 2),
+    (6, 0, 4, 0, 0, 2, 0),
+    (6, 4, 4, 1, 0, 2, 0),
+    (7, 0, 4, 0, 1, 3, 0),
+    (7, 4, 4, 0, 1, 1, 0),
+    (7, 8, 4, 1, 1, 3, 0),
+    (7, 12, 4, 1, 1, 1, 0),
+    (8, 0, 4, 0, 1, 0, 0),
+    (8, 4, 4, 1, 1, 0, 0),
+    (8, 8, 4, 0, 1, 2, 0),
+    (8, 12, 4, 1, 1, 2, 0),
 )
-NA, NB = 8, 10
+NA, NB = 7, 9
 
 
 def quantize(tiles, o_ref):
@@ -261,16 +256,17 @@
         a1p, a1m = to_x(near, 1), to_x(near, -1)
         b2p, b2m = to_y(pair, 1), to_y(pair, -1)
         far, a1p, a1m, b2p, b2m = lax.optimization_barrier((far, a1p, a1m, b2p, b2m))
+    even = row % 2 == 0
     with jax.named_scope("round2"):
         a2p, a2m = to_x(cat(a1p[:1], far), 1), to_x(cat(a1m[1:], far), -1)
-        b3p, b3m = to_y(cat(b1p[:2], b2p[:2]), 1), to_y(cat(b1m[2:], b2m[2:]), -1)
+        b3 = send(jnp.where(even, cat(b1p, b2p), cat(b1m, b2m)), lambda y, c, zl, x, zh: ((y + 1 - 2 * c) % 4, c, zl, x, zh))
         c12 = to_core(cat(b1p, b1m, b2p, b2m))
-        a2p, a2m, b3p, b3m, c12, late = lax.optimization_barrier((a2p, a2m, b3p, b3m, c12, pair))
+        a2p, a2m, b3, c12, late = lax.optimization_barrier((a2p, a2m, b3, c12, pair))
     with jax.named_scope("round3"):
-        a3p, a3m = to_x(a2p[1:2], 1), to_x(a2m[2:], -1)
-        c03 = to_core(cat(own, late, b3p, b3m))
-    a = (near, a1p, a1m, far, a2p, a2m, a3p, a3m)
-    b = (own, pair, b1p, b1m, b2p, b2m, b3p, b3m, c12, c03)
+        a3 = send(jnp.where(even, a2p[1:], a2m[1:]), lambda y, c, zl, x, zh: (y, c, zl, (x + 1 - 2 * c) % 4, zh))
+        c03 = to_core(cat(own, late, b3))
+    a = (near, a1p, a1m, far, a2p, a2m, a3)
+    b = (own, pair, b1p, b1m, b2p, b2m, b3, c12, c03)
     far_shape = [jax.ShapeDtypeStruct((8 * BS + PAD, BS), jnp.int16)]
     rest_shape = [jax.ShapeDtypeStruct((2, BS, 4 * BS), jnp.float32)] * 3
     got, = matmul(far_kernel, "matmul_far", 1, far_shape, pos, owner[0], a, b)

time: 168 us -> 176 us (1.048)
  the two profiles are of different devices: /device:TPU:31 before, /device:TPU:65 now
where the time goes in v11:
time: 176 us; the launch traced here: 175 us
  starting transfers between devices  95.5 us (54%)
  waiting for transfers between devices  55.4 us (31%)
  Pallas kernels  12.5 us (7%)
  local copies, waits for them, and re-layouts  6.74 us (4%)
  other arithmetic  4.55 us (3%)
    ppermute x21, starting transfers between devices, send(): return lax.ppermute(v, AXES, moves(f))  95.5 us
    ppermute x21, waiting for transfers between devices, send(): return lax.ppermute(v, AXES, moves(f))  55.4 us
    pallas_call x2, Pallas kernels, matmul(): pl.pallas_call(kernel, out_shape=out_shape, in_specs=[pl.BlockSpec(memory...  8.93 us
  transfers between devices with their start and end apart: 21, of which 10 were waited for; matrix products, arithmetic and copies ran while one was open for 3% of the time, Pallas kernels for 4%

profile of v11, /device:TPU:65, one launch (start us, length us, event | category | flops | bytes accessed | tf_op | source)
XLA Modules:
  0.0 175.1 jit_solution(18310654307224743480)
XLA Ops:
  0.0 3.5 %collective-permute-start.2 = (bf16[4,128,512]{2,1,0:T(8,128)(2,1)}, bf16[4,128,512]{2,1,0:T(8,128)(2,1)S(1)}, u32[]{:S(2)}, u32[]{:S(2)}) collective-permute-start(bf16[4,128,512]{2,1,0:T(8,128)(2,1)} %bitcast.14), channel_id=1, source_target_pairs={{0,16},{1,17},{2,18},{3,19},{4,20},{5,21},{6,22},{7,23},{8,24},{9,... | collective-permute-start | bytes 1572872 | tf_op jit(solution)/shard_map/round0/ppermute | solution.py:27
  3.5 3.2 %collective-permute-start.3 = (bf16[4,128,512]{2,1,0:T(8,128)(2,1)}, bf16[4,128,512]{2,1,0:T(8,128)(2,1)S(1)}, u32[]{:S(2)}, u32[]{:S(2)}) collective-permute-start(bf16[4,128,512]{2,1,0:T(8,128)(2,1)} %bitcast.15), channel_id=1, source_target_pairs={{0,128},{1,129},{2,130},{3,131},{4,132},{5,133},{6,134},{7,135},{8... | collective-permute-start | bytes 1572872 | tf_op jit(solution)/shard_map/round0/ppermute | solution.py:27
  6.8 3.4 %collective-permute-start.4 = (bf16[4,128,512]{2,1,0:T(8,128)(2,1)}, bf16[4,128,512]{2,1,0:T(8,128)(2,1)S(1)}, u32[]{:S(2)}, u32[]{:S(2)}) collective-permute-start(bf16[4,128,512]{2,1,0:T(8,128)(2,1)} %bitcast.16), channel_id=1, source_target_pairs={{0,384},{1,385},{2,386},{3,387},{4,388},{5,389},{6,390},{7,391},{8... | collective-permute-start | bytes 1572872 | tf_op jit(solution)/shard_map/round0/ppermute | solution.py:27
  12.7 3.1 %collective-permute-start = (bf16[512,256]{1,0:T(8,128)(2,1)S(1)}, bf16[512,256]{1,0:T(8,128)(2,1)S(1)}, u32[]{:S(2)}, u32[]{:S(2)}) collective-permute-start(bf16[512,256]{1,0:T(8,128)(2,1)S(1)} %get-tuple-element.29), channel_id=1, source_target_pairs={{0,0},{1,1},{2,2},{3,3},{4,4},{5,5},{6,6},{7,7},{8,8},{9,9},{10,10... | collective-permute-start | bytes 786440 | tf_op jit(solution)/shard_map/round0/ppermute | solution.py:27
  17.7 3.0 %collective-permute-done = bf16[512,256]{1,0:T(8,128)(2,1)S(1)} collective-permute-done((bf16[512,256]{1,0:T(8,128)(2,1)S(1)}, bf16[512,256]{1,0:T(8,128)(2,1)S(1)}, u32[]{:S(2)}, u32[]{:S(2)}) %collective-permute-start) | collective-permute-done | bytes 262176 | tf_op jit(solution)/shard_map/round0/ppermute | solution.py:27
  21.9 6.7 %collective-permute-start.5 = (bf16[2,512,256]{2,1,0:T(8,128)(2,1)S(1)}, bf16[2,512,256]{2,1,0:T(8,128)(2,1)S(1)}, u32[]{:S(2)}, u32[]{:S(2)}) collective-permute-start(bf16[2,512,256]{2,1,0:T(8,128)(2,1)S(1)} %pad_maximum_fusion.4.refs_0_), channel_id=1, source_target_pairs={{0,32},{1,33},{2,34},{3,35},{4,36},{5,37},{6,38},{7,39},{8,40},{9,... | collective-permute-start | bytes 1572872 | tf_op jit(solution)/shard_map/round1/ppermute | solution.py:27
  30.5 4.6 %collective-permute-start.7 = (bf16[2,512,256]{2,1,0:T(8,128)(2,1)S(1)}, bf16[2,512,256]{2,1,0:T(8,128)(2,1)}, u32[]{:S(2)}, u32[]{:S(2)}) collective-permute-start(bf16[2,512,256]{2,1,0:T(8,128)(2,1)S(1)} %pad_maximum_fusion.4.refs_0_), channel_id=1, source_target_pairs={{0,12},{1,13},{2,14},{3,15},{4,0},{5,1},{6,2},{7,3},{8,4},{9,5},{1... | collective-permute-start | bytes 1572872 | tf_op jit(solution)/shard_map/round1/ppermute | solution.py:27
  37.8 4.6 %collective-permute-start.9 = (bf16[4,128,512]{2,1,0:T(8,128)(2,1)S(1)}, bf16[4,128,512]{2,1,0:T(8,128)(2,1)S(1)}, u32[]{:S(2)}, u32[]{:S(2)}) collective-permute-start(bf16[4,128,512]{2,1,0:T(8,128)(2,1)S(1)} %collective-permute-done.2.refs_8_), channel_id=1, source_target_pairs={{0,384},{1,385},{2,386},{3,387},{4,388},{5,389},{6,390},{7,391},{8... | collective-permute-start | bytes 1572872 | tf_op jit(solution)/shard_map/round1/ppermute | solution.py:27
  42.4 8.1 %collective-permute-done.5.refs_3_ = bf16[2,512,256]{2,1,0:T(8,128)(2,1)S(1)} collective-permute-done((bf16[2,512,256]{2,1,0:T(8,128)(2,1)S(1)}, bf16[2,512,256]{2,1,0:T(8,128)(2,1)S(1)}, u32[]{:S(2)}, u32[]{:S(2)}) %collective-permute-start.5) | collective-permute-done | bytes 524320 | tf_op jit(solution)/shard_map/round1/ppermute | solution.py:27
  53.0 5.1 %collective-permute-start.13 = (bf16[16,128,512]{2,1,0:T(8,128)(2,1)}, bf16[16,128,512]{2,1,0:T(8,128)(2,1)S(1)}, u32[]{:S(2)}, u32[]{:S(2)}) collective-permute-start(bf16[16,128,512]{2,1,0:T(8,128)(2,1)} %pad_maximum_fusion), channel_id=1, source_target_pairs={{0,64},{1,65},{2,66},{3,67},{4,68},{5,69},{6,70},{7,71},{8,72},{9,... | collective-permute-start | bytes 6291464 | tf_op jit(solution)/shard_map/round2/ppermute | solution.py:27
  59.5 5.5 %collective-permute-start.12 = (bf16[8,128,512]{2,1,0:T(8,128)(2,1)S(1)}, bf16[8,128,512]{2,1,0:T(8,128)(2,1)S(1)}, u32[]{:S(2)}, u32[]{:S(2)}) collective-permute-start(bf16[8,128,512]{2,1,0:T(8,128)(2,1)S(1)} %maximum_select_fusion), channel_id=1, source_target_pairs={{0,128},{1,129},{2,130},{3,131},{4,132},{5,133},{6,134},{7,135},{8... | collective-permute-start | bytes 3145736 | tf_op jit(solution)/shard_map/round2/ppermute | solution.py:27
  71.4 4.7 %collective-permute-start.11 = (bf16[3,512,256]{2,1,0:T(8,128)(2,1)S(1)}, bf16[3,512,256]{2,1,0:T(8,128)(2,1)S(1)}, u32[]{:S(2)}, u32[]{:S(2)}) collective-permute-start(bf16[3,512,256]{2,1,0:T(8,128)(2,1)S(1)} %get-tuple-element.53), channel_id=1, source_target_pairs={{0,12},{1,13},{2,14},{3,15},{4,0},{5,1},{6,2},{7,3},{8,4},{9,5},{1... | collective-permute-start | bytes 2359304 | tf_op jit(solution)/shard_map/round2/ppermute | solution.py:27
  76.1 12.8 %collective-permute-done.10.refs_4_ = bf16[3,512,256]{2,1,0:T(8,128)(2,1)S(1)} collective-permute-done((bf16[3,512,256]{2,1,0:T(8,128)(2,1)S(1)}, bf16[3,512,256]{2,1,0:T(8,128)(2,1)S(1)}, u32[]{:S(2)}, u32[]{:S(2)}) %collective-permute-start.10) | collective-permute-done | bytes 786464 | tf_op jit(solution)/shard_map/round2/ppermute | solution.py:27
  88.9 1.9 %collective-permute-done.11.refs_5_ = bf16[3,512,256]{2,1,0:T(8,128)(2,1)S(1)} collective-permute-done((bf16[3,512,256]{2,1,0:T(8,128)(2,1)S(1)}, bf16[3,512,256]{2,1,0:T(8,128)(2,1)S(1)}, u32[]{:S(2)}, u32[]{:S(2)}) %collective-permute-start.11) | collective-permute-done | bytes 786464 | tf_op jit(solution)/shard_map/round2/ppermute | solution.py:27
  93.1 5.0 %collective-permute-start.14 = (bf16[2,512,256]{2,1,0:T(8,128)(2,1)S(1)}, bf16[2,512,256]{2,1,0:T(8,128)(2,1)S(1)}, u32[]{:S(2)}, u32[]{:S(2)}) collective-permute-start(bf16[2,512,256]{2,1,0:T(8,128)(2,1)S(1)} %slice_select_fusion), channel_id=1, source_target_pairs={{0,4},{1,5},{2,6},{3,7},{4,8},{5,9},{6,10},{7,11},{8,12},{9,13},{1... | collective-permute-start | bytes 1572872 | tf_op jit(solution)/shard_map/round3/ppermute | solution.py:27
  98.1 6.1 %collective-permute-done.14.refs_6_ = bf16[2,512,256]{2,1,0:T(8,128)(2,1)S(1)} collective-permute-done((bf16[2,512,256]{2,1,0:T(8,128)(2,1)S(1)}, bf16[2,512,256]{2,1,0:T(8,128)(2,1)S(1)}, u32[]{:S(2)}, u32[]{:S(2)}) %collective-permute-start.14) | collective-permute-done | bytes 524320 | tf_op jit(solution)/shard_map/round3/ppermute | solution.py:27
  104.2 3.2 %matmul_far.1 = s16[1040,128]{1,0:T(8,128)(2,1)S(1)} custom-call(s32[6]{0:T(128)S(1)} %stack.36.pos_ref, s32[32]{0:T(128)S(1)} %bitcast.21, bf16[2,512,256]{2,1,0:T(8,128)(2,1)S(1)} %copy-done.7, bf16[2,512,256]{2,1,0:T(8,128)(2,1)} %collective-permute-done.6.refs_1_, bf16[2,512,256]{2,1,0:T(8,128)(2,1)} %collective-permute-done.7.refs_2_, ...), custom_call_target="tpu_custom_call" | custom-call | flops 1073741824 | bytes 1048576 | tf_op jit(solution)/shard_map/matmul_far/pallas_call | solution.py:162
  107.4 8.3 %collective-permute-start.16 = (s16[1040,128]{1,0:T(8,128)(2,1)S(1)}, s16[1040,128]{1,0:T(8,128)(2,1)S(1)}, u32[]{:S(2)}, u32[]{:S(2)}) collective-permute-start(s16[1040,128]{1,0:T(8,128)(2,1)S(1)} %matmul_far.1), channel_id=1, source_target_pairs={{0,1},{1,2},{2,3},{3,0},{4,5},{5,6},{6,7},{7,4},{8,9},{9,10},{10,1... | collective-permute-start | bytes 798728 | tf_op jit(solution)/shard_map/layer_far/ppermute | solution.py:27
  115.6 5.8 %matmul_rest.1 = (f32[2,128,512]{2,1,0:T(8,128)S(1)}, f32[2,128,512]{2,1,0:T(8,128)S(1)}, f32[2,128,512]{2,1,0:T(8,128)S(1)}) custom-call(s32[6]{0:T(128)S(1)} %stack.36.pos_ref, s32[32]{0:T(128)S(1)} %bitcast.22, bf16[2,512,256]{2,1,0:T(8,128)(2,1)S(1)} %copy-done.7, bf16[2,512,256]{2,1,0:T(8,128)(2,1)} %collective-permute-done.6.refs_1_, ...), custom_call_target="tpu_custom_call" | custom-call | flops 3221225472 | bytes 1048576 | tf_op jit(solution)/shard_map/matmul_rest/pallas_call | solution.py:162
  122.3 7.8 %collective-permute-start.17 = (s16[1040,128]{1,0:T(8,128)(2,1)S(1)}, s16[1040,128]{1,0:T(8,128)(2,1)S(1)}, u32[]{:S(2)}, u32[]{:S(2)}) collective-permute-start(s16[1040,128]{1,0:T(8,128)(2,1)S(1)} %get-tuple-element.49), channel_id=1, source_target_pairs={{0,1},{1,2},{2,3},{3,0},{4,5},{5,6},{6,7},{7,4},{8,9},{9,10},{10,1... | collective-permute-start | bytes 798728 | tf_op jit(solution)/shard_map/layer_sums/ppermute | solution.py:27
  130.1 7.2 %collective-permute-start.18 = (s16[1040,128]{1,0:T(8,128)(2,1)S(1)}, s16[1040,128]{1,0:T(8,128)(2,1)S(1)}, u32[]{:S(2)}, u32[]{:S(2)}) collective-permute-start(s16[1040,128]{1,0:T(8,128)(2,1)S(1)} %get-tuple-element.50), channel_id=1, source_target_pairs={{0,3},{1,0},{2,1},{3,2},{4,7},{5,4},{6,5},{7,6},{8,11},{9,8},{10,9... | collective-permute-start | bytes 798728 | tf_op jit(solution)/shard_map/layer_sums/ppermute | solution.py:27
  137.3 16.8 %collective-permute-done.17.refs_0_ = s16[1040,128]{1,0:T(8,128)(2,1)S(1)} collective-permute-done((s16[1040,128]{1,0:T(8,128)(2,1)S(1)}, s16[1040,128]{1,0:T(8,128)(2,1)S(1)}, u32[]{:S(2)}, u32[]{:S(2)}) %collective-permute-start.17) | collective-permute-done | bytes 266272 | tf_op jit(solution)/shard_map/layer_sums/ppermute | solution.py:27
  156.5 11.6 %collective-permute-start.19 = (bf16[128,512]{1,0:T(8,128)(2,1)S(1)}, bf16[128,512]{1,0:T(8,128)(2,1)S(1)}, u32[]{:S(2)}, u32[]{:S(2)}) collective-permute-start(bf16[128,512]{1,0:T(8,128)(2,1)S(1)} %get-tuple-element.51), channel_id=1, source_target_pairs={{0,0},{1,1},{2,2},{3,3},{4,4},{5,5},{6,6},{7,7},{8,8},{9,9},{10,10... | collective-permute-start | bytes 393224 | tf_op jit(solution)/shard_map/product_pair/ppermute | solution.py:27
  170.7 3.1 %collective-permute-done.20.second_ref = bf16[128,512]{1,0:T(8,128)(2,1)S(1)} collective-permute-done((bf16[128,512]{1,0:T(8,128)(2,1)S(1)}, bf16[128,512]{1,0:T(8,128)(2,1)S(1)}, u32[]{:S(2)}, u32[]{:S(2)}) %collective-permute-start.20) | collective-permute-done | bytes 131104 | tf_op jit(solution)/shard_map/product_pair/ppermute | solution.py:27
  (63 shorter events, 30.0 us)
Async XLA Ops:
  0.0 21.9 %collective-permute-start.2 = (bf16[4,128,512]{2,1,0:T(8,128)(2,1)}, bf16[4,128,512]{2,1,0:T(8,128)(2,1)S(1)}, u32[]{:S(2)}, u32[]{:S(2)}) collective-permute-start(bf16[4,128,512]{2,1,0:T(8,128)(2,1)} %bitcast.14), channel_id=1, source_target_pairs={{0,16},{1,17},{2,18},{3,19},{4,20},{5,21},{6,22},{7,23},{8,24},{9,... | collective-permute-start | bytes 1572872 | tf_op jit(solution)/shard_map/round0/ppermute | solution.py:27
  3.5 18.3 %collective-permute-start.3 = (bf16[4,128,512]{2,1,0:T(8,128)(2,1)}, bf16[4,128,512]{2,1,0:T(8,128)(2,1)S(1)}, u32[]{:S(2)}, u32[]{:S(2)}) collective-permute-start(bf16[4,128,512]{2,1,0:T(8,128)(2,1)} %bitcast.15), channel_id=1, source_target_pairs={{0,128},{1,129},{2,130},{3,131},{4,132},{5,133},{6,134},{7,135},{8... | collective-permute-start | bytes 1572872 | tf_op jit(solution)/shard_map/round0/ppermute | solution.py:27
  6.8 15.1 %collective-permute-start.4 = (bf16[4,128,512]{2,1,0:T(8,128)(2,1)}, bf16[4,128,512]{2,1,0:T(8,128)(2,1)S(1)}, u32[]{:S(2)}, u32[]{:S(2)}) collective-permute-start(bf16[4,128,512]{2,1,0:T(8,128)(2,1)} %bitcast.16), channel_id=1, source_target_pairs={{0,384},{1,385},{2,386},{3,387},{4,388},{5,389},{6,390},{7,391},{8... | collective-permute-start | bytes 1572872 | tf_op jit(solution)/shard_map/round0/ppermute | solution.py:27
  12.7 8.0 %collective-permute-start = (bf16[512,256]{1,0:T(8,128)(2,1)S(1)}, bf16[512,256]{1,0:T(8,128)(2,1)S(1)}, u32[]{:S(2)}, u32[]{:S(2)}) collective-permute-start(bf16[512,256]{1,0:T(8,128)(2,1)S(1)} %get-tuple-element.29), channel_id=1, source_target_pairs={{0,0},{1,1},{2,2},{3,3},{4,4},{5,5},{6,6},{7,7},{8,8},{9,9},{10,10... | collective-permute-start | bytes 786440 | tf_op jit(solution)/shard_map/round0/ppermute | solution.py:27
  15.7 6.1 %collective-permute-start.1 = (bf16[512,256]{1,0:T(8,128)(2,1)S(1)}, bf16[512,256]{1,0:T(8,128)(2,1)S(1)}, u32[]{:S(2)}, u32[]{:S(2)}) collective-permute-start(bf16[512,256]{1,0:T(8,128)(2,1)S(1)} %get-tuple-element.30), channel_id=1, source_target_pairs={{0,64},{1,65},{2,66},{3,67},{4,68},{5,69},{6,70},{7,71},{8,72},{9,... | collective-permute-start | bytes 786440 | tf_op jit(solution)/shard_map/round0/ppermute | solution.py:27
  21.9 28.6 %collective-permute-start.5 = (bf16[2,512,256]{2,1,0:T(8,128)(2,1)S(1)}, bf16[2,512,256]{2,1,0:T(8,128)(2,1)S(1)}, u32[]{:S(2)}, u32[]{:S(2)}) collective-permute-start(bf16[2,512,256]{2,1,0:T(8,128)(2,1)S(1)} %pad_maximum_fusion.4.refs_0_), channel_id=1, source_target_pairs={{0,32},{1,33},{2,34},{3,35},{4,36},{5,37},{6,38},{7,39},{8,40},{9,... | collective-permute-start | bytes 1572872 | tf_op jit(solution)/shard_map/round1/ppermute | solution.py:27
  28.6 21.9 %collective-permute-start.6 = (bf16[2,512,256]{2,1,0:T(8,128)(2,1)S(1)}, bf16[2,512,256]{2,1,0:T(8,128)(2,1)}, u32[]{:S(2)}, u32[]{:S(2)}) collective-permute-start(bf16[2,512,256]{2,1,0:T(8,128)(2,1)S(1)} %pad_maximum_fusion.4.refs_0_), channel_id=1, source_target_pairs={{0,4},{1,5},{2,6},{3,7},{4,8},{5,9},{6,10},{7,11},{8,12},{9,13},{1... | collective-permute-start | bytes 1572872 | tf_op jit(solution)/shard_map/round1/ppermute | solution.py:27
  30.5 20.0 %collective-permute-start.7 = (bf16[2,512,256]{2,1,0:T(8,128)(2,1)S(1)}, bf16[2,512,256]{2,1,0:T(8,128)(2,1)}, u32[]{:S(2)}, u32[]{:S(2)}) collective-permute-start(bf16[2,512,256]{2,1,0:T(8,128)(2,1)S(1)} %pad_maximum_fusion.4.refs_0_), channel_id=1, source_target_pairs={{0,12},{1,13},{2,14},{3,15},{4,0},{5,1},{6,2},{7,3},{8,4},{9,5},{1... | collective-permute-start | bytes 1572872 | tf_op jit(solution)/shard_map/round1/ppermute | solution.py:27
  35.9 14.6 %collective-permute-start.8 = (bf16[4,128,512]{2,1,0:T(8,128)(2,1)S(1)}, bf16[4,128,512]{2,1,0:T(8,128)(2,1)S(1)}, u32[]{:S(2)}, u32[]{:S(2)}) collective-permute-start(bf16[4,128,512]{2,1,0:T(8,128)(2,1)S(1)} %collective-permute-done.2.refs_8_), channel_id=1, source_target_pairs={{0,128},{1,129},{2,130},{3,131},{4,132},{5,133},{6,134},{7,135},{8... | collective-permute-start | bytes 1572872 | tf_op jit(solution)/shard_map/round1/ppermute | solution.py:27
  37.8 13.5 %collective-permute-start.9 = (bf16[4,128,512]{2,1,0:T(8,128)(2,1)S(1)}, bf16[4,128,512]{2,1,0:T(8,128)(2,1)S(1)}, u32[]{:S(2)}, u32[]{:S(2)}) collective-permute-start(bf16[4,128,512]{2,1,0:T(8,128)(2,1)S(1)} %collective-permute-done.2.refs_8_), channel_id=1, source_target_pairs={{0,384},{1,385},{2,386},{3,387},{4,388},{5,389},{6,390},{7,391},{8... | collective-permute-start | bytes 1572872 | tf_op jit(solution)/shard_map/round1/ppermute | solution.py:27
  53.0 37.9 %collective-permute-start.13 = (bf16[16,128,512]{2,1,0:T(8,128)(2,1)}, bf16[16,128,512]{2,1,0:T(8,128)(2,1)S(1)}, u32[]{:S(2)}, u32[]{:S(2)}) collective-permute-start(bf16[16,128,512]{2,1,0:T(8,128)(2,1)} %pad_maximum_fusion), channel_id=1, source_target_pairs={{0,64},{1,65},{2,66},{3,67},{4,68},{5,69},{6,70},{7,71},{8,72},{9,... | collective-permute-start | bytes 6291464 | tf_op jit(solution)/shard_map/round2/ppermute | solution.py:27
  59.5 31.3 %collective-permute-start.12 = (bf16[8,128,512]{2,1,0:T(8,128)(2,1)S(1)}, bf16[8,128,512]{2,1,0:T(8,128)(2,1)S(1)}, u32[]{:S(2)}, u32[]{:S(2)}) collective-permute-start(bf16[8,128,512]{2,1,0:T(8,128)(2,1)S(1)} %maximum_select_fusion), channel_id=1, source_target_pairs={{0,128},{1,129},{2,130},{3,131},{4,132},{5,133},{6,134},{7,135},{8... | collective-permute-start | bytes 3145736 | tf_op jit(solution)/shard_map/round2/ppermute | solution.py:27
  69.4 19.4 %collective-permute-start.10 = (bf16[3,512,256]{2,1,0:T(8,128)(2,1)S(1)}, bf16[3,512,256]{2,1,0:T(8,128)(2,1)S(1)}, u32[]{:S(2)}, u32[]{:S(2)}) collective-permute-start(bf16[3,512,256]{2,1,0:T(8,128)(2,1)S(1)} %get-tuple-element.54), channel_id=1, source_target_pairs={{0,4},{1,5},{2,6},{3,7},{4,8},{5,9},{6,10},{7,11},{8,12},{9,13},{1... | collective-permute-start | bytes 2359304 | tf_op jit(solution)/shard_map/round2/ppermute | solution.py:27
  71.4 32.8 %copy-start.1 = (bf16[4,128,512]{2,1,0:T(8,128)(2,1)S(1)}, bf16[4,128,512]{2,1,0:T(8,128)(2,1)}, u32[]{:S(2)}) copy-start(bf16[4,128,512]{2,1,0:T(8,128)(2,1)} %copy-done) | copy-start | bytes 1572868
  71.4 32.8 %copy-start.3 = (bf16[4,128,512]{2,1,0:T(8,128)(2,1)S(1)}, bf16[4,128,512]{2,1,0:T(8,128)(2,1)}, u32[]{:S(2)}) copy-start(bf16[4,128,512]{2,1,0:T(8,128)(2,1)} %copy-done.2) | copy-start | bytes 1572868
  71.4 19.4 %collective-permute-start.11 = (bf16[3,512,256]{2,1,0:T(8,128)(2,1)S(1)}, bf16[3,512,256]{2,1,0:T(8,128)(2,1)S(1)}, u32[]{:S(2)}, u32[]{:S(2)}) collective-permute-start(bf16[3,512,256]{2,1,0:T(8,128)(2,1)S(1)} %get-tuple-element.53), channel_id=1, source_target_pairs={{0,12},{1,13},{2,14},{3,15},{4,0},{5,1},{6,2},{7,3},{8,4},{9,5},{1... | collective-permute-start | bytes 2359304 | tf_op jit(solution)/shard_map/round2/ppermute | solution.py:27
  91.1 13.1 %collective-permute-start.15 = (bf16[16,128,512]{2,1,0:T(8,128)(2,1)S(1)}, bf16[16,128,512]{2,1,0:T(8,128)(2,1)S(1)}, u32[]{:S(2)}, u32[]{:S(2)}) collective-permute-start(bf16[16,128,512]{2,1,0:T(8,128)(2,1)S(1)} %pad_maximum_fusion.1), channel_id=1, source_target_pairs={{0,64},{1,65},{2,66},{3,67},{4,68},{5,69},{6,70},{7,71},{8,72},{9,... | collective-permute-start | bytes 6291464 | tf_op jit(solution)/shard_map/round3/ppermute | solution.py:27
  93.1 11.1 %collective-permute-start.14 = (bf16[2,512,256]{2,1,0:T(8,128)(2,1)S(1)}, bf16[2,512,256]{2,1,0:T(8,128)(2,1)S(1)}, u32[]{:S(2)}, u32[]{:S(2)}) collective-permute-start(bf16[2,512,256]{2,1,0:T(8,128)(2,1)S(1)} %slice_select_fusion), channel_id=1, source_target_pairs={{0,4},{1,5},{2,6},{3,7},{4,8},{5,9},{6,10},{7,11},{8,12},{9,13},{1... | collective-permute-start | bytes 1572872 | tf_op jit(solution)/shard_map/round3/ppermute | solution.py:27
  107.4 14.1 %collective-permute-start.16 = (s16[1040,128]{1,0:T(8,128)(2,1)S(1)}, s16[1040,128]{1,0:T(8,128)(2,1)S(1)}, u32[]{:S(2)}, u32[]{:S(2)}) collective-permute-start(s16[1040,128]{1,0:T(8,128)(2,1)S(1)} %matmul_far.1), channel_id=1, source_target_pairs={{0,1},{1,2},{2,3},{3,0},{4,5},{5,6},{6,7},{7,4},{8,9},{9,10},{10,1... | collective-permute-start | bytes 798728 | tf_op jit(solution)/shard_map/layer_far/ppermute | solution.py:27
  121.4 52.4 %copy-start.14 = (s32[2,4]{1,0:T(2,128)S(1)}, s32[2,4]{1,0:T(2,128)}, u32[]{:S(2)}) copy-start(s32[2,4]{1,0:T(2,128)} %pat_ref.1) | copy-start | bytes 100
  122.3 31.8 %collective-permute-start.17 = (s16[1040,128]{1,0:T(8,128)(2,1)S(1)}, s16[1040,128]{1,0:T(8,128)(2,1)S(1)}, u32[]{:S(2)}, u32[]{:S(2)}) collective-permute-start(s16[1040,128]{1,0:T(8,128)(2,1)S(1)} %get-tuple-element.49), channel_id=1, source_target_pairs={{0,1},{1,2},{2,3},{3,0},{4,5},{5,6},{6,7},{7,4},{8,9},{9,10},{10,1... | collective-permute-start | bytes 798728 | tf_op jit(solution)/shard_map/layer_sums/ppermute | solution.py:27
  130.1 25.7 %collective-permute-start.18 = (s16[1040,128]{1,0:T(8,128)(2,1)S(1)}, s16[1040,128]{1,0:T(8,128)(2,1)S(1)}, u32[]{:S(2)}, u32[]{:S(2)}) collective-permute-start(s16[1040,128]{1,0:T(8,128)(2,1)S(1)} %get-tuple-element.50), channel_id=1, source_target_pairs={{0,3},{1,0},{2,1},{3,2},{4,7},{5,4},{6,5},{7,6},{8,11},{9,8},{10,9... | collective-permute-start | bytes 798728 | tf_op jit(solution)/shard_map/layer_sums/ppermute | solution.py:27
  156.5 14.2 %collective-permute-start.19 = (bf16[128,512]{1,0:T(8,128)(2,1)S(1)}, bf16[128,512]{1,0:T(8,128)(2,1)S(1)}, u32[]{:S(2)}, u32[]{:S(2)}) collective-permute-start(bf16[128,512]{1,0:T(8,128)(2,1)S(1)} %get-tuple-element.51), channel_id=1, source_target_pairs={{0,0},{1,1},{2,2},{3,3},{4,4},{5,5},{6,6},{7,7},{8,8},{9,9},{10,10... | collective-permute-start | bytes 393224 | tf_op jit(solution)/shard_map/product_pair/ppermute | solution.py:27
  168.1 5.7 %collective-permute-start.20 = (bf16[128,512]{1,0:T(8,128)(2,1)S(1)}, bf16[128,512]{1,0:T(8,128)(2,1)S(1)}, u32[]{:S(2)}, u32[]{:S(2)}) collective-permute-start(bf16[128,512]{1,0:T(8,128)(2,1)S(1)} %get-tuple-element.52), channel_id=1, source_target_pairs={{0,16},{1,17},{2,18},{3,19},{4,20},{5,21},{6,22},{7,23},{8,24},{9,... | collective-permute-start | bytes 393224 | tf_op jit(solution)/shard_map/product_pair/ppermute | solution.py:27
  (12 other events, 174.6 us)

commit v12 on v11

--- a/solution.py
+++ b/solution.py
@@ -237,6 +237,31 @@
     )(pos, pattern, first, second)
 
 
+def pick_kernel(pos_ref, *refs):
+    *in_refs, o_ref = refs
+    half = len(in_refs) // 2
+    for core, group in ((0, in_refs[:half]), (1, in_refs[half:])):
+
+        @pl.when(pos_ref[1] == core)
+        def _():
+            done = 0
+            for ref in group:
+                count = min(ref.shape[0], o_ref.shape[0])
+                o_ref[pl.ds(done, count)] = ref[pl.ds(ref.shape[0] - count, count)]
+                done += count
+
+
+def pick(pos, count, *v):
+    return pl.pallas_call(
+        pick_kernel,
+        out_shape=jax.ShapeDtypeStruct((count,) + v[0].shape[1:], v[0].dtype),
+        in_specs=[pl.BlockSpec(memory_space=pltpu.SMEM)] + [pl.BlockSpec(memory_space=pltpu.VMEM)] * len(v),
+        out_specs=pl.BlockSpec(memory_space=pltpu.VMEM),
+        compiler_params=pltpu.CompilerParams(vmem_limit_bytes=8 << 20),
+        name="pick",
+    )(pos, *v)
+
+
 def shards(panel, in_pattern, slab, owner, out_pattern):
     row, col = lax.axis_index("row"), lax.axis_index("col")
     zl = col // 4
@@ -256,14 +281,13 @@
         a1p, a1m = to_x(near, 1), to_x(near, -1)
         b2p, b2m = to_y(pair, 1), to_y(pair, -1)
         far, a1p, a1m, b2p, b2m = lax.optimization_barrier((far, a1p, a1m, b2p, b2m))
-    even = row % 2 == 0
     with jax.named_scope("round2"):
         a2p, a2m = to_x(cat(a1p[:1], far), 1), to_x(cat(a1m[1:], far), -1)
-        b3 = send(jnp.where(even, cat(b1p, b2p), cat(b1m, b2m)), lambda y, c, zl, x, zh: ((y + 1 - 2 * c) % 4, c, zl, x, zh))
+        b3 = send(pick(pos, 8, b1p, b2p, b1m, b2m), lambda y, c, zl, x, zh: ((y + 1 - 2 * c) % 4, c, zl, x, zh))
         c12 = to_core(cat(b1p, b1m, b2p, b2m))
         a2p, a2m, b3, c12, late = lax.optimization_barrier((a2p, a2m, b3, c12, pair))
     with jax.named_scope("round3"):
-        a3 = send(jnp.where(even, a2p[1:], a2m[1:]), lambda y, c, zl, x, zh: (y, c, zl, (x + 1 - 2 * c) % 4, zh))
+        a3 = send(pick(pos, 2, a2p, a2m), lambda y, c, zl, x, zh: (y, c, zl, (x + 1 - 2 * c) % 4, zh))
         c03 = to_core(cat(own, late, b3))
     a = (near, a1p, a1m, far, a2p, a2m, a3)
     b = (own, pair, b1p, b1m, b2p, b2m, b3, c12, c03)

time: 176 us -> 168 us (0.955)
  local copies, waits for them, and re-layouts: 6.74 us -> 1.86 us
  other arithmetic: 4.55 us -> 0.64 us
    slice x2, local copies, waits for them, and re-layouts: 3.33 us -> 0.04 us  [shards(): a2p, a2m = (to_x(cat(a1p[:1], far), 1), to_x(cat(a1m[1:], far), -1))]
    concatenate x3, other arithmetic: 3.02 us -> 0.59 us  [shards(): cat = lambda *v: jnp.concatenate(v, axis=0)]
  transfers between devices with their start and end apart: 21 -> 21, of which waited for: 10 -> 11; matrix products, arithmetic and copies ran while one was open for 3% -> 0% of each run, Pallas kernels for 4% -> 4%
where the time goes in v12:
time: 168 us
  starting transfers between devices  95.8 us (57%)
  waiting for transfers between devices  56.7 us (34%)
  Pallas kernels  12.3 us (7%)
  local copies, waits for them, and re-layouts  1.86 us (1%)
    ppermute x21, starting transfers between devices, send(): return lax.ppermute(v, AXES, moves(f))  95.8 us
    ppermute x21, waiting for transfers between devices, send(): return lax.ppermute(v, AXES, moves(f))  56.7 us
    pallas_call x2, Pallas kernels, matmul(): pl.pallas_call(kernel, out_shape=out_shape, in_specs=[pl.BlockSpec(memory...  7.46 us
  transfers between devices with their start and end apart: 21, of which 11 were waited for; matrix products, arithmetic and copies ran while one was open for 0% of the time, Pallas kernels for 4%

profile of v12, /device:TPU:65, one launch (start us, length us, event | category | flops | bytes accessed | tf_op | source)
XLA Modules:
  0.0 167.6 jit_solution(17527112506531115608)
XLA Ops:
  0.0 3.5 %collective-permute-start.2 = (bf16[4,128,512]{2,1,0:T(8,128)(2,1)}, bf16[4,128,512]{2,1,0:T(8,128)(2,1)S(1)}, u32[]{:S(2)}, u32[]{:S(2)}) collective-permute-start(bf16[4,128,512]{2,1,0:T(8,128)(2,1)} %bitcast.14), channel_id=1, source_target_pairs={{0,16},{1,17},{2,18},{3,19},{4,20},{5,21},{6,22},{7,23},{8,24},{9,... | collective-permute-start | bytes 1572872 | tf_op jit(solution)/shard_map/round0/ppermute | solution.py:27
  3.5 3.2 %collective-permute-start.3 = (bf16[4,128,512]{2,1,0:T(8,128)(2,1)}, bf16[4,128,512]{2,1,0:T(8,128)(2,1)S(1)}, u32[]{:S(2)}, u32[]{:S(2)}) collective-permute-start(bf16[4,128,512]{2,1,0:T(8,128)(2,1)} %bitcast.15), channel_id=1, source_target_pairs={{0,128},{1,129},{2,130},{3,131},{4,132},{5,133},{6,134},{7,135},{8... | collective-permute-start | bytes 1572872 | tf_op jit(solution)/shard_map/round0/ppermute | solution.py:27
  6.8 3.4 %collective-permute-start.4 = (bf16[4,128,512]{2,1,0:T(8,128)(2,1)}, bf16[4,128,512]{2,1,0:T(8,128)(2,1)S(1)}, u32[]{:S(2)}, u32[]{:S(2)}) collective-permute-start(bf16[4,128,512]{2,1,0:T(8,128)(2,1)} %bitcast.16), channel_id=1, source_target_pairs={{0,384},{1,385},{2,386},{3,387},{4,388},{5,389},{6,390},{7,391},{8... | collective-permute-start | bytes 1572872 | tf_op jit(solution)/shard_map/round0/ppermute | solution.py:27
  12.7 3.1 %collective-permute-start = (bf16[512,256]{1,0:T(8,128)(2,1)S(1)}, bf16[512,256]{1,0:T(8,128)(2,1)S(1)}, u32[]{:S(2)}, u32[]{:S(2)}) collective-permute-start(bf16[512,256]{1,0:T(8,128)(2,1)S(1)} %get-tuple-element.29), channel_id=1, source_target_pairs={{0,0},{1,1},{2,2},{3,3},{4,4},{5,5},{6,6},{7,7},{8,8},{9,9},{10,10... | collective-permute-start | bytes 786440 | tf_op jit(solution)/shard_map/round0/ppermute | solution.py:27
  17.7 3.0 %collective-permute-done = bf16[512,256]{1,0:T(8,128)(2,1)S(1)} collective-permute-done((bf16[512,256]{1,0:T(8,128)(2,1)S(1)}, bf16[512,256]{1,0:T(8,128)(2,1)S(1)}, u32[]{:S(2)}, u32[]{:S(2)}) %collective-permute-start) | collective-permute-done | bytes 262176 | tf_op jit(solution)/shard_map/round0/ppermute | solution.py:27
  21.9 6.7 %collective-permute-start.5 = (bf16[2,512,256]{2,1,0:T(8,128)(2,1)S(1)}, bf16[2,512,256]{2,1,0:T(8,128)(2,1)S(1)}, u32[]{:S(2)}, u32[]{:S(2)}) collective-permute-start(bf16[2,512,256]{2,1,0:T(8,128)(2,1)S(1)} %pad_maximum_fusion.4.refs_0_), channel_id=1, source_target_pairs={{0,32},{1,33},{2,34},{3,35},{4,36},{5,37},{6,38},{7,39},{8,40},{9,... | collective-permute-start | bytes 1572872 | tf_op jit(solution)/shard_map/round1/ppermute | solution.py:27
  30.5 4.6 %collective-permute-start.7 = (bf16[2,512,256]{2,1,0:T(8,128)(2,1)S(1)}, bf16[2,512,256]{2,1,0:T(8,128)(2,1)S(1)}, u32[]{:S(2)}, u32[]{:S(2)}) collective-permute-start(bf16[2,512,256]{2,1,0:T(8,128)(2,1)S(1)} %pad_maximum_fusion.4.refs_0_), channel_id=1, source_target_pairs={{0,12},{1,13},{2,14},{3,15},{4,0},{5,1},{6,2},{7,3},{8,4},{9,5},{1... | collective-permute-start | bytes 1572872 | tf_op jit(solution)/shard_map/round1/ppermute | solution.py:27
  37.0 4.6 %collective-permute-start.9 = (bf16[4,128,512]{2,1,0:T(8,128)(2,1)S(1)}, bf16[4,128,512]{2,1,0:T(8,128)(2,1)S(1)}, u32[]{:S(2)}, u32[]{:S(2)}) collective-permute-start(bf16[4,128,512]{2,1,0:T(8,128)(2,1)S(1)} %collective-permute-done.2.refs_8_), channel_id=1, source_target_pairs={{0,384},{1,385},{2,386},{3,387},{4,388},{5,389},{6,390},{7,391},{8... | collective-permute-start | bytes 1572872 | tf_op jit(solution)/shard_map/round1/ppermute | solution.py:27
  41.6 8.9 %collective-permute-done.5.refs_3_ = bf16[2,512,256]{2,1,0:T(8,128)(2,1)S(1)} collective-permute-done((bf16[2,512,256]{2,1,0:T(8,128)(2,1)S(1)}, bf16[2,512,256]{2,1,0:T(8,128)(2,1)S(1)}, u32[]{:S(2)}, u32[]{:S(2)}) %collective-permute-start.5) | collective-permute-done | bytes 524320 | tf_op jit(solution)/shard_map/round1/ppermute | solution.py:27
  50.8 5.1 %collective-permute-start.13 = (bf16[16,128,512]{2,1,0:T(8,128)(2,1)S(1)}, bf16[16,128,512]{2,1,0:T(8,128)(2,1)S(1)}, u32[]{:S(2)}, u32[]{:S(2)}) collective-permute-start(bf16[16,128,512]{2,1,0:T(8,128)(2,1)S(1)} %pad_maximum_fusion), channel_id=1, source_target_pairs={{0,64},{1,65},{2,66},{3,67},{4,68},{5,69},{6,70},{7,71},{8,72},{9,... | collective-permute-start | bytes 6291464 | tf_op jit(solution)/shard_map/round2/ppermute | solution.py:27
  56.5 5.5 %collective-permute-start.12 = (bf16[8,128,512]{2,1,0:T(8,128)(2,1)S(1)}, bf16[8,128,512]{2,1,0:T(8,128)(2,1)S(1)}, u32[]{:S(2)}, u32[]{:S(2)}) collective-permute-start(bf16[8,128,512]{2,1,0:T(8,128)(2,1)S(1)} %pick.2), channel_id=1, source_target_pairs={{0,128},{1,129},{2,130},{3,131},{4,132},{5,133},{6,134},{7,135},{8... | collective-permute-start | bytes 3145736 | tf_op jit(solution)/shard_map/round2/ppermute | solution.py:27
  64.1 4.6 %collective-permute-start.11 = (bf16[3,512,256]{2,1,0:T(8,128)(2,1)S(1)}, bf16[3,512,256]{2,1,0:T(8,128)(2,1)S(1)}, u32[]{:S(2)}, u32[]{:S(2)}) collective-permute-start(bf16[3,512,256]{2,1,0:T(8,128)(2,1)S(1)} %get-tuple-element.53), channel_id=1, source_target_pairs={{0,12},{1,13},{2,14},{3,15},{4,0},{5,1},{6,2},{7,3},{8,4},{9,5},{1... | collective-permute-start | bytes 2359304 | tf_op jit(solution)/shard_map/round2/ppermute | solution.py:27
  68.7 12.9 %collective-permute-done.10.refs_0_.refs_4_ = bf16[3,512,256]{2,1,0:T(8,128)(2,1)S(1)} collective-permute-done((bf16[3,512,256]{2,1,0:T(8,128)(2,1)S(1)}, bf16[3,512,256]{2,1,0:T(8,128)(2,1)S(1)}, u32[]{:S(2)}, u32[]{:S(2)}) %collective-permute-start.10) | collective-permute-done | bytes 786464 | tf_op jit(solution)/shard_map/round2/ppermute | solution.py:27
  86.1 5.0 %collective-permute-start.14 = (bf16[2,512,256]{2,1,0:T(8,128)(2,1)S(1)}, bf16[2,512,256]{2,1,0:T(8,128)(2,1)S(1)}, u32[]{:S(2)}, u32[]{:S(2)}) collective-permute-start(bf16[2,512,256]{2,1,0:T(8,128)(2,1)S(1)} %pick.3), channel_id=1, source_target_pairs={{0,4},{1,5},{2,6},{3,7},{4,8},{5,9},{6,10},{7,11},{8,12},{9,13},{1... | collective-permute-start | bytes 1572872 | tf_op jit(solution)/shard_map/round3/ppermute | solution.py:27
  91.2 6.1 %collective-permute-done.14.refs_6_ = bf16[2,512,256]{2,1,0:T(8,128)(2,1)S(1)} collective-permute-done((bf16[2,512,256]{2,1,0:T(8,128)(2,1)S(1)}, bf16[2,512,256]{2,1,0:T(8,128)(2,1)S(1)}, u32[]{:S(2)}, u32[]{:S(2)}) %collective-permute-start.14) | collective-permute-done | bytes 524320 | tf_op jit(solution)/shard_map/round3/ppermute | solution.py:27
  97.3 2.4 %matmul_far.1 = s16[1040,128]{1,0:T(8,128)(2,1)S(1)} custom-call(s32[6]{0:T(128)S(1)} %stack.36.pos_ref, s32[32]{0:T(128)S(1)} %bitcast.21, bf16[2,512,256]{2,1,0:T(8,128)(2,1)S(1)} %pad_maximum_fusion.4.refs_0_, bf16[2,512,256]{2,1,0:T(8,128)(2,1)S(1)} %collective-permute-done.6.refs_1_, bf16[2,512,256]{2,1,0:T(8,128)(2,1)S(1)} %collective-permute-done.7.refs_2_, ...), custom_call_target="tpu_custom_call" | custom-call | flops 1073741824 | bytes 1048576 | tf_op jit(solution)/shard_map/matmul_far/pallas_call | solution.py:162
  99.7 8.3 %collective-permute-start.16 = (s16[1040,128]{1,0:T(8,128)(2,1)S(1)}, s16[1040,128]{1,0:T(8,128)(2,1)S(1)}, u32[]{:S(2)}, u32[]{:S(2)}) collective-permute-start(s16[1040,128]{1,0:T(8,128)(2,1)S(1)} %matmul_far.1), channel_id=1, source_target_pairs={{0,1},{1,2},{2,3},{3,0},{4,5},{5,6},{6,7},{7,4},{8,9},{9,10},{10,1... | collective-permute-start | bytes 798728 | tf_op jit(solution)/shard_map/layer_far/ppermute | solution.py:27
  108.0 5.0 %matmul_rest.1 = (f32[2,128,512]{2,1,0:T(8,128)S(1)}, f32[2,128,512]{2,1,0:T(8,128)S(1)}, f32[2,128,512]{2,1,0:T(8,128)S(1)}) custom-call(s32[6]{0:T(128)S(1)} %stack.36.pos_ref, s32[32]{0:T(128)S(1)} %bitcast.22, bf16[2,512,256]{2,1,0:T(8,128)(2,1)S(1)} %pad_maximum_fusion.4.refs_0_, bf16[2,512,256]{2,1,0:T(8,128)(2,1)S(1)} %collective-permute-done.6.refs_1_, ...), custom_call_target="tpu_custom_call" | custom-call | flops 3221225472 | bytes 1048576 | tf_op jit(solution)/shard_map/matmul_rest/pallas_call | solution.py:162
  114.5 8.0 %collective-permute-start.17 = (s16[1040,128]{1,0:T(8,128)(2,1)S(1)}, s16[1040,128]{1,0:T(8,128)(2,1)S(1)}, u32[]{:S(2)}, u32[]{:S(2)}) collective-permute-start(s16[1040,128]{1,0:T(8,128)(2,1)S(1)} %get-tuple-element.49), channel_id=1, source_target_pairs={{0,1},{1,2},{2,3},{3,0},{4,5},{5,6},{6,7},{7,4},{8,9},{9,10},{10,1... | collective-permute-start | bytes 798728 | tf_op jit(solution)/shard_map/layer_sums/ppermute | solution.py:27
  122.5 7.1 %collective-permute-start.18 = (s16[1040,128]{1,0:T(8,128)(2,1)S(1)}, s16[1040,128]{1,0:T(8,128)(2,1)S(1)}, u32[]{:S(2)}, u32[]{:S(2)}) collective-permute-start(s16[1040,128]{1,0:T(8,128)(2,1)S(1)} %get-tuple-element.50), channel_id=1, source_target_pairs={{0,3},{1,0},{2,1},{3,2},{4,7},{5,4},{6,5},{7,6},{8,11},{9,8},{10,9... | collective-permute-start | bytes 798728 | tf_op jit(solution)/shard_map/layer_sums/ppermute | solution.py:27
  129.6 16.9 %collective-permute-done.17.refs_0_ = s16[1040,128]{1,0:T(8,128)(2,1)S(1)} collective-permute-done((s16[1040,128]{1,0:T(8,128)(2,1)S(1)}, s16[1040,128]{1,0:T(8,128)(2,1)S(1)}, u32[]{:S(2)}, u32[]{:S(2)}) %collective-permute-start.17) | collective-permute-done | bytes 266272 | tf_op jit(solution)/shard_map/layer_sums/ppermute | solution.py:27
  148.8 11.8 %collective-permute-start.19 = (bf16[128,512]{1,0:T(8,128)(2,1)S(1)}, bf16[128,512]{1,0:T(8,128)(2,1)S(1)}, u32[]{:S(2)}, u32[]{:S(2)}) collective-permute-start(bf16[128,512]{1,0:T(8,128)(2,1)S(1)} %get-tuple-element.51), channel_id=1, source_target_pairs={{0,0},{1,1},{2,2},{3,3},{4,4},{5,5},{6,6},{7,7},{8,8},{9,9},{10,10... | collective-permute-start | bytes 393224 | tf_op jit(solution)/shard_map/product_pair/ppermute | solution.py:27
  160.6 1.9 %collective-permute-start.20 = (bf16[128,512]{1,0:T(8,128)(2,1)S(1)}, bf16[128,512]{1,0:T(8,128)(2,1)S(1)}, u32[]{:S(2)}, u32[]{:S(2)}) collective-permute-start(bf16[128,512]{1,0:T(8,128)(2,1)S(1)} %get-tuple-element.52), channel_id=1, source_target_pairs={{0,16},{1,17},{2,18},{3,19},{4,20},{5,21},{6,22},{7,23},{8,24},{9,... | collective-permute-start | bytes 393224 | tf_op jit(solution)/shard_map/product_pair/ppermute | solution.py:27
  163.2 3.1 %collective-permute-done.20.second_ref = bf16[128,512]{1,0:T(8,128)(2,1)S(1)} collective-permute-done((bf16[128,512]{1,0:T(8,128)(2,1)S(1)}, bf16[128,512]{1,0:T(8,128)(2,1)S(1)}, u32[]{:S(2)}, u32[]{:S(2)}) %collective-permute-start.20) | collective-permute-done | bytes 131104 | tf_op jit(solution)/shard_map/product_pair/ppermute | solution.py:27
  (43 shorter events, 22.8 us)
Async XLA Ops:
  0.0 21.9 %collective-permute-start.2 = (bf16[4,128,512]{2,1,0:T(8,128)(2,1)}, bf16[4,128,512]{2,1,0:T(8,128)(2,1)S(1)}, u32[]{:S(2)}, u32[]{:S(2)}) collective-permute-start(bf16[4,128,512]{2,1,0:T(8,128)(2,1)} %bitcast.14), channel_id=1, source_target_pairs={{0,16},{1,17},{2,18},{3,19},{4,20},{5,21},{6,22},{7,23},{8,24},{9,... | collective-permute-start | bytes 1572872 | tf_op jit(solution)/shard_map/round0/ppermute | solution.py:27
  3.5 18.3 %collective-permute-start.3 = (bf16[4,128,512]{2,1,0:T(8,128)(2,1)}, bf16[4,128,512]{2,1,0:T(8,128)(2,1)S(1)}, u32[]{:S(2)}, u32[]{:S(2)}) collective-permute-start(bf16[4,128,512]{2,1,0:T(8,128)(2,1)} %bitcast.15), channel_id=1, source_target_pairs={{0,128},{1,129},{2,130},{3,131},{4,132},{5,133},{6,134},{7,135},{8... | collective-permute-start | bytes 1572872 | tf_op jit(solution)/shard_map/round0/ppermute | solution.py:27
  6.8 15.1 %collective-permute-start.4 = (bf16[4,128,512]{2,1,0:T(8,128)(2,1)}, bf16[4,128,512]{2,1,0:T(8,128)(2,1)S(1)}, u32[]{:S(2)}, u32[]{:S(2)}) collective-permute-start(bf16[4,128,512]{2,1,0:T(8,128)(2,1)} %bitcast.16), channel_id=1, source_target_pairs={{0,384},{1,385},{2,386},{3,387},{4,388},{5,389},{6,390},{7,391},{8... | collective-permute-start | bytes 1572872 | tf_op jit(solution)/shard_map/round0/ppermute | solution.py:27
  12.7 8.0 %collective-permute-start = (bf16[512,256]{1,0:T(8,128)(2,1)S(1)}, bf16[512,256]{1,0:T(8,128)(2,1)S(1)}, u32[]{:S(2)}, u32[]{:S(2)}) collective-permute-start(bf16[512,256]{1,0:T(8,128)(2,1)S(1)} %get-tuple-element.29), channel_id=1, source_target_pairs={{0,0},{1,1},{2,2},{3,3},{4,4},{5,5},{6,6},{7,7},{8,8},{9,9},{10,10... | collective-permute-start | bytes 786440 | tf_op jit(solution)/shard_map/round0/ppermute | solution.py:27
  15.7 6.1 %collective-permute-start.1 = (bf16[512,256]{1,0:T(8,128)(2,1)S(1)}, bf16[512,256]{1,0:T(8,128)(2,1)S(1)}, u32[]{:S(2)}, u32[]{:S(2)}) collective-permute-start(bf16[512,256]{1,0:T(8,128)(2,1)S(1)} %get-tuple-element.30), channel_id=1, source_target_pairs={{0,64},{1,65},{2,66},{3,67},{4,68},{5,69},{6,70},{7,71},{8,72},{9,... | collective-permute-start | bytes 786440 | tf_op jit(solution)/shard_map/round0/ppermute | solution.py:27
  21.9 28.6 %collective-permute-start.5 = (bf16[2,512,256]{2,1,0:T(8,128)(2,1)S(1)}, bf16[2,512,256]{2,1,0:T(8,128)(2,1)S(1)}, u32[]{:S(2)}, u32[]{:S(2)}) collective-permute-start(bf16[2,512,256]{2,1,0:T(8,128)(2,1)S(1)} %pad_maximum_fusion.4.refs_0_), channel_id=1, source_target_pairs={{0,32},{1,33},{2,34},{3,35},{4,36},{5,37},{6,38},{7,39},{8,40},{9,... | collective-permute-start | bytes 1572872 | tf_op jit(solution)/shard_map/round1/ppermute | solution.py:27
  28.6 21.9 %collective-permute-start.6 = (bf16[2,512,256]{2,1,0:T(8,128)(2,1)S(1)}, bf16[2,512,256]{2,1,0:T(8,128)(2,1)S(1)}, u32[]{:S(2)}, u32[]{:S(2)}) collective-permute-start(bf16[2,512,256]{2,1,0:T(8,128)(2,1)S(1)} %pad_maximum_fusion.4.refs_0_), channel_id=1, source_target_pairs={{0,4},{1,5},{2,6},{3,7},{4,8},{5,9},{6,10},{7,11},{8,12},{9,13},{1... | collective-permute-start | bytes 1572872 | tf_op jit(solution)/shard_map/round1/ppermute | solution.py:27
  30.5 20.0 %collective-permute-start.7 = (bf16[2,512,256]{2,1,0:T(8,128)(2,1)S(1)}, bf16[2,512,256]{2,1,0:T(8,128)(2,1)S(1)}, u32[]{:S(2)}, u32[]{:S(2)}) collective-permute-start(bf16[2,512,256]{2,1,0:T(8,128)(2,1)S(1)} %pad_maximum_fusion.4.refs_0_), channel_id=1, source_target_pairs={{0,12},{1,13},{2,14},{3,15},{4,0},{5,1},{6,2},{7,3},{8,4},{9,5},{1... | collective-permute-start | bytes 1572872 | tf_op jit(solution)/shard_map/round1/ppermute | solution.py:27
  35.1 15.4 %collective-permute-start.8 = (bf16[4,128,512]{2,1,0:T(8,128)(2,1)S(1)}, bf16[4,128,512]{2,1,0:T(8,128)(2,1)S(1)}, u32[]{:S(2)}, u32[]{:S(2)}) collective-permute-start(bf16[4,128,512]{2,1,0:T(8,128)(2,1)S(1)} %collective-permute-done.2.refs_8_), channel_id=1, source_target_pairs={{0,128},{1,129},{2,130},{3,131},{4,132},{5,133},{6,134},{7,135},{8... | collective-permute-start | bytes 1572872 | tf_op jit(solution)/shard_map/round1/ppermute | solution.py:27
  37.0 13.5 %collective-permute-start.9 = (bf16[4,128,512]{2,1,0:T(8,128)(2,1)S(1)}, bf16[4,128,512]{2,1,0:T(8,128)(2,1)S(1)}, u32[]{:S(2)}, u32[]{:S(2)}) collective-permute-start(bf16[4,128,512]{2,1,0:T(8,128)(2,1)S(1)} %collective-permute-done.2.refs_8_), channel_id=1, source_target_pairs={{0,384},{1,385},{2,386},{3,387},{4,388},{5,389},{6,390},{7,391},{8... | collective-permute-start | bytes 1572872 | tf_op jit(solution)/shard_map/round1/ppermute | solution.py:27
  50.8 32.6 %collective-permute-start.13 = (bf16[16,128,512]{2,1,0:T(8,128)(2,1)S(1)}, bf16[16,128,512]{2,1,0:T(8,128)(2,1)S(1)}, u32[]{:S(2)}, u32[]{:S(2)}) collective-permute-start(bf16[16,128,512]{2,1,0:T(8,128)(2,1)S(1)} %pad_maximum_fusion), channel_id=1, source_target_pairs={{0,64},{1,65},{2,66},{3,67},{4,68},{5,69},{6,70},{7,71},{8,72},{9,... | collective-permute-start | bytes 6291464 | tf_op jit(solution)/shard_map/round2/ppermute | solution.py:27
  56.5 26.9 %copy-start = (bf16[1,4,128,512]{3,2,1,0:T(8,128)(2,1)S(1)}, bf16[1,4,128,512]{3,2,1,0:T(8,128)(2,1)}, u32[]{:S(2)}) copy-start(bf16[1,4,128,512]{3,2,1,0:T(8,128)(2,1)} %param.7) | copy-start | bytes 1572868
  56.5 26.8 %collective-permute-start.12 = (bf16[8,128,512]{2,1,0:T(8,128)(2,1)S(1)}, bf16[8,128,512]{2,1,0:T(8,128)(2,1)S(1)}, u32[]{:S(2)}, u32[]{:S(2)}) collective-permute-start(bf16[8,128,512]{2,1,0:T(8,128)(2,1)S(1)} %pick.2), channel_id=1, source_target_pairs={{0,128},{1,129},{2,130},{3,131},{4,132},{5,133},{6,134},{7,135},{8... | collective-permute-start | bytes 3145736 | tf_op jit(solution)/shard_map/round2/ppermute | solution.py:27
  62.2 19.4 %collective-permute-start.10 = (bf16[3,512,256]{2,1,0:T(8,128)(2,1)S(1)}, bf16[3,512,256]{2,1,0:T(8,128)(2,1)S(1)}, u32[]{:S(2)}, u32[]{:S(2)}) collective-permute-start(bf16[3,512,256]{2,1,0:T(8,128)(2,1)S(1)} %get-tuple-element.54), channel_id=1, source_target_pairs={{0,4},{1,5},{2,6},{3,7},{4,8},{5,9},{6,10},{7,11},{8,12},{9,13},{1... | collective-permute-start | bytes 2359304 | tf_op jit(solution)/shard_map/round2/ppermute | solution.py:27
  64.1 19.3 %collective-permute-start.11 = (bf16[3,512,256]{2,1,0:T(8,128)(2,1)S(1)}, bf16[3,512,256]{2,1,0:T(8,128)(2,1)S(1)}, u32[]{:S(2)}, u32[]{:S(2)}) collective-permute-start(bf16[3,512,256]{2,1,0:T(8,128)(2,1)S(1)} %get-tuple-element.53), channel_id=1, source_target_pairs={{0,12},{1,13},{2,14},{3,15},{4,0},{5,1},{6,2},{7,3},{8,4},{9,5},{1... | collective-permute-start | bytes 2359304 | tf_op jit(solution)/shard_map/round2/ppermute | solution.py:27
  83.6 13.7 %copy-start.2 = (s32[1,32]{1,0:T(1,128)S(1)}, s32[1,32]{1,0:T(1,128)}, u32[]{:S(2)}) copy-start(s32[1,32]{1,0:T(1,128)} %param.8) | copy-start | bytes 388
  83.6 13.7 %collective-permute-start.15 = (bf16[16,128,512]{2,1,0:T(8,128)(2,1)S(1)}, bf16[16,128,512]{2,1,0:T(8,128)(2,1)S(1)}, u32[]{:S(2)}, u32[]{:S(2)}) collective-permute-start(bf16[16,128,512]{2,1,0:T(8,128)(2,1)S(1)} %pad_maximum_fusion.1), channel_id=1, source_target_pairs={{0,64},{1,65},{2,66},{3,67},{4,68},{5,69},{6,70},{7,71},{8,72},{9,... | collective-permute-start | bytes 6291464 | tf_op jit(solution)/shard_map/round3/ppermute | solution.py:27
  86.1 11.1 %collective-permute-start.14 = (bf16[2,512,256]{2,1,0:T(8,128)(2,1)S(1)}, bf16[2,512,256]{2,1,0:T(8,128)(2,1)S(1)}, u32[]{:S(2)}, u32[]{:S(2)}) collective-permute-start(bf16[2,512,256]{2,1,0:T(8,128)(2,1)S(1)} %pick.3), channel_id=1, source_target_pairs={{0,4},{1,5},{2,6},{3,7},{4,8},{5,9},{6,10},{7,11},{8,12},{9,13},{1... | collective-permute-start | bytes 1572872 | tf_op jit(solution)/shard_map/round3/ppermute | solution.py:27
  99.7 13.9 %collective-permute-start.16 = (s16[1040,128]{1,0:T(8,128)(2,1)S(1)}, s16[1040,128]{1,0:T(8,128)(2,1)S(1)}, u32[]{:S(2)}, u32[]{:S(2)}) collective-permute-start(s16[1040,128]{1,0:T(8,128)(2,1)S(1)} %matmul_far.1), channel_id=1, source_target_pairs={{0,1},{1,2},{2,3},{3,0},{4,5},{5,6},{6,7},{7,4},{8,9},{9,10},{10,1... | collective-permute-start | bytes 798728 | tf_op jit(solution)/shard_map/layer_far/ppermute | solution.py:27
  113.0 53.3 %copy-start.4 = (s32[2,4]{1,0:T(2,128)S(1)}, s32[2,4]{1,0:T(2,128)}, u32[]{:S(2)}) copy-start(s32[2,4]{1,0:T(2,128)} %pat_ref.1) | copy-start | bytes 100
  114.5 32.0 %collective-permute-start.17 = (s16[1040,128]{1,0:T(8,128)(2,1)S(1)}, s16[1040,128]{1,0:T(8,128)(2,1)S(1)}, u32[]{:S(2)}, u32[]{:S(2)}) collective-permute-start(s16[1040,128]{1,0:T(8,128)(2,1)S(1)} %get-tuple-element.49), channel_id=1, source_target_pairs={{0,1},{1,2},{2,3},{3,0},{4,5},{5,6},{6,7},{7,4},{8,9},{9,10},{10,1... | collective-permute-start | bytes 798728 | tf_op jit(solution)/shard_map/layer_sums/ppermute | solution.py:27
  122.5 25.6 %collective-permute-start.18 = (s16[1040,128]{1,0:T(8,128)(2,1)S(1)}, s16[1040,128]{1,0:T(8,128)(2,1)S(1)}, u32[]{:S(2)}, u32[]{:S(2)}) collective-permute-start(s16[1040,128]{1,0:T(8,128)(2,1)S(1)} %get-tuple-element.50), channel_id=1, source_target_pairs={{0,3},{1,0},{2,1},{3,2},{4,7},{5,4},{6,5},{7,6},{8,11},{9,8},{10,9... | collective-permute-start | bytes 798728 | tf_op jit(solution)/shard_map/layer_sums/ppermute | solution.py:27
  148.8 14.4 %collective-permute-start.19 = (bf16[128,512]{1,0:T(8,128)(2,1)S(1)}, bf16[128,512]{1,0:T(8,128)(2,1)S(1)}, u32[]{:S(2)}, u32[]{:S(2)}) collective-permute-start(bf16[128,512]{1,0:T(8,128)(2,1)S(1)} %get-tuple-element.51), channel_id=1, source_target_pairs={{0,0},{1,1},{2,2},{3,3},{4,4},{5,5},{6,6},{7,7},{8,8},{9,9},{10,10... | collective-permute-start | bytes 393224 | tf_op jit(solution)/shard_map/product_pair/ppermute | solution.py:27
  160.6 5.7 %collective-permute-start.20 = (bf16[128,512]{1,0:T(8,128)(2,1)S(1)}, bf16[128,512]{1,0:T(8,128)(2,1)S(1)}, u32[]{:S(2)}, u32[]{:S(2)}) collective-permute-start(bf16[128,512]{1,0:T(8,128)(2,1)S(1)} %get-tuple-element.52), channel_id=1, source_target_pairs={{0,16},{1,17},{2,18},{3,19},{4,20},{5,21},{6,22},{7,23},{8,24},{9,... | collective-permute-start | bytes 393224 | tf_op jit(solution)/shard_map/product_pair/ppermute | solution.py:27
  (2 other events, 1.7 us)

commit v13 on v12

--- a/solution.py
+++ b/solution.py
@@ -70,9 +70,10 @@
     ((0, 0, 0), (0, 0, 1)),
     ((0, 3, 0), (0, 3, 1)),
     ((0, 1, 0), (0, 1, 1)),
+    ((0, 2, 0), (0, 2, 1)),
     ((1, 0, 0), (1, 0, 1)),
-    ((0, 2, 0), (1, 3, 0), (1, 3, 1)),
-    ((0, 2, 1), (1, 1, 0), (1, 1, 1)),
+    ((1, 3, 0), (1, 3, 1)),
+    ((1, 1, 0), (1, 1, 1)),
     ((1, 2, 0), (1, 2, 1)),
 )
 SLAB = (
@@ -93,7 +94,7 @@
     (8, 8, 4, 0, 1, 2, 0),
     (8, 12, 4, 1, 1, 2, 0),
 )
-NA, NB = 7, 9
+NA, NB = 8, 9
 
 
 def quantize(tiles, o_ref):
@@ -280,16 +281,17 @@
         far = send(near, lambda y, c, zl, x, zh: (y, c, zl ^ 2, x, zh))
         a1p, a1m = to_x(near, 1), to_x(near, -1)
         b2p, b2m = to_y(pair, 1), to_y(pair, -1)
-        far, a1p, a1m, b2p, b2m = lax.optimization_barrier((far, a1p, a1m, b2p, b2m))
+        a1h = send(pick(pos, 2, a1p, a1m), lambda y, c, zl, x, zh: (y, c, zl, (x + 1 - 2 * c) % 4, zh))
+        far, a1p, a1m, a1h, b2p, b2m = lax.optimization_barrier((far, a1p, a1m, a1h, b2p, b2m))
     with jax.named_scope("round2"):
-        a2p, a2m = to_x(cat(a1p[:1], far), 1), to_x(cat(a1m[1:], far), -1)
+        a2p, a2m = to_x(far, 1), to_x(far, -1)
         b3 = send(pick(pos, 8, b1p, b2p, b1m, b2m), lambda y, c, zl, x, zh: ((y + 1 - 2 * c) % 4, c, zl, x, zh))
         c12 = to_core(cat(b1p, b1m, b2p, b2m))
         a2p, a2m, b3, c12, late = lax.optimization_barrier((a2p, a2m, b3, c12, pair))
     with jax.named_scope("round3"):
         a3 = send(pick(pos, 2, a2p, a2m), lambda y, c, zl, x, zh: (y, c, zl, (x + 1 - 2 * c) % 4, zh))
         c03 = to_core(cat(own, late, b3))
-    a = (near, a1p, a1m, far, a2p, a2m, a3)
+    a = (near, a1p, a1m, a1h, far, a2p, a2m, a3)
     b = (own, pair, b1p, b1m, b2p, b2m, b3, c12, c03)
     far_shape = [jax.ShapeDtypeStruct((8 * BS + PAD, BS), jnp.int16)]
     rest_shape = [jax.ShapeDtypeStruct((2, BS, 4 * BS), jnp.float32)] * 3

time: 168 us -> 167 us (level)
  the two profiles are of different devices: /device:TPU:65 before, /device:TPU:87 now
where the time goes in v13:
time: 167 us; the launch traced here: 166 us
  starting transfers between devices  84.9 us (51%)
  waiting for transfers between devices  65.6 us (39%)
  Pallas kernels  12.8 us (8%)
  local copies, waits for them, and re-layouts  1.83 us (1%)
    ppermute x22, starting transfers between devices, send(): return lax.ppermute(v, AXES, moves(f))  84.9 us
    ppermute x22, waiting for transfers between devices, send(): return lax.ppermute(v, AXES, moves(f))  65.6 us
    pallas_call x2, Pallas kernels, matmul(): pl.pallas_call(kernel, out_shape=out_shape, in_specs=[pl.BlockSpec(memory...  7.46 us
  transfers between devices with their start and end apart: 22, of which 12 were waited for; matrix products, arithmetic and copies ran while one was open for 0% of the time, Pallas kernels for 5%

profile of v13, /device:TPU:87, one launch (start us, length us, event | category | flops | bytes accessed | tf_op | source)
XLA Modules:
  0.0 166.0 jit_solution(8585846502622254193)
XLA Ops:
  0.0 3.5 %collective-permute-start.2 = (bf16[4,128,512]{2,1,0:T(8,128)(2,1)}, bf16[4,128,512]{2,1,0:T(8,128)(2,1)S(1)}, u32[]{:S(2)}, u32[]{:S(2)}) collective-permute-start(bf16[4,128,512]{2,1,0:T(8,128)(2,1)} %bitcast.14), channel_id=1, source_target_pairs={{0,16},{1,17},{2,18},{3,19},{4,20},{5,21},{6,22},{7,23},{8,24},{9,... | collective-permute-start | bytes 1572872 | tf_op jit(solution)/shard_map/round0/ppermute | solution.py:27
  3.5 2.9 %collective-permute-start.3 = (bf16[4,128,512]{2,1,0:T(8,128)(2,1)}, bf16[4,128,512]{2,1,0:T(8,128)(2,1)S(1)}, u32[]{:S(2)}, u32[]{:S(2)}) collective-permute-start(bf16[4,128,512]{2,1,0:T(8,128)(2,1)} %bitcast.15), channel_id=1, source_target_pairs={{0,128},{1,129},{2,130},{3,131},{4,132},{5,133},{6,134},{7,135},{8... | collective-permute-start | bytes 1572872 | tf_op jit(solution)/shard_map/round0/ppermute | solution.py:27
  11.4 3.1 %collective-permute-start = (bf16[512,256]{1,0:T(8,128)(2,1)S(1)}, bf16[512,256]{1,0:T(8,128)(2,1)S(1)}, u32[]{:S(2)}, u32[]{:S(2)}) collective-permute-start(bf16[512,256]{1,0:T(8,128)(2,1)S(1)} %get-tuple-element.30), channel_id=1, source_target_pairs={{0,0},{1,1},{2,2},{3,3},{4,4},{5,5},{6,6},{7,7},{8,8},{9,9},{10,10... | collective-permute-start | bytes 786440 | tf_op jit(solution)/shard_map/round0/ppermute | solution.py:27
  16.5 2.9 %collective-permute-done = bf16[512,256]{1,0:T(8,128)(2,1)S(1)} collective-permute-done((bf16[512,256]{1,0:T(8,128)(2,1)S(1)}, bf16[512,256]{1,0:T(8,128)(2,1)S(1)}, u32[]{:S(2)}, u32[]{:S(2)}) %collective-permute-start) | collective-permute-done | bytes 262176 | tf_op jit(solution)/shard_map/round0/ppermute | solution.py:27
  23.3 3.2 %collective-permute-start.7 = (bf16[2,512,256]{2,1,0:T(8,128)(2,1)S(1)}, bf16[2,512,256]{2,1,0:T(8,128)(2,1)S(1)}, u32[]{:S(2)}, u32[]{:S(2)}) collective-permute-start(bf16[2,512,256]{2,1,0:T(8,128)(2,1)S(1)} %pad_maximum_fusion.2.refs_0_), channel_id=1, source_target_pairs={{0,12},{1,13},{2,14},{3,15},{4,0},{5,1},{6,2},{7,3},{8,4},{9,5},{1... | collective-permute-start | bytes 1572872 | tf_op jit(solution)/shard_map/round1/ppermute | solution.py:27
  28.4 3.5 %collective-permute-start.10 = (bf16[4,128,512]{2,1,0:T(8,128)(2,1)S(1)}, bf16[4,128,512]{2,1,0:T(8,128)(2,1)S(1)}, u32[]{:S(2)}, u32[]{:S(2)}) collective-permute-start(bf16[4,128,512]{2,1,0:T(8,128)(2,1)S(1)} %collective-permute-done.2.refs_9_), channel_id=1, source_target_pairs={{0,384},{1,385},{2,386},{3,387},{4,388},{5,389},{6,390},{7,391},{8... | collective-permute-start | bytes 1572872 | tf_op jit(solution)/shard_map/round1/ppermute | solution.py:27
  31.9 2.5 %collective-permute-start.9 = (bf16[4,128,512]{2,1,0:T(8,128)(2,1)S(1)}, bf16[4,128,512]{2,1,0:T(8,128)(2,1)S(1)}, u32[]{:S(2)}, u32[]{:S(2)}) collective-permute-start(bf16[4,128,512]{2,1,0:T(8,128)(2,1)S(1)} %collective-permute-done.2.refs_9_), channel_id=1, source_target_pairs={{0,128},{1,129},{2,130},{3,131},{4,132},{5,133},{6,134},{7,135},{8... | collective-permute-start | bytes 1572872 | tf_op jit(solution)/shard_map/round1/ppermute | solution.py:27
  34.7 3.0 %collective-permute-done.7.refs_1_.refs_2_ = bf16[2,512,256]{2,1,0:T(8,128)(2,1)S(1)} collective-permute-done((bf16[2,512,256]{2,1,0:T(8,128)(2,1)S(1)}, bf16[2,512,256]{2,1,0:T(8,128)(2,1)S(1)}, u32[]{:S(2)}, u32[]{:S(2)}) %collective-permute-start.7) | collective-permute-done | bytes 524320 | tf_op jit(solution)/shard_map/round1/ppermute | solution.py:27
  40.3 9.3 %collective-permute-done.5.refs_4_ = bf16[2,512,256]{2,1,0:T(8,128)(2,1)S(1)} collective-permute-done((bf16[2,512,256]{2,1,0:T(8,128)(2,1)S(1)}, bf16[2,512,256]{2,1,0:T(8,128)(2,1)S(1)}, u32[]{:S(2)}, u32[]{:S(2)}) %collective-permute-start.5) | collective-permute-done | bytes 524320 | tf_op jit(solution)/shard_map/round1/ppermute | solution.py:27
  49.9 4.9 %collective-permute-start.14 = (bf16[16,128,512]{2,1,0:T(8,128)(2,1)S(1)}, bf16[16,128,512]{2,1,0:T(8,128)(2,1)S(1)}, u32[]{:S(2)}, u32[]{:S(2)}) collective-permute-start(bf16[16,128,512]{2,1,0:T(8,128)(2,1)S(1)} %pad_maximum_fusion), channel_id=1, source_target_pairs={{0,64},{1,65},{2,66},{3,67},{4,68},{5,69},{6,70},{7,71},{8,72},{9,... | collective-permute-start | bytes 6291464 | tf_op jit(solution)/shard_map/round2/ppermute | solution.py:27
  55.4 2.9 %collective-permute-start.13 = (bf16[8,128,512]{2,1,0:T(8,128)(2,1)S(1)}, bf16[8,128,512]{2,1,0:T(8,128)(2,1)S(1)}, u32[]{:S(2)}, u32[]{:S(2)}) collective-permute-start(bf16[8,128,512]{2,1,0:T(8,128)(2,1)S(1)} %pick.4), channel_id=1, source_target_pairs={{0,128},{1,129},{2,130},{3,131},{4,132},{5,133},{6,134},{7,135},{8... | collective-permute-start | bytes 3145736 | tf_op jit(solution)/shard_map/round2/ppermute | solution.py:27
  58.3 4.6 %collective-permute-start.11 = (bf16[2,512,256]{2,1,0:T(8,128)(2,1)S(1)}, bf16[2,512,256]{2,1,0:T(8,128)(2,1)S(1)}, u32[]{:S(2)}, u32[]{:S(2)}) collective-permute-start(bf16[2,512,256]{2,1,0:T(8,128)(2,1)S(1)} %collective-permute-done.5.refs_4_), channel_id=1, source_target_pairs={{0,4},{1,5},{2,6},{3,7},{4,8},{5,9},{6,10},{7,11},{8,12},{9,13},{1... | collective-permute-start | bytes 1572872 | tf_op jit(solution)/shard_map/round2/ppermute | solution.py:27
  64.8 8.4 %collective-permute-done.11.refs_0_.refs_5_ = bf16[2,512,256]{2,1,0:T(8,128)(2,1)S(1)} collective-permute-done((bf16[2,512,256]{2,1,0:T(8,128)(2,1)S(1)}, bf16[2,512,256]{2,1,0:T(8,128)(2,1)S(1)}, u32[]{:S(2)}, u32[]{:S(2)}) %collective-permute-start.11) | collective-permute-done | bytes 524320 | tf_op jit(solution)/shard_map/round2/ppermute | solution.py:27
  73.2 5.0 %collective-permute-done.12.refs_1_.refs_6_ = bf16[2,512,256]{2,1,0:T(8,128)(2,1)S(1)} collective-permute-done((bf16[2,512,256]{2,1,0:T(8,128)(2,1)S(1)}, bf16[2,512,256]{2,1,0:T(8,128)(2,1)S(1)}, u32[]{:S(2)}, u32[]{:S(2)}) %collective-permute-start.12) | collective-permute-done | bytes 524320 | tf_op jit(solution)/shard_map/round2/ppermute | solution.py:27
  78.4 4.0 %collective-permute-start.16 = (bf16[16,128,512]{2,1,0:T(8,128)(2,1)S(1)}, bf16[16,128,512]{2,1,0:T(8,128)(2,1)S(1)}, u32[]{:S(2)}, u32[]{:S(2)}) collective-permute-start(bf16[16,128,512]{2,1,0:T(8,128)(2,1)S(1)} %pad_maximum_fusion.1), channel_id=1, source_target_pairs={{0,64},{1,65},{2,66},{3,67},{4,68},{5,69},{6,70},{7,71},{8,72},{9,... | collective-permute-start | bytes 6291464 | tf_op jit(solution)/shard_map/round3/ppermute | solution.py:27
  85.0 9.2 %collective-permute-done.15.refs_7_ = bf16[2,512,256]{2,1,0:T(8,128)(2,1)S(1)} collective-permute-done((bf16[2,512,256]{2,1,0:T(8,128)(2,1)S(1)}, bf16[2,512,256]{2,1,0:T(8,128)(2,1)S(1)}, u32[]{:S(2)}, u32[]{:S(2)}) %collective-permute-start.15) | collective-permute-done | bytes 524320 | tf_op jit(solution)/shard_map/round3/ppermute | solution.py:27
  96.6 8.6 %collective-permute-start.17 = (s16[1040,128]{1,0:T(8,128)(2,1)S(1)}, s16[1040,128]{1,0:T(8,128)(2,1)S(1)}, u32[]{:S(2)}, u32[]{:S(2)}) collective-permute-start(s16[1040,128]{1,0:T(8,128)(2,1)S(1)} %matmul_far.1), channel_id=1, source_target_pairs={{0,1},{1,2},{2,3},{3,0},{4,5},{5,6},{6,7},{7,4},{8,9},{9,10},{10,1... | collective-permute-start | bytes 798728 | tf_op jit(solution)/shard_map/layer_far/ppermute | solution.py:27
  105.3 5.0 %matmul_rest.1 = (f32[2,128,512]{2,1,0:T(8,128)S(1)}, f32[2,128,512]{2,1,0:T(8,128)S(1)}, f32[2,128,512]{2,1,0:T(8,128)S(1)}) custom-call(s32[6]{0:T(128)S(1)} %stack.36.pos_ref, s32[32]{0:T(128)S(1)} %bitcast.22, bf16[2,512,256]{2,1,0:T(8,128)(2,1)S(1)} %pad_maximum_fusion.2.refs_0_, bf16[2,512,256]{2,1,0:T(8,128)(2,1)S(1)} %collective-permute-done.6.refs_0_.refs_1_, ...), custom_call_target="tpu_custom_call" | custom-call | flops 3221225472 | bytes 1048576 | tf_op jit(solution)/shard_map/matmul_rest/pallas_call | solution.py:163
  111.2 4.3 %collective-permute-start.18 = (s16[1040,128]{1,0:T(8,128)(2,1)S(1)}, s16[1040,128]{1,0:T(8,128)(2,1)S(1)}, u32[]{:S(2)}, u32[]{:S(2)}) collective-permute-start(s16[1040,128]{1,0:T(8,128)(2,1)S(1)} %get-tuple-element.51), channel_id=1, source_target_pairs={{0,1},{1,2},{2,3},{3,0},{4,5},{5,6},{6,7},{7,4},{8,9},{9,10},{10,1... | collective-permute-start | bytes 798728 | tf_op jit(solution)/shard_map/layer_sums/ppermute | solution.py:27
  115.5 12.3 %collective-permute-start.19 = (s16[1040,128]{1,0:T(8,128)(2,1)S(1)}, s16[1040,128]{1,0:T(8,128)(2,1)S(1)}, u32[]{:S(2)}, u32[]{:S(2)}) collective-permute-start(s16[1040,128]{1,0:T(8,128)(2,1)S(1)} %get-tuple-element.52), channel_id=1, source_target_pairs={{0,3},{1,0},{2,1},{3,2},{4,7},{5,4},{6,5},{7,6},{8,11},{9,8},{10,9... | collective-permute-start | bytes 798728 | tf_op jit(solution)/shard_map/layer_sums/ppermute | solution.py:27
  127.8 13.3 %collective-permute-done.18.refs_0_ = s16[1040,128]{1,0:T(8,128)(2,1)S(1)} collective-permute-done((s16[1040,128]{1,0:T(8,128)(2,1)S(1)}, s16[1040,128]{1,0:T(8,128)(2,1)S(1)}, u32[]{:S(2)}, u32[]{:S(2)}) %collective-permute-start.18) | collective-permute-done | bytes 266272 | tf_op jit(solution)/shard_map/layer_sums/ppermute | solution.py:27
  141.1 8.7 %collective-permute-done.19.refs_1_ = s16[1040,128]{1,0:T(8,128)(2,1)S(1)} collective-permute-done((s16[1040,128]{1,0:T(8,128)(2,1)S(1)}, s16[1040,128]{1,0:T(8,128)(2,1)S(1)}, u32[]{:S(2)}, u32[]{:S(2)}) %collective-permute-start.19) | collective-permute-done | bytes 266272 | tf_op jit(solution)/shard_map/layer_sums/ppermute | solution.py:27
  150.5 8.5 %collective-permute-start.20 = (bf16[128,512]{1,0:T(8,128)(2,1)S(1)}, bf16[128,512]{1,0:T(8,128)(2,1)S(1)}, u32[]{:S(2)}, u32[]{:S(2)}) collective-permute-start(bf16[128,512]{1,0:T(8,128)(2,1)S(1)} %get-tuple-element.53), channel_id=1, source_target_pairs={{0,0},{1,1},{2,2},{3,3},{4,4},{5,5},{6,6},{7,7},{8,8},{9,9},{10,10... | collective-permute-start | bytes 393224 | tf_op jit(solution)/shard_map/product_pair/ppermute | solution.py:27
  161.6 3.1 %collective-permute-done.21.second_ref = bf16[128,512]{1,0:T(8,128)(2,1)S(1)} collective-permute-done((bf16[128,512]{1,0:T(8,128)(2,1)S(1)}, bf16[128,512]{1,0:T(8,128)(2,1)S(1)}, u32[]{:S(2)}, u32[]{:S(2)}) %collective-permute-start.21) | collective-permute-done | bytes 131104 | tf_op jit(solution)/shard_map/product_pair/ppermute | solution.py:27
  (43 shorter events, 28.9 us)
Async XLA Ops:
  0.0 21.1 %collective-permute-start.2 = (bf16[4,128,512]{2,1,0:T(8,128)(2,1)}, bf16[4,128,512]{2,1,0:T(8,128)(2,1)S(1)}, u32[]{:S(2)}, u32[]{:S(2)}) collective-permute-start(bf16[4,128,512]{2,1,0:T(8,128)(2,1)} %bitcast.14), channel_id=1, source_target_pairs={{0,16},{1,17},{2,18},{3,19},{4,20},{5,21},{6,22},{7,23},{8,24},{9,... | collective-permute-start | bytes 1572872 | tf_op jit(solution)/shard_map/round0/ppermute | solution.py:27
  3.5 17.6 %collective-permute-start.3 = (bf16[4,128,512]{2,1,0:T(8,128)(2,1)}, bf16[4,128,512]{2,1,0:T(8,128)(2,1)S(1)}, u32[]{:S(2)}, u32[]{:S(2)}) collective-permute-start(bf16[4,128,512]{2,1,0:T(8,128)(2,1)} %bitcast.15), channel_id=1, source_target_pairs={{0,128},{1,129},{2,130},{3,131},{4,132},{5,133},{6,134},{7,135},{8... | collective-permute-start | bytes 1572872 | tf_op jit(solution)/shard_map/round0/ppermute | solution.py:27
  6.5 14.6 %collective-permute-start.4 = (bf16[4,128,512]{2,1,0:T(8,128)(2,1)}, bf16[4,128,512]{2,1,0:T(8,128)(2,1)S(1)}, u32[]{:S(2)}, u32[]{:S(2)}) collective-permute-start(bf16[4,128,512]{2,1,0:T(8,128)(2,1)} %bitcast.16), channel_id=1, source_target_pairs={{0,384},{1,385},{2,386},{3,387},{4,388},{5,389},{6,390},{7,391},{8... | collective-permute-start | bytes 1572872 | tf_op jit(solution)/shard_map/round0/ppermute | solution.py:27
  11.4 8.0 %collective-permute-start = (bf16[512,256]{1,0:T(8,128)(2,1)S(1)}, bf16[512,256]{1,0:T(8,128)(2,1)S(1)}, u32[]{:S(2)}, u32[]{:S(2)}) collective-permute-start(bf16[512,256]{1,0:T(8,128)(2,1)S(1)} %get-tuple-element.30), channel_id=1, source_target_pairs={{0,0},{1,1},{2,2},{3,3},{4,4},{5,5},{6,6},{7,7},{8,8},{9,9},{10,10... | collective-permute-start | bytes 786440 | tf_op jit(solution)/shard_map/round0/ppermute | solution.py:27
  14.5 6.6 %collective-permute-start.1 = (bf16[512,256]{1,0:T(8,128)(2,1)S(1)}, bf16[512,256]{1,0:T(8,128)(2,1)S(1)}, u32[]{:S(2)}, u32[]{:S(2)}) collective-permute-start(bf16[512,256]{1,0:T(8,128)(2,1)S(1)} %get-tuple-element.31), channel_id=1, source_target_pairs={{0,64},{1,65},{2,66},{3,67},{4,68},{5,69},{6,70},{7,71},{8,72},{9,... | collective-permute-start | bytes 786440 | tf_op jit(solution)/shard_map/round0/ppermute | solution.py:27
  21.2 13.5 %collective-permute-start.6 = (bf16[2,512,256]{2,1,0:T(8,128)(2,1)S(1)}, bf16[2,512,256]{2,1,0:T(8,128)(2,1)S(1)}, u32[]{:S(2)}, u32[]{:S(2)}) collective-permute-start(bf16[2,512,256]{2,1,0:T(8,128)(2,1)S(1)} %pad_maximum_fusion.2.refs_0_), channel_id=1, source_target_pairs={{0,4},{1,5},{2,6},{3,7},{4,8},{5,9},{6,10},{7,11},{8,12},{9,13},{1... | collective-permute-start | bytes 1572872 | tf_op jit(solution)/shard_map/round1/ppermute | solution.py:27
  23.3 14.4 %collective-permute-start.7 = (bf16[2,512,256]{2,1,0:T(8,128)(2,1)S(1)}, bf16[2,512,256]{2,1,0:T(8,128)(2,1)S(1)}, u32[]{:S(2)}, u32[]{:S(2)}) collective-permute-start(bf16[2,512,256]{2,1,0:T(8,128)(2,1)S(1)} %pad_maximum_fusion.2.refs_0_), channel_id=1, source_target_pairs={{0,12},{1,13},{2,14},{3,15},{4,0},{5,1},{6,2},{7,3},{8,4},{9,5},{1... | collective-permute-start | bytes 1572872 | tf_op jit(solution)/shard_map/round1/ppermute | solution.py:27
  26.5 23.1 %collective-permute-start.5 = (bf16[2,512,256]{2,1,0:T(8,128)(2,1)S(1)}, bf16[2,512,256]{2,1,0:T(8,128)(2,1)S(1)}, u32[]{:S(2)}, u32[]{:S(2)}) collective-permute-start(bf16[2,512,256]{2,1,0:T(8,128)(2,1)S(1)} %pad_maximum_fusion.2.refs_0_), channel_id=1, source_target_pairs={{0,32},{1,33},{2,34},{3,35},{4,36},{5,37},{6,38},{7,39},{8,40},{9,... | collective-permute-start | bytes 1572872 | tf_op jit(solution)/shard_map/round1/ppermute | solution.py:27
  28.4 21.2 %collective-permute-start.10 = (bf16[4,128,512]{2,1,0:T(8,128)(2,1)S(1)}, bf16[4,128,512]{2,1,0:T(8,128)(2,1)S(1)}, u32[]{:S(2)}, u32[]{:S(2)}) collective-permute-start(bf16[4,128,512]{2,1,0:T(8,128)(2,1)S(1)} %collective-permute-done.2.refs_9_), channel_id=1, source_target_pairs={{0,384},{1,385},{2,386},{3,387},{4,388},{5,389},{6,390},{7,391},{8... | collective-permute-start | bytes 1572872 | tf_op jit(solution)/shard_map/round1/ppermute | solution.py:27
  31.9 17.6 %collective-permute-start.9 = (bf16[4,128,512]{2,1,0:T(8,128)(2,1)S(1)}, bf16[4,128,512]{2,1,0:T(8,128)(2,1)S(1)}, u32[]{:S(2)}, u32[]{:S(2)}) collective-permute-start(bf16[4,128,512]{2,1,0:T(8,128)(2,1)S(1)} %collective-permute-done.2.refs_9_), channel_id=1, source_target_pairs={{0,128},{1,129},{2,130},{3,131},{4,132},{5,133},{6,134},{7,135},{8... | collective-permute-start | bytes 1572872 | tf_op jit(solution)/shard_map/round1/ppermute | solution.py:27
  38.3 11.3 %collective-permute-start.8 = (bf16[2,512,256]{2,1,0:T(8,128)(2,1)S(1)}, bf16[2,512,256]{2,1,0:T(8,128)(2,1)S(1)}, u32[]{:S(2)}, u32[]{:S(2)}) collective-permute-start(bf16[2,512,256]{2,1,0:T(8,128)(2,1)S(1)} %pick.3), channel_id=1, source_target_pairs={{0,4},{1,5},{2,6},{3,7},{4,8},{5,9},{6,10},{7,11},{8,12},{9,13},{1... | collective-permute-start | bytes 1572872 | tf_op jit(solution)/shard_map/round1/ppermute | solution.py:27
  49.9 28.3 %collective-permute-start.14 = (bf16[16,128,512]{2,1,0:T(8,128)(2,1)S(1)}, bf16[16,128,512]{2,1,0:T(8,128)(2,1)S(1)}, u32[]{:S(2)}, u32[]{:S(2)}) collective-permute-start(bf16[16,128,512]{2,1,0:T(8,128)(2,1)S(1)} %pad_maximum_fusion), channel_id=1, source_target_pairs={{0,64},{1,65},{2,66},{3,67},{4,68},{5,69},{6,70},{7,71},{8,72},{9,... | collective-permute-start | bytes 6291464 | tf_op jit(solution)/shard_map/round2/ppermute | solution.py:27
  55.3 38.8 %copy-start.2 = (s32[1,32]{1,0:T(1,128)S(1)}, s32[1,32]{1,0:T(1,128)}, u32[]{:S(2)}) copy-start(s32[1,32]{1,0:T(1,128)} %param.8) | copy-start | bytes 388
  55.4 22.8 %collective-permute-start.13 = (bf16[8,128,512]{2,1,0:T(8,128)(2,1)S(1)}, bf16[8,128,512]{2,1,0:T(8,128)(2,1)S(1)}, u32[]{:S(2)}, u32[]{:S(2)}) collective-permute-start(bf16[8,128,512]{2,1,0:T(8,128)(2,1)S(1)} %pick.4), channel_id=1, source_target_pairs={{0,128},{1,129},{2,130},{3,131},{4,132},{5,133},{6,134},{7,135},{8... | collective-permute-start | bytes 3145736 | tf_op jit(solution)/shard_map/round2/ppermute | solution.py:27
  58.3 14.9 %collective-permute-start.11 = (bf16[2,512,256]{2,1,0:T(8,128)(2,1)S(1)}, bf16[2,512,256]{2,1,0:T(8,128)(2,1)S(1)}, u32[]{:S(2)}, u32[]{:S(2)}) collective-permute-start(bf16[2,512,256]{2,1,0:T(8,128)(2,1)S(1)} %collective-permute-done.5.refs_4_), channel_id=1, source_target_pairs={{0,4},{1,5},{2,6},{3,7},{4,8},{5,9},{6,10},{7,11},{8,12},{9,13},{1... | collective-permute-start | bytes 1572872 | tf_op jit(solution)/shard_map/round2/ppermute | solution.py:27
  62.9 15.3 %collective-permute-start.12 = (bf16[2,512,256]{2,1,0:T(8,128)(2,1)S(1)}, bf16[2,512,256]{2,1,0:T(8,128)(2,1)S(1)}, u32[]{:S(2)}, u32[]{:S(2)}) collective-permute-start(bf16[2,512,256]{2,1,0:T(8,128)(2,1)S(1)} %collective-permute-done.5.refs_4_), channel_id=1, source_target_pairs={{0,12},{1,13},{2,14},{3,15},{4,0},{5,1},{6,2},{7,3},{8,4},{9,5},{1... | collective-permute-start | bytes 1572872 | tf_op jit(solution)/shard_map/round2/ppermute | solution.py:27
  78.4 15.8 %collective-permute-start.16 = (bf16[16,128,512]{2,1,0:T(8,128)(2,1)S(1)}, bf16[16,128,512]{2,1,0:T(8,128)(2,1)S(1)}, u32[]{:S(2)}, u32[]{:S(2)}) collective-permute-start(bf16[16,128,512]{2,1,0:T(8,128)(2,1)S(1)} %pad_maximum_fusion.1), channel_id=1, source_target_pairs={{0,64},{1,65},{2,66},{3,67},{4,68},{5,69},{6,70},{7,71},{8,72},{9,... | collective-permute-start | bytes 6291464 | tf_op jit(solution)/shard_map/round3/ppermute | solution.py:27
  83.0 11.1 %collective-permute-start.15 = (bf16[2,512,256]{2,1,0:T(8,128)(2,1)S(1)}, bf16[2,512,256]{2,1,0:T(8,128)(2,1)S(1)}, u32[]{:S(2)}, u32[]{:S(2)}) collective-permute-start(bf16[2,512,256]{2,1,0:T(8,128)(2,1)S(1)} %pick.5), channel_id=1, source_target_pairs={{0,4},{1,5},{2,6},{3,7},{4,8},{5,9},{6,10},{7,11},{8,12},{9,13},{1... | collective-permute-start | bytes 1572872 | tf_op jit(solution)/shard_map/round3/ppermute | solution.py:27
  96.6 13.7 %collective-permute-start.17 = (s16[1040,128]{1,0:T(8,128)(2,1)S(1)}, s16[1040,128]{1,0:T(8,128)(2,1)S(1)}, u32[]{:S(2)}, u32[]{:S(2)}) collective-permute-start(s16[1040,128]{1,0:T(8,128)(2,1)S(1)} %matmul_far.1), channel_id=1, source_target_pairs={{0,1},{1,2},{2,3},{3,0},{4,5},{5,6},{6,7},{7,4},{8,9},{9,10},{10,1... | collective-permute-start | bytes 798728 | tf_op jit(solution)/shard_map/layer_far/ppermute | solution.py:27
  110.3 54.4 %copy-start.4 = (s32[2,4]{1,0:T(2,128)S(1)}, s32[2,4]{1,0:T(2,128)}, u32[]{:S(2)}) copy-start(s32[2,4]{1,0:T(2,128)} %pat_ref.1) | copy-start | bytes 100
  111.2 29.9 %collective-permute-start.18 = (s16[1040,128]{1,0:T(8,128)(2,1)S(1)}, s16[1040,128]{1,0:T(8,128)(2,1)S(1)}, u32[]{:S(2)}, u32[]{:S(2)}) collective-permute-start(s16[1040,128]{1,0:T(8,128)(2,1)S(1)} %get-tuple-element.51), channel_id=1, source_target_pairs={{0,1},{1,2},{2,3},{3,0},{4,5},{5,6},{6,7},{7,4},{8,9},{9,10},{10,1... | collective-permute-start | bytes 798728 | tf_op jit(solution)/shard_map/layer_sums/ppermute | solution.py:27
  115.5 34.3 %collective-permute-start.19 = (s16[1040,128]{1,0:T(8,128)(2,1)S(1)}, s16[1040,128]{1,0:T(8,128)(2,1)S(1)}, u32[]{:S(2)}, u32[]{:S(2)}) collective-permute-start(s16[1040,128]{1,0:T(8,128)(2,1)S(1)} %get-tuple-element.52), channel_id=1, source_target_pairs={{0,3},{1,0},{2,1},{3,2},{4,7},{5,4},{6,5},{7,6},{8,11},{9,8},{10,9... | collective-permute-start | bytes 798728 | tf_op jit(solution)/shard_map/layer_sums/ppermute | solution.py:27
  150.5 11.1 %collective-permute-start.20 = (bf16[128,512]{1,0:T(8,128)(2,1)S(1)}, bf16[128,512]{1,0:T(8,128)(2,1)S(1)}, u32[]{:S(2)}, u32[]{:S(2)}) collective-permute-start(bf16[128,512]{1,0:T(8,128)(2,1)S(1)} %get-tuple-element.53), channel_id=1, source_target_pairs={{0,0},{1,1},{2,2},{3,3},{4,4},{5,5},{6,6},{7,7},{8,8},{9,9},{10,10... | collective-permute-start | bytes 393224 | tf_op jit(solution)/shard_map/product_pair/ppermute | solution.py:27
  159.0 5.7 %collective-permute-start.21 = (bf16[128,512]{1,0:T(8,128)(2,1)S(1)}, bf16[128,512]{1,0:T(8,128)(2,1)S(1)}, u32[]{:S(2)}, u32[]{:S(2)}) collective-permute-start(bf16[128,512]{1,0:T(8,128)(2,1)S(1)} %get-tuple-element.54), channel_id=1, source_target_pairs={{0,16},{1,17},{2,18},{3,19},{4,20},{5,21},{6,22},{7,23},{8,24},{9,... | collective-permute-start | bytes 393224 | tf_op jit(solution)/shard_map/product_pair/ppermute | solution.py:27
  (3 other events, 30.1 us)

commit v14 on v13

--- a/solution.py
+++ b/solution.py
@@ -85,12 +85,12 @@
     (5, 0, 4, 1, 0, 1, 0),
     (6, 0, 4, 0, 0, 2, 0),
     (6, 4, 4, 1, 0, 2, 0),
-    (7, 0, 4, 0, 1, 3, 0),
-    (7, 4, 4, 0, 1, 1, 0),
-    (7, 8, 4, 1, 1, 3, 0),
-    (7, 12, 4, 1, 1, 1, 0),
-    (8, 0, 4, 0, 1, 0, 0),
-    (8, 4, 4, 1, 1, 0, 0),
+    (7, 0, 4, 0, 1, 0, 0),
+    (7, 4, 4, 1, 1, 0, 0),
+    (7, 8, 4, 0, 1, 3, 0),
+    (7, 12, 4, 0, 1, 1, 0),
+    (8, 0, 4, 1, 1, 3, 0),
+    (8, 4, 4, 1, 1, 1, 0),
     (8, 8, 4, 0, 1, 2, 0),
     (8, 12, 4, 1, 1, 2, 0),
 )
@@ -282,17 +282,18 @@
         a1p, a1m = to_x(near, 1), to_x(near, -1)
         b2p, b2m = to_y(pair, 1), to_y(pair, -1)
         a1h = send(pick(pos, 2, a1p, a1m), lambda y, c, zl, x, zh: (y, c, zl, (x + 1 - 2 * c) % 4, zh))
-        far, a1p, a1m, a1h, b2p, b2m = lax.optimization_barrier((far, a1p, a1m, a1h, b2p, b2m))
+        a1p, late = lax.optimization_barrier((a1p, pair))
+        c01 = to_core(cat(own, late, b1p, b1m))
+        far, a1p, a1m, a1h, c01, b2p, b2m = lax.optimization_barrier((far, a1p, a1m, a1h, c01, b2p, b2m))
     with jax.named_scope("round2"):
         a2p, a2m = to_x(far, 1), to_x(far, -1)
         b3 = send(pick(pos, 8, b1p, b2p, b1m, b2m), lambda y, c, zl, x, zh: ((y + 1 - 2 * c) % 4, c, zl, x, zh))
-        c12 = to_core(cat(b1p, b1m, b2p, b2m))
-        a2p, a2m, b3, c12, late = lax.optimization_barrier((a2p, a2m, b3, c12, pair))
+        a2p, a2m, b3 = lax.optimization_barrier((a2p, a2m, b3))
     with jax.named_scope("round3"):
         a3 = send(pick(pos, 2, a2p, a2m), lambda y, c, zl, x, zh: (y, c, zl, (x + 1 - 2 * c) % 4, zh))
-        c03 = to_core(cat(own, late, b3))
+        c23 = to_core(cat(b2p, b2m, b3))
     a = (near, a1p, a1m, a1h, far, a2p, a2m, a3)
-    b = (own, pair, b1p, b1m, b2p, b2m, b3, c12, c03)
+    b = (own, pair, b1p, b1m, b2p, b2m, b3, c01, c23)
     far_shape = [jax.ShapeDtypeStruct((8 * BS + PAD, BS), jnp.int16)]
     rest_shape = [jax.ShapeDtypeStruct((2, BS, 4 * BS), jnp.float32)] * 3
     got, = matmul(far_kernel, "matmul_far", 1, far_shape, pos, owner[0], a, b)

time: 167 us -> 184 us (1.10)
  the two profiles are of different devices: /device:TPU:87 before, /device:TPU:65 now
where the time goes in v14:
time: 184 us; the launch traced here: 183 us
  starting transfers between devices  93.6 us (51%)
  waiting for transfers between devices  72.9 us (40%)
  Pallas kernels  12.9 us (7%)
    ppermute x22, starting transfers between devices, send(): return lax.ppermute(v, AXES, moves(f))  93.6 us
    ppermute x22, waiting for transfers between devices, send(): return lax.ppermute(v, AXES, moves(f))  72.9 us
    pallas_call x2, Pallas kernels, matmul(): pl.pallas_call(kernel, out_shape=out_shape, in_specs=[pl.BlockSpec(memory...  7.5 us
  transfers between devices with their start and end apart: 22, of which 12 were waited for; matrix products, arithmetic and copies ran while one was open for 0% of the time, Pallas kernels for 4%

profile of v14, /device:TPU:65, one launch (start us, length us, event | category | flops | bytes accessed | tf_op | source)
XLA Modules:
  0.0 183.1 jit_solution(3830392442449130669)
XLA Ops:
  0.0 3.5 %collective-permute-start.2 = (bf16[4,128,512]{2,1,0:T(8,128)(2,1)}, bf16[4,128,512]{2,1,0:T(8,128)(2,1)S(1)}, u32[]{:S(2)}, u32[]{:S(2)}) collective-permute-start(bf16[4,128,512]{2,1,0:T(8,128)(2,1)} %bitcast.14), channel_id=1, source_target_pairs={{0,16},{1,17},{2,18},{3,19},{4,20},{5,21},{6,22},{7,23},{8,24},{9,... | collective-permute-start | bytes 1572872 | tf_op jit(solution)/shard_map/round0/ppermute | solution.py:27
  3.5 3.2 %collective-permute-start.3 = (bf16[4,128,512]{2,1,0:T(8,128)(2,1)}, bf16[4,128,512]{2,1,0:T(8,128)(2,1)S(1)}, u32[]{:S(2)}, u32[]{:S(2)}) collective-permute-start(bf16[4,128,512]{2,1,0:T(8,128)(2,1)} %bitcast.15), channel_id=1, source_target_pairs={{0,128},{1,129},{2,130},{3,131},{4,132},{5,133},{6,134},{7,135},{8... | collective-permute-start | bytes 1572872 | tf_op jit(solution)/shard_map/round0/ppermute | solution.py:27
  6.8 3.4 %collective-permute-start.4 = (bf16[4,128,512]{2,1,0:T(8,128)(2,1)}, bf16[4,128,512]{2,1,0:T(8,128)(2,1)S(1)}, u32[]{:S(2)}, u32[]{:S(2)}) collective-permute-start(bf16[4,128,512]{2,1,0:T(8,128)(2,1)} %bitcast.16), channel_id=1, source_target_pairs={{0,384},{1,385},{2,386},{3,387},{4,388},{5,389},{6,390},{7,391},{8... | collective-permute-start | bytes 1572872 | tf_op jit(solution)/shard_map/round0/ppermute | solution.py:27
  21.9 3.1 %collective-permute-start.6 = (bf16[2,512,256]{2,1,0:T(8,128)(2,1)S(1)}, bf16[2,512,256]{2,1,0:T(8,128)(2,1)S(1)}, u32[]{:S(2)}, u32[]{:S(2)}) collective-permute-start(bf16[2,512,256]{2,1,0:T(8,128)(2,1)S(1)} %pad_maximum_fusion.2.refs_0_), channel_id=1, source_target_pairs={{0,4},{1,5},{2,6},{3,7},{4,8},{5,9},{6,10},{7,11},{8,12},{9,13},{1... | collective-permute-start | bytes 1572872 | tf_op jit(solution)/shard_map/round1/ppermute | solution.py:27
  25.1 11.4 %collective-permute-done.6.refs_0_.refs_1_ = bf16[2,512,256]{2,1,0:T(8,128)(2,1)S(1)} collective-permute-done((bf16[2,512,256]{2,1,0:T(8,128)(2,1)S(1)}, bf16[2,512,256]{2,1,0:T(8,128)(2,1)S(1)}, u32[]{:S(2)}, u32[]{:S(2)}) %collective-permute-start.6) | collective-permute-done | bytes 524320 | tf_op jit(solution)/shard_map/round1/ppermute | solution.py:27
  37.7 4.8 %collective-permute-start.9 = (bf16[16,128,512]{2,1,0:T(8,128)(2,1)S(1)}, bf16[16,128,512]{2,1,0:T(8,128)(2,1)S(1)}, u32[]{:S(2)}, u32[]{:S(2)}) collective-permute-start(bf16[16,128,512]{2,1,0:T(8,128)(2,1)S(1)} %pad_maximum_fusion), channel_id=1, source_target_pairs={{0,64},{1,65},{2,66},{3,67},{4,68},{5,69},{6,70},{7,71},{8,72},{9,... | collective-permute-start | bytes 6291464 | tf_op jit(solution)/shard_map/round1/ppermute | solution.py:27
  42.6 3.2 %collective-permute-start.7 = (bf16[2,512,256]{2,1,0:T(8,128)(2,1)S(1)}, bf16[2,512,256]{2,1,0:T(8,128)(2,1)S(1)}, u32[]{:S(2)}, u32[]{:S(2)}) collective-permute-start(bf16[2,512,256]{2,1,0:T(8,128)(2,1)S(1)} %pad_maximum_fusion.2.refs_0_), channel_id=1, source_target_pairs={{0,12},{1,13},{2,14},{3,15},{4,0},{5,1},{6,2},{7,3},{8,4},{9,5},{1... | collective-permute-start | bytes 1572872 | tf_op jit(solution)/shard_map/round1/ppermute | solution.py:27
  45.8 5.4 %collective-permute-start.5 = (bf16[2,512,256]{2,1,0:T(8,128)(2,1)S(1)}, bf16[2,512,256]{2,1,0:T(8,128)(2,1)S(1)}, u32[]{:S(2)}, u32[]{:S(2)}) collective-permute-start(bf16[2,512,256]{2,1,0:T(8,128)(2,1)S(1)} %pad_maximum_fusion.2.refs_0_), channel_id=1, source_target_pairs={{0,32},{1,33},{2,34},{3,35},{4,36},{5,37},{6,38},{7,39},{8,40},{9,... | collective-permute-start | bytes 1572872 | tf_op jit(solution)/shard_map/round1/ppermute | solution.py:27
  53.1 4.6 %collective-permute-start.11 = (bf16[4,128,512]{2,1,0:T(8,128)(2,1)S(1)}, bf16[4,128,512]{2,1,0:T(8,128)(2,1)S(1)}, u32[]{:S(2)}, u32[]{:S(2)}) collective-permute-start(bf16[4,128,512]{2,1,0:T(8,128)(2,1)S(1)} %collective-permute-done.2.refs_9_), channel_id=1, source_target_pairs={{0,384},{1,385},{2,386},{3,387},{4,388},{5,389},{6,390},{7,391},{8... | collective-permute-start | bytes 1572872 | tf_op jit(solution)/shard_map/round1/ppermute | solution.py:27
  58.6 4.4 %collective-permute-start.8 = (bf16[2,512,256]{2,1,0:T(8,128)(2,1)S(1)}, bf16[2,512,256]{2,1,0:T(8,128)(2,1)S(1)}, u32[]{:S(2)}, u32[]{:S(2)}) collective-permute-start(bf16[2,512,256]{2,1,0:T(8,128)(2,1)S(1)} %pick.3), channel_id=1, source_target_pairs={{0,4},{1,5},{2,6},{3,7},{4,8},{5,9},{6,10},{7,11},{8,12},{9,13},{1... | collective-permute-start | bytes 1572872 | tf_op jit(solution)/shard_map/round1/ppermute | solution.py:27
  63.0 10.8 %collective-permute-done.5.refs_4_ = bf16[2,512,256]{2,1,0:T(8,128)(2,1)S(1)} collective-permute-done((bf16[2,512,256]{2,1,0:T(8,128)(2,1)S(1)}, bf16[2,512,256]{2,1,0:T(8,128)(2,1)S(1)}, u32[]{:S(2)}, u32[]{:S(2)}) %collective-permute-start.5) | collective-permute-done | bytes 524320 | tf_op jit(solution)/shard_map/round1/ppermute | solution.py:27
  76.6 3.4 %collective-permute-start.12 = (bf16[2,512,256]{2,1,0:T(8,128)(2,1)S(1)}, bf16[2,512,256]{2,1,0:T(8,128)(2,1)S(1)}, u32[]{:S(2)}, u32[]{:S(2)}) collective-permute-start(bf16[2,512,256]{2,1,0:T(8,128)(2,1)S(1)} %collective-permute-done.5.refs_4_), channel_id=1, source_target_pairs={{0,4},{1,5},{2,6},{3,7},{4,8},{5,9},{6,10},{7,11},{8,12},{9,13},{1... | collective-permute-start | bytes 1572872 | tf_op jit(solution)/shard_map/round2/ppermute | solution.py:27
  79.9 3.1 %collective-permute-start.13 = (bf16[2,512,256]{2,1,0:T(8,128)(2,1)S(1)}, bf16[2,512,256]{2,1,0:T(8,128)(2,1)S(1)}, u32[]{:S(2)}, u32[]{:S(2)}) collective-permute-start(bf16[2,512,256]{2,1,0:T(8,128)(2,1)S(1)} %collective-permute-done.5.refs_4_), channel_id=1, source_target_pairs={{0,12},{1,13},{2,14},{3,15},{4,0},{5,1},{6,2},{7,3},{8,4},{9,5},{1... | collective-permute-start | bytes 1572872 | tf_op jit(solution)/shard_map/round2/ppermute | solution.py:27
  83.1 9.4 %collective-permute-done.12.refs_0_.refs_5_ = bf16[2,512,256]{2,1,0:T(8,128)(2,1)S(1)} collective-permute-done((bf16[2,512,256]{2,1,0:T(8,128)(2,1)S(1)}, bf16[2,512,256]{2,1,0:T(8,128)(2,1)S(1)}, u32[]{:S(2)}, u32[]{:S(2)}) %collective-permute-start.12) | collective-permute-done | bytes 524320 | tf_op jit(solution)/shard_map/round2/ppermute | solution.py:27
  94.5 3.8 %collective-permute-start.16 = (bf16[16,128,512]{2,1,0:T(8,128)(2,1)S(1)}, bf16[16,128,512]{2,1,0:T(8,128)(2,1)S(1)}, u32[]{:S(2)}, u32[]{:S(2)}) collective-permute-start(bf16[16,128,512]{2,1,0:T(8,128)(2,1)S(1)} %pad_maximum_fusion.1), channel_id=1, source_target_pairs={{0,64},{1,65},{2,66},{3,67},{4,68},{5,69},{6,70},{7,71},{8,72},{9,... | collective-permute-start | bytes 6291464 | tf_op jit(solution)/shard_map/round3/ppermute | solution.py:27
  98.9 4.3 %collective-permute-start.15 = (bf16[2,512,256]{2,1,0:T(8,128)(2,1)S(1)}, bf16[2,512,256]{2,1,0:T(8,128)(2,1)S(1)}, u32[]{:S(2)}, u32[]{:S(2)}) collective-permute-start(bf16[2,512,256]{2,1,0:T(8,128)(2,1)S(1)} %pick.5), channel_id=1, source_target_pairs={{0,4},{1,5},{2,6},{3,7},{4,8},{5,9},{6,10},{7,11},{8,12},{9,13},{1... | collective-permute-start | bytes 1572872 | tf_op jit(solution)/shard_map/round3/ppermute | solution.py:27
  103.3 6.1 %collective-permute-done.15.refs_7_ = bf16[2,512,256]{2,1,0:T(8,128)(2,1)S(1)} collective-permute-done((bf16[2,512,256]{2,1,0:T(8,128)(2,1)S(1)}, bf16[2,512,256]{2,1,0:T(8,128)(2,1)S(1)}, u32[]{:S(2)}, u32[]{:S(2)}) %collective-permute-start.15) | collective-permute-done | bytes 524320 | tf_op jit(solution)/shard_map/round3/ppermute | solution.py:27
  111.8 9.4 %collective-permute-start.17 = (s16[1040,128]{1,0:T(8,128)(2,1)S(1)}, s16[1040,128]{1,0:T(8,128)(2,1)S(1)}, u32[]{:S(2)}, u32[]{:S(2)}) collective-permute-start(s16[1040,128]{1,0:T(8,128)(2,1)S(1)} %matmul_far.1), channel_id=1, source_target_pairs={{0,1},{1,2},{2,3},{3,0},{4,5},{5,6},{6,7},{7,4},{8,9},{9,10},{10,1... | collective-permute-start | bytes 798728 | tf_op jit(solution)/shard_map/layer_far/ppermute | solution.py:27
  121.3 5.0 %matmul_rest.1 = (f32[2,128,512]{2,1,0:T(8,128)S(1)}, f32[2,128,512]{2,1,0:T(8,128)S(1)}, f32[2,128,512]{2,1,0:T(8,128)S(1)}) custom-call(s32[6]{0:T(128)S(1)} %stack.36.pos_ref, s32[32]{0:T(128)S(1)} %bitcast.22, bf16[2,512,256]{2,1,0:T(8,128)(2,1)S(1)} %pad_maximum_fusion.2.refs_0_, bf16[2,512,256]{2,1,0:T(8,128)(2,1)S(1)} %collective-permute-done.6.refs_0_.refs_1_, ...), custom_call_target="tpu_custom_call" | custom-call | flops 3221225472 | bytes 1048576 | tf_op jit(solution)/shard_map/matmul_rest/pallas_call | solution.py:163
  126.3 6.6 %collective-permute-done.17.got_ref = s16[1040,128]{1,0:T(8,128)(2,1)S(1)} collective-permute-done((s16[1040,128]{1,0:T(8,128)(2,1)S(1)}, s16[1040,128]{1,0:T(8,128)(2,1)S(1)}, u32[]{:S(2)}, u32[]{:S(2)}) %collective-permute-start.17) | collective-permute-done | bytes 266272 | tf_op jit(solution)/shard_map/layer_far/ppermute | solution.py:27
  135.8 7.8 %collective-permute-start.19 = (s16[1040,128]{1,0:T(8,128)(2,1)S(1)}, s16[1040,128]{1,0:T(8,128)(2,1)S(1)}, u32[]{:S(2)}, u32[]{:S(2)}) collective-permute-start(s16[1040,128]{1,0:T(8,128)(2,1)S(1)} %get-tuple-element.54), channel_id=1, source_target_pairs={{0,3},{1,0},{2,1},{3,2},{4,7},{5,4},{6,5},{7,6},{8,11},{9,8},{10,9... | collective-permute-start | bytes 798728 | tf_op jit(solution)/shard_map/layer_sums/ppermute | solution.py:27
  143.6 18.4 %collective-permute-done.18.refs_0_ = s16[1040,128]{1,0:T(8,128)(2,1)S(1)} collective-permute-done((s16[1040,128]{1,0:T(8,128)(2,1)S(1)}, s16[1040,128]{1,0:T(8,128)(2,1)S(1)}, u32[]{:S(2)}, u32[]{:S(2)}) %collective-permute-start.18) | collective-permute-done | bytes 266272 | tf_op jit(solution)/shard_map/layer_sums/ppermute | solution.py:27
  162.8 13.3 %collective-permute-start.20 = (bf16[128,512]{1,0:T(8,128)(2,1)S(1)}, bf16[128,512]{1,0:T(8,128)(2,1)S(1)}, u32[]{:S(2)}, u32[]{:S(2)}) collective-permute-start(bf16[128,512]{1,0:T(8,128)(2,1)S(1)} %get-tuple-element.55), channel_id=1, source_target_pairs={{0,0},{1,1},{2,2},{3,3},{4,4},{5,5},{6,6},{7,7},{8,8},{9,9},{10,10... | collective-permute-start | bytes 393224 | tf_op jit(solution)/shard_map/product_pair/ppermute | solution.py:27
  178.7 3.1 %collective-permute-done.21.second_ref = bf16[128,512]{1,0:T(8,128)(2,1)S(1)} collective-permute-done((bf16[128,512]{1,0:T(8,128)(2,1)S(1)}, bf16[128,512]{1,0:T(8,128)(2,1)S(1)}, u32[]{:S(2)}, u32[]{:S(2)}) %collective-permute-start.21) | collective-permute-done | bytes 131104 | tf_op jit(solution)/shard_map/product_pair/ppermute | solution.py:27
  (43 shorter events, 31.1 us)
Async XLA Ops:
  0.0 21.9 %collective-permute-start.2 = (bf16[4,128,512]{2,1,0:T(8,128)(2,1)}, bf16[4,128,512]{2,1,0:T(8,128)(2,1)S(1)}, u32[]{:S(2)}, u32[]{:S(2)}) collective-permute-start(bf16[4,128,512]{2,1,0:T(8,128)(2,1)} %bitcast.14), channel_id=1, source_target_pairs={{0,16},{1,17},{2,18},{3,19},{4,20},{5,21},{6,22},{7,23},{8,24},{9,... | collective-permute-start | bytes 1572872 | tf_op jit(solution)/shard_map/round0/ppermute | solution.py:27
  3.5 18.3 %collective-permute-start.3 = (bf16[4,128,512]{2,1,0:T(8,128)(2,1)}, bf16[4,128,512]{2,1,0:T(8,128)(2,1)S(1)}, u32[]{:S(2)}, u32[]{:S(2)}) collective-permute-start(bf16[4,128,512]{2,1,0:T(8,128)(2,1)} %bitcast.15), channel_id=1, source_target_pairs={{0,128},{1,129},{2,130},{3,131},{4,132},{5,133},{6,134},{7,135},{8... | collective-permute-start | bytes 1572872 | tf_op jit(solution)/shard_map/round0/ppermute | solution.py:27
  6.8 15.1 %collective-permute-start.4 = (bf16[4,128,512]{2,1,0:T(8,128)(2,1)}, bf16[4,128,512]{2,1,0:T(8,128)(2,1)S(1)}, u32[]{:S(2)}, u32[]{:S(2)}) collective-permute-start(bf16[4,128,512]{2,1,0:T(8,128)(2,1)} %bitcast.16), channel_id=1, source_target_pairs={{0,384},{1,385},{2,386},{3,387},{4,388},{5,389},{6,390},{7,391},{8... | collective-permute-start | bytes 1572872 | tf_op jit(solution)/shard_map/round0/ppermute | solution.py:27
  12.7 8.0 %collective-permute-start = (bf16[512,256]{1,0:T(8,128)(2,1)S(1)}, bf16[512,256]{1,0:T(8,128)(2,1)S(1)}, u32[]{:S(2)}, u32[]{:S(2)}) collective-permute-start(bf16[512,256]{1,0:T(8,128)(2,1)S(1)} %get-tuple-element.31), channel_id=1, source_target_pairs={{0,0},{1,1},{2,2},{3,3},{4,4},{5,5},{6,6},{7,7},{8,8},{9,9},{10,10... | collective-permute-start | bytes 786440 | tf_op jit(solution)/shard_map/round0/ppermute | solution.py:27
  15.7 6.1 %collective-permute-start.1 = (bf16[512,256]{1,0:T(8,128)(2,1)S(1)}, bf16[512,256]{1,0:T(8,128)(2,1)S(1)}, u32[]{:S(2)}, u32[]{:S(2)}) collective-permute-start(bf16[512,256]{1,0:T(8,128)(2,1)S(1)} %get-tuple-element.32), channel_id=1, source_target_pairs={{0,64},{1,65},{2,66},{3,67},{4,68},{5,69},{6,70},{7,71},{8,72},{9,... | collective-permute-start | bytes 786440 | tf_op jit(solution)/shard_map/round0/ppermute | solution.py:27
  21.9 14.5 %collective-permute-start.6 = (bf16[2,512,256]{2,1,0:T(8,128)(2,1)S(1)}, bf16[2,512,256]{2,1,0:T(8,128)(2,1)S(1)}, u32[]{:S(2)}, u32[]{:S(2)}) collective-permute-start(bf16[2,512,256]{2,1,0:T(8,128)(2,1)S(1)} %pad_maximum_fusion.2.refs_0_), channel_id=1, source_target_pairs={{0,4},{1,5},{2,6},{3,7},{4,8},{5,9},{6,10},{7,11},{8,12},{9,13},{1... | collective-permute-start | bytes 1572872 | tf_op jit(solution)/shard_map/round1/ppermute | solution.py:27
  37.7 36.1 %collective-permute-start.9 = (bf16[16,128,512]{2,1,0:T(8,128)(2,1)S(1)}, bf16[16,128,512]{2,1,0:T(8,128)(2,1)S(1)}, u32[]{:S(2)}, u32[]{:S(2)}) collective-permute-start(bf16[16,128,512]{2,1,0:T(8,128)(2,1)S(1)} %pad_maximum_fusion), channel_id=1, source_target_pairs={{0,64},{1,65},{2,66},{3,67},{4,68},{5,69},{6,70},{7,71},{8,72},{9,... | collective-permute-start | bytes 6291464 | tf_op jit(solution)/shard_map/round1/ppermute | solution.py:27
  42.6 15.4 %collective-permute-start.7 = (bf16[2,512,256]{2,1,0:T(8,128)(2,1)S(1)}, bf16[2,512,256]{2,1,0:T(8,128)(2,1)S(1)}, u32[]{:S(2)}, u32[]{:S(2)}) collective-permute-start(bf16[2,512,256]{2,1,0:T(8,128)(2,1)S(1)} %pad_maximum_fusion.2.refs_0_), channel_id=1, source_target_pairs={{0,12},{1,13},{2,14},{3,15},{4,0},{5,1},{6,2},{7,3},{8,4},{9,5},{1... | collective-permute-start | bytes 1572872 | tf_op jit(solution)/shard_map/round1/ppermute | solution.py:27
  45.8 28.1 %collective-permute-start.5 = (bf16[2,512,256]{2,1,0:T(8,128)(2,1)S(1)}, bf16[2,512,256]{2,1,0:T(8,128)(2,1)S(1)}, u32[]{:S(2)}, u32[]{:S(2)}) collective-permute-start(bf16[2,512,256]{2,1,0:T(8,128)(2,1)S(1)} %pad_maximum_fusion.2.refs_0_), channel_id=1, source_target_pairs={{0,32},{1,33},{2,34},{3,35},{4,36},{5,37},{6,38},{7,39},{8,40},{9,... | collective-permute-start | bytes 1572872 | tf_op jit(solution)/shard_map/round1/ppermute | solution.py:27
  51.2 22.7 %collective-permute-start.10 = (bf16[4,128,512]{2,1,0:T(8,128)(2,1)S(1)}, bf16[4,128,512]{2,1,0:T(8,128)(2,1)S(1)}, u32[]{:S(2)}, u32[]{:S(2)}) collective-permute-start(bf16[4,128,512]{2,1,0:T(8,128)(2,1)S(1)} %collective-permute-done.2.refs_9_), channel_id=1, source_target_pairs={{0,128},{1,129},{2,130},{3,131},{4,132},{5,133},{6,134},{7,135},{8... | collective-permute-start | bytes 1572872 | tf_op jit(solution)/shard_map/round1/ppermute | solution.py:27
  53.1 20.7 %collective-permute-start.11 = (bf16[4,128,512]{2,1,0:T(8,128)(2,1)S(1)}, bf16[4,128,512]{2,1,0:T(8,128)(2,1)S(1)}, u32[]{:S(2)}, u32[]{:S(2)}) collective-permute-start(bf16[4,128,512]{2,1,0:T(8,128)(2,1)S(1)} %collective-permute-done.2.refs_9_), channel_id=1, source_target_pairs={{0,384},{1,385},{2,386},{3,387},{4,388},{5,389},{6,390},{7,391},{8... | collective-permute-start | bytes 1572872 | tf_op jit(solution)/shard_map/round1/ppermute | solution.py:27
  58.6 15.2 %collective-permute-start.8 = (bf16[2,512,256]{2,1,0:T(8,128)(2,1)S(1)}, bf16[2,512,256]{2,1,0:T(8,128)(2,1)S(1)}, u32[]{:S(2)}, u32[]{:S(2)}) collective-permute-start(bf16[2,512,256]{2,1,0:T(8,128)(2,1)S(1)} %pick.3), channel_id=1, source_target_pairs={{0,4},{1,5},{2,6},{3,7},{4,8},{5,9},{6,10},{7,11},{8,12},{9,13},{1... | collective-permute-start | bytes 1572872 | tf_op jit(solution)/shard_map/round1/ppermute | solution.py:27
  74.5 34.9 %copy-start = (bf16[1,4,128,512]{3,2,1,0:T(8,128)(2,1)S(1)}, bf16[1,4,128,512]{3,2,1,0:T(8,128)(2,1)}, u32[]{:S(2)}) copy-start(bf16[1,4,128,512]{3,2,1,0:T(8,128)(2,1)} %param.7) | copy-start | bytes 1572868
  74.5 19.8 %collective-permute-start.14 = (bf16[8,128,512]{2,1,0:T(8,128)(2,1)S(1)}, bf16[8,128,512]{2,1,0:T(8,128)(2,1)S(1)}, u32[]{:S(2)}, u32[]{:S(2)}) collective-permute-start(bf16[8,128,512]{2,1,0:T(8,128)(2,1)S(1)} %pick.4), channel_id=1, source_target_pairs={{0,128},{1,129},{2,130},{3,131},{4,132},{5,133},{6,134},{7,135},{8... | collective-permute-start | bytes 3145736 | tf_op jit(solution)/shard_map/round2/ppermute | solution.py:27
  76.6 15.9 %collective-permute-start.12 = (bf16[2,512,256]{2,1,0:T(8,128)(2,1)S(1)}, bf16[2,512,256]{2,1,0:T(8,128)(2,1)S(1)}, u32[]{:S(2)}, u32[]{:S(2)}) collective-permute-start(bf16[2,512,256]{2,1,0:T(8,128)(2,1)S(1)} %collective-permute-done.5.refs_4_), channel_id=1, source_target_pairs={{0,4},{1,5},{2,6},{3,7},{4,8},{5,9},{6,10},{7,11},{8,12},{9,13},{1... | collective-permute-start | bytes 1572872 | tf_op jit(solution)/shard_map/round2/ppermute | solution.py:27
  79.9 14.3 %collective-permute-start.13 = (bf16[2,512,256]{2,1,0:T(8,128)(2,1)S(1)}, bf16[2,512,256]{2,1,0:T(8,128)(2,1)S(1)}, u32[]{:S(2)}, u32[]{:S(2)}) collective-permute-start(bf16[2,512,256]{2,1,0:T(8,128)(2,1)S(1)} %collective-permute-done.5.refs_4_), channel_id=1, source_target_pairs={{0,12},{1,13},{2,14},{3,15},{4,0},{5,1},{6,2},{7,3},{8,4},{9,5},{1... | collective-permute-start | bytes 1572872 | tf_op jit(solution)/shard_map/round2/ppermute | solution.py:27
  94.5 14.9 %collective-permute-start.16 = (bf16[16,128,512]{2,1,0:T(8,128)(2,1)S(1)}, bf16[16,128,512]{2,1,0:T(8,128)(2,1)S(1)}, u32[]{:S(2)}, u32[]{:S(2)}) collective-permute-start(bf16[16,128,512]{2,1,0:T(8,128)(2,1)S(1)} %pad_maximum_fusion.1), channel_id=1, source_target_pairs={{0,64},{1,65},{2,66},{3,67},{4,68},{5,69},{6,70},{7,71},{8,72},{9,... | collective-permute-start | bytes 6291464 | tf_op jit(solution)/shard_map/round3/ppermute | solution.py:27
  98.9 10.5 %collective-permute-start.15 = (bf16[2,512,256]{2,1,0:T(8,128)(2,1)S(1)}, bf16[2,512,256]{2,1,0:T(8,128)(2,1)S(1)}, u32[]{:S(2)}, u32[]{:S(2)}) collective-permute-start(bf16[2,512,256]{2,1,0:T(8,128)(2,1)S(1)} %pick.5), channel_id=1, source_target_pairs={{0,4},{1,5},{2,6},{3,7},{4,8},{5,9},{6,10},{7,11},{8,12},{9,13},{1... | collective-permute-start | bytes 1572872 | tf_op jit(solution)/shard_map/round3/ppermute | solution.py:27
  111.8 21.1 %collective-permute-start.17 = (s16[1040,128]{1,0:T(8,128)(2,1)S(1)}, s16[1040,128]{1,0:T(8,128)(2,1)S(1)}, u32[]{:S(2)}, u32[]{:S(2)}) collective-permute-start(s16[1040,128]{1,0:T(8,128)(2,1)S(1)} %matmul_far.1), channel_id=1, source_target_pairs={{0,1},{1,2},{2,3},{3,0},{4,5},{5,6},{6,7},{7,4},{8,9},{9,10},{10,1... | collective-permute-start | bytes 798728 | tf_op jit(solution)/shard_map/layer_far/ppermute | solution.py:27
  126.3 55.5 %copy-start.4 = (s32[2,4]{1,0:T(2,128)S(1)}, s32[2,4]{1,0:T(2,128)}, u32[]{:S(2)}) copy-start(s32[2,4]{1,0:T(2,128)} %pat_ref.1) | copy-start | bytes 100
  133.9 28.2 %collective-permute-start.18 = (s16[1040,128]{1,0:T(8,128)(2,1)S(1)}, s16[1040,128]{1,0:T(8,128)(2,1)S(1)}, u32[]{:S(2)}, u32[]{:S(2)}) collective-permute-start(s16[1040,128]{1,0:T(8,128)(2,1)S(1)} %get-tuple-element.53), channel_id=1, source_target_pairs={{0,1},{1,2},{2,3},{3,0},{4,5},{5,6},{6,7},{7,4},{8,9},{9,10},{10,1... | collective-permute-start | bytes 798728 | tf_op jit(solution)/shard_map/layer_sums/ppermute | solution.py:27
  135.8 26.2 %collective-permute-start.19 = (s16[1040,128]{1,0:T(8,128)(2,1)S(1)}, s16[1040,128]{1,0:T(8,128)(2,1)S(1)}, u32[]{:S(2)}, u32[]{:S(2)}) collective-permute-start(s16[1040,128]{1,0:T(8,128)(2,1)S(1)} %get-tuple-element.54), channel_id=1, source_target_pairs={{0,3},{1,0},{2,1},{3,2},{4,7},{5,4},{6,5},{7,6},{8,11},{9,8},{10,9... | collective-permute-start | bytes 798728 | tf_op jit(solution)/shard_map/layer_sums/ppermute | solution.py:27
  162.8 15.9 %collective-permute-start.20 = (bf16[128,512]{1,0:T(8,128)(2,1)S(1)}, bf16[128,512]{1,0:T(8,128)(2,1)S(1)}, u32[]{:S(2)}, u32[]{:S(2)}) collective-permute-start(bf16[128,512]{1,0:T(8,128)(2,1)S(1)} %get-tuple-element.55), channel_id=1, source_target_pairs={{0,0},{1,1},{2,2},{3,3},{4,4},{5,5},{6,6},{7,7},{8,8},{9,9},{10,10... | collective-permute-start | bytes 393224 | tf_op jit(solution)/shard_map/product_pair/ppermute | solution.py:27
  176.1 5.7 %collective-permute-start.21 = (bf16[128,512]{1,0:T(8,128)(2,1)S(1)}, bf16[128,512]{1,0:T(8,128)(2,1)S(1)}, u32[]{:S(2)}, u32[]{:S(2)}) collective-permute-start(bf16[128,512]{1,0:T(8,128)(2,1)S(1)} %get-tuple-element.56), channel_id=1, source_target_pairs={{0,16},{1,17},{2,18},{3,19},{4,20},{5,21},{6,22},{7,23},{8,24},{9,... | collective-permute-start | bytes 393224 | tf_op jit(solution)/shard_map/product_pair/ppermute | solution.py:27
  (3 other events, 36.6 us)
